TPU v7x, 128 devices: a whole 4x4x4 slice. The times are simulated.
128 devices in a mesh: dp: 64 (over z, y, x_hi, core), tower: 2 (over x_lo).
Axes of the slice: x: 4 (x_hi: 2, x_lo: 2; x = x_hi * 2 + x_lo), y: 4, z: 4, core: 2. Of those that a mesh axis runs over, the one named last changes fastest.
Arguments:
- img_feats: bfloat16 [8192, 1152], P('dp'), may hold values from -8 to 8
- txt_feats: bfloat16 [8192, 1152], P('dp'), may hold values from -8 to 8
- img_proj: bfloat16 [1152, 1152], P(None, 'tower'), may hold values from -1 to 1
- txt_proj: bfloat16 [1152, 1152], P(None, 'tower'), may hold values from -1 to 1
Outputs:
- img_proj_grad: float32 [1152, 1152], P('dp', 'tower')
- txt_proj_grad: float32 [1152, 1152], P('dp', 'tower')
All inputs are finite; a program needn't handle non-finite values.
Results may differ from a plain program's by a relative error of at most 0.004.
Values may be sent and summed in bfloat16 or wider, within the bound.
No kernel may reach another device: no remote copies, remote signals or barrier semaphores. Data moves between devices by JAX's collectives and lax.ppermute only.
A program may use at most 64 MiB of HBM per device.

v0:
```python
import jax
import jax.numpy as jnp
from jax import lax
from jax.sharding import PartitionSpec as P

logit_scale = 10.0
logit_bias = -10.0
norm_eps = 1e-06


def from_behind(value, axis, by):
    size = lax.axis_size(axis)
    return lax.ppermute(value, axis, [(i, (i + by) % size) for i in range(size)])


def normalize(raw):
    wide = raw.astype(jnp.float32)
    norm = jnp.sqrt(jnp.sum(wide * wide, axis=1, keepdims=True) + norm_eps)
    unit = wide / norm
    return (unit.astype(jnp.bfloat16), unit, norm)


def pair_coef(block_img, block_txt, positive):
    logits = (
        logit_scale
        * lax.dot_general(
            block_img, block_txt, (((1,), (1,)), ((), ())), preferred_element_type=jnp.float32
        )
        + logit_bias
    )
    label = 2.0 * positive - 1.0
    return (-logit_scale * label * jax.nn.sigmoid(-label * logits)).astype(jnp.bfloat16)


def advance_text(block, stride):
    return from_behind(block, "dp", stride)


def advance_image(block, stride):
    return from_behind(block, "dp", stride)


def local(img_feats, txt_feats, img_proj, txt_proj):
    rows = img_feats.shape[0]
    ndp = lax.axis_size("dp")
    ntower = lax.axis_size("tower")
    dp_id = lax.axis_index("dp")
    tower_id = lax.axis_index("tower")
    img_half = jnp.dot(img_feats, img_proj, preferred_element_type=jnp.float32).astype(jnp.bfloat16)
    txt_half = jnp.dot(txt_feats, txt_proj, preferred_element_type=jnp.float32).astype(jnp.bfloat16)
    img_raw, txt_raw = (
        lax.all_gather(img_half, "tower", axis=1, tiled=True),
        lax.all_gather(txt_half, "tower", axis=1, tiled=True),
    )
    img_emb, img_unit, img_norm = normalize(img_raw)
    txt_emb, txt_unit, txt_norm = normalize(txt_raw)
    emb = img_emb.shape[1]
    counter = lax.broadcasted_iota(jnp.int32, (rows, rows), 0)
    diagonal = (counter == lax.broadcasted_iota(jnp.int32, (rows, rows), 1)).astype(jnp.float32)
    direction = 1
    text_first = from_behind(txt_emb, "dp", 1)
    text_start = jnp.where(tower_id == 1, text_first, txt_emb)
    image_first = from_behind(img_emb, "dp", direction)
    image_start = jnp.where(tower_id == 1, image_first, img_emb)
    turns = ndp // (2 * ntower)
    empty = jnp.zeros((rows, emb), jnp.float32)

    def image_side(total, block, visit):
        positive = diagonal * (visit == dp_id).astype(jnp.float32)
        coef = pair_coef(img_emb, block, positive)
        return total + jnp.dot(coef, block, preferred_element_type=jnp.float32)

    def text_side(total, block, visit):
        positive = diagonal * (visit == dp_id).astype(jnp.float32)
        coef = pair_coef(block, txt_emb, positive)
        return total + lax.dot_general(
            coef, block, (((0,), (0,)), ((), ())), preferred_element_type=jnp.float32
        )

    def text_visit(step):
        return (dp_id - tower_id - ntower * step) % ndp

    def image_visit(step):
        return (dp_id - direction * (tower_id + ntower * step)) % ndp

    def text_turn(turn, state):
        block, total = state
        for sub in range(2):
            total = image_side(total, block, text_visit(2 * turn + sub))
            block = advance_text(block, ntower)
        return (block, total)

    def image_turn(turn, state):
        block, total = state
        for sub in range(2):
            total = text_side(total, block, image_visit(2 * turn + sub))
            block = advance_image(block, direction * ntower)
        return (block, total)

    img_dir = lax.fori_loop(0, turns, text_turn, (text_start, empty))[1]
    txt_dir = lax.fori_loop(0, turns, image_turn, (image_start, empty))[1]
    width = emb // ntower
    start = tower_id * width
    img_full, txt_full = lax.psum((img_dir, txt_dir), "tower")
    img_inner = jnp.sum(img_unit * img_full, axis=1, keepdims=True)
    txt_inner = jnp.sum(txt_unit * txt_full, axis=1, keepdims=True)
    img_share = lax.dynamic_slice_in_dim(img_full, start, width, 1)
    txt_share = lax.dynamic_slice_in_dim(txt_full, start, width, 1)
    img_unit_share = lax.dynamic_slice_in_dim(img_unit, start, width, 1)
    txt_unit_share = lax.dynamic_slice_in_dim(txt_unit, start, width, 1)
    img_raw_grad = ((img_share - img_unit_share * img_inner) / img_norm).astype(jnp.bfloat16)
    txt_raw_grad = ((txt_share - txt_unit_share * txt_inner) / txt_norm).astype(jnp.bfloat16)
    img_terms = lax.dot_general(
        img_feats, img_raw_grad, (((0,), (0,)), ((), ())), preferred_element_type=jnp.float32
    )
    txt_terms = lax.dot_general(
        txt_feats, txt_raw_grad, (((0,), (0,)), ((), ())), preferred_element_type=jnp.float32
    )
    img_proj_grad, txt_proj_grad = (
        lax.psum_scatter(img_terms, "dp", scatter_dimension=0, tiled=True),
        lax.psum_scatter(txt_terms, "dp", scatter_dimension=0, tiled=True),
    )
    return (img_proj_grad, txt_proj_grad)


def solution(mesh):
    return jax.shard_map(
        local,
        mesh=mesh,
        in_specs=(P("dp", None), P("dp", None), P(None, "tower"), P(None, "tower")),
        out_specs=(P("dp", "tower"), P("dp", "tower")),
        check_vma=False,
    )
```

profile of v0, /device:TPU:1, one launch (start us, length us, event | category | flops | bytes accessed | tf_op | source)
XLA Modules:
  0.0 1612.7 jit_solution(10580421362990573971)
XLA Ops:
  33.0 389.6 %while.40 = (s32[]{:T(128)}, bf16[128,1152]{1,0:T(8,128)(2,1)S(1)}, f32[128,1152]{1,0:T(8,128)}, s32[]{:T(128)}, s32[]{:T(128)}, /*index=5*/bf16[128,1152]{1,0:T...) while((s32[]{:T(128)}, bf16[128,1152]{1,0:T(8,128)(2,1)S(1)}, ...), condition=%wide.region_3.4_spmd.clone.clone, body=%wide.region_2.3_spmd.clone.clone.sunk | while | flops 151896080 | bytes 6488597 | solution.py:100
  35.7 11.2 collective-permute-done
  48.8 10.9 collective-permute-done.1
  59.9 11.9 collective-permute-done
  83.3 11.3 collective-permute-done
  106.0 11.3 collective-permute-done
  128.7 11.3 collective-permute-done
  152.6 13.5 collective-permute-done
  169.1 11.4 collective-permute-done.1
  180.7 13.6 collective-permute-done
  207.0 11.8 collective-permute-done
  230.2 11.3 collective-permute-done
  252.9 11.3 collective-permute-done
  275.6 11.5 collective-permute-done
  299.9 13.7 collective-permute-done
  316.6 11.4 collective-permute-done.1
  328.1 13.5 collective-permute-done
  354.3 11.6 collective-permute-done
  377.3 11.3 collective-permute-done
  400.0 11.3 collective-permute-done
  426.7 408.0 %while.41 = (s32[]{:T(128)}, bf16[128,1152]{1,0:T(8,128)(2,1)}, f32[128,1152]{1,0:T(8,128)S(1)}, s32[]{:T(128)}, s32[]{:T(128)}, /*index=5*/bf16[128,1152]{1,0:T...) while((s32[]{:T(128)}, bf16[128,1152]{1,0:T(8,128)(2,1)}, ...), condition=%wide.region_8.9_spmd.clone.clone, body=%wide.region_7.8_spmd.clone.clone.sunk | while | flops 151896080 | bytes 6488621 | solution.py:101
  427.7 11.3 collective-permute-done.2
  451.4 11.3 collective-permute-done.2
  463.9 13.0 collective-permute-done.3
  477.9 14.5 collective-permute-done.2
  493.6 11.6 collective-permute-done.3
  506.2 13.0 collective-permute-done.2
  531.6 11.3 collective-permute-done.2
  555.3 11.3 collective-permute-done.2
  578.9 11.3 collective-permute-done.2
  591.5 10.4 collective-permute-done.3
  602.8 12.6 collective-permute-done.2
  616.6 12.5 collective-permute-done.3
  630.1 14.4 collective-permute-done.2
  645.8 12.4 collective-permute-done.3
  659.2 12.6 collective-permute-done.2
  673.1 10.6 collective-permute-done.3
  684.6 11.3 collective-permute-done.2
  708.3 11.3 collective-permute-done.2
  732.0 11.3 collective-permute-done.2
  744.5 10.5 collective-permute-done.3
  756.0 11.6 collective-permute-done.2
  768.9 12.6 collective-permute-done.3
  782.5 13.9 collective-permute-done.2
  797.7 11.7 collective-permute-done.3
  810.3 13.1 collective-permute-done.2
  835.9 113.8 %all-reduce.9.cloned.1.call-done = (f32[128,1152]{0,1:T(8,128)}, f32[128,1152]{0,1:T(8,128)}) async-done(((f32[128,1152]{0,1:T(8,128)}, f32[128,1152]{0,1:T(8,128)}), (f32[128,1152]{0,1:T(8,128)}, f32[128,1152]{0,1:T(8,128)})) %all-reduce.9.cloned.1.call-update) | async-done | bytes 1179664 | tf_op jit(solution)/shard_map/psum | solution.py:104
  957.4 644.5 %all-reduce.7.cloned.1.call-done = (f32[1152,576]{0,1:T(8,128)}, f32[1152,576]{0,1:T(8,128)}) async-done(((f32[1152,576]{0,1:T(8,128)}, f32[1152,576]{0,1:T(8,128)}), (f32[1152,576]{0,1:T(8,128)}, f32[1152,576]{0,1:T(8,128)})) %all-reduce.7.cloned.1.call-update) | async-done | bytes 5308432
  (238 shorter events, 311.5 us)
Async XLA Ops:
  7.2 942.5 %all-reduce.9.cloned.1.call-start = ((), (), s32[]{:S(2)}) async-start(), calls=%async_computation.1 | async-start | bytes 2359296 | tf_op jit(solution)/shard_map/psum | solution.py:104
  16.7 15.9 collective-permute-start.4
  30.2 394.6 %collective-permute-start.5 = (bf16[128,1152]{0,1:T(8,128)(2,1)}, bf16[128,1152]{0,1:T(8,128)(2,1)}, u32[]{:S(2)}, u32[]{:S(2)}) collective-permute-start(bf16[128,1152]{0,1:T(8,128)(2,1)} %fusion.117), channel_id=1, source_target_pairs={{0,2},{2,4},{4,6},{6,8},{8,10},{10,12},{12,14},{14,16},{16,18},{18... | collective-permute-start | bytes 884744 | tf_op jit(solution)/shard_map/ppermute | solution.py:13
  33.0 13.9 collective-permute-start
  46.9 12.9 collective-permute-start.1
  59.8 12.1 collective-permute-start
  83.2 11.4 collective-permute-start
  105.9 11.4 collective-permute-start
  128.6 11.4 collective-permute-start
  139.9 12.5 collective-permute-start.1
  152.5 13.6 collective-permute-start
  166.1 14.4 collective-permute-start.1
  180.5 13.7 collective-permute-start
  194.3 12.6 collective-permute-start.1
  206.9 11.9 collective-permute-start
  230.1 11.4 collective-permute-start
  275.5 11.6 collective-permute-start
  287.1 12.6 collective-permute-start.1
  299.8 13.8 collective-permute-start
  313.6 14.4 collective-permute-start.1
  328.0 13.6 collective-permute-start
  341.6 12.6 collective-permute-start.1
  354.2 11.7 collective-permute-start
  439.0 11.4 collective-permute-start.3
  462.7 14.3 collective-permute-start.3
  477.9 14.5 collective-permute-start.2
  492.4 12.9 collective-permute-start.3
  506.2 13.0 collective-permute-start.2
  519.2 11.4 collective-permute-start.3
  542.9 11.4 collective-permute-start.3
  566.5 11.4 collective-permute-start.3
  590.2 11.6 collective-permute-start.3
  602.8 12.6 collective-permute-start.2
  615.4 13.8 collective-permute-start.3
  630.1 14.4 collective-permute-start.2
  644.6 13.7 collective-permute-start.3
  659.2 12.7 collective-permute-start.2
  671.8 11.8 collective-permute-start.3
  695.9 11.4 collective-permute-start.3
  719.6 11.4 collective-permute-start.3
  743.3 11.7 collective-permute-start.3
  756.0 11.6 collective-permute-start.2
  767.6 13.9 collective-permute-start.3
  782.5 13.9 collective-permute-start.2
  796.4 12.9 collective-permute-start.3
  810.3 13.1 collective-permute-start.2
  823.4 11.4 collective-permute-start.3
  835.9 766.0 %all-reduce.7.cloned.1.call-start = ((), (), s32[]{:S(2)}) async-start(), calls=%async_computation | async-start | bytes 10616832
  (31 other events, 405.5 us)
Sparse Core Ops, SparseCore 0:
  836.0 113.6 all-reduce.8
  955.7 646.1 all-reduce.6
where the time goes:
time: 1620 us; the launch traced here: 1610 us
  waiting for transfers between devices  1470 us (91%)
  matrix products  72 us (4%)
  local copies, waits for them, and re-layouts  28.9 us (2%)
    ppermute x66, waiting for transfers between devices, from_behind(): lax.ppermute(value, axis, [(i, (i + by) % size) for i in range(size)])  710 us
    unnamed x3, waiting for transfers between devices  644 us
    psum x1, waiting for transfers between devices, local(): img_full, txt_full = lax.psum((img_dir, txt_dir), 'tower')  114 us
    dot_general x32, matrix products, image_side(): return total + jnp.dot(coef, block, preferred_element_type=jnp.float32)  46.5 us
  transfers between devices with their start and end apart: 68, of which 66 were waited for; matrix products, arithmetic and copies ran while one was open for 5% of the time, Pallas kernels for 0%

commit v1 on v0

v1 whole, which is shorter than its diff:
```python
import functools

import jax
import jax.numpy as jnp
from jax import lax
from jax.experimental import pallas as pl
from jax.experimental.pallas import tpu as pltpu
from jax.sharding import PartitionSpec as P

logit_scale = 10.0
logit_bias = -10.0
norm_eps = 1e-06
AXES = ("dp", "tower")
RING = 4
UNITS = 8
MIB = 1 << 20


def device(z, y, x, core):
    return (((z % 4 * 4 + y % 4) * 2 + x // 2) * 2 + core) * 2 + x % 2


def chips():
    return [(z, y, x) for z in range(RING) for y in range(RING) for x in range(RING)]


def swap_cores():
    return [(device(*chip, core), device(*chip, 1 - core)) for chip in chips() for core in range(2)]


def swap_towers():
    return [
        (device(z, y, x, core), device(z, y, x ^ 1, core)) for z, y, x in chips() for core in range(2)
    ]


def gather_pairs(turn, flip):
    pairs = []
    for z, y, x in chips():
        pairs.append((device(z + turn, y, x ^ 1 if flip else x, 0), device(z, y, x, 0)))
        pairs.append((device(z, y + turn, 3 - x if flip else x, 1), device(z, y, x, 1)))
    return pairs


def reduce_pairs(turn, flip):
    return [
        (device(z, y, x, core), device(z + turn, y, x ^ 1 if flip else x, core))
        for z, y, x in chips()
        for core in range(2)
    ]


def reduce_groups():
    return [
        [device(z, y, 2 * hi + lo, core) for y in range(RING) for hi in range(2)]
        for z in range(RING)
        for lo in range(2)
        for core in range(2)
    ]


OFFSETS = [(turn, flip) for flip in range(2) for turn in range(RING)]


def embed_kernel(*refs):
    units, (own_ref, far_ref), (emb_ref, raw_ref, norm_ref), head = (
        refs[:UNITS], refs[UNITS : UNITS + 2], refs[UNITS + 2 : UNITS + 5], refs[UNITS + 5]
    )
    width = own_ref.shape[1]
    rows = units[0].shape[0]
    head[:, :width] = own_ref[...]
    head[:, width:] = far_ref[...]
    for i in range(0, UNITS, 2):
        feats = jnp.concatenate([units[i][...], units[i + 1][...]], axis=0)
        raw = jnp.dot(feats, head[...], preferred_element_type=jnp.float32).astype(jnp.bfloat16)
        wide = raw.astype(jnp.float32)
        norm = jnp.sqrt(jnp.sum(wide * wide, axis=1, keepdims=True) + norm_eps)
        here = pl.ds(i * rows, 2 * rows)
        emb_ref[here, :] = (wide / norm).astype(jnp.bfloat16)
        raw_ref[here, :] = raw
        norm_ref[here, :] = norm


def score_kernel(*refs):
    (where_ref, emb_ref, far_ref, raw_ref, norm_ref), units, pieces, (flipped, grads, coefs) = (
        refs[:5], refs[5 : 5 + UNITS], refs[5 + UNITS : 5 + 2 * UNITS], refs[5 + 2 * UNITS :]
    )
    rows = units[0].shape[0]
    tile = 2 * rows
    for i in range(UNITS):
        flipped[:, i * rows : (i + 1) * rows] = units[i][...].T

    def step(i, carry):
        here = pl.ds(pl.multiple_of(i * tile, tile), tile)
        logits = (
            logit_scale
            * lax.dot_general(
                emb_ref[here, :], far_ref[...], (((1,), (1,)), ((), ())), preferred_element_type=jnp.float32
            )
            + logit_bias
        )
        coefs[...] = (logit_scale / (1.0 + jnp.exp(-logits))).astype(jnp.bfloat16)

        @pl.when(i == 0)
        def _():
            block = logits[:rows, :rows]
            match = lax.broadcasted_iota(jnp.int32, (rows, rows), 0) == lax.broadcasted_iota(
                jnp.int32, (rows, rows), 1
            )
            value = logit_scale / (1.0 + jnp.exp(jnp.where(match, block, -block)))
            coefs[:rows, :rows] = jnp.where(match, -value, value).astype(jnp.bfloat16)

        direction = jnp.dot(coefs[...], far_ref[...], preferred_element_type=jnp.float32)
        norm = norm_ref[here, :]
        unit = raw_ref[here, :].astype(jnp.float32) / norm
        inner = jnp.sum(unit * direction, axis=1, keepdims=True)
        grads[here, :] = ((direction - unit * inner) / norm).astype(jnp.bfloat16)
        return carry

    lax.fori_loop(0, UNITS // 2, step, 0)
    depth, width = pieces[0].shape
    for k, (turn, flip) in enumerate(OFFSETS):
        ring = lax.rem(where_ref[0] + turn, RING)
        feats = flipped[pl.ds(pl.multiple_of(ring * depth, 32), depth), :]
        pieces[k][...] = jnp.dot(
            feats, grads[:, flip * width : (flip + 1) * width], preferred_element_type=jnp.float32
        ).astype(jnp.bfloat16)


def sum_kernel(*refs):
    total = refs[0][...].astype(jnp.float32)
    for ref in refs[1:-1]:
        total += ref[...].astype(jnp.float32)
    out_ref = refs[-1]
    part = out_ref.shape[1]
    for j in range(UNITS):
        out_ref[j] = total[j * part : (j + 1) * part, :]


def local(img_feats, txt_feats, img_proj, txt_proj):
    rows, depth = img_feats.shape
    width = img_proj.shape[1]
    batch = UNITS * rows
    dp_id = lax.axis_index("dp")
    tower_id = lax.axis_index("tower")
    core = lax.rem(dp_id, 2)
    high = lax.rem(lax.div(dp_id, 2), 2)
    is_img = core == 0

    head = jnp.where(is_img, img_proj, txt_proj)
    head_far = lax.ppermute(head, AXES, swap_towers())
    mine = jnp.where(is_img, img_feats, txt_feats)
    other = lax.ppermute(jnp.where(is_img, txt_feats, img_feats), AXES, swap_cores())
    pick = (high == tower_id).astype(jnp.int32)
    unit = jnp.where(pick == core, mine, other)
    units = [unit] + [lax.ppermute(unit, AXES, gather_pairs(*offset)) for offset in OFFSETS[1:]]

    emb, raw, norm = pl.pallas_call(
        embed_kernel,
        out_shape=(
            jax.ShapeDtypeStruct((batch, 2 * width), jnp.bfloat16),
            jax.ShapeDtypeStruct((batch, 2 * width), jnp.bfloat16),
            jax.ShapeDtypeStruct((batch, 1), jnp.float32),
        ),
        scratch_shapes=[pltpu.VMEM((depth, 2 * width), jnp.bfloat16)],
        compiler_params=pltpu.CompilerParams(vmem_limit_bytes=40 * MIB),
        cost_estimate=pl.CostEstimate(
            flops=4 * batch * depth * width, bytes_accessed=10 * MIB, transcendentals=0
        ),
        name="embed",
    )(*units, head, head_far)
    emb_far = lax.ppermute(emb, AXES, swap_cores())

    place = lax.div(dp_id, 16).astype(jnp.int32).reshape(1)
    part = depth // RING
    vmem = pl.BlockSpec(memory_space=pltpu.VMEM)
    pieces = pl.pallas_call(
        score_kernel,
        out_shape=[jax.ShapeDtypeStruct((part, width), jnp.bfloat16)] * UNITS,
        in_specs=[pl.BlockSpec(memory_space=pltpu.SMEM)] + [vmem] * (4 + UNITS),
        out_specs=[vmem] * UNITS,
        scratch_shapes=[
            pltpu.VMEM((depth, batch), jnp.bfloat16),
            pltpu.VMEM((batch, 2 * width), jnp.bfloat16),
            pltpu.VMEM((2 * rows, batch), jnp.bfloat16),
        ],
        compiler_params=pltpu.CompilerParams(vmem_limit_bytes=48 * MIB),
        cost_estimate=pl.CostEstimate(
            flops=8 * batch * batch * width + 4 * batch * depth * width,
            bytes_accessed=14 * MIB,
            transcendentals=batch * batch,
        ),
        name="score",
    )(place, emb, emb_far, raw, norm, *units)
    terms = [pieces[0]] + [
        lax.ppermute(piece, AXES, reduce_pairs(*offset)) for piece, offset in zip(pieces[1:], OFFSETS[1:])
    ]
    sums = pl.pallas_call(
        sum_kernel,
        out_shape=jax.ShapeDtypeStruct((UNITS, part // UNITS, width), jnp.float32),
        compiler_params=pltpu.CompilerParams(vmem_limit_bytes=24 * MIB),
        name="sum_pieces",
    )(*terms)
    swapped = lax.all_to_all(
        sums, AXES, 0, 0, axis_index_groups=reduce_groups(), tiled=True
    )
    total = jnp.sum(swapped, axis=0)
    half = total.shape[0] // 2
    low, top = total[:half], total[half:]
    keep = jnp.where(is_img, low, top)
    got = lax.ppermute(jnp.where(is_img, top, low), AXES, swap_cores())
    return (jnp.where(is_img, keep, got), jnp.where(is_img, got, keep))


def solution(mesh):
    return jax.shard_map(
        local,
        mesh=mesh,
        in_specs=(P("dp", None), P("dp", None), P(None, "tower"), P(None, "tower")),
        out_specs=(P("dp", "tower"), P("dp", "tower")),
        check_vma=False,
    )
```

time: 1620 us -> 165 us (0.10)
  waiting for transfers between devices: 1470 us -> 60.7 us
  matrix products: 72 us -> 0 us
  starting transfers between devices: 8.66 us -> 43.1 us
  Pallas kernels: 0 us -> 23.1 us
    ppermute x66 -> x18, waiting for transfers between devices: 710 us -> 60.7 us  [the longest x7 36.8 us: local(): lax.ppermute(piece, AXES, reduce_pairs(*offset))]
    unnamed x3 -> x0, waiting for transfers between devices: 644 us -> none
    psum x1 -> x0, waiting for transfers between devices: 114 us -> none  [local(): img_full, txt_full = lax.psum((img_dir, txt_dir), 'tower')]
    dot_general x68 -> x0, matrix products: 72 us -> none  [the longest x32 46.5 us: image_side(): return total + jnp.dot(coef, block, preferred_element_type=jnp.float32)]
    ppermute x66 -> x18, starting transfers between devices: 8.58 us -> 43.1 us  [the longest x7 14.2 us: local(): lax.ppermute(unit, AXES, gather_pairs(*offset))]
    pallas_call x0 -> x3, Pallas kernels: none -> 23.1 us  [the longest x1 16 us: local(): pl.pallas_call(score_kernel, out_shape=[jax.ShapeDtypeStruct((part, width...]
    while x34 -> x0, local copies, waits for them, and re-layouts: 19 us -> none
    all_to_all x0 -> x1, blocking collectives: none -> 18.8 us  [local(): lax.all_to_all(sums, AXES, 0, 0, axis_index_groups=reduce_groups(), tiled...]
  transfers between devices with their start and end apart: 68 -> 18, of which waited for: 66 -> 9; matrix products, arithmetic and copies ran while one was open for 5% -> 2% of each run, Pallas kernels for 0% -> 0%
where the time goes in v1:
time: 165 us; the launch traced here: 164 us
  waiting for transfers between devices  60.7 us (37%)
  starting transfers between devices  43.1 us (26%)
  Pallas kernels  23.1 us (14%)
  blocking collectives  18.8 us (11%)
  local copies, waits for them, and re-layouts  14.7 us (9%)
  other arithmetic  3.06 us (2%)
    ppermute x7, waiting for transfers between devices, local(): lax.ppermute(piece, AXES, reduce_pairs(*offset))  36.8 us
    all_to_all x1, blocking collectives, local(): lax.all_to_all(sums, AXES, 0, 0, axis_index_groups=reduce_groups(), tiled...  18.8 us
    pallas_call x1, Pallas kernels, local(): pl.pallas_call(score_kernel, out_shape=[jax.ShapeDtypeStruct((part, width...  16 us
    ppermute x7, starting transfers between devices, local(): lax.ppermute(unit, AXES, gather_pairs(*offset))  14.2 us
    ppermute x1, starting transfers between devices, local(): emb_far = lax.ppermute(emb, AXES, swap_cores())  13.9 us
    ppermute x1, waiting for transfers between devices, local(): head_far = lax.ppermute(head, AXES, swap_towers())  11.5 us
    unnamed x22, local copies, waits for them, and re-layouts  10.9 us
    ppermute x7, starting transfers between devices, local(): lax.ppermute(piece, AXES, reduce_pairs(*offset))  9.32 us
  transfers between devices with their start and end apart: 18, of which 9 were waited for; matrix products, arithmetic and copies ran while one was open for 2% of the time, Pallas kernels for 0%

profile of v1, /device:TPU:1, one launch (start us, length us, event | category | flops | bytes accessed | tf_op | source)
XLA Modules:
  0.0 164.2 jit_solution(12826547488547545124)
XLA Ops:
  0.6 2.2 %copy.8 = bf16[1152,576]{1,0:T(8,128)(2,1)S(1)} copy(bf16[1152,576]{0,1:T(8,128)(2,1)} %param.6) | data formatting | bytes 2654208 | tf_op args[2]
  2.9 1.7 %copy.9 = bf16[1152,576]{1,0:T(8,128)(2,1)} copy(bf16[1152,576]{0,1:T(8,128)(2,1)S(1)} %copy-done.6) | data formatting | bytes 2654208 | tf_op args[3]
  4.5 1.5 broadcast_select_fusion.refs_8_
  6.0 0.0 copy-start.8
  6.1 0.0 copy-start.9
  6.1 1.8 %copy.10 = bf16[1152,576]{0,1:T(8,128)(2,1)} copy(bf16[1152,576]{1,0:T(8,128)(2,1)S(1)} %broadcast_select_fusion.refs_8_) | data formatting | bytes 2654208 | tf_op jit(solution)/shard_map/jit(_where)/select_n | solution.py:150
  7.9 2.0 %collective-permute-start.8 = (bf16[1152,576]{0,1:T(8,128)(2,1)}, bf16[1152,576]{0,1:T(8,128)(2,1)S(1)}, u32[]{:S(2)}, u32[]{:S(2)}) collective-permute-start(bf16[1152,576]{0,1:T(8,128)(2,1)} %copy.10), channel_id=1, source_target_pairs={{0,1},{2,3},{1,0},{3,2},{4,5},{6,7},{5,4},{7,6},{8,9},{10,11},{9,8... | collective-permute-start | bytes 3981320 | tf_op jit(solution)/shard_map/ppermute | solution.py:151
  9.9 0.8 broadcast_select_fusion.1
  10.7 0.0 collective-permute-start
  10.7 1.9 %collective-permute-done = bf16[128,1152]{1,0:T(8,128)(2,1)} collective-permute-done((bf16[128,1152]{1,0:T(8,128)(2,1)}, bf16[128,1152]{1,0:T(8,128)(2,1)}, u32[]{:S(2)}, u32[]{:S(2)}) %collective-permute-start) | collective-permute-done | bytes 294944 | tf_op jit(solution)/shard_map/ppermute | solution.py:153
  12.6 0.1 select_select_fusion.refs_0_.refs_5_
  12.7 2.9 %collective-permute-start.7 = (bf16[128,1152]{1,0:T(8,128)(2,1)S(1)}, bf16[128,1152]{1,0:T(8,128)(2,1)S(1)}, u32[]{:S(2)}, u32[]{:S(2)}) collective-permute-start(bf16[128,1152]{1,0:T(8,128)(2,1)S(1)} %select_select_fusion.refs_0_.refs_5_), channel_id=1, source_target_pairs={{97,0},{31,2},{96,1},{30,3},{101,4},{27,6},{100,5},{26,7},{105,8},... | collective-permute-start | bytes 884744 | tf_op jit(solution)/shard_map/ppermute | solution.py:156
  15.6 3.2 %collective-permute-start.6 = (bf16[128,1152]{1,0:T(8,128)(2,1)S(1)}, bf16[128,1152]{1,0:T(8,128)(2,1)S(1)}, u32[]{:S(2)}, u32[]{:S(2)}) collective-permute-start(bf16[128,1152]{1,0:T(8,128)(2,1)S(1)} %select_select_fusion.refs_0_.refs_5_), channel_id=1, source_target_pairs={{65,0},{23,2},{64,1},{22,3},{69,4},{19,6},{68,5},{18,7},{73,8},{31... | collective-permute-start | bytes 884744 | tf_op jit(solution)/shard_map/ppermute | solution.py:156
  18.8 2.6 %collective-permute-start.5 = (bf16[128,1152]{1,0:T(8,128)(2,1)S(1)}, bf16[128,1152]{1,0:T(8,128)(2,1)}, u32[]{:S(2)}, u32[]{:S(2)}) collective-permute-start(bf16[128,1152]{1,0:T(8,128)(2,1)S(1)} %select_select_fusion.refs_0_.refs_5_), channel_id=1, source_target_pairs={{33,0},{15,2},{32,1},{14,3},{37,4},{11,6},{36,5},{10,7},{41,8},{23... | collective-permute-start | bytes 884744 | tf_op jit(solution)/shard_map/ppermute | solution.py:156
  21.4 0.9 collective-permute-start.4
  22.2 0.4 collective-permute-start.3
  22.6 3.5 %collective-permute-done.6.refs_6_.refs_11_ = bf16[128,1152]{1,0:T(8,128)(2,1)S(1)} collective-permute-done((bf16[128,1152]{1,0:T(8,128)(2,1)S(1)}, bf16[128,1152]{1,0:T(8,128)(2,1)S(1)}, u32[]{:S(2)}, u32[]{:S(2)}) %collective-permute-start.6) | collective-permute-done | bytes 294944 | tf_op jit(solution)/shard_map/ppermute | solution.py:156
  26.1 0.7 copy-done
  26.8 1.4 collective-permute-start.2
  28.2 11.5 %collective-permute-done.8 = bf16[1152,576]{0,1:T(8,128)(2,1)S(1)} collective-permute-done((bf16[1152,576]{0,1:T(8,128)(2,1)}, bf16[1152,576]{0,1:T(8,128)(2,1)S(1)}, u32[]{:S(2)}, u32[]{:S(2)}) %collective-permute-start.8) | collective-permute-done | bytes 1327136 | tf_op jit(solution)/shard_map/ppermute | solution.py:151
  39.7 1.1 copy-done.7
  40.8 2.8 %collective-permute-start.1 = (bf16[128,1152]{1,0:T(8,128)(2,1)S(1)}, bf16[128,1152]{1,0:T(8,128)(2,1)}, u32[]{:S(2)}, u32[]{:S(2)}) collective-permute-start(bf16[128,1152]{1,0:T(8,128)(2,1)S(1)} %select_select_fusion.refs_0_.refs_5_), channel_id=1, source_target_pairs={{32,0},{10,2},{33,1},{11,3},{36,4},{14,6},{37,5},{15,7},{40,8},{18... | collective-permute-start | bytes 884744 | tf_op jit(solution)/shard_map/ppermute | solution.py:156
  43.6 2.1 %copy.11.refs_9_ = bf16[1152,576]{1,0:T(8,128)(2,1)S(1)} copy(bf16[1152,576]{0,1:T(8,128)(2,1)} %copy-done.7) | data formatting | bytes 2654208 | tf_op jit(solution)/shard_map/ppermute | solution.py:151
  45.7 0.0 collective-permute-done.4.refs_4_.refs_9_
  45.7 1.5 collective-permute-done.1.refs_1_.refs_6_
  47.3 1.0 copy-done.1
  48.2 6.7 %embed.1 = (bf16[1024,1152]{1,0:T(8,128)(2,1)}, bf16[1024,1152]{1,0:T(8,128)(2,1)S(1)}, f32[1024,1]{1,0:T(8,128)S(1)}) custom-call(bf16[128,1152]{1,0:T(8,128)(2,1)S(1)} %select_select_fusion.refs_0_.refs_5_, bf16[128,1152]{1,0:T(8,128)(2,1)} %collective-permute-done.1.refs_1_.refs_6_, bf16[128,1152]{1,0:T(8,128)(2,1)} %collective-permute-done.2.refs_2_.refs_7_, ...), custom_call_target="tpu_custom_call" | custom-call | flops 2717908992 | bytes 10485760 | tf_op jit(solution)/shard_map/embed/pallas_call | solution.py:158
  55.0 1.4 copy-done.3
  56.4 0.8 copy-done.4
  57.2 13.9 %collective-permute-start.9 = (bf16[1024,1152]{1,0:T(8,128)(2,1)}, bf16[1024,1152]{1,0:T(8,128)(2,1)}, u32[]{:S(2)}, u32[]{:S(2)}) collective-permute-start(bf16[1024,1152]{1,0:T(8,128)(2,1)} %get-tuple-element.13.refs_1_), channel_id=1, source_target_pairs={{0,2},{2,0},{1,3},{3,1},{4,6},{6,4},{5,7},{7,5},{8,10},{10,8},{9,1... | collective-permute-start | bytes 7077896 | tf_op jit(solution)/shard_map/ppermute | solution.py:172
  71.0 4.5 %collective-permute-done.9.refs_2_ = bf16[1024,1152]{1,0:T(8,128)(2,1)} collective-permute-done((bf16[1024,1152]{1,0:T(8,128)(2,1)}, bf16[1024,1152]{1,0:T(8,128)(2,1)}, u32[]{:S(2)}, u32[]{:S(2)}) %collective-permute-start.9) | collective-permute-done | bytes 2359328 | tf_op jit(solution)/shard_map/ppermute | solution.py:172
  75.5 1.0 copy-done.2
  76.5 1.0 copy-done.5
  77.6 16.0 %score.1 = (bf16[288,576]{1,0:T(8,128)(2,1)S(1)}, bf16[288,576]{1,0:T(8,128)(2,1)S(1)}, bf16[288,576]{1,0:T(8,128)(2,1)S(1)}, bf16[288,576]{1,0:T(8,128)(2,1)S(1...) custom-call(s32[1]{0:T(128)} %bitcast.refs_0_, ...), custom_call_target="tpu_custom_call" | custom-call | flops 7549747200 | bytes 14680064 | tf_op jit(solution)/shard_map/score/pallas_call | solution.py:177
  93.5 2.8 %collective-permute-start.10 = (bf16[288,576]{1,0:T(8,128)(2,1)S(1)}, bf16[288,576]{1,0:T(8,128)(2,1)S(1)}, u32[]{:S(2)}, u32[]{:S(2)}) collective-permute-start(bf16[288,576]{1,0:T(8,128)(2,1)S(1)} %get-tuple-element.17), channel_id=1, source_target_pairs={{0,32},{2,34},{1,33},{3,35},{4,36},{6,38},{5,37},{7,39},{8,40},{10... | collective-permute-start | bytes 995336 | tf_op jit(solution)/shard_map/ppermute | solution.py:196
  96.3 1.5 collective-permute-start.11
  97.8 1.2 collective-permute-start.12
  99.0 1.2 collective-permute-start.13
  100.2 0.2 collective-permute-start.14
  100.4 4.8 %collective-permute-done.10.refs_1_ = bf16[288,576]{1,0:T(8,128)(2,1)S(1)} collective-permute-done((bf16[288,576]{1,0:T(8,128)(2,1)S(1)}, bf16[288,576]{1,0:T(8,128)(2,1)S(1)}, u32[]{:S(2)}, u32[]{:S(2)}) %collective-permute-start.10) | collective-permute-done | bytes 331808 | tf_op jit(solution)/shard_map/ppermute | solution.py:196
  105.3 2.4 %collective-permute-start.15 = (bf16[288,576]{1,0:T(8,128)(2,1)S(1)}, bf16[288,576]{1,0:T(8,128)(2,1)S(1)}, u32[]{:S(2)}, u32[]{:S(2)}) collective-permute-start(bf16[288,576]{1,0:T(8,128)(2,1)S(1)} %get-tuple-element.22), channel_id=1, source_target_pairs={{0,65},{2,67},{1,64},{3,66},{4,69},{6,71},{5,68},{7,70},{8,73},{10... | collective-permute-start | bytes 995336 | tf_op jit(solution)/shard_map/ppermute | solution.py:196
  107.7 22.3 %collective-permute-done.11.refs_2_ = bf16[288,576]{1,0:T(8,128)(2,1)S(1)} collective-permute-done((bf16[288,576]{1,0:T(8,128)(2,1)S(1)}, bf16[288,576]{1,0:T(8,128)(2,1)S(1)}, u32[]{:S(2)}, u32[]{:S(2)}) %collective-permute-start.11) | collective-permute-done | bytes 331808 | tf_op jit(solution)/shard_map/ppermute | solution.py:196
  130.0 9.7 %collective-permute-done.16.refs_7_ = bf16[288,576]{1,0:T(8,128)(2,1)S(1)} collective-permute-done((bf16[288,576]{1,0:T(8,128)(2,1)S(1)}, bf16[288,576]{1,0:T(8,128)(2,1)S(1)}, u32[]{:S(2)}, u32[]{:S(2)}) %collective-permute-start.16) | collective-permute-done | bytes 331808 | tf_op jit(solution)/shard_map/ppermute | solution.py:196
  139.7 0.4 sum_pieces.1
  140.1 18.8 %all_to_all.5 = f32[8,36,576]{2,1,0:T(8,128)S(1)} all-to-all(f32[8,36,576]{2,1,0:T(8,128)S(1)} %sum_pieces.1), channel_id=1, replica_groups={{0,4,8,12,16,20,24,28},{2,6,10,14,18,22,26,30},{1,5,9,13,17,21,25,29},{..., dimensions={0} | all-to-all | bytes 1327104 | tf_op jit(solution)/shard_map/all_to_all | solution.py:204
  159.0 3.7 %collective-permute-start.17 = (f32[18,576]{1,0:T(8,128)S(1)}, f32[18,576]{1,0:T(8,128)S(1)}, u32[]{:S(2)}, u32[]{:S(2)}) collective-permute-start(f32[18,576]{1,0:T(8,128)S(1)} %slice_select_fusion), channel_id=1, source_target_pairs={{0,2},{2,0},{1,3},{3,1},{4,6},{6,4},{5,7},{7,5},{8,10},{10,8},{9,1... | collective-permute-start | bytes 124424 | tf_op jit(solution)/shard_map/ppermute | solution.py:211
  162.6 0.9 collective-permute-done.17
  163.5 0.7 broadcast_select_fusion.2
  (22 shorter events, 0.1 us)
Async XLA Ops:
  0.6 2.2 %copy-start.6 = (bf16[1152,576]{0,1:T(8,128)(2,1)S(1)}, bf16[1152,576]{0,1:T(8,128)(2,1)}, u32[]{:S(2)}) copy-start(bf16[1152,576]{0,1:T(8,128)(2,1)} %param.7) | copy-start | bytes 3981316
  6.0 3.9 %copy-start.8 = (bf16[128,1152]{1,0:T(8,128)(2,1)S(1)}, bf16[128,1152]{1,0:T(8,128)(2,1)}, u32[]{:S(2)}) copy-start(bf16[128,1152]{1,0:T(8,128)(2,1)} %param.5) | copy-start | bytes 884740
  6.1 3.9 %copy-start.9 = (bf16[128,1152]{1,0:T(8,128)(2,1)S(1)}, bf16[128,1152]{1,0:T(8,128)(2,1)}, u32[]{:S(2)}) copy-start(bf16[128,1152]{1,0:T(8,128)(2,1)} %param.4) | copy-start | bytes 884740
  7.9 31.8 %collective-permute-start.8 = (bf16[1152,576]{0,1:T(8,128)(2,1)}, bf16[1152,576]{0,1:T(8,128)(2,1)S(1)}, u32[]{:S(2)}, u32[]{:S(2)}) collective-permute-start(bf16[1152,576]{0,1:T(8,128)(2,1)} %copy.10), channel_id=1, source_target_pairs={{0,1},{2,3},{1,0},{3,2},{4,5},{6,7},{5,4},{7,6},{8,9},{10,11},{9,8... | collective-permute-start | bytes 3981320 | tf_op jit(solution)/shard_map/ppermute | solution.py:151
  10.7 1.9 %collective-permute-start = (bf16[128,1152]{1,0:T(8,128)(2,1)}, bf16[128,1152]{1,0:T(8,128)(2,1)}, u32[]{:S(2)}, u32[]{:S(2)}) collective-permute-start(bf16[128,1152]{1,0:T(8,128)(2,1)} %broadcast_select_fusion.1), channel_id=1, source_target_pairs={{0,2},{2,0},{1,3},{3,1},{4,6},{6,4},{5,7},{7,5},{8,10},{10,8},{9,1... | collective-permute-start | bytes 884744 | tf_op jit(solution)/shard_map/ppermute | solution.py:153
  12.7 9.6 %collective-permute-start.7 = (bf16[128,1152]{1,0:T(8,128)(2,1)S(1)}, bf16[128,1152]{1,0:T(8,128)(2,1)S(1)}, u32[]{:S(2)}, u32[]{:S(2)}) collective-permute-start(bf16[128,1152]{1,0:T(8,128)(2,1)S(1)} %select_select_fusion.refs_0_.refs_5_), channel_id=1, source_target_pairs={{97,0},{31,2},{96,1},{30,3},{101,4},{27,6},{100,5},{26,7},{105,8},... | collective-permute-start | bytes 884744 | tf_op jit(solution)/shard_map/ppermute | solution.py:156
  15.6 10.5 %collective-permute-start.6 = (bf16[128,1152]{1,0:T(8,128)(2,1)S(1)}, bf16[128,1152]{1,0:T(8,128)(2,1)S(1)}, u32[]{:S(2)}, u32[]{:S(2)}) collective-permute-start(bf16[128,1152]{1,0:T(8,128)(2,1)S(1)} %select_select_fusion.refs_0_.refs_5_), channel_id=1, source_target_pairs={{65,0},{23,2},{64,1},{22,3},{69,4},{19,6},{68,5},{18,7},{73,8},{31... | collective-permute-start | bytes 884744 | tf_op jit(solution)/shard_map/ppermute | solution.py:156
  18.8 26.9 %collective-permute-start.5 = (bf16[128,1152]{1,0:T(8,128)(2,1)S(1)}, bf16[128,1152]{1,0:T(8,128)(2,1)}, u32[]{:S(2)}, u32[]{:S(2)}) collective-permute-start(bf16[128,1152]{1,0:T(8,128)(2,1)S(1)} %select_select_fusion.refs_0_.refs_5_), channel_id=1, source_target_pairs={{33,0},{15,2},{32,1},{14,3},{37,4},{11,6},{36,5},{10,7},{41,8},{23... | collective-permute-start | bytes 884744 | tf_op jit(solution)/shard_map/ppermute | solution.py:156
  21.4 24.3 %collective-permute-start.4 = (bf16[128,1152]{1,0:T(8,128)(2,1)S(1)}, bf16[128,1152]{1,0:T(8,128)(2,1)}, u32[]{:S(2)}, u32[]{:S(2)}) collective-permute-start(bf16[128,1152]{1,0:T(8,128)(2,1)S(1)} %select_select_fusion.refs_0_.refs_5_), channel_id=1, source_target_pairs={{1,0},{7,2},{0,1},{6,3},{5,4},{3,6},{4,5},{2,7},{9,8},{15,10},{8,9... | collective-permute-start | bytes 884744 | tf_op jit(solution)/shard_map/ppermute | solution.py:156
  22.2 23.5 %collective-permute-start.3 = (bf16[128,1152]{1,0:T(8,128)(2,1)S(1)}, bf16[128,1152]{1,0:T(8,128)(2,1)}, u32[]{:S(2)}, u32[]{:S(2)}) collective-permute-start(bf16[128,1152]{1,0:T(8,128)(2,1)S(1)} %select_select_fusion.refs_0_.refs_5_), channel_id=1, source_target_pairs={{96,0},{26,2},{97,1},{27,3},{100,4},{30,6},{101,5},{31,7},{104,8},... | collective-permute-start | bytes 884744 | tf_op jit(solution)/shard_map/ppermute | solution.py:156
  26.1 0.7 copy-start
  26.8 18.9 %collective-permute-start.2 = (bf16[128,1152]{1,0:T(8,128)(2,1)S(1)}, bf16[128,1152]{1,0:T(8,128)(2,1)}, u32[]{:S(2)}, u32[]{:S(2)}) collective-permute-start(bf16[128,1152]{1,0:T(8,128)(2,1)S(1)} %select_select_fusion.refs_0_.refs_5_), channel_id=1, source_target_pairs={{64,0},{18,2},{65,1},{19,3},{68,4},{22,6},{69,5},{23,7},{72,8},{26... | collective-permute-start | bytes 884744 | tf_op jit(solution)/shard_map/ppermute | solution.py:156
  39.7 1.1 copy-start.7
  40.8 6.5 %collective-permute-start.1 = (bf16[128,1152]{1,0:T(8,128)(2,1)S(1)}, bf16[128,1152]{1,0:T(8,128)(2,1)}, u32[]{:S(2)}, u32[]{:S(2)}) collective-permute-start(bf16[128,1152]{1,0:T(8,128)(2,1)S(1)} %select_select_fusion.refs_0_.refs_5_), channel_id=1, source_target_pairs={{32,0},{10,2},{33,1},{11,3},{36,4},{14,6},{37,5},{15,7},{40,8},{18... | collective-permute-start | bytes 884744 | tf_op jit(solution)/shard_map/ppermute | solution.py:156
  47.3 1.0 copy-start.1
  54.9 1.4 copy-start.3
  56.4 0.8 copy-start.4
  57.2 18.4 %collective-permute-start.9 = (bf16[1024,1152]{1,0:T(8,128)(2,1)}, bf16[1024,1152]{1,0:T(8,128)(2,1)}, u32[]{:S(2)}, u32[]{:S(2)}) collective-permute-start(bf16[1024,1152]{1,0:T(8,128)(2,1)} %get-tuple-element.13.refs_1_), channel_id=1, source_target_pairs={{0,2},{2,0},{1,3},{3,1},{4,6},{6,4},{5,7},{7,5},{8,10},{10,8},{9,1... | collective-permute-start | bytes 7077896 | tf_op jit(solution)/shard_map/ppermute | solution.py:172
  75.5 1.0 copy-start.2
  76.5 1.0 copy-start.5
  93.5 11.7 %collective-permute-start.10 = (bf16[288,576]{1,0:T(8,128)(2,1)S(1)}, bf16[288,576]{1,0:T(8,128)(2,1)S(1)}, u32[]{:S(2)}, u32[]{:S(2)}) collective-permute-start(bf16[288,576]{1,0:T(8,128)(2,1)S(1)} %get-tuple-element.17), channel_id=1, source_target_pairs={{0,32},{2,34},{1,33},{3,35},{4,36},{6,38},{5,37},{7,39},{8,40},{10... | collective-permute-start | bytes 995336 | tf_op jit(solution)/shard_map/ppermute | solution.py:196
  96.3 33.7 %collective-permute-start.11 = (bf16[288,576]{1,0:T(8,128)(2,1)S(1)}, bf16[288,576]{1,0:T(8,128)(2,1)S(1)}, u32[]{:S(2)}, u32[]{:S(2)}) collective-permute-start(bf16[288,576]{1,0:T(8,128)(2,1)S(1)} %get-tuple-element.18), channel_id=1, source_target_pairs={{0,64},{2,66},{1,65},{3,67},{4,68},{6,70},{5,69},{7,71},{8,72},{10... | collective-permute-start | bytes 995336 | tf_op jit(solution)/shard_map/ppermute | solution.py:196
  97.8 32.2 %collective-permute-start.12 = (bf16[288,576]{1,0:T(8,128)(2,1)S(1)}, bf16[288,576]{1,0:T(8,128)(2,1)S(1)}, u32[]{:S(2)}, u32[]{:S(2)}) collective-permute-start(bf16[288,576]{1,0:T(8,128)(2,1)S(1)} %get-tuple-element.19), channel_id=1, source_target_pairs={{0,96},{2,98},{1,97},{3,99},{4,100},{6,102},{5,101},{7,103},{8,104... | collective-permute-start | bytes 995336 | tf_op jit(solution)/shard_map/ppermute | solution.py:196
  99.0 31.0 %collective-permute-start.13 = (bf16[288,576]{1,0:T(8,128)(2,1)S(1)}, bf16[288,576]{1,0:T(8,128)(2,1)S(1)}, u32[]{:S(2)}, u32[]{:S(2)}) collective-permute-start(bf16[288,576]{1,0:T(8,128)(2,1)S(1)} %get-tuple-element.20), channel_id=1, source_target_pairs={{0,1},{2,3},{1,0},{3,2},{4,5},{6,7},{5,4},{7,6},{8,9},{10,11},{9,8... | collective-permute-start | bytes 995336 | tf_op jit(solution)/shard_map/ppermute | solution.py:196
  100.2 29.8 %collective-permute-start.14 = (bf16[288,576]{1,0:T(8,128)(2,1)S(1)}, bf16[288,576]{1,0:T(8,128)(2,1)S(1)}, u32[]{:S(2)}, u32[]{:S(2)}) collective-permute-start(bf16[288,576]{1,0:T(8,128)(2,1)S(1)} %get-tuple-element.21), channel_id=1, source_target_pairs={{0,33},{2,35},{1,32},{3,34},{4,37},{6,39},{5,36},{7,38},{8,41},{10... | collective-permute-start | bytes 995336 | tf_op jit(solution)/shard_map/ppermute | solution.py:196
  105.3 24.8 %collective-permute-start.15 = (bf16[288,576]{1,0:T(8,128)(2,1)S(1)}, bf16[288,576]{1,0:T(8,128)(2,1)S(1)}, u32[]{:S(2)}, u32[]{:S(2)}) collective-permute-start(bf16[288,576]{1,0:T(8,128)(2,1)S(1)} %get-tuple-element.22), channel_id=1, source_target_pairs={{0,65},{2,67},{1,64},{3,66},{4,69},{6,71},{5,68},{7,70},{8,73},{10... | collective-permute-start | bytes 995336 | tf_op jit(solution)/shard_map/ppermute | solution.py:196
  130.0 9.7 %collective-permute-start.16 = (bf16[288,576]{1,0:T(8,128)(2,1)S(1)}, bf16[288,576]{1,0:T(8,128)(2,1)S(1)}, u32[]{:S(2)}, u32[]{:S(2)}) collective-permute-start(bf16[288,576]{1,0:T(8,128)(2,1)S(1)} %get-tuple-element.23), channel_id=1, source_target_pairs={{0,97},{2,99},{1,96},{3,98},{4,101},{6,103},{5,100},{7,102},{8,105... | collective-permute-start | bytes 995336 | tf_op jit(solution)/shard_map/ppermute | solution.py:196
  159.0 4.6 %collective-permute-start.17 = (f32[18,576]{1,0:T(8,128)S(1)}, f32[18,576]{1,0:T(8,128)S(1)}, u32[]{:S(2)}, u32[]{:S(2)}) collective-permute-start(f32[18,576]{1,0:T(8,128)S(1)} %slice_select_fusion), channel_id=1, source_target_pairs={{0,2},{2,0},{1,3},{3,1},{4,6},{6,4},{5,7},{7,5},{8,10},{10,8},{9,1... | collective-permute-start | bytes 124424 | tf_op jit(solution)/shard_map/ppermute | solution.py:211

commit v2 on v0

v2 whole, which is shorter than its diff:
```python
import jax
import jax.numpy as jnp
from jax import lax
from jax.experimental import pallas as pl
from jax.experimental.pallas import tpu as pltpu
from jax.sharding import PartitionSpec as P

logit_scale = 10.0
logit_bias = -10.0
norm_eps = 1e-06
AXES = ("dp", "tower")
RING = 4
MIB = 1 << 20
F32, BF16 = jnp.float32, jnp.bfloat16


def device(z, y, x, core):
    return (((z % 4 * 4 + y % 4) * 2 + x // 2) * 2 + core) * 2 + x % 2


CHIPS = [(z, y, x) for z in range(RING) for y in range(RING) for x in range(RING)]
CORES_SWAP = [(device(*chip, core), device(*chip, 1 - core)) for chip in CHIPS for core in range(2)]
TOWERS_SWAP = [(device(z, y, x, core), device(z, y, x ^ 1, core)) for z, y, x in CHIPS for core in range(2)]


def gather_pairs(turn):
    source = (0, 2, 1, 3)
    pairs = []
    for z, y, x in CHIPS:
        pairs.append((device(z + turn, y, x, 0), device(z, y, x, 0)))
        pairs.append((device(z, y + turn, source[x], 1), device(z, y, x, 1)))
    return pairs


def reduce_pairs(turn, flip):
    pairs = []
    for z, y, x in CHIPS:
        pairs.append((device(z, y, x, 0), device(z + turn, y, x ^ flip, 0)))
        pairs.append((device(z, y, x, 1), device(z, y + turn, x ^ (2 * flip), 1)))
    return pairs


REDUCE_GROUPS = [
    [device(z, y, 2 * high + tower, 0) for y in range(RING) for high in range(2)]
    for z in range(RING)
    for tower in range(2)
] + [
    [device(z, y, 2 * high + tower, 1) for z in range(RING) for tower in range(2)]
    for y in range(RING)
    for high in range(2)
]


def position():
    dp = lax.axis_index("dp")
    return (
        lax.div(dp, 16),
        lax.rem(lax.div(dp, 4), 4),
        lax.rem(lax.div(dp, 2), 2),
        lax.rem(dp, 2),
        lax.axis_index("tower"),
    )


def vmem():
    return pl.BlockSpec(memory_space=pltpu.VMEM)


def pick_kernel(img_feats, txt_feats, img_proj, txt_proj, mine, give, top, bottom, head, sems):
    core = position()[3]

    def copies(feats, other, proj):
        return [
            pltpu.make_async_copy(proj, head, sems.at[0]),
            pltpu.make_async_copy(other, give, sems.at[1]),
            pltpu.make_async_copy(feats, mine, sems.at[2]),
        ]

    @pl.when(core == 0)
    def _():
        for copy in copies(img_feats, txt_feats, img_proj):
            copy.start()

    @pl.when(core == 1)
    def _():
        for copy in copies(txt_feats, img_feats, txt_proj):
            copy.start()

    for copy in copies(img_feats, txt_feats, img_proj):
        copy.wait()
    part, width = top.shape[0], head.shape[1]
    top[:, :width] = head[:part, :]
    bottom[:, :width] = head[part : 2 * part, :]
    top[:, width:] = head[2 * part : 3 * part, :]
    bottom[:, width:] = head[3 * part :, :]


def flip_rows(feats, flip_ref, lane):
    z, y, high, core, _ = position()
    part = flip_ref.shape[2] // RING
    turned = feats.T

    def store(own, ring_first):
        for block in range(2 * RING * RING):
            first, second, side = block // 8, block // 2 % 4, block % 2
            ring, other = (first, second) if ring_first else (second, first)
            turn = lax.rem(ring - own + RING, RING)
            flip_ref[turn, lax.rem(side + high, 2), pl.ds(other * part, part), pl.ds(lane, feats.shape[0])] = (
                turned[block * part : (block + 1) * part, :]
            )

    @pl.when(core == 0)
    def _():
        store(z, True)

    @pl.when(core == 1)
    def _():
        store(y, False)


def embed_rows(feats, head, here, emb_ref, raw_ref):
    raw = jnp.dot(feats, head, preferred_element_type=F32).astype(BF16)
    wide = raw.astype(F32)
    norm = jnp.sqrt(jnp.sum(wide * wide, axis=1, keepdims=True) + norm_eps)
    emb_ref[here, :] = (wide / norm).astype(BF16)
    raw_ref[here, :] = raw


def embed_first_kernel(top, bottom, far_top, far_bottom, one, two, emb_ref, raw_ref, flip_ref, head_ref):
    part, width = top.shape[0], top.shape[1] // 2
    for column, (upper, lower) in ((0, (top, bottom)), (width, (far_top, far_bottom))):
        head_ref[0:part, column : column + width] = upper[:, :width]
        head_ref[part : 2 * part, column : column + width] = lower[:, :width]
        head_ref[2 * part : 3 * part, column : column + width] = upper[:, width:]
        head_ref[3 * part :, column : column + width] = lower[:, width:]
    rows = one.shape[0]
    for i, unit in enumerate((one, two)):
        embed_rows(unit[...], head_ref[...], pl.ds(i * rows, rows), emb_ref, raw_ref)
        flip_rows(unit[...], flip_ref, i * rows)


def embed_second_kernel(head_ref, one, two, emb_ref, raw_ref, flip_ref):
    rows = one.shape[0]
    for i, unit in enumerate((one, two)):
        embed_rows(unit[...], head_ref[...], pl.ds(i * rows, rows), emb_ref, raw_ref)
        flip_rows(unit[...], flip_ref, i * rows)


def score_kernel(emb_a, emb_b, far_a, far_b, raw_a, raw_b, grad_a, grad_b, turned_a, turned_b):
    _, _, high, _, tower = position()
    turned_a[...] = far_a[...].T
    turned_b[...] = far_b[...].T
    rows = emb_a.shape[0] // 2

    def coef(logits):
        return (logit_scale / (1.0 + jnp.exp(-(logit_scale * logits + logit_bias)))).astype(BF16)

    for emb, raw, grad, i in ((emb_a, raw_a, grad_a, 0), (emb_a, raw_a, grad_a, 1), (emb_b, raw_b, grad_b, 0), (emb_b, raw_b, grad_b, 1)):
        here = pl.ds(i * rows, rows)
        own = emb[here, :]
        coef_a = coef(jnp.dot(own, turned_a[...], preferred_element_type=F32))
        logits_b = jnp.dot(own, turned_b[...], preferred_element_type=F32)
        if emb is emb_b and i == 0:
            row = lax.broadcasted_iota(jnp.int32, (rows, rows), 0)
            column = lax.broadcasted_iota(jnp.int32, (rows, rows), 1)
            match = (jnp.abs(row - column) == rows // 2) & (high == tower)
            logits = logit_scale * logits_b[:, :rows] + logit_bias
            value = logit_scale / (1.0 + jnp.exp(jnp.where(match, logits, -logits)))
            coef_b = jnp.concatenate(
                [jnp.where(match, -value, value).astype(BF16), coef(logits_b[:, rows:])], axis=1
            )
        else:
            coef_b = coef(logits_b)
        direction = jnp.dot(coef_a, far_a[...], preferred_element_type=F32) + jnp.dot(
            coef_b, far_b[...], preferred_element_type=F32
        )
        wide = raw[here, :].astype(F32)
        norm = jnp.sqrt(jnp.sum(wide * wide, axis=1, keepdims=True) + norm_eps)
        unit = wide / norm
        inner = jnp.sum(unit * direction, axis=1, keepdims=True)
        grad[here, :] = ((direction - unit * inner) / norm).astype(BF16)


def terms_kernel(turns, flip_a, flip_b, grad_a, grad_b, *pieces):
    core = position()[3]
    for k, turn in enumerate(turns):
        half, rows = flip_a.shape[2], grad_a.shape[0]
        width = grad_a.shape[1] // 2
        term = jnp.dot(
            flip_a[turn].reshape(2 * half, rows), grad_a[...], preferred_element_type=F32
        ) + jnp.dot(flip_b[turn].reshape(2 * half, rows), grad_b[...], preferred_element_type=F32)
        term = term.astype(BF16)
        straight, crossed = pieces[2 * k], pieces[2 * k + 1]
        straight[:, :width] = term[:half, :width]
        crossed[:, width:] = term[half:, width:]

        @pl.when(core == 0)
        def _():
            straight[:, width:] = term[half:, :width]
            crossed[:, :width] = term[:half, width:]

        @pl.when(core == 1)
        def _():
            straight[:, width:] = term[:half, width:]
            crossed[:, :width] = term[half:, :width]


def sum_kernel(*refs):
    _, _, high, core, tower = position()
    out_ref = refs[-1]
    total = refs[0][...].astype(F32)
    for ref in refs[1:-1]:
        total += ref[...].astype(F32)
    total = total.astype(out_ref.dtype)
    twist = jnp.where(core == 0, high, tower)
    part, width = out_ref.shape[1], out_ref.shape[2] // 2
    for j in range(RING):
        for side in range(2):
            slot = 2 * j + lax.rem(side + twist, 2)
            columns = slice(side * width, (side + 1) * width)
            out_ref[slot, :, :width] = total[2 * j * part : (2 * j + 1) * part, columns]
            out_ref[slot, :, width:] = total[(2 * j + 1) * part : (2 * j + 2) * part, columns]


def kernel_call(body, name, shapes, operands, scratch=(), flops=0, exps=0, specs=None, limit=40):
    shapes = [jax.ShapeDtypeStruct(*shape) for shape in shapes]
    touched = sum(a.size * a.dtype.itemsize for a in (*shapes, *operands))
    return pl.pallas_call(
        body,
        out_shape=shapes,
        in_specs=[vmem()] * len(operands) if specs is None else specs,
        out_specs=[vmem()] * len(shapes),
        scratch_shapes=list(scratch),
        compiler_params=pltpu.CompilerParams(vmem_limit_bytes=limit * MIB),
        cost_estimate=pl.CostEstimate(flops=flops, bytes_accessed=touched, transcendentals=exps),
        name=name,
    )(*operands)


def local(img_feats, txt_feats, img_proj, txt_proj):
    rows, depth = img_feats.shape
    width = img_proj.shape[1]
    full = 2 * width
    unit = 2 * rows
    pair = 2 * unit
    part = depth // (2 * RING * RING)

    def swap(value):
        return lax.ppermute(value, AXES, CORES_SWAP)

    mine, give, top, bottom = kernel_call(
        pick_kernel,
        "pick",
        [((rows, depth), BF16)] * 2 + [((depth // 4, full), BF16)] * 2,
        (img_feats, txt_feats, img_proj, txt_proj),
        scratch=(pltpu.VMEM((depth, width), BF16), pltpu.SemaphoreType.DMA((3,))),
        specs=[pl.BlockSpec(memory_space=pl.ANY)] * 4,
    )
    far_top = lax.ppermute(top, AXES, TOWERS_SWAP)
    far_bottom = lax.ppermute(bottom, AXES, TOWERS_SWAP)
    own = jnp.concatenate([mine, swap(give)], axis=0)
    units = [lax.ppermute(own, AXES, gather_pairs(turn)) for turn in range(RING)]

    flips = ((RING, 2, RING * part, pair), BF16)
    block = ((pair, full), BF16)
    work = 2 * pair * depth * full
    emb_a, raw_a, flip_a, head = kernel_call(
        embed_first_kernel,
        "embed_first",
        [block, block, flips, ((depth, full), BF16)],
        (top, bottom, far_top, far_bottom, units[1], units[3]),
        flops=work,
    )
    far_a = swap(emb_a)
    emb_b, raw_b, flip_b = kernel_call(
        embed_second_kernel, "embed_second", [block, block, flips], (head, units[0], units[2]), flops=work
    )
    far_b = swap(emb_b)
    grad_a, grad_b = kernel_call(
        score_kernel,
        "score",
        [block, block],
        (emb_a, emb_b, far_a, far_b, raw_a, raw_b),
        scratch=[pltpu.VMEM((full, pair), BF16)] * 2,
        flops=16 * pair * pair * full,
        exps=4 * pair * pair,
    )

    def terms(name, turns):
        return kernel_call(
            lambda *refs: terms_kernel(turns, *refs),
            name,
            [((RING * part, full), BF16)] * (2 * len(turns)),
            (flip_a, flip_b, grad_a, grad_b),
            flops=len(turns) * work // 2,
        )

    def send(pieces, turns):
        return [
            lax.ppermute(pieces[2 * k + flip], AXES, reduce_pairs(turn, flip)) if turn or flip else pieces[0]
            for k, turn in enumerate(turns)
            for flip in range(2)
        ]

    first = send(terms("terms_first", (1, 3)), (1, 3))
    second = send(terms("terms_second", (0, 2)), (0, 2))
    (sums,) = kernel_call(
        sum_kernel, "sum_terms", [((2 * RING, part // 2, full), BF16)], (*first, *second)
    )
    swapped = lax.all_to_all(sums, AXES, 0, 0, axis_index_groups=REDUCE_GROUPS, tiled=True)
    total = jnp.sum(swapped.astype(F32), axis=0)
    is_img = position()[3] == 0
    low, high = total[:, :width], total[:, width:]
    keep = jnp.where(is_img, low, high)
    got = swap(jnp.where(is_img, high, low))
    return (jnp.where(is_img, keep, got), jnp.where(is_img, got, keep))


def solution(mesh):
    return jax.shard_map(
        local,
        mesh=mesh,
        in_specs=(P("dp", None), P("dp", None), P(None, "tower"), P(None, "tower")),
        out_specs=(P("dp", "tower"), P("dp", "tower")),
        check_vma=False,
    )
```

time: 1620 us -> 113 us (0.07)
  waiting for transfers between devices: 1470 us -> 47.5 us
  matrix products: 72 us -> 0 us
  starting transfers between devices: 8.66 us -> 39.8 us
  local copies, waits for them, and re-layouts: 28.9 us -> 4.29 us
  Pallas kernels: 0 us -> 19.1 us
    ppermute x66 -> x17, waiting for transfers between devices: 710 us -> 39.7 us  [the longest x7 15.6 us: send(): lax.ppermute(pieces[2 * k + flip], AXES, reduce_pairs(turn, flip))]
    unnamed x3 -> x0, waiting for transfers between devices: 644 us -> none
    psum x1 -> x0, waiting for transfers between devices: 114 us -> none  [local(): img_full, txt_full = lax.psum((img_dir, txt_dir), 'tower')]
    dot_general x68 -> x0, matrix products: 72 us -> none  [the longest x32 46.5 us: image_side(): return total + jnp.dot(coef, block, preferred_element_type=jnp.float32)]
    ppermute x66 -> x17, starting transfers between devices: 8.58 us -> 31.7 us  [the longest x7 16.1 us: send(): lax.ppermute(pieces[2 * k + flip], AXES, reduce_pairs(turn, flip))]
    pallas_call x0 -> x7, Pallas kernels: none -> 19.1 us  [kernel_call(): pl.pallas_call(body, out_shape=shapes, in_specs=[vmem()] * len(operands)...]
    while x34 -> x0, local copies, waits for them, and re-layouts: 19 us -> none
  transfers between devices with their start and end apart: 68 -> 18, of which waited for: 66 -> 9; matrix products, arithmetic and copies ran while one was open for 5% -> 0% of each run, Pallas kernels for 0% -> 7%
where the time goes in v2:
time: 113 us; the launch traced here: 112 us
  waiting for transfers between devices  47.5 us (42%)
  starting transfers between devices  39.8 us (35%)
  Pallas kernels  19.1 us (17%)
  local copies, waits for them, and re-layouts  4.29 us (4%)
    pallas_call x7, Pallas kernels, kernel_call(): pl.pallas_call(body, out_shape=shapes, in_specs=[vmem()] * len(operands)...  19.1 us
    ppermute x7, starting transfers between devices, send(): lax.ppermute(pieces[2 * k + flip], AXES, reduce_pairs(turn, flip))  16.1 us
    ppermute x7, waiting for transfers between devices, send(): lax.ppermute(pieces[2 * k + flip], AXES, reduce_pairs(turn, flip))  15.6 us
    ppermute x1, waiting for transfers between devices, local(): far_bottom = lax.ppermute(bottom, AXES, TOWERS_SWAP)  10.9 us
    ppermute x1, waiting for transfers between devices, local(): far_top = lax.ppermute(top, AXES, TOWERS_SWAP)  8.42 us
    all_to_all x1, starting transfers between devices, local(): lax.all_to_all(sums, AXES, 0, 0, axis_index_groups=REDUCE_GROUPS, tiled=T...  8.04 us
    all_to_all x1, waiting for transfers between devices, local(): lax.all_to_all(sums, AXES, 0, 0, axis_index_groups=REDUCE_GROUPS, tiled=T...  7.84 us
    ppermute x4, starting transfers between devices, local(): lax.ppermute(own, AXES, gather_pairs(turn))  6.85 us
  transfers between devices with their start and end apart: 18, of which 9 were waited for; matrix products, arithmetic and copies ran while one was open for 0% of the time, Pallas kernels for 7%

profile of v2, /device:TPU:1, one launch (start us, length us, event | category | flops | bytes accessed | tf_op | source)
XLA Modules:
  0.0 112.3 jit_solution(18350996138314186573)
XLA Ops:
  0.6 2.1 %copy.6.img_proj = bf16[1152,576]{1,0:T(8,128)(2,1)S(1)} copy(bf16[1152,576]{0,1:T(8,128)(2,1)} %param.6) | data formatting | bytes 2654208 | tf_op args[2]
  2.7 0.0 copy-start
  2.7 0.0 copy-start.1
  2.7 2.1 %copy.7.txt_proj = bf16[1152,576]{1,0:T(8,128)(2,1)S(1)} copy(bf16[1152,576]{0,1:T(8,128)(2,1)} %param.7) | data formatting | bytes 2654208 | tf_op args[3]
  4.9 0.8 pick.1
  5.7 2.1 %collective-permute-start = (bf16[288,1152]{1,0:T(8,128)(2,1)S(1)}, bf16[288,1152]{1,0:T(8,128)(2,1)S(1)}, u32[]{:S(2)}, u32[]{:S(2)}) collective-permute-start(bf16[288,1152]{1,0:T(8,128)(2,1)S(1)} %get-tuple-element.23.top), channel_id=1, source_target_pairs={{0,1},{2,3},{1,0},{3,2},{4,5},{6,7},{5,4},{7,6},{8,9},{10,11},{9,8... | collective-permute-start | bytes 1990664 | tf_op jit(solution)/shard_map/ppermute | solution.py:259
  7.8 1.0 collective-permute-start.2
  8.8 0.2 collective-permute-start.1
  9.0 1.0 collective-permute-done.2
  10.0 2.8 %collective-permute-start.3 = (bf16[256,1152]{1,0:T(8,128)(2,1)S(1)}, bf16[256,1152]{1,0:T(8,128)(2,1)S(1)}, u32[]{:S(2)}, u32[]{:S(2)}) collective-permute-start(bf16[256,1152]{1,0:T(8,128)(2,1)S(1)} %constant_dynamic-update-slice_fusion), channel_id=1, source_target_pairs={{32,0},{10,2},{33,1},{14,3},{36,4},{11,6},{37,5},{15,7},{40,8},{18... | collective-permute-start | bytes 1769480 | tf_op jit(solution)/shard_map/ppermute | solution.py:262
  12.9 0.0 collective-permute-start.4
  12.9 0.7 collective-permute-start.5
  13.5 8.4 %collective-permute-done.far_top = bf16[288,1152]{1,0:T(8,128)(2,1)S(1)} collective-permute-done((bf16[288,1152]{1,0:T(8,128)(2,1)S(1)}, bf16[288,1152]{1,0:T(8,128)(2,1)S(1)}, u32[]{:S(2)}, u32[]{:S(2)}) %collective-permute-start) | collective-permute-done | bytes 663584 | tf_op jit(solution)/shard_map/ppermute | solution.py:259
  22.0 3.4 %collective-permute-start.6 = (bf16[256,1152]{1,0:T(8,128)(2,1)S(1)}, bf16[256,1152]{1,0:T(8,128)(2,1)S(1)}, u32[]{:S(2)}, u32[]{:S(2)}) collective-permute-start(bf16[256,1152]{1,0:T(8,128)(2,1)S(1)} %constant_dynamic-update-slice_fusion), channel_id=1, source_target_pairs={{64,0},{18,2},{65,1},{22,3},{68,4},{19,6},{69,5},{23,7},{72,8},{26... | collective-permute-start | bytes 1769480 | tf_op jit(solution)/shard_map/ppermute | solution.py:262
  25.3 10.9 %collective-permute-done.1.far_bottom = bf16[288,1152]{1,0:T(8,128)(2,1)S(1)} collective-permute-done((bf16[288,1152]{1,0:T(8,128)(2,1)S(1)}, bf16[288,1152]{1,0:T(8,128)(2,1)S(1)}, u32[]{:S(2)}, u32[]{:S(2)}) %collective-permute-start.1) | collective-permute-done | bytes 663584 | tf_op jit(solution)/shard_map/ppermute | solution.py:260
  36.2 0.0 collective-permute-done.3.one
  36.2 0.0 collective-permute-done.4.two
  36.2 2.7 %embed_first.1 = (bf16[512,1152]{1,0:T(8,128)(2,1)S(1)}, bf16[512,1152]{1,0:T(8,128)(2,1)S(1)}, bf16[4,2,144,512]{3,2,1,0:T(8,128)(2,1)S(1)}, bf16[1152,1152]{1,0:T(8,128)(2,1)S(1)}) custom-call(bf16[288,1152]{1,0:T(8,128)(2,1)S(1)} %get-tuple-element.23.top, bf16[288,1152]{1,0:T(8,128)(2,1)S(1)} %get-tuple-element.24.bottom, ...), custom_call_target="tpu_custom_call" | custom-call | flops 1358954496 | bytes 10027008 | tf_op jit(solution)/shard_map/embed_first/pallas_call | solution.py:228
  38.9 1.8 %collective-permute-start.7 = (bf16[512,1152]{1,0:T(8,128)(2,1)S(1)}, bf16[512,1152]{1,0:T(8,128)(2,1)S(1)}, u32[]{:S(2)}, u32[]{:S(2)}) collective-permute-start(bf16[512,1152]{1,0:T(8,128)(2,1)S(1)} %get-tuple-element.30.emb_a), channel_id=1, source_target_pairs={{0,2},{2,0},{1,3},{3,1},{4,6},{6,4},{5,7},{7,5},{8,10},{10,8},{9,1... | collective-permute-start | bytes 3538952 | tf_op jit(solution)/shard_map/ppermute | solution.py:249
  40.7 0.0 collective-permute-done.5.one
  40.7 0.0 collective-permute-done.6.two
  40.7 2.6 %embed_second.1 = (bf16[512,1152]{1,0:T(8,128)(2,1)S(1)}, bf16[512,1152]{1,0:T(8,128)(2,1)S(1)}, bf16[4,2,144,512]{3,2,1,0:T(8,128)(2,1)S(1)}) custom-call(bf16[1152,1152]{1,0:T(8,128)(2,1)S(1)} %get-tuple-element.28.head_ref, bf16[256,1152]{1,0:T(8,128)(2,1)S(1)} %collective-permute-done.5.one, bf16[256,1152]{1,0:T(8,128)(2,1)S(1)} %collective-permute-done.6.two), custom_call_target="tpu_custom_call" | custom-call | flops 1358954496 | bytes 7372800 | tf_op jit(solution)/shard_map/embed_second/pallas_call | solution.py:228
  43.4 0.3 collective-permute-start.8
  43.7 0.0 collective-permute-done.7.far_a
  43.7 2.8 %collective-permute-done.8.far_b = bf16[512,1152]{1,0:T(8,128)(2,1)S(1)} collective-permute-done((bf16[512,1152]{1,0:T(8,128)(2,1)S(1)}, bf16[512,1152]{1,0:T(8,128)(2,1)S(1)}, u32[]{:S(2)}, u32[]{:S(2)}) %collective-permute-start.8) | collective-permute-done | bytes 1179680 | tf_op jit(solution)/shard_map/ppermute | solution.py:249
  46.5 7.2 %score.1 = (bf16[512,1152]{1,0:T(8,128)(2,1)S(1)}, bf16[512,1152]{1,0:T(8,128)(2,1)S(1)}) custom-call(bf16[512,1152]{1,0:T(8,128)(2,1)S(1)} %get-tuple-element.30.emb_a, bf16[512,1152]{1,0:T(8,128)(2,1)S(1)} %get-tuple-element.31.emb_b, bf16[512,1152]{1,0:T(8,128)(2,1)S(1)} %collective-permute-done.7.far_a, ...), custom_call_target="tpu_custom_call" | custom-call | flops 4831838208 | bytes 9437184 | tf_op jit(solution)/shard_map/score/pallas_call | solution.py:228
  53.7 2.3 %terms_first.1 = (bf16[144,1152]{1,0:T(8,128)(2,1)S(1)}, bf16[144,1152]{1,0:T(8,128)(2,1)S(1)}, bf16[144,1152]{1,0:T(8,128)(2,1)S(1)}, bf16[144,1152]{1,0:T(8,128)(2,1)S(1)}) custom-call(bf16[4,2,144,512]{3,2,1,0:T(8,128)(2,1)S(1)} %get-tuple-element.27.refs_0_, bf16[4,2,144,512]{3,2,1,0:T(8,128)(2,1)S(1)} %get-tuple-element.29.refs_1_, ...), custom_call_target="tpu_custom_call" | custom-call | flops 1358954496 | bytes 6045696 | tf_op jit(solution)/shard_map/terms_first/pallas_call | solution.py:228
  56.0 1.6 %collective-permute-start.9 = (bf16[144,1152]{1,0:T(8,128)(2,1)S(1)}, bf16[144,1152]{1,0:T(8,128)(2,1)S(1)}, u32[]{:S(2)}, u32[]{:S(2)}) collective-permute-start(bf16[144,1152]{1,0:T(8,128)(2,1)S(1)} %get-tuple-element.36), channel_id=1, source_target_pairs={{0,32},{2,10},{1,33},{3,11},{4,36},{6,14},{5,37},{7,15},{8,40},{10... | collective-permute-start | bytes 995336 | tf_op jit(solution)/shard_map/ppermute | solution.py:300
  57.6 3.7 %collective-permute-start.10 = (bf16[144,1152]{1,0:T(8,128)(2,1)S(1)}, bf16[144,1152]{1,0:T(8,128)(2,1)S(1)}, u32[]{:S(2)}, u32[]{:S(2)}) collective-permute-start(bf16[144,1152]{1,0:T(8,128)(2,1)S(1)} %get-tuple-element.37), channel_id=1, source_target_pairs={{0,33},{2,14},{1,32},{3,15},{4,37},{6,10},{5,36},{7,11},{8,41},{10... | collective-permute-start | bytes 995336 | tf_op jit(solution)/shard_map/ppermute | solution.py:300
  61.3 1.4 %collective-permute-start.11 = (bf16[144,1152]{1,0:T(8,128)(2,1)S(1)}, bf16[144,1152]{1,0:T(8,128)(2,1)S(1)}, u32[]{:S(2)}, u32[]{:S(2)}) collective-permute-start(bf16[144,1152]{1,0:T(8,128)(2,1)S(1)} %get-tuple-element.38), channel_id=1, source_target_pairs={{0,96},{2,26},{1,97},{3,27},{4,100},{6,30},{5,101},{7,31},{8,104},... | collective-permute-start | bytes 995336 | tf_op jit(solution)/shard_map/ppermute | solution.py:300
  62.7 0.2 collective-permute-start.12
  63.0 2.3 %terms_second.1 = (bf16[144,1152]{1,0:T(8,128)(2,1)S(1)}, bf16[144,1152]{1,0:T(8,128)(2,1)S(1)}, bf16[144,1152]{1,0:T(8,128)(2,1)S(1)}, bf16[144,1152]{1,0:T(8,128)(2,1)S(1)}) custom-call(bf16[4,2,144,512]{3,2,1,0:T(8,128)(2,1)S(1)} %get-tuple-element.27.refs_0_, bf16[4,2,144,512]{3,2,1,0:T(8,128)(2,1)S(1)} %get-tuple-element.29.refs_1_, ...), custom_call_target="tpu_custom_call" | custom-call | flops 1358954496 | bytes 6045696 | tf_op jit(solution)/shard_map/terms_second/pallas_call | solution.py:228
  65.2 2.8 %collective-permute-start.13 = (bf16[144,1152]{1,0:T(8,128)(2,1)S(1)}, bf16[144,1152]{1,0:T(8,128)(2,1)S(1)}, u32[]{:S(2)}, u32[]{:S(2)}) collective-permute-start(bf16[144,1152]{1,0:T(8,128)(2,1)S(1)} %get-tuple-element.41), channel_id=1, source_target_pairs={{0,1},{2,6},{1,0},{3,7},{4,5},{6,2},{5,4},{7,3},{8,9},{10,14},{9,8... | collective-permute-start | bytes 995336 | tf_op jit(solution)/shard_map/ppermute | solution.py:300
  68.1 0.0 collective-permute-done.9.refs_0_
  68.1 1.6 %collective-permute-start.14 = (bf16[144,1152]{1,0:T(8,128)(2,1)S(1)}, bf16[144,1152]{1,0:T(8,128)(2,1)S(1)}, u32[]{:S(2)}, u32[]{:S(2)}) collective-permute-start(bf16[144,1152]{1,0:T(8,128)(2,1)S(1)} %get-tuple-element.42), channel_id=1, source_target_pairs={{0,64},{2,18},{1,65},{3,19},{4,68},{6,22},{5,69},{7,23},{8,72},{10... | collective-permute-start | bytes 995336 | tf_op jit(solution)/shard_map/ppermute | solution.py:300
  69.6 0.0 collective-permute-done.10.refs_1_
  69.6 4.7 %collective-permute-start.15 = (bf16[144,1152]{1,0:T(8,128)(2,1)S(1)}, bf16[144,1152]{1,0:T(8,128)(2,1)S(1)}, u32[]{:S(2)}, u32[]{:S(2)}) collective-permute-start(bf16[144,1152]{1,0:T(8,128)(2,1)S(1)} %get-tuple-element.43), channel_id=1, source_target_pairs={{0,65},{2,22},{1,64},{3,23},{4,69},{6,18},{5,68},{7,19},{8,73},{10... | collective-permute-start | bytes 995336 | tf_op jit(solution)/shard_map/ppermute | solution.py:300
  74.3 1.4 %collective-permute-done.12.refs_3_ = bf16[144,1152]{1,0:T(8,128)(2,1)S(1)} collective-permute-done((bf16[144,1152]{1,0:T(8,128)(2,1)S(1)}, bf16[144,1152]{1,0:T(8,128)(2,1)S(1)}, u32[]{:S(2)}, u32[]{:S(2)}) %collective-permute-start.12) | collective-permute-done | bytes 331808 | tf_op jit(solution)/shard_map/ppermute | solution.py:300
  75.7 7.1 %collective-permute-done.13.refs_5_ = bf16[144,1152]{1,0:T(8,128)(2,1)S(1)} collective-permute-done((bf16[144,1152]{1,0:T(8,128)(2,1)S(1)}, bf16[144,1152]{1,0:T(8,128)(2,1)S(1)}, u32[]{:S(2)}, u32[]{:S(2)}) %collective-permute-start.13) | collective-permute-done | bytes 331808 | tf_op jit(solution)/shard_map/ppermute | solution.py:300
  82.9 7.1 %collective-permute-done.15.refs_7_ = bf16[144,1152]{1,0:T(8,128)(2,1)S(1)} collective-permute-done((bf16[144,1152]{1,0:T(8,128)(2,1)S(1)}, bf16[144,1152]{1,0:T(8,128)(2,1)S(1)}, u32[]{:S(2)}, u32[]{:S(2)}) %collective-permute-start.15) | collective-permute-done | bytes 331808 | tf_op jit(solution)/shard_map/ppermute | solution.py:300
  90.0 1.2 %sum_terms.1 = bf16[8,18,1152]{2,1,0:T(8,128)(2,1)} custom-call(bf16[144,1152]{1,0:T(8,128)(2,1)S(1)} %collective-permute-done.9.refs_0_, bf16[144,1152]{1,0:T(8,128)(2,1)S(1)} %collective-permute-done.10.refs_1_, bf16[144,1152]{1,0:T(8,128)(2,1)S(1)} %collective-permute-done.11.refs_2_, bf16[144,1152]{1,0:T(8,128)(2,1)S(1)} %collective-permute-done.12.refs_3_, ...), custom_call_target="tpu_custom_call" | custom-call | bytes 2985984 | tf_op jit(solution)/shard_map/sum_terms/pallas_call | solution.py:228
  91.2 8.0 %all-to-all-start = ((bf16[8,18,1152]{2,1,0:T(8,128)(2,1)}), bf16[8,18,1152]{2,1,0:T(8,128)(2,1)S(1)}, u32[]{:S(2)}, u32[]{:S(2)}) async-start(bf16[8,18,1152]{2,1,0:T(8,128)(2,1)} %sum_terms.1), calls=%async_computation | async-start | bytes 884736 | tf_op jit(solution)/shard_map/all_to_all | solution.py:310
  99.2 7.8 %all-to-all-done = bf16[8,18,1152]{2,1,0:T(8,128)(2,1)S(1)} async-done(((bf16[8,18,1152]{2,1,0:T(8,128)(2,1)}), bf16[8,18,1152]{2,1,0:T(8,128)(2,1)S(1)}, u32[]{:S(2)}, u32[]{:S(2)}) %all-to-all-start) | async-done | bytes 331808 | tf_op jit(solution)/shard_map/all_to_all | solution.py:310
  107.0 0.1 convert_reduce_fusion
  107.1 0.1 slice_select_fusion
  107.2 3.5 %collective-permute-start.16 = (f32[18,576]{1,0:T(8,128)S(1)}, f32[18,576]{1,0:T(8,128)S(1)}, u32[]{:S(2)}, u32[]{:S(2)}) collective-permute-start(f32[18,576]{1,0:T(8,128)S(1)} %slice_select_fusion), channel_id=1, source_target_pairs={{0,2},{2,0},{1,3},{3,1},{4,6},{6,4},{5,7},{7,5},{8,10},{10,8},{9,1... | collective-permute-start | bytes 124424 | tf_op jit(solution)/shard_map/ppermute | solution.py:249
  110.7 0.9 collective-permute-done.16
  111.5 0.7 broadcast_select_fusion
  (6 shorter events, 0.1 us)
Async XLA Ops:
  2.7 2.2 %copy-start = (bf16[128,1152]{1,0:T(8,128)(2,1)S(1)}, bf16[128,1152]{1,0:T(8,128)(2,1)}, u32[]{:S(2)}) copy-start(bf16[128,1152]{1,0:T(8,128)(2,1)} %img_feats.1) | copy-start | bytes 884740
  2.7 2.2 %copy-start.1 = (bf16[128,1152]{1,0:T(8,128)(2,1)S(1)}, bf16[128,1152]{1,0:T(8,128)(2,1)}, u32[]{:S(2)}) copy-start(bf16[128,1152]{1,0:T(8,128)(2,1)} %txt_feats.1) | copy-start | bytes 884740
  5.7 16.2 %collective-permute-start = (bf16[288,1152]{1,0:T(8,128)(2,1)S(1)}, bf16[288,1152]{1,0:T(8,128)(2,1)S(1)}, u32[]{:S(2)}, u32[]{:S(2)}) collective-permute-start(bf16[288,1152]{1,0:T(8,128)(2,1)S(1)} %get-tuple-element.23.top), channel_id=1, source_target_pairs={{0,1},{2,3},{1,0},{3,2},{4,5},{6,7},{5,4},{7,6},{8,9},{10,11},{9,8... | collective-permute-start | bytes 1990664 | tf_op jit(solution)/shard_map/ppermute | solution.py:259
  7.8 2.2 %collective-permute-start.2 = (bf16[128,1152]{1,0:T(8,128)(2,1)S(1)}, bf16[128,1152]{1,0:T(8,128)(2,1)S(1)}, u32[]{:S(2)}, u32[]{:S(2)}) collective-permute-start(bf16[128,1152]{1,0:T(8,128)(2,1)S(1)} %get-tuple-element.26), channel_id=1, source_target_pairs={{0,2},{2,0},{1,3},{3,1},{4,6},{6,4},{5,7},{7,5},{8,10},{10,8},{9,1... | collective-permute-start | bytes 884744 | tf_op jit(solution)/shard_map/ppermute | solution.py:249
  8.8 27.4 %collective-permute-start.1 = (bf16[288,1152]{1,0:T(8,128)(2,1)S(1)}, bf16[288,1152]{1,0:T(8,128)(2,1)S(1)}, u32[]{:S(2)}, u32[]{:S(2)}) collective-permute-start(bf16[288,1152]{1,0:T(8,128)(2,1)S(1)} %get-tuple-element.24.bottom), channel_id=1, source_target_pairs={{0,1},{2,3},{1,0},{3,2},{4,5},{6,7},{5,4},{7,6},{8,9},{10,11},{9,8... | collective-permute-start | bytes 1990664 | tf_op jit(solution)/shard_map/ppermute | solution.py:260
  10.0 26.1 %collective-permute-start.3 = (bf16[256,1152]{1,0:T(8,128)(2,1)S(1)}, bf16[256,1152]{1,0:T(8,128)(2,1)S(1)}, u32[]{:S(2)}, u32[]{:S(2)}) collective-permute-start(bf16[256,1152]{1,0:T(8,128)(2,1)S(1)} %constant_dynamic-update-slice_fusion), channel_id=1, source_target_pairs={{32,0},{10,2},{33,1},{14,3},{36,4},{11,6},{37,5},{15,7},{40,8},{18... | collective-permute-start | bytes 1769480 | tf_op jit(solution)/shard_map/ppermute | solution.py:262
  12.9 23.3 %collective-permute-start.4 = (bf16[256,1152]{1,0:T(8,128)(2,1)S(1)}, bf16[256,1152]{1,0:T(8,128)(2,1)S(1)}, u32[]{:S(2)}, u32[]{:S(2)}) collective-permute-start(bf16[256,1152]{1,0:T(8,128)(2,1)S(1)} %constant_dynamic-update-slice_fusion), channel_id=1, source_target_pairs={{96,0},{26,2},{97,1},{30,3},{100,4},{27,6},{101,5},{31,7},{104,8},... | collective-permute-start | bytes 1769480 | tf_op jit(solution)/shard_map/ppermute | solution.py:262
  12.9 27.9 %collective-permute-start.5 = (bf16[256,1152]{1,0:T(8,128)(2,1)S(1)}, bf16[256,1152]{1,0:T(8,128)(2,1)S(1)}, u32[]{:S(2)}, u32[]{:S(2)}) collective-permute-start(bf16[256,1152]{1,0:T(8,128)(2,1)S(1)} %constant_dynamic-update-slice_fusion), channel_id=1, source_target_pairs={{0,0},{2,2},{1,1},{6,3},{4,4},{3,6},{5,5},{7,7},{8,8},{10,10},{9,9... | collective-permute-start | bytes 1769480 | tf_op jit(solution)/shard_map/ppermute | solution.py:262
  22.0 18.8 %collective-permute-start.6 = (bf16[256,1152]{1,0:T(8,128)(2,1)S(1)}, bf16[256,1152]{1,0:T(8,128)(2,1)S(1)}, u32[]{:S(2)}, u32[]{:S(2)}) collective-permute-start(bf16[256,1152]{1,0:T(8,128)(2,1)S(1)} %constant_dynamic-update-slice_fusion), channel_id=1, source_target_pairs={{64,0},{18,2},{65,1},{22,3},{68,4},{19,6},{69,5},{23,7},{72,8},{26... | collective-permute-start | bytes 1769480 | tf_op jit(solution)/shard_map/ppermute | solution.py:262
  38.9 4.8 %collective-permute-start.7 = (bf16[512,1152]{1,0:T(8,128)(2,1)S(1)}, bf16[512,1152]{1,0:T(8,128)(2,1)S(1)}, u32[]{:S(2)}, u32[]{:S(2)}) collective-permute-start(bf16[512,1152]{1,0:T(8,128)(2,1)S(1)} %get-tuple-element.30.emb_a), channel_id=1, source_target_pairs={{0,2},{2,0},{1,3},{3,1},{4,6},{6,4},{5,7},{7,5},{8,10},{10,8},{9,1... | collective-permute-start | bytes 3538952 | tf_op jit(solution)/shard_map/ppermute | solution.py:249
  43.4 3.1 %collective-permute-start.8 = (bf16[512,1152]{1,0:T(8,128)(2,1)S(1)}, bf16[512,1152]{1,0:T(8,128)(2,1)S(1)}, u32[]{:S(2)}, u32[]{:S(2)}) collective-permute-start(bf16[512,1152]{1,0:T(8,128)(2,1)S(1)} %get-tuple-element.31.emb_b), channel_id=1, source_target_pairs={{0,2},{2,0},{1,3},{3,1},{4,6},{6,4},{5,7},{7,5},{8,10},{10,8},{9,1... | collective-permute-start | bytes 3538952 | tf_op jit(solution)/shard_map/ppermute | solution.py:249
  56.0 12.1 %collective-permute-start.9 = (bf16[144,1152]{1,0:T(8,128)(2,1)S(1)}, bf16[144,1152]{1,0:T(8,128)(2,1)S(1)}, u32[]{:S(2)}, u32[]{:S(2)}) collective-permute-start(bf16[144,1152]{1,0:T(8,128)(2,1)S(1)} %get-tuple-element.36), channel_id=1, source_target_pairs={{0,32},{2,10},{1,33},{3,11},{4,36},{6,14},{5,37},{7,15},{8,40},{10... | collective-permute-start | bytes 995336 | tf_op jit(solution)/shard_map/ppermute | solution.py:300
  57.6 12.0 %collective-permute-start.10 = (bf16[144,1152]{1,0:T(8,128)(2,1)S(1)}, bf16[144,1152]{1,0:T(8,128)(2,1)S(1)}, u32[]{:S(2)}, u32[]{:S(2)}) collective-permute-start(bf16[144,1152]{1,0:T(8,128)(2,1)S(1)} %get-tuple-element.37), channel_id=1, source_target_pairs={{0,33},{2,14},{1,32},{3,15},{4,37},{6,10},{5,36},{7,11},{8,41},{10... | collective-permute-start | bytes 995336 | tf_op jit(solution)/shard_map/ppermute | solution.py:300
  61.3 13.0 %collective-permute-start.11 = (bf16[144,1152]{1,0:T(8,128)(2,1)S(1)}, bf16[144,1152]{1,0:T(8,128)(2,1)S(1)}, u32[]{:S(2)}, u32[]{:S(2)}) collective-permute-start(bf16[144,1152]{1,0:T(8,128)(2,1)S(1)} %get-tuple-element.38), channel_id=1, source_target_pairs={{0,96},{2,26},{1,97},{3,27},{4,100},{6,30},{5,101},{7,31},{8,104},... | collective-permute-start | bytes 995336 | tf_op jit(solution)/shard_map/ppermute | solution.py:300
  62.7 13.0 %collective-permute-start.12 = (bf16[144,1152]{1,0:T(8,128)(2,1)S(1)}, bf16[144,1152]{1,0:T(8,128)(2,1)S(1)}, u32[]{:S(2)}, u32[]{:S(2)}) collective-permute-start(bf16[144,1152]{1,0:T(8,128)(2,1)S(1)} %get-tuple-element.39), channel_id=1, source_target_pairs={{0,97},{2,30},{1,96},{3,31},{4,101},{6,26},{5,100},{7,27},{8,105},... | collective-permute-start | bytes 995336 | tf_op jit(solution)/shard_map/ppermute | solution.py:300
  65.2 17.6 %collective-permute-start.13 = (bf16[144,1152]{1,0:T(8,128)(2,1)S(1)}, bf16[144,1152]{1,0:T(8,128)(2,1)S(1)}, u32[]{:S(2)}, u32[]{:S(2)}) collective-permute-start(bf16[144,1152]{1,0:T(8,128)(2,1)S(1)} %get-tuple-element.41), channel_id=1, source_target_pairs={{0,1},{2,6},{1,0},{3,7},{4,5},{6,2},{5,4},{7,3},{8,9},{10,14},{9,8... | collective-permute-start | bytes 995336 | tf_op jit(solution)/shard_map/ppermute | solution.py:300
  68.1 14.8 %collective-permute-start.14 = (bf16[144,1152]{1,0:T(8,128)(2,1)S(1)}, bf16[144,1152]{1,0:T(8,128)(2,1)S(1)}, u32[]{:S(2)}, u32[]{:S(2)}) collective-permute-start(bf16[144,1152]{1,0:T(8,128)(2,1)S(1)} %get-tuple-element.42), channel_id=1, source_target_pairs={{0,64},{2,18},{1,65},{3,19},{4,68},{6,22},{5,69},{7,23},{8,72},{10... | collective-permute-start | bytes 995336 | tf_op jit(solution)/shard_map/ppermute | solution.py:300
  69.6 20.3 %collective-permute-start.15 = (bf16[144,1152]{1,0:T(8,128)(2,1)S(1)}, bf16[144,1152]{1,0:T(8,128)(2,1)S(1)}, u32[]{:S(2)}, u32[]{:S(2)}) collective-permute-start(bf16[144,1152]{1,0:T(8,128)(2,1)S(1)} %get-tuple-element.43), channel_id=1, source_target_pairs={{0,65},{2,22},{1,64},{3,23},{4,69},{6,18},{5,68},{7,19},{8,73},{10... | collective-permute-start | bytes 995336 | tf_op jit(solution)/shard_map/ppermute | solution.py:300
  91.2 15.9 %all-to-all-start = ((bf16[8,18,1152]{2,1,0:T(8,128)(2,1)}), bf16[8,18,1152]{2,1,0:T(8,128)(2,1)S(1)}, u32[]{:S(2)}, u32[]{:S(2)}) async-start(bf16[8,18,1152]{2,1,0:T(8,128)(2,1)} %sum_terms.1), calls=%async_computation | async-start | bytes 884736 | tf_op jit(solution)/shard_map/all_to_all | solution.py:310
  107.2 4.4 %collective-permute-start.16 = (f32[18,576]{1,0:T(8,128)S(1)}, f32[18,576]{1,0:T(8,128)S(1)}, u32[]{:S(2)}, u32[]{:S(2)}) collective-permute-start(f32[18,576]{1,0:T(8,128)S(1)} %slice_select_fusion), channel_id=1, source_target_pairs={{0,2},{2,0},{1,3},{3,1},{4,6},{6,4},{5,7},{7,5},{8,10},{10,8},{9,1... | collective-permute-start | bytes 124424 | tf_op jit(solution)/shard_map/ppermute | solution.py:249

commit v3 on v2

--- a/solution.py
+++ b/solution.py
@@ -19,36 +19,32 @@
 
 
 CHIPS = [(z, y, x) for z in range(RING) for y in range(RING) for x in range(RING)]
+
+
+def per_core(images, texts):
+    return [
+        (device(*chip, core), device(*to(*chip), core)) for chip in CHIPS for core, to in enumerate((images, texts))
+    ]
+
+
+def ring(turn):
+    return per_core(lambda z, y, x: (z - turn, y, x), lambda z, y, x: (z, y - turn, x))
+
+
+def reduce_pairs(turn, flip):
+    return per_core(
+        lambda z, y, x: (z + turn, y, x ^ flip), lambda z, y, x: (z, y + turn, 3 - x if flip else x)
+    )
+
+
 CORES_SWAP = [(device(*chip, core), device(*chip, 1 - core)) for chip in CHIPS for core in range(2)]
-TOWERS_SWAP = [(device(z, y, x, core), device(z, y, x ^ 1, core)) for z, y, x in CHIPS for core in range(2)]
-
-
-def gather_pairs(turn):
-    source = (0, 2, 1, 3)
-    pairs = []
-    for z, y, x in CHIPS:
-        pairs.append((device(z + turn, y, x, 0), device(z, y, x, 0)))
-        pairs.append((device(z, y + turn, source[x], 1), device(z, y, x, 1)))
-    return pairs
-
-
-def reduce_pairs(turn, flip):
-    pairs = []
-    for z, y, x in CHIPS:
-        pairs.append((device(z, y, x, 0), device(z + turn, y, x ^ flip, 0)))
-        pairs.append((device(z, y, x, 1), device(z, y + turn, x ^ (2 * flip), 1)))
-    return pairs
-
+NEAR_SWAP = per_core(*[lambda z, y, x: (z, y, x ^ 1)] * 2)
+FAR_SWAP = per_core(*[lambda z, y, x: (z, y, 3 - x)] * 2)
+TEXTS_SWAP = per_core(lambda z, y, x: (z, y, x), lambda z, y, x: (z, y, 3 - x))
 
 REDUCE_GROUPS = [
-    [device(z, y, 2 * high + tower, 0) for y in range(RING) for high in range(2)]
-    for z in range(RING)
-    for tower in range(2)
-] + [
-    [device(z, y, 2 * high + tower, 1) for z in range(RING) for tower in range(2)]
-    for y in range(RING)
-    for high in range(2)
-]
+    [device(z, y, x, 0) for y in range(RING) for x in pair] for z in range(RING) for pair in ((0, 3), (1, 2))
+] + [[device(z, y, x, 1) for z in range(RING) for x in pair] for y in range(RING) for pair in ((0, 1), (2, 3))]
 
 
 def position():
@@ -66,33 +62,26 @@
     return pl.BlockSpec(memory_space=pltpu.VMEM)
 
 
-def pick_kernel(img_feats, txt_feats, img_proj, txt_proj, mine, give, top, bottom, head, sems):
+def pick_kernel(img_feats, txt_feats, img_head, txt_head, mine, give, top, bottom, sems):
     core = position()[3]
-
-    def copies(feats, other, proj):
-        return [
-            pltpu.make_async_copy(proj, head, sems.at[0]),
-            pltpu.make_async_copy(other, give, sems.at[1]),
-            pltpu.make_async_copy(feats, mine, sems.at[2]),
-        ]
+    part = top.shape[0]
+
+    def copies(feats, other, head):
+        moves = ((other, give), (head.at[:part], top), (head.at[part:], bottom), (feats, mine))
+        return [pltpu.make_async_copy(*move, sems.at[i]) for i, move in enumerate(moves)]
 
     @pl.when(core == 0)
     def _():
-        for copy in copies(img_feats, txt_feats, img_proj):
+        for copy in copies(img_feats, txt_feats, img_head):
             copy.start()
 
     @pl.when(core == 1)
     def _():
-        for copy in copies(txt_feats, img_feats, txt_proj):
+        for copy in copies(txt_feats, img_feats, txt_head):
             copy.start()
 
-    for copy in copies(img_feats, txt_feats, img_proj):
+    for copy in copies(img_feats, txt_feats, img_head):
         copy.wait()
-    part, width = top.shape[0], head.shape[1]
-    top[:, :width] = head[:part, :]
-    bottom[:, :width] = head[part : 2 * part, :]
-    top[:, width:] = head[2 * part : 3 * part, :]
-    bottom[:, width:] = head[3 * part :, :]
 
 
 def flip_rows(feats, flip_ref, lane):
@@ -126,28 +115,26 @@
     raw_ref[here, :] = raw
 
 
-def embed_first_kernel(top, bottom, far_top, far_bottom, one, two, emb_ref, raw_ref, flip_ref, head_ref):
-    part, width = top.shape[0], top.shape[1] // 2
-    for column, (upper, lower) in ((0, (top, bottom)), (width, (far_top, far_bottom))):
-        head_ref[0:part, column : column + width] = upper[:, :width]
-        head_ref[part : 2 * part, column : column + width] = lower[:, :width]
-        head_ref[2 * part : 3 * part, column : column + width] = upper[:, width:]
-        head_ref[3 * part :, column : column + width] = lower[:, width:]
-    rows = one.shape[0]
-    for i, unit in enumerate((one, two)):
-        embed_rows(unit[...], head_ref[...], pl.ds(i * rows, rows), emb_ref, raw_ref)
-        flip_rows(unit[...], flip_ref, i * rows)
-
-
-def embed_second_kernel(head_ref, one, two, emb_ref, raw_ref, flip_ref):
-    rows = one.shape[0]
-    for i, unit in enumerate((one, two)):
-        embed_rows(unit[...], head_ref[...], pl.ds(i * rows, rows), emb_ref, raw_ref)
-        flip_rows(unit[...], flip_ref, i * rows)
+def embed_units(head, units, emb_ref, raw_ref, flip_ref):
+    rows = units[0].shape[0]
+    for i in range(0, len(units), 2):
+        feats = jnp.concatenate([units[i][...], units[i + 1][...]], axis=0)
+        embed_rows(feats, head, pl.ds(i * rows, 2 * rows), emb_ref, raw_ref)
+        flip_rows(feats, flip_ref, i * rows)
+
+
+def embed_first_kernel(top, bottom, far_top, far_bottom, *refs):
+    *units, emb_ref, raw_ref, flip_ref, head_ref = refs
+    head_ref[...] = jnp.concatenate([top[...], bottom[...], far_top[...], far_bottom[...]], axis=0).T
+    embed_units(head_ref[...], units, emb_ref, raw_ref, flip_ref)
+
+
+def embed_second_kernel(head_ref, *refs):
+    *units, emb_ref, raw_ref, flip_ref = refs
+    embed_units(head_ref[...], units, emb_ref, raw_ref, flip_ref)
 
 
 def score_kernel(emb_a, emb_b, far_a, far_b, raw_a, raw_b, grad_a, grad_b, turned_a, turned_b):
-    _, _, high, _, tower = position()
     turned_a[...] = far_a[...].T
     turned_b[...] = far_b[...].T
     rows = emb_a.shape[0] // 2
@@ -158,19 +145,21 @@
     for emb, raw, grad, i in ((emb_a, raw_a, grad_a, 0), (emb_a, raw_a, grad_a, 1), (emb_b, raw_b, grad_b, 0), (emb_b, raw_b, grad_b, 1)):
         here = pl.ds(i * rows, rows)
         own = emb[here, :]
-        coef_a = coef(jnp.dot(own, turned_a[...], preferred_element_type=F32))
+        logits_a = jnp.dot(own, turned_a[...], preferred_element_type=F32)
+        coef_a = coef(logits_a)
+        if emb is emb_a and i == 0:
+            block = rows // 2
+            match = lax.broadcasted_iota(jnp.int32, (block, block), 0) == lax.broadcasted_iota(
+                jnp.int32, (block, block), 1
+            )
+            logits = logit_scale * logits_a[:block, :block] + logit_bias
+            value = logit_scale / (1.0 + jnp.exp(jnp.where(match, logits, -logits)))
+            upper = jnp.concatenate(
+                [jnp.where(match, -value, value).astype(BF16), coef_a[:block, block:]], axis=1
+            )
+            coef_a = jnp.concatenate([upper, coef_a[block:, :]], axis=0)
         logits_b = jnp.dot(own, turned_b[...], preferred_element_type=F32)
-        if emb is emb_b and i == 0:
-            row = lax.broadcasted_iota(jnp.int32, (rows, rows), 0)
-            column = lax.broadcasted_iota(jnp.int32, (rows, rows), 1)
-            match = (jnp.abs(row - column) == rows // 2) & (high == tower)
-            logits = logit_scale * logits_b[:, :rows] + logit_bias
-            value = logit_scale / (1.0 + jnp.exp(jnp.where(match, logits, -logits)))
-            coef_b = jnp.concatenate(
-                [jnp.where(match, -value, value).astype(BF16), coef(logits_b[:, rows:])], axis=1
-            )
-        else:
-            coef_b = coef(logits_b)
+        coef_b = coef(logits_b)
         direction = jnp.dot(coef_a, far_a[...], preferred_element_type=F32) + jnp.dot(
             coef_b, far_b[...], preferred_element_type=F32
         )
@@ -192,17 +181,17 @@
         term = term.astype(BF16)
         straight, crossed = pieces[2 * k], pieces[2 * k + 1]
         straight[:, :width] = term[:half, :width]
-        crossed[:, width:] = term[half:, width:]
+        crossed[:, width:] = term[half:, :width]
 
         @pl.when(core == 0)
         def _():
-            straight[:, width:] = term[half:, :width]
+            straight[:, width:] = term[half:, width:]
             crossed[:, :width] = term[:half, width:]
 
         @pl.when(core == 1)
         def _():
             straight[:, width:] = term[:half, width:]
-            crossed[:, :width] = term[half:, :width]
+            crossed[:, :width] = term[half:, width:]
 
 
 def sum_kernel(*refs):
@@ -241,8 +230,7 @@
     rows, depth = img_feats.shape
     width = img_proj.shape[1]
     full = 2 * width
-    unit = 2 * rows
-    pair = 2 * unit
+    pair = RING * rows
     part = depth // (2 * RING * RING)
 
     def swap(value):
@@ -251,15 +239,22 @@
     mine, give, top, bottom = kernel_call(
         pick_kernel,
         "pick",
-        [((rows, depth), BF16)] * 2 + [((depth // 4, full), BF16)] * 2,
-        (img_feats, txt_feats, img_proj, txt_proj),
-        scratch=(pltpu.VMEM((depth, width), BF16), pltpu.SemaphoreType.DMA((3,))),
+        [((rows, depth), BF16)] * 2 + [((width // 2, depth), BF16)] * 2,
+        (img_feats, txt_feats, img_proj.T, txt_proj.T),
+        scratch=(pltpu.SemaphoreType.DMA((4,)),),
         specs=[pl.BlockSpec(memory_space=pl.ANY)] * 4,
     )
-    far_top = lax.ppermute(top, AXES, TOWERS_SWAP)
-    far_bottom = lax.ppermute(bottom, AXES, TOWERS_SWAP)
-    own = jnp.concatenate([mine, swap(give)], axis=0)
-    units = [lax.ppermute(own, AXES, gather_pairs(turn)) for turn in range(RING)]
+    other = swap(give)
+    _, _, high, core, tower = position()
+    is_mine = (high == tower).astype(jnp.int32) == core
+    straight = jnp.where(is_mine, mine, other)
+    crossed = jnp.where((core == 0) & is_mine, other, jnp.where((core == 0) | is_mine, mine, other))
+    crossed = lax.ppermute(crossed, AXES, TEXTS_SWAP)
+    turns = (0, 1, 3, 2)
+    units_a = [lax.ppermute(straight, AXES, ring(turn)) if turn else straight for turn in turns]
+    far_top = lax.ppermute(top, AXES, NEAR_SWAP)
+    far_bottom = lax.ppermute(bottom, AXES, FAR_SWAP)
+    units_b = [lax.ppermute(crossed, AXES, ring(turn)) if turn else crossed for turn in turns]
 
     flips = ((RING, 2, RING * part, pair), BF16)
     block = ((pair, full), BF16)
@@ -268,12 +263,12 @@
         embed_first_kernel,
         "embed_first",
         [block, block, flips, ((depth, full), BF16)],
-        (top, bottom, far_top, far_bottom, units[1], units[3]),
+        (top, bottom, far_top, far_bottom, *units_a),
         flops=work,
     )
     far_a = swap(emb_a)
     emb_b, raw_b, flip_b = kernel_call(
-        embed_second_kernel, "embed_second", [block, block, flips], (head, units[0], units[2]), flops=work
+        embed_second_kernel, "embed_second", [block, block, flips], (head, *units_b), flops=work
     )
     far_b = swap(emb_b)
     grad_a, grad_b = kernel_call(

time: 113 us -> 94.8 us (0.84)
  waiting for transfers between devices: 47.5 us -> 16.7 us
  blocking collectives: 0 us -> 12 us
    ppermute x6 -> x9, waiting for transfers between devices: 19.3 us -> 6.36 us  [the longest x3 3.4 us: local(): lax.ppermute(straight, AXES, ring(turn))]
    all_to_all x0 -> x1, blocking collectives: none -> 12 us  [local(): lax.all_to_all(sums, AXES, 0, 0, axis_index_groups=REDUCE_GROUPS, tiled=T...]
    ppermute x7, waiting for transfers between devices: 15.6 us -> 5.37 us  [send(): lax.ppermute(pieces[2 * k + flip], AXES, reduce_pairs(turn, flip))]
    ppermute x6 -> x9, starting transfers between devices: 9.14 us -> 18.4 us  [the longest x3 6.84 us: local(): lax.ppermute(crossed, AXES, ring(turn))]
    all_to_all x1 -> x0, starting transfers between devices: 8.04 us -> none  [local(): lax.all_to_all(sums, AXES, 0, 0, axis_index_groups=REDUCE_GROUPS, tiled=T...]
    all_to_all x1 -> x0, waiting for transfers between devices: 7.84 us -> none  [local(): lax.all_to_all(sums, AXES, 0, 0, axis_index_groups=REDUCE_GROUPS, tiled=T...]
    unnamed x7 -> x8, local copies, waits for them, and re-layouts: 4.26 us -> 4.56 us
  transfers between devices with their start and end apart: 18 -> 20, of which waited for: 9 -> 9; matrix products, arithmetic and copies ran while one was open for 0% -> 0% of each run, Pallas kernels for 7% -> 8%
where the time goes in v3:
time: 94.8 us; the launch traced here: 93.5 us
  starting transfers between devices  40.2 us (42%)
  Pallas kernels  18.3 us (19%)
  waiting for transfers between devices  16.7 us (18%)
  blocking collectives  12 us (13%)
  local copies, waits for them, and re-layouts  4.56 us (5%)
  other arithmetic  0.95 us (1%)
    pallas_call x7, Pallas kernels, kernel_call(): pl.pallas_call(body, out_shape=shapes, in_specs=[vmem()] * len(operands)...  18.3 us
    ppermute x7, starting transfers between devices, send(): lax.ppermute(pieces[2 * k + flip], AXES, reduce_pairs(turn, flip))  15.1 us
    all_to_all x1, blocking collectives, local(): lax.all_to_all(sums, AXES, 0, 0, axis_index_groups=REDUCE_GROUPS, tiled=T...  12 us
    ppermute x3, starting transfers between devices, local(): lax.ppermute(crossed, AXES, ring(turn))  6.84 us
    ppermute x4, starting transfers between devices, swap(): return lax.ppermute(value, AXES, CORES_SWAP)  6.7 us
    ppermute x3, starting transfers between devices, local(): lax.ppermute(straight, AXES, ring(turn))  6.22 us
    ppermute x7, waiting for transfers between devices, send(): lax.ppermute(pieces[2 * k + flip], AXES, reduce_pairs(turn, flip))  5.37 us
    ppermute x4, waiting for transfers between devices, swap(): return lax.ppermute(value, AXES, CORES_SWAP)  4.93 us
  transfers between devices with their start and end apart: 20, of which 9 were waited for; matrix products, arithmetic and copies ran while one was open for 0% of the time, Pallas kernels for 8%

profile of v3, /device:TPU:1, one launch (start us, length us, event | category | flops | bytes accessed | tf_op | source)
XLA Modules:
  0.0 93.5 jit_solution(10011822917636357294)
XLA Ops:
  0.6 1.3 %copy-done = bf16[1152,576]{0,1:T(8,128)(2,1)S(1)} copy-done((bf16[1152,576]{0,1:T(8,128)(2,1)S(1)}, bf16[1152,576]{0,1:T(8,128)(2,1)}, u32[]{:S(2)}) %copy-start) | copy-done | bytes 1327128
  2.0 1.3 %copy-done.1 = bf16[1152,576]{0,1:T(8,128)(2,1)S(1)} copy-done((bf16[1152,576]{0,1:T(8,128)(2,1)S(1)}, bf16[1152,576]{0,1:T(8,128)(2,1)}, u32[]{:S(2)}) %copy-start.1) | copy-done | bytes 1327128
  3.3 1.0 %copy-done.2 = bf16[128,1152]{1,0:T(8,128)(2,1)S(1)} copy-done((bf16[128,1152]{1,0:T(8,128)(2,1)S(1)}, bf16[128,1152]{1,0:T(8,128)(2,1)}, u32[]{:S(2)}) %copy-start.2) | copy-done | bytes 294936
  4.2 1.0 %copy-done.3 = bf16[128,1152]{1,0:T(8,128)(2,1)S(1)} copy-done((bf16[128,1152]{1,0:T(8,128)(2,1)S(1)}, bf16[128,1152]{1,0:T(8,128)(2,1)}, u32[]{:S(2)}) %copy-start.3) | copy-done | bytes 294936
  5.2 0.6 pick.1
  5.8 1.5 %collective-permute-start.2 = (bf16[128,1152]{1,0:T(8,128)(2,1)S(1)}, bf16[128,1152]{1,0:T(8,128)(2,1)S(1)}, u32[]{:S(2)}, u32[]{:S(2)}) collective-permute-start(bf16[128,1152]{1,0:T(8,128)(2,1)S(1)} %get-tuple-element.26), channel_id=1, source_target_pairs={{0,2},{2,0},{1,3},{3,1},{4,6},{6,4},{5,7},{7,5},{8,10},{10,8},{9,1... | collective-permute-start | bytes 884744 | tf_op jit(solution)/shard_map/ppermute | solution.py:237
  7.3 1.2 %collective-permute-done.2 = bf16[128,1152]{1,0:T(8,128)(2,1)S(1)} collective-permute-done((bf16[128,1152]{1,0:T(8,128)(2,1)S(1)}, bf16[128,1152]{1,0:T(8,128)(2,1)S(1)}, u32[]{:S(2)}, u32[]{:S(2)}) %collective-permute-start.2) | collective-permute-done | bytes 294944 | tf_op jit(solution)/shard_map/ppermute | solution.py:237
  8.5 0.1 select_select_fusion
  8.6 4.5 %collective-permute-start.6 = (bf16[128,1152]{1,0:T(8,128)(2,1)S(1)}, bf16[128,1152]{1,0:T(8,128)(2,1)S(1)}, u32[]{:S(2)}, u32[]{:S(2)}) collective-permute-start(bf16[128,1152]{1,0:T(8,128)(2,1)S(1)} %get-tuple-element.44), channel_id=1, source_target_pairs={{0,0},{2,7},{1,1},{3,6},{4,4},{6,3},{5,5},{7,2},{8,8},{10,15},{9,9... | collective-permute-start | bytes 884744 | tf_op jit(solution)/shard_map/ppermute | solution.py:252
  13.1 0.1 collective-permute-start
  13.2 0.8 collective-permute-start.1
  13.9 2.9 %collective-permute-start.5 = (bf16[128,1152]{1,0:T(8,128)(2,1)S(1)}, bf16[128,1152]{1,0:T(8,128)(2,1)S(1)}, u32[]{:S(2)}, u32[]{:S(2)}) collective-permute-start(bf16[128,1152]{1,0:T(8,128)(2,1)S(1)} %get-tuple-element.45.refs_0_), channel_id=1, source_target_pairs={{0,64},{2,18},{1,65},{3,19},{4,68},{6,22},{5,69},{7,23},{8,72},{10... | collective-permute-start | bytes 884744 | tf_op jit(solution)/shard_map/ppermute | solution.py:254
  16.9 0.4 collective-permute-start.4
  17.3 2.1 %collective-permute-done.6.refs_0_ = bf16[128,1152]{1,0:T(8,128)(2,1)S(1)} collective-permute-done((bf16[128,1152]{1,0:T(8,128)(2,1)S(1)}, bf16[128,1152]{1,0:T(8,128)(2,1)S(1)}, u32[]{:S(2)}, u32[]{:S(2)}) %collective-permute-start.6) | collective-permute-done | bytes 294944 | tf_op jit(solution)/shard_map/ppermute | solution.py:252
  19.4 2.9 %collective-permute-start.3 = (bf16[128,1152]{1,0:T(8,128)(2,1)S(1)}, bf16[128,1152]{1,0:T(8,128)(2,1)S(1)}, u32[]{:S(2)}, u32[]{:S(2)}) collective-permute-start(bf16[128,1152]{1,0:T(8,128)(2,1)S(1)} %get-tuple-element.45.refs_0_), channel_id=1, source_target_pairs={{0,96},{2,26},{1,97},{3,27},{4,100},{6,30},{5,101},{7,31},{8,104},... | collective-permute-start | bytes 884744 | tf_op jit(solution)/shard_map/ppermute | solution.py:254
  22.3 0.0 collective-permute-done.5.refs_3_
  22.3 2.0 %collective-permute-start.9 = (bf16[128,1152]{1,0:T(8,128)(2,1)S(1)}, bf16[128,1152]{1,0:T(8,128)(2,1)S(1)}, u32[]{:S(2)}, u32[]{:S(2)}) collective-permute-start(bf16[128,1152]{1,0:T(8,128)(2,1)S(1)} %collective-permute-done.6.refs_0_), channel_id=1, source_target_pairs={{0,64},{2,18},{1,65},{3,19},{4,68},{6,22},{5,69},{7,23},{8,72},{10... | collective-permute-start | bytes 884744 | tf_op jit(solution)/shard_map/ppermute | solution.py:257
  24.3 0.2 collective-permute-done.4.refs_2_
  24.5 1.5 %collective-permute-start.8 = (bf16[128,1152]{1,0:T(8,128)(2,1)S(1)}, bf16[128,1152]{1,0:T(8,128)(2,1)S(1)}, u32[]{:S(2)}, u32[]{:S(2)}) collective-permute-start(bf16[128,1152]{1,0:T(8,128)(2,1)S(1)} %collective-permute-done.6.refs_0_), channel_id=1, source_target_pairs={{0,32},{2,10},{1,33},{3,11},{4,36},{6,14},{5,37},{7,15},{8,40},{10... | collective-permute-start | bytes 884744 | tf_op jit(solution)/shard_map/ppermute | solution.py:257
  25.9 3.2 %collective-permute-done.3.refs_1_ = bf16[128,1152]{1,0:T(8,128)(2,1)S(1)} collective-permute-done((bf16[128,1152]{1,0:T(8,128)(2,1)S(1)}, bf16[128,1152]{1,0:T(8,128)(2,1)S(1)}, u32[]{:S(2)}, u32[]{:S(2)}) %collective-permute-start.3) | collective-permute-done | bytes 294944 | tf_op jit(solution)/shard_map/ppermute | solution.py:254
  29.1 3.4 %collective-permute-start.7 = (bf16[128,1152]{1,0:T(8,128)(2,1)S(1)}, bf16[128,1152]{1,0:T(8,128)(2,1)S(1)}, u32[]{:S(2)}, u32[]{:S(2)}) collective-permute-start(bf16[128,1152]{1,0:T(8,128)(2,1)S(1)} %collective-permute-done.6.refs_0_), channel_id=1, source_target_pairs={{0,96},{2,26},{1,97},{3,27},{4,100},{6,30},{5,101},{7,31},{8,104},... | collective-permute-start | bytes 884744 | tf_op jit(solution)/shard_map/ppermute | solution.py:257
  32.6 2.7 %embed_first.1 = (bf16[512,1152]{1,0:T(8,128)(2,1)S(1)}, bf16[512,1152]{1,0:T(8,128)(2,1)S(1)}, bf16[4,2,144,512]{3,2,1,0:T(8,128)(2,1)S(1)}, bf16[1152,1152]{1,0:T(8,128)(2,1)S(1)}) custom-call(bf16[288,1152]{1,0:T(8,128)(2,1)S(1)} %get-tuple-element.23.top, bf16[288,1152]{1,0:T(8,128)(2,1)S(1)} %get-tuple-element.24.bottom, ...), custom_call_target="tpu_custom_call" | custom-call | flops 1358954496 | bytes 10027008 | tf_op jit(solution)/shard_map/embed_first/pallas_call | solution.py:217
  35.3 0.1 collective-permute-start.10
  35.4 0.0 collective-permute-done.9.refs_3_
  35.4 0.8 collective-permute-done.7.refs_1_
  36.2 2.7 %embed_second.1 = (bf16[512,1152]{1,0:T(8,128)(2,1)S(1)}, bf16[512,1152]{1,0:T(8,128)(2,1)S(1)}, bf16[4,2,144,512]{3,2,1,0:T(8,128)(2,1)S(1)}) custom-call(bf16[1152,1152]{1,0:T(8,128)(2,1)S(1)} %get-tuple-element.28.head_ref, bf16[128,1152]{1,0:T(8,128)(2,1)S(1)} %collective-permute-done.6.refs_0_, bf16[128,1152]{1,0:T(8,128)(2,1)S(1)} %collective-permute-done.7.refs_1_, ...), custom_call_target="tpu_custom_call" | custom-call | flops 1358954496 | bytes 7372800 | tf_op jit(solution)/shard_map/embed_second/pallas_call | solution.py:217
  38.9 0.3 collective-permute-start.11
  39.2 2.8 %collective-permute-done.11.far_b = bf16[512,1152]{1,0:T(8,128)(2,1)S(1)} collective-permute-done((bf16[512,1152]{1,0:T(8,128)(2,1)S(1)}, bf16[512,1152]{1,0:T(8,128)(2,1)S(1)}, u32[]{:S(2)}, u32[]{:S(2)}) %collective-permute-start.11) | collective-permute-done | bytes 1179680 | tf_op jit(solution)/shard_map/ppermute | solution.py:237
  42.0 7.1 %score.1 = (bf16[512,1152]{1,0:T(8,128)(2,1)S(1)}, bf16[512,1152]{1,0:T(8,128)(2,1)S(1)}) custom-call(bf16[512,1152]{1,0:T(8,128)(2,1)S(1)} %get-tuple-element.30.emb_a, bf16[512,1152]{1,0:T(8,128)(2,1)S(1)} %get-tuple-element.31.emb_b, bf16[512,1152]{1,0:T(8,128)(2,1)S(1)} %collective-permute-done.10.far_a, ...), custom_call_target="tpu_custom_call" | custom-call | flops 4831838208 | bytes 9437184 | tf_op jit(solution)/shard_map/score/pallas_call | solution.py:217
  49.1 2.4 %terms_second.1 = (bf16[144,1152]{1,0:T(8,128)(2,1)S(1)}, bf16[144,1152]{1,0:T(8,128)(2,1)S(1)}, bf16[144,1152]{1,0:T(8,128)(2,1)S(1)}, bf16[144,1152]{1,0:T(8,128)(2,1)S(1)}) custom-call(bf16[4,2,144,512]{3,2,1,0:T(8,128)(2,1)S(1)} %get-tuple-element.27.refs_0_, bf16[4,2,144,512]{3,2,1,0:T(8,128)(2,1)S(1)} %get-tuple-element.29.refs_1_, ...), custom_call_target="tpu_custom_call" | custom-call | flops 1358954496 | bytes 6045696 | tf_op jit(solution)/shard_map/terms_second/pallas_call | solution.py:217
  51.5 3.3 %collective-permute-start.16 = (bf16[144,1152]{1,0:T(8,128)(2,1)S(1)}, bf16[144,1152]{1,0:T(8,128)(2,1)S(1)}, u32[]{:S(2)}, u32[]{:S(2)}) collective-permute-start(bf16[144,1152]{1,0:T(8,128)(2,1)S(1)} %get-tuple-element.41), channel_id=1, source_target_pairs={{0,1},{2,7},{1,0},{3,6},{4,5},{6,3},{5,4},{7,2},{8,9},{10,15},{9,8... | collective-permute-start | bytes 995336 | tf_op jit(solution)/shard_map/ppermute | solution.py:295
  54.8 1.6 %collective-permute-start.17 = (bf16[144,1152]{1,0:T(8,128)(2,1)S(1)}, bf16[144,1152]{1,0:T(8,128)(2,1)S(1)}, u32[]{:S(2)}, u32[]{:S(2)}) collective-permute-start(bf16[144,1152]{1,0:T(8,128)(2,1)S(1)} %get-tuple-element.42), channel_id=1, source_target_pairs={{0,64},{2,18},{1,65},{3,19},{4,68},{6,22},{5,69},{7,23},{8,72},{10... | collective-permute-start | bytes 995336 | tf_op jit(solution)/shard_map/ppermute | solution.py:295
  56.4 1.2 %collective-permute-start.18 = (bf16[144,1152]{1,0:T(8,128)(2,1)S(1)}, bf16[144,1152]{1,0:T(8,128)(2,1)S(1)}, u32[]{:S(2)}, u32[]{:S(2)}) collective-permute-start(bf16[144,1152]{1,0:T(8,128)(2,1)S(1)} %get-tuple-element.43), channel_id=1, source_target_pairs={{0,65},{2,23},{1,64},{3,22},{4,69},{6,19},{5,68},{7,18},{8,73},{10... | collective-permute-start | bytes 995336 | tf_op jit(solution)/shard_map/ppermute | solution.py:295
  57.6 2.4 %terms_first.1 = (bf16[144,1152]{1,0:T(8,128)(2,1)S(1)}, bf16[144,1152]{1,0:T(8,128)(2,1)S(1)}, bf16[144,1152]{1,0:T(8,128)(2,1)S(1)}, bf16[144,1152]{1,0:T(8,128)(2,1)S(1)}) custom-call(bf16[4,2,144,512]{3,2,1,0:T(8,128)(2,1)S(1)} %get-tuple-element.27.refs_0_, bf16[4,2,144,512]{3,2,1,0:T(8,128)(2,1)S(1)} %get-tuple-element.29.refs_1_, ...), custom_call_target="tpu_custom_call" | custom-call | flops 1358954496 | bytes 6045696 | tf_op jit(solution)/shard_map/terms_first/pallas_call | solution.py:217
  60.0 1.0 %collective-permute-start.12 = (bf16[144,1152]{1,0:T(8,128)(2,1)S(1)}, bf16[144,1152]{1,0:T(8,128)(2,1)S(1)}, u32[]{:S(2)}, u32[]{:S(2)}) collective-permute-start(bf16[144,1152]{1,0:T(8,128)(2,1)S(1)} %get-tuple-element.36), channel_id=1, source_target_pairs={{0,32},{2,10},{1,33},{3,11},{4,36},{6,14},{5,37},{7,15},{8,40},{10... | collective-permute-start | bytes 995336 | tf_op jit(solution)/shard_map/ppermute | solution.py:295
  61.0 2.7 %collective-permute-start.13 = (bf16[144,1152]{1,0:T(8,128)(2,1)S(1)}, bf16[144,1152]{1,0:T(8,128)(2,1)S(1)}, u32[]{:S(2)}, u32[]{:S(2)}) collective-permute-start(bf16[144,1152]{1,0:T(8,128)(2,1)S(1)} %get-tuple-element.37), channel_id=1, source_target_pairs={{0,33},{2,15},{1,32},{3,14},{4,37},{6,11},{5,36},{7,10},{8,41},{10... | collective-permute-start | bytes 995336 | tf_op jit(solution)/shard_map/ppermute | solution.py:295
  63.7 0.0 collective-permute-done.16.refs_5_
  63.7 2.1 %collective-permute-start.14 = (bf16[144,1152]{1,0:T(8,128)(2,1)S(1)}, bf16[144,1152]{1,0:T(8,128)(2,1)S(1)}, u32[]{:S(2)}, u32[]{:S(2)}) collective-permute-start(bf16[144,1152]{1,0:T(8,128)(2,1)S(1)} %get-tuple-element.38), channel_id=1, source_target_pairs={{0,96},{2,26},{1,97},{3,27},{4,100},{6,30},{5,101},{7,31},{8,104},... | collective-permute-start | bytes 995336 | tf_op jit(solution)/shard_map/ppermute | solution.py:295
  65.8 3.3 %collective-permute-start.15 = (bf16[144,1152]{1,0:T(8,128)(2,1)S(1)}, bf16[144,1152]{1,0:T(8,128)(2,1)S(1)}, u32[]{:S(2)}, u32[]{:S(2)}) collective-permute-start(bf16[144,1152]{1,0:T(8,128)(2,1)S(1)} %get-tuple-element.39), channel_id=1, source_target_pairs={{0,97},{2,31},{1,96},{3,30},{4,101},{6,27},{5,100},{7,26},{8,105},... | collective-permute-start | bytes 995336 | tf_op jit(solution)/shard_map/ppermute | solution.py:295
  69.1 4.2 %collective-permute-done.12.refs_0_ = bf16[144,1152]{1,0:T(8,128)(2,1)S(1)} collective-permute-done((bf16[144,1152]{1,0:T(8,128)(2,1)S(1)}, bf16[144,1152]{1,0:T(8,128)(2,1)S(1)}, u32[]{:S(2)}, u32[]{:S(2)}) %collective-permute-start.12) | collective-permute-done | bytes 331808 | tf_op jit(solution)/shard_map/ppermute | solution.py:295
  73.3 1.1 %collective-permute-done.14.refs_2_ = bf16[144,1152]{1,0:T(8,128)(2,1)S(1)} collective-permute-done((bf16[144,1152]{1,0:T(8,128)(2,1)S(1)}, bf16[144,1152]{1,0:T(8,128)(2,1)S(1)}, u32[]{:S(2)}, u32[]{:S(2)}) %collective-permute-start.14) | collective-permute-done | bytes 331808 | tf_op jit(solution)/shard_map/ppermute | solution.py:295
  74.4 0.4 sum_terms.1
  74.9 12.0 %all_to_all.5 = bf16[8,18,1152]{2,1,0:T(8,128)(2,1)S(1)} all-to-all(bf16[8,18,1152]{2,1,0:T(8,128)(2,1)S(1)} %sum_terms.1), channel_id=1, replica_groups={{0,5,8,13,16,21,24,29},{1,4,9,12,17,20,25,28},{32,37,40,45,48,53,56,61}..., dimensions={0} | all-to-all | bytes 663552 | tf_op jit(solution)/shard_map/all_to_all | solution.py:305
  86.8 0.1 convert_reduce_fusion
  86.9 0.1 slice_select_fusion
  87.0 4.8 %collective-permute-start.19 = (f32[18,576]{1,0:T(8,128)S(1)}, f32[18,576]{1,0:T(8,128)S(1)}, u32[]{:S(2)}, u32[]{:S(2)}) collective-permute-start(f32[18,576]{1,0:T(8,128)S(1)} %slice_select_fusion), channel_id=1, source_target_pairs={{0,2},{2,0},{1,3},{3,1},{4,6},{6,4},{5,7},{7,5},{8,10},{10,8},{9,1... | collective-permute-start | bytes 124424 | tf_op jit(solution)/shard_map/ppermute | solution.py:237
  91.8 0.9 collective-permute-done.19
  92.7 0.7 broadcast_select_fusion.1
  (12 shorter events, 0.0 us)
Async XLA Ops:
  0.6 1.3 %copy-start = (bf16[1152,576]{0,1:T(8,128)(2,1)S(1)}, bf16[1152,576]{0,1:T(8,128)(2,1)}, u32[]{:S(2)}) copy-start(bf16[1152,576]{0,1:T(8,128)(2,1)} %param.6) | copy-start | bytes 3981316
  2.0 1.3 %copy-start.1 = (bf16[1152,576]{0,1:T(8,128)(2,1)S(1)}, bf16[1152,576]{0,1:T(8,128)(2,1)}, u32[]{:S(2)}) copy-start(bf16[1152,576]{0,1:T(8,128)(2,1)} %param.7) | copy-start | bytes 3981316
  3.3 1.0 %copy-start.2 = (bf16[128,1152]{1,0:T(8,128)(2,1)S(1)}, bf16[128,1152]{1,0:T(8,128)(2,1)}, u32[]{:S(2)}) copy-start(bf16[128,1152]{1,0:T(8,128)(2,1)} %img_feats.1) | copy-start | bytes 884740
  4.2 1.0 %copy-start.3 = (bf16[128,1152]{1,0:T(8,128)(2,1)S(1)}, bf16[128,1152]{1,0:T(8,128)(2,1)}, u32[]{:S(2)}) copy-start(bf16[128,1152]{1,0:T(8,128)(2,1)} %txt_feats.1) | copy-start | bytes 884740
  5.8 2.7 %collective-permute-start.2 = (bf16[128,1152]{1,0:T(8,128)(2,1)S(1)}, bf16[128,1152]{1,0:T(8,128)(2,1)S(1)}, u32[]{:S(2)}, u32[]{:S(2)}) collective-permute-start(bf16[128,1152]{1,0:T(8,128)(2,1)S(1)} %get-tuple-element.26), channel_id=1, source_target_pairs={{0,2},{2,0},{1,3},{3,1},{4,6},{6,4},{5,7},{7,5},{8,10},{10,8},{9,1... | collective-permute-start | bytes 884744 | tf_op jit(solution)/shard_map/ppermute | solution.py:237
  8.6 10.8 %collective-permute-start.6 = (bf16[128,1152]{1,0:T(8,128)(2,1)S(1)}, bf16[128,1152]{1,0:T(8,128)(2,1)S(1)}, u32[]{:S(2)}, u32[]{:S(2)}) collective-permute-start(bf16[128,1152]{1,0:T(8,128)(2,1)S(1)} %get-tuple-element.44), channel_id=1, source_target_pairs={{0,0},{2,7},{1,1},{3,6},{4,4},{6,3},{5,5},{7,2},{8,8},{10,15},{9,9... | collective-permute-start | bytes 884744 | tf_op jit(solution)/shard_map/ppermute | solution.py:252
  13.1 19.5 %collective-permute-start = (bf16[288,1152]{1,0:T(8,128)(2,1)S(1)}, bf16[288,1152]{1,0:T(8,128)(2,1)S(1)}, u32[]{:S(2)}, u32[]{:S(2)}) collective-permute-start(bf16[288,1152]{1,0:T(8,128)(2,1)S(1)} %get-tuple-element.23.top), channel_id=1, source_target_pairs={{0,1},{2,3},{1,0},{3,2},{4,5},{6,7},{5,4},{7,6},{8,9},{10,11},{9,8... | collective-permute-start | bytes 1990664 | tf_op jit(solution)/shard_map/ppermute | solution.py:255
  13.2 19.4 %collective-permute-start.1 = (bf16[288,1152]{1,0:T(8,128)(2,1)S(1)}, bf16[288,1152]{1,0:T(8,128)(2,1)S(1)}, u32[]{:S(2)}, u32[]{:S(2)}) collective-permute-start(bf16[288,1152]{1,0:T(8,128)(2,1)S(1)} %get-tuple-element.24.bottom), channel_id=1, source_target_pairs={{0,5},{2,7},{1,4},{3,6},{4,1},{6,3},{5,0},{7,2},{8,13},{10,15},{9,... | collective-permute-start | bytes 1990664 | tf_op jit(solution)/shard_map/ppermute | solution.py:256
  13.9 8.4 %collective-permute-start.5 = (bf16[128,1152]{1,0:T(8,128)(2,1)S(1)}, bf16[128,1152]{1,0:T(8,128)(2,1)S(1)}, u32[]{:S(2)}, u32[]{:S(2)}) collective-permute-start(bf16[128,1152]{1,0:T(8,128)(2,1)S(1)} %get-tuple-element.45.refs_0_), channel_id=1, source_target_pairs={{0,64},{2,18},{1,65},{3,19},{4,68},{6,22},{5,69},{7,23},{8,72},{10... | collective-permute-start | bytes 884744 | tf_op jit(solution)/shard_map/ppermute | solution.py:254
  16.9 7.6 %collective-permute-start.4 = (bf16[128,1152]{1,0:T(8,128)(2,1)S(1)}, bf16[128,1152]{1,0:T(8,128)(2,1)S(1)}, u32[]{:S(2)}, u32[]{:S(2)}) collective-permute-start(bf16[128,1152]{1,0:T(8,128)(2,1)S(1)} %get-tuple-element.45.refs_0_), channel_id=1, source_target_pairs={{0,32},{2,10},{1,33},{3,11},{4,36},{6,14},{5,37},{7,15},{8,40},{10... | collective-permute-start | bytes 884744 | tf_op jit(solution)/shard_map/ppermute | solution.py:254
  19.4 9.7 %collective-permute-start.3 = (bf16[128,1152]{1,0:T(8,128)(2,1)S(1)}, bf16[128,1152]{1,0:T(8,128)(2,1)S(1)}, u32[]{:S(2)}, u32[]{:S(2)}) collective-permute-start(bf16[128,1152]{1,0:T(8,128)(2,1)S(1)} %get-tuple-element.45.refs_0_), channel_id=1, source_target_pairs={{0,96},{2,26},{1,97},{3,27},{4,100},{6,30},{5,101},{7,31},{8,104},... | collective-permute-start | bytes 884744 | tf_op jit(solution)/shard_map/ppermute | solution.py:254
  22.3 13.1 %collective-permute-start.9 = (bf16[128,1152]{1,0:T(8,128)(2,1)S(1)}, bf16[128,1152]{1,0:T(8,128)(2,1)S(1)}, u32[]{:S(2)}, u32[]{:S(2)}) collective-permute-start(bf16[128,1152]{1,0:T(8,128)(2,1)S(1)} %collective-permute-done.6.refs_0_), channel_id=1, source_target_pairs={{0,64},{2,18},{1,65},{3,19},{4,68},{6,22},{5,69},{7,23},{8,72},{10... | collective-permute-start | bytes 884744 | tf_op jit(solution)/shard_map/ppermute | solution.py:257
  24.5 10.9 %collective-permute-start.8 = (bf16[128,1152]{1,0:T(8,128)(2,1)S(1)}, bf16[128,1152]{1,0:T(8,128)(2,1)S(1)}, u32[]{:S(2)}, u32[]{:S(2)}) collective-permute-start(bf16[128,1152]{1,0:T(8,128)(2,1)S(1)} %collective-permute-done.6.refs_0_), channel_id=1, source_target_pairs={{0,32},{2,10},{1,33},{3,11},{4,36},{6,14},{5,37},{7,15},{8,40},{10... | collective-permute-start | bytes 884744 | tf_op jit(solution)/shard_map/ppermute | solution.py:257
  29.1 7.1 %collective-permute-start.7 = (bf16[128,1152]{1,0:T(8,128)(2,1)S(1)}, bf16[128,1152]{1,0:T(8,128)(2,1)S(1)}, u32[]{:S(2)}, u32[]{:S(2)}) collective-permute-start(bf16[128,1152]{1,0:T(8,128)(2,1)S(1)} %collective-permute-done.6.refs_0_), channel_id=1, source_target_pairs={{0,96},{2,26},{1,97},{3,27},{4,100},{6,30},{5,101},{7,31},{8,104},... | collective-permute-start | bytes 884744 | tf_op jit(solution)/shard_map/ppermute | solution.py:257
  35.3 3.9 %collective-permute-start.10 = (bf16[512,1152]{1,0:T(8,128)(2,1)S(1)}, bf16[512,1152]{1,0:T(8,128)(2,1)S(1)}, u32[]{:S(2)}, u32[]{:S(2)}) collective-permute-start(bf16[512,1152]{1,0:T(8,128)(2,1)S(1)} %get-tuple-element.30.emb_a), channel_id=1, source_target_pairs={{0,2},{2,0},{1,3},{3,1},{4,6},{6,4},{5,7},{7,5},{8,10},{10,8},{9,1... | collective-permute-start | bytes 3538952 | tf_op jit(solution)/shard_map/ppermute | solution.py:237
  38.9 3.1 %collective-permute-start.11 = (bf16[512,1152]{1,0:T(8,128)(2,1)S(1)}, bf16[512,1152]{1,0:T(8,128)(2,1)S(1)}, u32[]{:S(2)}, u32[]{:S(2)}) collective-permute-start(bf16[512,1152]{1,0:T(8,128)(2,1)S(1)} %get-tuple-element.31.emb_b), channel_id=1, source_target_pairs={{0,2},{2,0},{1,3},{3,1},{4,6},{6,4},{5,7},{7,5},{8,10},{10,8},{9,1... | collective-permute-start | bytes 3538952 | tf_op jit(solution)/shard_map/ppermute | solution.py:237
  51.5 12.2 %collective-permute-start.16 = (bf16[144,1152]{1,0:T(8,128)(2,1)S(1)}, bf16[144,1152]{1,0:T(8,128)(2,1)S(1)}, u32[]{:S(2)}, u32[]{:S(2)}) collective-permute-start(bf16[144,1152]{1,0:T(8,128)(2,1)S(1)} %get-tuple-element.41), channel_id=1, source_target_pairs={{0,1},{2,7},{1,0},{3,6},{4,5},{6,3},{5,4},{7,2},{8,9},{10,15},{9,8... | collective-permute-start | bytes 995336 | tf_op jit(solution)/shard_map/ppermute | solution.py:295
  54.8 11.0 %collective-permute-start.17 = (bf16[144,1152]{1,0:T(8,128)(2,1)S(1)}, bf16[144,1152]{1,0:T(8,128)(2,1)S(1)}, u32[]{:S(2)}, u32[]{:S(2)}) collective-permute-start(bf16[144,1152]{1,0:T(8,128)(2,1)S(1)} %get-tuple-element.42), channel_id=1, source_target_pairs={{0,64},{2,18},{1,65},{3,19},{4,68},{6,22},{5,69},{7,23},{8,72},{10... | collective-permute-start | bytes 995336 | tf_op jit(solution)/shard_map/ppermute | solution.py:295
  56.4 12.6 %collective-permute-start.18 = (bf16[144,1152]{1,0:T(8,128)(2,1)S(1)}, bf16[144,1152]{1,0:T(8,128)(2,1)S(1)}, u32[]{:S(2)}, u32[]{:S(2)}) collective-permute-start(bf16[144,1152]{1,0:T(8,128)(2,1)S(1)} %get-tuple-element.43), channel_id=1, source_target_pairs={{0,65},{2,23},{1,64},{3,22},{4,69},{6,19},{5,68},{7,18},{8,73},{10... | collective-permute-start | bytes 995336 | tf_op jit(solution)/shard_map/ppermute | solution.py:295
  60.0 13.3 %collective-permute-start.12 = (bf16[144,1152]{1,0:T(8,128)(2,1)S(1)}, bf16[144,1152]{1,0:T(8,128)(2,1)S(1)}, u32[]{:S(2)}, u32[]{:S(2)}) collective-permute-start(bf16[144,1152]{1,0:T(8,128)(2,1)S(1)} %get-tuple-element.36), channel_id=1, source_target_pairs={{0,32},{2,10},{1,33},{3,11},{4,36},{6,14},{5,37},{7,15},{8,40},{10... | collective-permute-start | bytes 995336 | tf_op jit(solution)/shard_map/ppermute | solution.py:295
  61.0 12.3 %collective-permute-start.13 = (bf16[144,1152]{1,0:T(8,128)(2,1)S(1)}, bf16[144,1152]{1,0:T(8,128)(2,1)S(1)}, u32[]{:S(2)}, u32[]{:S(2)}) collective-permute-start(bf16[144,1152]{1,0:T(8,128)(2,1)S(1)} %get-tuple-element.37), channel_id=1, source_target_pairs={{0,33},{2,15},{1,32},{3,14},{4,37},{6,11},{5,36},{7,10},{8,41},{10... | collective-permute-start | bytes 995336 | tf_op jit(solution)/shard_map/ppermute | solution.py:295
  63.7 10.7 %collective-permute-start.14 = (bf16[144,1152]{1,0:T(8,128)(2,1)S(1)}, bf16[144,1152]{1,0:T(8,128)(2,1)S(1)}, u32[]{:S(2)}, u32[]{:S(2)}) collective-permute-start(bf16[144,1152]{1,0:T(8,128)(2,1)S(1)} %get-tuple-element.38), channel_id=1, source_target_pairs={{0,96},{2,26},{1,97},{3,27},{4,100},{6,30},{5,101},{7,31},{8,104},... | collective-permute-start | bytes 995336 | tf_op jit(solution)/shard_map/ppermute | solution.py:295
  65.8 8.6 %collective-permute-start.15 = (bf16[144,1152]{1,0:T(8,128)(2,1)S(1)}, bf16[144,1152]{1,0:T(8,128)(2,1)S(1)}, u32[]{:S(2)}, u32[]{:S(2)}) collective-permute-start(bf16[144,1152]{1,0:T(8,128)(2,1)S(1)} %get-tuple-element.39), channel_id=1, source_target_pairs={{0,97},{2,31},{1,96},{3,30},{4,101},{6,27},{5,100},{7,26},{8,105},... | collective-permute-start | bytes 995336 | tf_op jit(solution)/shard_map/ppermute | solution.py:295
  87.0 5.7 %collective-permute-start.19 = (f32[18,576]{1,0:T(8,128)S(1)}, f32[18,576]{1,0:T(8,128)S(1)}, u32[]{:S(2)}, u32[]{:S(2)}) collective-permute-start(f32[18,576]{1,0:T(8,128)S(1)} %slice_select_fusion), channel_id=1, source_target_pairs={{0,2},{2,0},{1,3},{3,1},{4,6},{6,4},{5,7},{7,5},{8,10},{10,8},{9,1... | collective-permute-start | bytes 124424 | tf_op jit(solution)/shard_map/ppermute | solution.py:237

commit v4 on v3

v4 whole, which is shorter than its diff:
```python
import jax
import jax.numpy as jnp
from jax import lax
from jax.experimental import pallas as pl
from jax.experimental.pallas import tpu as pltpu
from jax.sharding import PartitionSpec as P

logit_scale = 10.0
logit_bias = -10.0
norm_eps = 1e-06
AXES = ("dp", "tower")
RING = 4
MIB = 1 << 20
F32, BF16 = jnp.float32, jnp.bfloat16


def device(z, y, x, core):
    return (((z % 4 * 4 + y % 4) * 2 + x // 2) * 2 + core) * 2 + x % 2


CHIPS = [(z, y, x) for z in range(RING) for y in range(RING) for x in range(RING)]


def block_of(x):
    return int(x // 2 == x % 2)


def per_core(images, texts):
    return [
        (device(*chip, core), device(*to(*chip), core)) for chip in CHIPS for core, to in enumerate((images, texts))
    ]


def ring(turn):
    return per_core(lambda z, y, x: (z + turn, y, x), lambda z, y, x: (z, y + turn, x))


def first_ring(turn):
    return [(device(z, y, x, 1 - block_of(x)), device(z + turn, y, x, 0)) for z, y, x in CHIPS] + [
        (device(z, y, x, block_of(x)), device(z, y + turn, x, 1)) for z, y, x in CHIPS
    ]


CORES_SWAP = [(device(*chip, core), device(*chip, 1 - core)) for chip in CHIPS for core in range(2)]
NEAR_SWAP = per_core(*[lambda z, y, x: (z, y, x ^ 1)] * 2)
FAR_SWAP = per_core(*[lambda z, y, x: (z, y, 3 - x)] * 2)
TEXTS_SWAP = [(device(z, y, x, block_of(x)), device(z, y, 3 - x, 1)) for z, y, x in CHIPS]

REDUCE_GROUPS = [[device(z, y, x, 0) for y in range(RING) for x in range(RING)] for z in range(RING)] + [
    [device(z, y, x, 1) for z in range(RING) for x in range(RING)] for y in range(RING)
]


def position():
    dp = lax.axis_index("dp")
    return (
        lax.div(dp, 16),
        lax.rem(lax.div(dp, 4), 4),
        lax.rem(lax.div(dp, 2), 2),
        lax.rem(dp, 2),
        lax.axis_index("tower"),
    )


def vmem():
    return pl.BlockSpec(memory_space=pltpu.VMEM)


def pick_kernel(img_feats, txt_feats, img_head, txt_head, mine, give, send, top, bottom, sems):
    _, _, high, core, tower = position()
    part = top.shape[0]

    def copies(feats, other, head):
        moves = ((head.at[:part], top), (head.at[part:], bottom), (other, give), (feats, mine))
        return [pltpu.make_async_copy(*move, sems.at[i]) for i, move in enumerate(moves)]

    def choice(feats):
        return pltpu.make_async_copy(feats, send, sems.at[4])

    @pl.when(core == 0)
    def _():
        for copy in copies(img_feats, txt_feats, img_head):
            copy.start()

    @pl.when(core == 1)
    def _():
        for copy in copies(txt_feats, img_feats, txt_head):
            copy.start()

    holds_block = (high == tower).astype(jnp.int32) == core

    @pl.when(holds_block)
    def _():
        choice(txt_feats).start()

    @pl.when(jnp.logical_not(holds_block))
    def _():
        choice(img_feats).start()

    for copy in copies(img_feats, txt_feats, img_head):
        copy.wait()
    choice(img_feats).wait()


def embed_units(head, units, emb_ref, raw_ref):
    rows = units[0].shape[0]
    for i in range(0, len(units), 2):
        here = pl.ds(i * rows, 2 * rows)
        feats = jnp.concatenate([units[i][...], units[i + 1][...]], axis=0)
        raw = jnp.dot(feats, head, preferred_element_type=F32).astype(BF16)
        wide = raw.astype(F32)
        norm = jnp.sqrt(jnp.sum(wide * wide, axis=1, keepdims=True) + norm_eps)
        emb_ref[here, :] = (wide / norm).astype(BF16)
        raw_ref[here, :] = raw


def embed_first_kernel(top, bottom, far_top, far_bottom, *refs):
    *units, emb_ref, raw_ref, head_ref = refs
    head_ref[...] = jnp.concatenate([top[...], bottom[...], far_top[...], far_bottom[...]], axis=0).T
    embed_units(head_ref[...], units, emb_ref, raw_ref)


def embed_second_kernel(head_ref, *refs):
    *units, emb_ref, raw_ref = refs
    embed_units(head_ref[...], units, emb_ref, raw_ref)


def flip_rows(feats, flip_ref, lane):
    z, y, _, core, _ = position()
    part = flip_ref.shape[1] // RING
    turned = feats.T

    def store(own, ring_first):
        for block in range(RING * RING):
            first, second = divmod(block, RING)
            place, other = (first, second) if ring_first else (second, first)
            turn = lax.rem(place - own + RING, RING)
            flip_ref[turn, pl.ds(other * part, part), pl.ds(lane, feats.shape[0])] = (
                turned[block * part : (block + 1) * part, :]
            )

    @pl.when(core == 0)
    def _():
        store(z, True)

    @pl.when(core == 1)
    def _():
        store(y, False)


def coefs(products):
    return (logit_scale / (1.0 + jnp.exp(-(logit_scale * products + logit_bias)))).astype(BF16)


def with_positives(products, result, here):
    block = result.shape[0] // 2
    match = lax.broadcasted_iota(jnp.int32, (block, block), 0) == lax.broadcasted_iota(
        jnp.int32, (block, block), 1
    )
    match = match & here
    logits = logit_scale * products[:block, :block] + logit_bias
    value = logit_scale / (1.0 + jnp.exp(jnp.where(match, logits, -logits)))
    upper = jnp.concatenate([jnp.where(match, -value, value).astype(BF16), result[:block, block:]], axis=1)
    return jnp.concatenate([upper, result[block:, :]], axis=0)


def score_first_kernel(*refs):
    core = position()[3]
    emb_a, emb_b, far_a = refs[:3]
    *units, coef_a, coef_b, flip_a, flip_b, turned = refs[3:]
    turned[...] = far_a[...].T
    rows = emb_a.shape[0] // 2
    for emb, coef_ref in ((emb_a, coef_a), (emb_b, coef_b)):
        for i in range(2):
            here = pl.ds(i * rows, rows)
            products = jnp.dot(emb[here, :], turned[...], preferred_element_type=F32)
            result = coefs(products)
            if emb is emb_b and i == 0:
                result = with_positives(products, result, core == 0)
            coef_ref[here, :] = result
    for i, unit in enumerate(units):
        flip_rows(unit[...], flip_a if i < RING else flip_b, i % RING * unit.shape[0])


def score_second_kernel(emb_a, emb_b, far_a, far_b, raw_a, raw_b, coef_a, coef_b, grad_a, grad_b, turned):
    core = position()[3]
    turned[...] = far_b[...].T
    rows = emb_a.shape[0] // 2
    for emb, raw, coef, grad in ((emb_a, raw_a, coef_a, grad_a), (emb_b, raw_b, coef_b, grad_b)):
        for i in range(2):
            here = pl.ds(i * rows, rows)
            products = jnp.dot(emb[here, :], turned[...], preferred_element_type=F32)
            result = coefs(products)
            if emb is emb_a and i == 0:
                result = with_positives(products, result, core == 1)
            direction = jnp.dot(coef[here, :], far_a[...], preferred_element_type=F32) + jnp.dot(
                result, far_b[...], preferred_element_type=F32
            )
            wide = raw[here, :].astype(F32)
            norm = jnp.sqrt(jnp.sum(wide * wide, axis=1, keepdims=True) + norm_eps)
            unit = wide / norm
            inner = jnp.sum(unit * direction, axis=1, keepdims=True)
            grad[here, :] = ((direction - unit * inner) / norm).astype(BF16)


def term_kernel(turn, flip_a, flip_b, grad_a, grad_b, piece):
    piece[...] = (
        jnp.dot(flip_a[turn], grad_a[...], preferred_element_type=F32)
        + jnp.dot(flip_b[turn], grad_b[...], preferred_element_type=F32)
    ).astype(piece.dtype)


def sum_kernel(*refs):
    tower = position()[4]
    out_ref = refs[-1]
    total = refs[0][...].astype(F32)
    for ref in refs[1:-1]:
        total += ref[...].astype(F32)
    total = total.astype(out_ref.dtype)
    part, width = out_ref.shape[1], out_ref.shape[2] // 2
    for j in range(2 * RING):
        for half in range(2):
            slot = 2 * j + lax.rem(half + tower, 2)
            columns = slice(half * width, (half + 1) * width)
            out_ref[slot, :, :width] = total[2 * j * part : (2 * j + 1) * part, columns]
            out_ref[slot, :, width:] = total[(2 * j + 1) * part : (2 * j + 2) * part, columns]


def kernel_call(body, name, shapes, operands, scratch=(), flops=0, exps=0, specs=None, limit=40):
    shapes = [jax.ShapeDtypeStruct(*shape) for shape in shapes]
    touched = sum(a.size * a.dtype.itemsize for a in (*shapes, *operands))
    return pl.pallas_call(
        body,
        out_shape=shapes,
        in_specs=[vmem()] * len(operands) if specs is None else specs,
        out_specs=[vmem()] * len(shapes),
        scratch_shapes=list(scratch),
        compiler_params=pltpu.CompilerParams(vmem_limit_bytes=limit * MIB),
        cost_estimate=pl.CostEstimate(flops=flops, bytes_accessed=touched, transcendentals=exps),
        name=name,
    )(*operands)


def local(img_feats, txt_feats, img_proj, txt_proj):
    rows, depth = img_feats.shape
    width = img_proj.shape[1]
    full = 2 * width
    pair = RING * rows
    part = depth // RING

    def swap(value):
        return lax.ppermute(value, AXES, CORES_SWAP)

    mine, give, send, top, bottom = kernel_call(
        pick_kernel,
        "pick",
        [((rows, depth), BF16)] * 3 + [((5 * depth // 18, depth), BF16), ((2 * depth // 9, depth), BF16)],
        (img_feats, txt_feats, img_proj.T, txt_proj.T),
        scratch=(pltpu.SemaphoreType.DMA((5,)),),
        specs=[pl.BlockSpec(memory_space=pltpu.HBM)] * 4,
        limit=60,
    )
    far_top = lax.ppermute(top, AXES, NEAR_SWAP)
    far_bottom = lax.ppermute(bottom, AXES, FAR_SWAP)
    far_texts = lax.ppermute(send, AXES, TEXTS_SWAP)
    turns = (1, 3, 2)
    units_a = [lax.ppermute(send, AXES, first_ring(turn)) for turn in turns]
    other = swap(give)
    _, _, high, core, tower = position()
    block = (high == tower).astype(jnp.int32)
    first = jnp.where(block == 1, mine, other)
    second = jnp.where(core == 1, far_texts, jnp.where(block == 0, mine, other))
    units_a = [first, *units_a]
    units_b = [second] + [lax.ppermute(second, AXES, ring(turn)) for turn in turns]

    rows_of = ((pair, full), BF16)
    work = 2 * pair * depth * full
    emb_a, raw_a, head = kernel_call(
        embed_first_kernel,
        "embed_first",
        [rows_of, rows_of, ((depth, full), BF16)],
        (top, bottom, far_top, far_bottom, *units_a),
        flops=work,
    )
    far_a = swap(emb_a)
    emb_b, raw_b = kernel_call(
        embed_second_kernel, "embed_second", [rows_of, rows_of], (head, *units_b), flops=work
    )
    far_b = swap(emb_b)
    square = ((pair, pair), BF16)
    flips = ((RING, part, pair), BF16)
    turned = pltpu.VMEM((full, pair), BF16)
    coef_a, coef_b, flip_a, flip_b = kernel_call(
        score_first_kernel,
        "score_first",
        [square, square, flips, flips],
        (emb_a, emb_b, far_a, *units_a, *units_b),
        scratch=[turned],
        flops=4 * pair * pair * full,
        exps=2 * pair * pair,
    )
    grad_a, grad_b = kernel_call(
        score_second_kernel,
        "score_second",
        [rows_of, rows_of],
        (emb_a, emb_b, far_a, far_b, raw_a, raw_b, coef_a, coef_b),
        scratch=[turned],
        flops=12 * pair * pair * full,
        exps=2 * pair * pair,
    )

    def term(turn):
        return kernel_call(
            lambda *refs: term_kernel(turn, *refs),
            "term_" + str(turn),
            [((part, full), BF16)],
            (flip_a, flip_b, grad_a, grad_b),
            flops=work // 2,
        )[0]

    sent = [lax.ppermute(term(turn), AXES, ring(turn)) for turn in (2, 1, 3)]
    (sums,) = kernel_call(
        sum_kernel, "sum_terms", [((RING * RING, part // RING // 4, full), BF16)], (term(0), *sent)
    )
    swapped = lax.all_to_all(sums, AXES, 0, 0, axis_index_groups=REDUCE_GROUPS, tiled=True)
    total = jnp.sum(swapped.astype(F32), axis=0)
    is_img = position()[3] == 0
    low, high = total[:, :width], total[:, width:]
    keep = jnp.where(is_img, low, high)
    got = swap(jnp.where(is_img, high, low))
    return (jnp.where(is_img, keep, got), jnp.where(is_img, got, keep))


def solution(mesh):
    return jax.shard_map(
        local,
        mesh=mesh,
        in_specs=(P("dp", None), P("dp", None), P(None, "tower"), P(None, "tower")),
        out_specs=(P("dp", "tower"), P("dp", "tower")),
        check_vma=False,
    )
```

time: 94.8 us -> 92.6 us (0.977); the launches traced: 93.5 us -> 92.3 us
  waiting for transfers between devices: 16.7 us -> 33.5 us
  blocking collectives: 12 us -> 0 us
  starting transfers between devices: 40.2 us -> 34.7 us
  local copies, waits for them, and re-layouts: 4.56 us -> 0.01 us
  Pallas kernels: 18.3 us -> 21.3 us
  other arithmetic: 0.95 us -> 1.98 us
    all_to_all x0 -> x1, waiting for transfers between devices: none -> 13.8 us  [local(): lax.all_to_all(sums, AXES, 0, 0, axis_index_groups=REDUCE_GROUPS, tiled=T...]
    ppermute x14 -> x10, starting transfers between devices: 32.7 us -> 19.9 us  [the longest x3 5.66 us: local(): sent = [lax.ppermute(term(turn), AXES, ring(turn)) for turn in (2, 1, 3)]]
    all_to_all x1 -> x0, blocking collectives: 12 us -> none  [local(): lax.all_to_all(sums, AXES, 0, 0, axis_index_groups=REDUCE_GROUPS, tiled=T...]
    ppermute x1, waiting for transfers between devices: 0.01 us -> 6.46 us  [local(): far_bottom = lax.ppermute(bottom, AXES, FAR_SWAP)]
    all_to_all x0 -> x1, starting transfers between devices: none -> 5.77 us  [local(): lax.all_to_all(sums, AXES, 0, 0, axis_index_groups=REDUCE_GROUPS, tiled=T...]
    unnamed x8 -> x4, local copies, waits for them, and re-layouts: 4.56 us -> 0.01 us
    ppermute x4, waiting for transfers between devices: 4.93 us -> 0.97 us  [swap(): return lax.ppermute(value, AXES, CORES_SWAP)]
    pallas_call x7 -> x10, Pallas kernels: 18.3 us -> 21.3 us  [kernel_call(): pl.pallas_call(body, out_shape=shapes, in_specs=[vmem()] * len(operands)...]
  transfers between devices with their start and end apart: 20 -> 17, of which waited for: 9 -> 7; matrix products, arithmetic and copies ran while one was open for 0% -> 1% of each run, Pallas kernels for 8% -> 9%
where the time goes in v4:
time: 92.6 us; the launch traced here: 92.3 us
  starting transfers between devices  34.7 us (37%)
  waiting for transfers between devices  33.5 us (36%)
  Pallas kernels  21.3 us (23%)
  other arithmetic  1.98 us (2%)
    pallas_call x10, Pallas kernels, kernel_call(): pl.pallas_call(body, out_shape=shapes, in_specs=[vmem()] * len(operands)...  21.3 us
    all_to_all x1, waiting for transfers between devices, local(): lax.all_to_all(sums, AXES, 0, 0, axis_index_groups=REDUCE_GROUPS, tiled=T...  13.8 us
    ppermute x3, waiting for transfers between devices, local(): sent = [lax.ppermute(term(turn), AXES, ring(turn)) for turn in (2, 1, 3)]  12.3 us
    ppermute x1, waiting for transfers between devices, local(): far_bottom = lax.ppermute(bottom, AXES, FAR_SWAP)  6.46 us
    ppermute x4, starting transfers between devices, swap(): return lax.ppermute(value, AXES, CORES_SWAP)  6.28 us
    all_to_all x1, starting transfers between devices, local(): lax.all_to_all(sums, AXES, 0, 0, axis_index_groups=REDUCE_GROUPS, tiled=T...  5.77 us
    ppermute x3, starting transfers between devices, local(): sent = [lax.ppermute(term(turn), AXES, ring(turn)) for turn in (2, 1, 3)]  5.66 us
    ppermute x3, starting transfers between devices, local(): lax.ppermute(second, AXES, ring(turn))  5.32 us
  transfers between devices with their start and end apart: 17, of which 7 were waited for; matrix products, arithmetic and copies ran while one was open for 1% of the time, Pallas kernels for 9%

profile of v4, /device:TPU:1, one launch (start us, length us, event | category | flops | bytes accessed | tf_op | source)
XLA Modules:
  0.0 92.3 jit_solution(16564939129993887674)
XLA Ops:
  0.6 3.0 %pick.1 = (bf16[128,1152]{1,0:T(8,128)(2,1)}, bf16[128,1152]{1,0:T(8,128)(2,1)}, bf16[128,1152]{1,0:T(8,128)(2,1)}, bf16[320,1152]{1,0:T(8,128)(2,1)}, bf16[256,1152]{1,0:T(8,128)(2,1)}) custom-call(bf16[128,1152]{1,0:T(8,128)(2,1)} %img_feats.1, bf16[128,1152]{1,0:T(8,128)(2,1)} %txt_feats.1, bf16[576,1152]{1,0:T(8,128)(2,1)} %bitcast.2, ...), custom_call_target="tpu_custom_call" | custom-call | bytes 5455872 | tf_op jit(solution)/shard_map/pick/pallas_call | solution.py:232
  3.6 1.5 %collective-permute-start.2 = (bf16[128,1152]{1,0:T(8,128)(2,1)}, bf16[128,1152]{1,0:T(8,128)(2,1)S(1)}, u32[]{:S(2)}, u32[]{:S(2)}) collective-permute-start(bf16[128,1152]{1,0:T(8,128)(2,1)} %get-tuple-element.21), channel_id=1, source_target_pairs={{0,2},{2,0},{1,3},{3,1},{4,6},{6,4},{5,7},{7,5},{8,10},{10,8},{9,1... | collective-permute-start | bytes 884744 | tf_op jit(solution)/shard_map/ppermute | solution.py:252
  5.1 4.5 %collective-permute-start.6 = (bf16[128,1152]{1,0:T(8,128)(2,1)}, bf16[128,1152]{1,0:T(8,128)(2,1)S(1)}, u32[]{:S(2)}, u32[]{:S(2)}) collective-permute-start(bf16[128,1152]{1,0:T(8,128)(2,1)} %get-tuple-element.22), channel_id=1, source_target_pairs={{2,7},{1,6},{4,3},{7,2},{10,15},{9,14},{12,11},{15,10},{18,23},{17... | collective-permute-start | bytes 884744 | tf_op jit(solution)/shard_map/ppermute | solution.py:265
  9.6 0.1 collective-permute-start
  9.7 3.0 %collective-permute-start.5 = (bf16[128,1152]{1,0:T(8,128)(2,1)}, bf16[128,1152]{1,0:T(8,128)(2,1)S(1)}, u32[]{:S(2)}, u32[]{:S(2)}) collective-permute-start(bf16[128,1152]{1,0:T(8,128)(2,1)} %get-tuple-element.22), channel_id=1, source_target_pairs={{0,64},{3,65},{6,68},{5,69},{8,72},{11,73},{14,76},{13,77},{16,80}... | collective-permute-start | bytes 884744 | tf_op jit(solution)/shard_map/ppermute | solution.py:267
  12.7 0.8 collective-permute-start.4
  13.5 0.0 collective-permute-done.2
  13.5 0.7 collective-permute-start.3
  14.2 0.0 collective-permute-done.6
  14.2 2.7 %collective-permute-start.1 = (bf16[256,1152]{1,0:T(8,128)(2,1)}, bf16[256,1152]{1,0:T(8,128)(2,1)S(1)}, u32[]{:S(2)}, u32[]{:S(2)}) collective-permute-start(bf16[256,1152]{1,0:T(8,128)(2,1)} %get-tuple-element.19.bottom), channel_id=1, source_target_pairs={{0,5},{2,7},{1,4},{3,6},{4,1},{6,3},{5,0},{7,2},{8,13},{10,15},{9,... | collective-permute-start | bytes 1769480 | tf_op jit(solution)/shard_map/ppermute | solution.py:264
  16.9 1.0 %select_select_fusion = (bf16[128,1152]{1,0:T(8,128)(2,1)S(1)}, bf16[128,1152]{1,0:T(8,128)(2,1)S(1)}) fusion(bf16[128,1152]{1,0:T(8,128)(2,1)S(1)} %collective-permute-done.6, bf16[128,1152]{1,0:T(8,128)(2,1)} %get-tuple-element.20, bf16[128,1152]{1,0:T(8,128)(2,1)S(1)} %collective-permute-done.2, pred[]{:T(512)S(6)} %eq.19, pred[]{:T(512)S(6)} %eq.18, ...), kind=kLoop, calls=%fused_computation.1 | loop fusion | flops 442368 | bytes 1474563 | tf_op jit(solution)/shard_map/jit(_where)/select_n | solution.py:272
  17.9 0.0 collective-permute-done.5.refs_3_.refs_6_
  17.9 3.0 %collective-permute-start.9 = (bf16[128,1152]{1,0:T(8,128)(2,1)S(1)}, bf16[128,1152]{1,0:T(8,128)(2,1)S(1)}, u32[]{:S(2)}, u32[]{:S(2)}) collective-permute-start(bf16[128,1152]{1,0:T(8,128)(2,1)S(1)} %get-tuple-element.34.refs_0_.refs_7_), channel_id=1, source_target_pairs={{0,64},{2,18},{1,65},{3,19},{4,68},{6,22},{5,69},{7,23},{8,72},{10... | collective-permute-start | bytes 884744 | tf_op jit(solution)/shard_map/ppermute | solution.py:274
  20.9 0.0 collective-permute-done.4.refs_2_.refs_5_
  20.9 2.3 %collective-permute-start.8 = (bf16[128,1152]{1,0:T(8,128)(2,1)S(1)}, bf16[128,1152]{1,0:T(8,128)(2,1)S(1)}, u32[]{:S(2)}, u32[]{:S(2)}) collective-permute-start(bf16[128,1152]{1,0:T(8,128)(2,1)S(1)} %get-tuple-element.34.refs_0_.refs_7_), channel_id=1, source_target_pairs={{0,96},{2,26},{1,97},{3,27},{4,100},{6,30},{5,101},{7,31},{8,104},... | collective-permute-start | bytes 884744 | tf_op jit(solution)/shard_map/ppermute | solution.py:274
  23.2 0.0 collective-permute-done.3.refs_1_.refs_4_
  23.2 0.0 collective-permute-start.7
  23.3 6.5 %collective-permute-done.1.far_bottom = bf16[256,1152]{1,0:T(8,128)(2,1)S(1)} collective-permute-done((bf16[256,1152]{1,0:T(8,128)(2,1)}, bf16[256,1152]{1,0:T(8,128)(2,1)S(1)}, u32[]{:S(2)}, u32[]{:S(2)}) %collective-permute-start.1) | collective-permute-done | bytes 589856 | tf_op jit(solution)/shard_map/ppermute | solution.py:264
  29.7 0.0 collective-permute-done.far_top
  29.7 2.2 %embed_first.1 = (bf16[512,1152]{1,0:T(8,128)(2,1)S(1)}, bf16[512,1152]{1,0:T(8,128)(2,1)S(1)}, bf16[1152,1152]{1,0:T(8,128)(2,1)S(1)}) custom-call(bf16[320,1152]{1,0:T(8,128)(2,1)S(1)} %copy-done, bf16[256,1152]{1,0:T(8,128)(2,1)S(1)} %copy-done.1, bf16[320,1152]{1,0:T(8,128)(2,1)S(1)} %collective-permute-done.far_top, ...), custom_call_target="tpu_custom_call" | custom-call | flops 1358954496 | bytes 8847360 | tf_op jit(solution)/shard_map/embed_first/pallas_call | solution.py:232
  31.9 1.7 %collective-permute-start.10 = (bf16[512,1152]{1,0:T(8,128)(2,1)S(1)}, bf16[512,1152]{1,0:T(8,128)(2,1)S(1)}, u32[]{:S(2)}, u32[]{:S(2)}) collective-permute-start(bf16[512,1152]{1,0:T(8,128)(2,1)S(1)} %get-tuple-element.23.refs_0_.emb_a), channel_id=1, source_target_pairs={{0,2},{2,0},{1,3},{3,1},{4,6},{6,4},{5,7},{7,5},{8,10},{10,8},{9,1... | collective-permute-start | bytes 3538952 | tf_op jit(solution)/shard_map/ppermute | solution.py:252
  33.7 0.0 collective-permute-done.9.refs_3_.refs_10_
  33.7 0.0 collective-permute-done.8.refs_2_.refs_9_
  33.7 0.0 collective-permute-done.7.refs_1_.refs_8_
  33.7 2.1 %embed_second.1 = (bf16[512,1152]{1,0:T(8,128)(2,1)S(1)}, bf16[512,1152]{1,0:T(8,128)(2,1)S(1)}) custom-call(bf16[1152,1152]{1,0:T(8,128)(2,1)S(1)} %get-tuple-element.24.head_ref, bf16[128,1152]{1,0:T(8,128)(2,1)S(1)} %get-tuple-element.34.refs_0_.refs_7_, bf16[128,1152]{1,0:T(8,128)(2,1)S(1)} %collective-permute-done.7.refs_1_.refs_8_, ...), custom_call_target="tpu_custom_call" | custom-call | flops 1358954496 | bytes 6193152 | tf_op jit(solution)/shard_map/embed_second/pallas_call | solution.py:232
  35.8 0.3 collective-permute-start.11
  36.1 0.1 collective-permute-done.10.refs_2_.far_a
  36.2 3.3 %score_first.1 = (bf16[512,512]{1,0:T(8,128)(2,1)S(1)}, bf16[512,512]{1,0:T(8,128)(2,1)S(1)}, bf16[4,288,512]{2,1,0:T(8,128)(2,1)S(1)}, bf16[4,288,512]{2,1,0:T(8,128)(2,1)S(1)}) custom-call(bf16[512,1152]{1,0:T(8,128)(2,1)S(1)} %get-tuple-element.23.refs_0_.emb_a, bf16[512,1152]{1,0:T(8,128)(2,1)S(1)} %get-tuple-element.25.refs_1_.emb_b, ...), custom_call_target="tpu_custom_call" | custom-call | flops 1207959552 | bytes 9306112 | tf_op jit(solution)/shard_map/score_first/pallas_call | solution.py:232
  39.4 0.0 collective-permute-done.11.far_b
  39.4 5.6 %score_second.1 = (bf16[512,1152]{1,0:T(8,128)(2,1)S(1)}, bf16[512,1152]{1,0:T(8,128)(2,1)S(1)}) custom-call(bf16[512,1152]{1,0:T(8,128)(2,1)S(1)} %get-tuple-element.23.refs_0_.emb_a, bf16[512,1152]{1,0:T(8,128)(2,1)S(1)} %get-tuple-element.25.refs_1_.emb_b, bf16[512,1152]{1,0:T(8,128)(2,1)S(1)} %collective-permute-done.10.refs_2_.far_a, ...), custom_call_target="tpu_custom_call" | custom-call | flops 3623878656 | bytes 10485760 | tf_op jit(solution)/shard_map/score_second/pallas_call | solution.py:232
  45.0 0.9 %term_3.1 = bf16[288,1152]{1,0:T(8,128)(2,1)S(1)} custom-call(bf16[4,288,512]{2,1,0:T(8,128)(2,1)S(1)} %get-tuple-element.26.refs_0_, bf16[4,288,512]{2,1,0:T(8,128)(2,1)S(1)} %get-tuple-element.27.refs_1_, bf16[512,1152]{1,0:T(8,128)(2,1)S(1)} %get-tuple-element.32.refs_2_, bf16[512,1152]{1,0:T(8,128)(2,1)S(1)} %get-tuple-element.33.refs_3_), custom_call_target="tpu_custom_call" | custom-call | flops 679477248 | bytes 5382144 | tf_op jit(solution)/shard_map/term_3/pallas_call | solution.py:232
  46.0 0.9 %term_1.1 = bf16[288,1152]{1,0:T(8,128)(2,1)S(1)} custom-call(bf16[4,288,512]{2,1,0:T(8,128)(2,1)S(1)} %get-tuple-element.26.refs_0_, bf16[4,288,512]{2,1,0:T(8,128)(2,1)S(1)} %get-tuple-element.27.refs_1_, bf16[512,1152]{1,0:T(8,128)(2,1)S(1)} %get-tuple-element.32.refs_2_, bf16[512,1152]{1,0:T(8,128)(2,1)S(1)} %get-tuple-element.33.refs_3_), custom_call_target="tpu_custom_call" | custom-call | flops 679477248 | bytes 5382144 | tf_op jit(solution)/shard_map/term_1/pallas_call | solution.py:232
  46.9 0.9 %term_2.1 = bf16[288,1152]{1,0:T(8,128)(2,1)S(1)} custom-call(bf16[4,288,512]{2,1,0:T(8,128)(2,1)S(1)} %get-tuple-element.26.refs_0_, bf16[4,288,512]{2,1,0:T(8,128)(2,1)S(1)} %get-tuple-element.27.refs_1_, bf16[512,1152]{1,0:T(8,128)(2,1)S(1)} %get-tuple-element.32.refs_2_, bf16[512,1152]{1,0:T(8,128)(2,1)S(1)} %get-tuple-element.33.refs_3_), custom_call_target="tpu_custom_call" | custom-call | flops 679477248 | bytes 5382144 | tf_op jit(solution)/shard_map/term_2/pallas_call | solution.py:232
  47.8 3.0 %collective-permute-start.12 = (bf16[288,1152]{1,0:T(8,128)(2,1)S(1)}, bf16[288,1152]{1,0:T(8,128)(2,1)S(1)}, u32[]{:S(2)}, u32[]{:S(2)}) collective-permute-start(bf16[288,1152]{1,0:T(8,128)(2,1)S(1)} %term_2.1), channel_id=1, source_target_pairs={{0,64},{2,18},{1,65},{3,19},{4,68},{6,22},{5,69},{7,23},{8,72},{10... | collective-permute-start | bytes 1990664 | tf_op jit(solution)/shard_map/ppermute | solution.py:321
  50.8 0.4 collective-permute-start.13
  51.2 2.3 %collective-permute-start.14 = (bf16[288,1152]{1,0:T(8,128)(2,1)S(1)}, bf16[288,1152]{1,0:T(8,128)(2,1)S(1)}, u32[]{:S(2)}, u32[]{:S(2)}) collective-permute-start(bf16[288,1152]{1,0:T(8,128)(2,1)S(1)} %term_3.1), channel_id=1, source_target_pairs={{0,96},{2,26},{1,97},{3,27},{4,100},{6,30},{5,101},{7,31},{8,104},... | collective-permute-start | bytes 1990664 | tf_op jit(solution)/shard_map/ppermute | solution.py:321
  53.5 0.9 %term_0.1.refs_0_ = bf16[288,1152]{1,0:T(8,128)(2,1)S(1)} custom-call(bf16[4,288,512]{2,1,0:T(8,128)(2,1)S(1)} %get-tuple-element.26.refs_0_, bf16[4,288,512]{2,1,0:T(8,128)(2,1)S(1)} %get-tuple-element.27.refs_1_, bf16[512,1152]{1,0:T(8,128)(2,1)S(1)} %get-tuple-element.32.refs_2_, bf16[512,1152]{1,0:T(8,128)(2,1)S(1)} %get-tuple-element.33.refs_3_), custom_call_target="tpu_custom_call" | custom-call | flops 679477248 | bytes 5382144 | tf_op jit(solution)/shard_map/term_0/pallas_call | solution.py:232
  54.4 4.8 %collective-permute-done.12.refs_1_ = bf16[288,1152]{1,0:T(8,128)(2,1)S(1)} collective-permute-done((bf16[288,1152]{1,0:T(8,128)(2,1)S(1)}, bf16[288,1152]{1,0:T(8,128)(2,1)S(1)}, u32[]{:S(2)}, u32[]{:S(2)}) %collective-permute-start.12) | collective-permute-done | bytes 663584 | tf_op jit(solution)/shard_map/ppermute | solution.py:321
  59.3 7.1 %collective-permute-done.13.refs_2_ = bf16[288,1152]{1,0:T(8,128)(2,1)S(1)} collective-permute-done((bf16[288,1152]{1,0:T(8,128)(2,1)S(1)}, bf16[288,1152]{1,0:T(8,128)(2,1)S(1)}, u32[]{:S(2)}, u32[]{:S(2)}) %collective-permute-start.13) | collective-permute-done | bytes 663584 | tf_op jit(solution)/shard_map/ppermute | solution.py:321
  66.4 0.4 collective-permute-done.14.refs_3_
  66.7 1.4 %sum_terms.1 = bf16[16,18,1152]{2,1,0:T(8,128)(2,1)} custom-call(bf16[288,1152]{1,0:T(8,128)(2,1)S(1)} %term_0.1.refs_0_, bf16[288,1152]{1,0:T(8,128)(2,1)S(1)} %collective-permute-done.12.refs_1_, bf16[288,1152]{1,0:T(8,128)(2,1)S(1)} %collective-permute-done.13.refs_2_, bf16[288,1152]{1,0:T(8,128)(2,1)S(1)} %collective-permute-done.14.refs_3_), custom_call_target="tpu_custom_call" | custom-call | bytes 3317760 | tf_op jit(solution)/shard_map/sum_terms/pallas_call | solution.py:232
  68.1 5.8 %all-to-all-start = ((bf16[16,18,1152]{2,1,0:T(8,128)(2,1)}), bf16[16,18,1152]{2,1,0:T(8,128)(2,1)S(1)}, u32[]{:S(2)}, u32[]{:S(2)}) async-start(bf16[16,18,1152]{2,1,0:T(8,128)(2,1)} %sum_terms.1), calls=%async_computation | async-start | bytes 1769472 | tf_op jit(solution)/shard_map/all_to_all | solution.py:325
  73.9 13.8 %all-to-all-done = bf16[16,18,1152]{2,1,0:T(8,128)(2,1)S(1)} async-done(((bf16[16,18,1152]{2,1,0:T(8,128)(2,1)}), bf16[16,18,1152]{2,1,0:T(8,128)(2,1)S(1)}, u32[]{:S(2)}, u32[]{:S(2)}) %all-to-all-start) | async-done | bytes 663584 | tf_op jit(solution)/shard_map/all_to_all | solution.py:325
  87.7 0.1 convert_reduce_fusion
  87.9 0.1 slice_select_fusion
  88.0 2.8 %collective-permute-start.15 = (f32[18,576]{1,0:T(8,128)S(1)}, f32[18,576]{1,0:T(8,128)S(1)}, u32[]{:S(2)}, u32[]{:S(2)}) collective-permute-start(f32[18,576]{1,0:T(8,128)S(1)} %slice_select_fusion), channel_id=1, source_target_pairs={{0,2},{2,0},{1,3},{3,1},{4,6},{6,4},{5,7},{7,5},{8,10},{10,8},{9,1... | collective-permute-start | bytes 124424 | tf_op jit(solution)/shard_map/ppermute | solution.py:252
  90.7 0.9 collective-permute-done.15
  91.6 0.7 broadcast_select_fusion.1
  (4 shorter events, 0.0 us)
Async XLA Ops:
  3.6 26.1 %copy-start = (bf16[320,1152]{1,0:T(8,128)(2,1)S(1)}, bf16[320,1152]{1,0:T(8,128)(2,1)}, u32[]{:S(2)}) copy-start(bf16[320,1152]{1,0:T(8,128)(2,1)} %get-tuple-element.18.top) | copy-start | bytes 2211844
  3.6 26.1 %copy-start.1 = (bf16[256,1152]{1,0:T(8,128)(2,1)S(1)}, bf16[256,1152]{1,0:T(8,128)(2,1)}, u32[]{:S(2)}) copy-start(bf16[256,1152]{1,0:T(8,128)(2,1)} %get-tuple-element.19.bottom) | copy-start | bytes 1769476
  3.6 9.8 %collective-permute-start.2 = (bf16[128,1152]{1,0:T(8,128)(2,1)}, bf16[128,1152]{1,0:T(8,128)(2,1)S(1)}, u32[]{:S(2)}, u32[]{:S(2)}) collective-permute-start(bf16[128,1152]{1,0:T(8,128)(2,1)} %get-tuple-element.21), channel_id=1, source_target_pairs={{0,2},{2,0},{1,3},{3,1},{4,6},{6,4},{5,7},{7,5},{8,10},{10,8},{9,1... | collective-permute-start | bytes 884744 | tf_op jit(solution)/shard_map/ppermute | solution.py:252
  5.1 9.0 %collective-permute-start.6 = (bf16[128,1152]{1,0:T(8,128)(2,1)}, bf16[128,1152]{1,0:T(8,128)(2,1)S(1)}, u32[]{:S(2)}, u32[]{:S(2)}) collective-permute-start(bf16[128,1152]{1,0:T(8,128)(2,1)} %get-tuple-element.22), channel_id=1, source_target_pairs={{2,7},{1,6},{4,3},{7,2},{10,15},{9,14},{12,11},{15,10},{18,23},{17... | collective-permute-start | bytes 884744 | tf_op jit(solution)/shard_map/ppermute | solution.py:265
  9.6 20.1 %collective-permute-start = (bf16[320,1152]{1,0:T(8,128)(2,1)}, bf16[320,1152]{1,0:T(8,128)(2,1)S(1)}, u32[]{:S(2)}, u32[]{:S(2)}) collective-permute-start(bf16[320,1152]{1,0:T(8,128)(2,1)} %get-tuple-element.18.top), channel_id=1, source_target_pairs={{0,1},{2,3},{1,0},{3,2},{4,5},{6,7},{5,4},{7,6},{8,9},{10,11},{9,8... | collective-permute-start | bytes 2211848 | tf_op jit(solution)/shard_map/ppermute | solution.py:263
  9.7 8.2 %collective-permute-start.5 = (bf16[128,1152]{1,0:T(8,128)(2,1)}, bf16[128,1152]{1,0:T(8,128)(2,1)S(1)}, u32[]{:S(2)}, u32[]{:S(2)}) collective-permute-start(bf16[128,1152]{1,0:T(8,128)(2,1)} %get-tuple-element.22), channel_id=1, source_target_pairs={{0,64},{3,65},{6,68},{5,69},{8,72},{11,73},{14,76},{13,77},{16,80}... | collective-permute-start | bytes 884744 | tf_op jit(solution)/shard_map/ppermute | solution.py:267
  12.7 8.2 %collective-permute-start.4 = (bf16[128,1152]{1,0:T(8,128)(2,1)}, bf16[128,1152]{1,0:T(8,128)(2,1)S(1)}, u32[]{:S(2)}, u32[]{:S(2)}) collective-permute-start(bf16[128,1152]{1,0:T(8,128)(2,1)} %get-tuple-element.22), channel_id=1, source_target_pairs={{0,96},{3,97},{6,100},{5,101},{8,104},{11,105},{14,108},{13,109},{... | collective-permute-start | bytes 884744 | tf_op jit(solution)/shard_map/ppermute | solution.py:267
  13.5 9.8 %collective-permute-start.3 = (bf16[128,1152]{1,0:T(8,128)(2,1)}, bf16[128,1152]{1,0:T(8,128)(2,1)S(1)}, u32[]{:S(2)}, u32[]{:S(2)}) collective-permute-start(bf16[128,1152]{1,0:T(8,128)(2,1)} %get-tuple-element.22), channel_id=1, source_target_pairs={{0,32},{3,33},{6,36},{5,37},{8,40},{11,41},{14,44},{13,45},{16,48}... | collective-permute-start | bytes 884744 | tf_op jit(solution)/shard_map/ppermute | solution.py:267
  14.2 15.6 %collective-permute-start.1 = (bf16[256,1152]{1,0:T(8,128)(2,1)}, bf16[256,1152]{1,0:T(8,128)(2,1)S(1)}, u32[]{:S(2)}, u32[]{:S(2)}) collective-permute-start(bf16[256,1152]{1,0:T(8,128)(2,1)} %get-tuple-element.19.bottom), channel_id=1, source_target_pairs={{0,5},{2,7},{1,4},{3,6},{4,1},{6,3},{5,0},{7,2},{8,13},{10,15},{9,... | collective-permute-start | bytes 1769480 | tf_op jit(solution)/shard_map/ppermute | solution.py:264
  17.9 15.8 %collective-permute-start.9 = (bf16[128,1152]{1,0:T(8,128)(2,1)S(1)}, bf16[128,1152]{1,0:T(8,128)(2,1)S(1)}, u32[]{:S(2)}, u32[]{:S(2)}) collective-permute-start(bf16[128,1152]{1,0:T(8,128)(2,1)S(1)} %get-tuple-element.34.refs_0_.refs_7_), channel_id=1, source_target_pairs={{0,64},{2,18},{1,65},{3,19},{4,68},{6,22},{5,69},{7,23},{8,72},{10... | collective-permute-start | bytes 884744 | tf_op jit(solution)/shard_map/ppermute | solution.py:274
  20.9 12.8 %collective-permute-start.8 = (bf16[128,1152]{1,0:T(8,128)(2,1)S(1)}, bf16[128,1152]{1,0:T(8,128)(2,1)S(1)}, u32[]{:S(2)}, u32[]{:S(2)}) collective-permute-start(bf16[128,1152]{1,0:T(8,128)(2,1)S(1)} %get-tuple-element.34.refs_0_.refs_7_), channel_id=1, source_target_pairs={{0,96},{2,26},{1,97},{3,27},{4,100},{6,30},{5,101},{7,31},{8,104},... | collective-permute-start | bytes 884744 | tf_op jit(solution)/shard_map/ppermute | solution.py:274
  23.2 10.4 %collective-permute-start.7 = (bf16[128,1152]{1,0:T(8,128)(2,1)S(1)}, bf16[128,1152]{1,0:T(8,128)(2,1)S(1)}, u32[]{:S(2)}, u32[]{:S(2)}) collective-permute-start(bf16[128,1152]{1,0:T(8,128)(2,1)S(1)} %get-tuple-element.34.refs_0_.refs_7_), channel_id=1, source_target_pairs={{0,32},{2,10},{1,33},{3,11},{4,36},{6,14},{5,37},{7,15},{8,40},{10... | collective-permute-start | bytes 884744 | tf_op jit(solution)/shard_map/ppermute | solution.py:274
  31.9 4.2 %collective-permute-start.10 = (bf16[512,1152]{1,0:T(8,128)(2,1)S(1)}, bf16[512,1152]{1,0:T(8,128)(2,1)S(1)}, u32[]{:S(2)}, u32[]{:S(2)}) collective-permute-start(bf16[512,1152]{1,0:T(8,128)(2,1)S(1)} %get-tuple-element.23.refs_0_.emb_a), channel_id=1, source_target_pairs={{0,2},{2,0},{1,3},{3,1},{4,6},{6,4},{5,7},{7,5},{8,10},{10,8},{9,1... | collective-permute-start | bytes 3538952 | tf_op jit(solution)/shard_map/ppermute | solution.py:252
  35.8 3.6 %collective-permute-start.11 = (bf16[512,1152]{1,0:T(8,128)(2,1)S(1)}, bf16[512,1152]{1,0:T(8,128)(2,1)S(1)}, u32[]{:S(2)}, u32[]{:S(2)}) collective-permute-start(bf16[512,1152]{1,0:T(8,128)(2,1)S(1)} %get-tuple-element.25.refs_1_.emb_b), channel_id=1, source_target_pairs={{0,2},{2,0},{1,3},{3,1},{4,6},{6,4},{5,7},{7,5},{8,10},{10,8},{9,1... | collective-permute-start | bytes 3538952 | tf_op jit(solution)/shard_map/ppermute | solution.py:252
  47.8 11.4 %collective-permute-start.12 = (bf16[288,1152]{1,0:T(8,128)(2,1)S(1)}, bf16[288,1152]{1,0:T(8,128)(2,1)S(1)}, u32[]{:S(2)}, u32[]{:S(2)}) collective-permute-start(bf16[288,1152]{1,0:T(8,128)(2,1)S(1)} %term_2.1), channel_id=1, source_target_pairs={{0,64},{2,18},{1,65},{3,19},{4,68},{6,22},{5,69},{7,23},{8,72},{10... | collective-permute-start | bytes 1990664 | tf_op jit(solution)/shard_map/ppermute | solution.py:321
  50.8 15.5 %collective-permute-start.13 = (bf16[288,1152]{1,0:T(8,128)(2,1)S(1)}, bf16[288,1152]{1,0:T(8,128)(2,1)S(1)}, u32[]{:S(2)}, u32[]{:S(2)}) collective-permute-start(bf16[288,1152]{1,0:T(8,128)(2,1)S(1)} %term_1.1), channel_id=1, source_target_pairs={{0,32},{2,10},{1,33},{3,11},{4,36},{6,14},{5,37},{7,15},{8,40},{10... | collective-permute-start | bytes 1990664 | tf_op jit(solution)/shard_map/ppermute | solution.py:321
  51.2 15.5 %collective-permute-start.14 = (bf16[288,1152]{1,0:T(8,128)(2,1)S(1)}, bf16[288,1152]{1,0:T(8,128)(2,1)S(1)}, u32[]{:S(2)}, u32[]{:S(2)}) collective-permute-start(bf16[288,1152]{1,0:T(8,128)(2,1)S(1)} %term_3.1), channel_id=1, source_target_pairs={{0,96},{2,26},{1,97},{3,27},{4,100},{6,30},{5,101},{7,31},{8,104},... | collective-permute-start | bytes 1990664 | tf_op jit(solution)/shard_map/ppermute | solution.py:321
  68.1 19.6 %all-to-all-start = ((bf16[16,18,1152]{2,1,0:T(8,128)(2,1)}), bf16[16,18,1152]{2,1,0:T(8,128)(2,1)S(1)}, u32[]{:S(2)}, u32[]{:S(2)}) async-start(bf16[16,18,1152]{2,1,0:T(8,128)(2,1)} %sum_terms.1), calls=%async_computation | async-start | bytes 1769472 | tf_op jit(solution)/shard_map/all_to_all | solution.py:325
  88.0 3.7 %collective-permute-start.15 = (f32[18,576]{1,0:T(8,128)S(1)}, f32[18,576]{1,0:T(8,128)S(1)}, u32[]{:S(2)}, u32[]{:S(2)}) collective-permute-start(f32[18,576]{1,0:T(8,128)S(1)} %slice_select_fusion), channel_id=1, source_target_pairs={{0,2},{2,0},{1,3},{3,1},{4,6},{6,4},{5,7},{7,5},{8,10},{10,8},{9,1... | collective-permute-start | bytes 124424 | tf_op jit(solution)/shard_map/ppermute | solution.py:252

commit v5 on v4

--- a/solution.py
+++ b/solution.py
@@ -62,20 +62,31 @@
     )
 
 
-def vmem():
-    return pl.BlockSpec(memory_space=pltpu.VMEM)
-
-
 def pick_kernel(img_feats, txt_feats, img_head, txt_head, mine, give, send, top, bottom, sems):
     _, _, high, core, tower = position()
-    part = top.shape[0]
+    split, step = top.shape[0], 64
 
     def copies(feats, other, head):
-        moves = ((head.at[:part], top), (head.at[part:], bottom), (other, give), (feats, mine))
+        moves = [(head.at[pl.ds(i, step)], top.at[pl.ds(i, step)]) for i in range(0, split, step)]
+        moves += [
+            (head.at[pl.ds(split + i, step)], bottom.at[pl.ds(i, step)])
+            for i in range(0, bottom.shape[0], step)
+        ]
+        moves += [(other, give), (feats, mine)]
         return [pltpu.make_async_copy(*move, sems.at[i]) for i, move in enumerate(moves)]
 
     def choice(feats):
-        return pltpu.make_async_copy(feats, send, sems.at[4])
+        return pltpu.make_async_copy(feats, send, sems.at[sems.shape[0] - 1])
+
+    holds_block = (high == tower).astype(jnp.int32) == core
+
+    @pl.when(holds_block)
+    def _():
+        choice(txt_feats).start()
+
+    @pl.when(jnp.logical_not(holds_block))
+    def _():
+        choice(img_feats).start()
 
     @pl.when(core == 0)
     def _():
@@ -86,16 +97,6 @@
     def _():
         for copy in copies(txt_feats, img_feats, txt_head):
             copy.start()
-
-    holds_block = (high == tower).astype(jnp.int32) == core
-
-    @pl.when(holds_block)
-    def _():
-        choice(txt_feats).start()
-
-    @pl.when(jnp.logical_not(holds_block))
-    def _():
-        choice(img_feats).start()
 
     for copy in copies(img_feats, txt_feats, img_head):
         copy.wait()
@@ -114,13 +115,11 @@
         raw_ref[here, :] = raw
 
 
-def embed_first_kernel(top, bottom, far_top, far_bottom, *refs):
-    *units, emb_ref, raw_ref, head_ref = refs
+def head_kernel(top, bottom, far_top, far_bottom, head_ref):
     head_ref[...] = jnp.concatenate([top[...], bottom[...], far_top[...], far_bottom[...]], axis=0).T
-    embed_units(head_ref[...], units, emb_ref, raw_ref)
-
-
-def embed_second_kernel(head_ref, *refs):
+
+
+def embed_kernel(head_ref, *refs):
     *units, emb_ref, raw_ref = refs
     embed_units(head_ref[...], units, emb_ref, raw_ref)
 
@@ -182,7 +181,7 @@
         flip_rows(unit[...], flip_a if i < RING else flip_b, i % RING * unit.shape[0])
 
 
-def score_second_kernel(emb_a, emb_b, far_a, far_b, raw_a, raw_b, coef_a, coef_b, grad_a, grad_b, turned):
+def score_second_kernel(emb_a, emb_b, far_a, far_b, raw_a, raw_b, coef_a, coef_b, flip_a, flip_b, grad_a, grad_b, piece, turned):
     core = position()[3]
     turned[...] = far_b[...].T
     rows = emb_a.shape[0] // 2
@@ -201,13 +200,19 @@
             unit = wide / norm
             inner = jnp.sum(unit * direction, axis=1, keepdims=True)
             grad[here, :] = ((direction - unit * inner) / norm).astype(BF16)
-
-
-def term_kernel(turn, flip_a, flip_b, grad_a, grad_b, piece):
-    piece[...] = (
-        jnp.dot(flip_a[turn], grad_a[...], preferred_element_type=F32)
-        + jnp.dot(flip_b[turn], grad_b[...], preferred_element_type=F32)
-    ).astype(piece.dtype)
+    terms_kernel((2,), flip_a, flip_b, grad_a, grad_b, piece)
+
+
+def terms_kernel(turns, flip_a, flip_b, grad_a, grad_b, *pieces):
+    for turn, piece in zip(turns, pieces):
+        piece[...] = (
+            jnp.dot(flip_a[turn], grad_a[...], preferred_element_type=F32)
+            + jnp.dot(flip_b[turn], grad_b[...], preferred_element_type=F32)
+        ).astype(piece.dtype)
+
+
+def add_kernel(left, right, out_ref):
+    out_ref[...] = left[...].astype(F32) + right[...].astype(F32)
 
 
 def sum_kernel(*refs):
@@ -226,14 +231,15 @@
             out_ref[slot, :, width:] = total[(2 * j + 1) * part : (2 * j + 2) * part, columns]
 
 
-def kernel_call(body, name, shapes, operands, scratch=(), flops=0, exps=0, specs=None, limit=40):
+def kernel_call(body, name, shapes, operands, scratch=(), flops=0, exps=0, anywhere=False, limit=40):
     shapes = [jax.ShapeDtypeStruct(*shape) for shape in shapes]
+    space = pl.BlockSpec(memory_space=pl.ANY if anywhere else pltpu.VMEM)
     touched = sum(a.size * a.dtype.itemsize for a in (*shapes, *operands))
     return pl.pallas_call(
         body,
         out_shape=shapes,
-        in_specs=[vmem()] * len(operands) if specs is None else specs,
-        out_specs=[vmem()] * len(shapes),
+        in_specs=[space] * len(operands),
+        out_specs=[space] * len(shapes),
         scratch_shapes=list(scratch),
         compiler_params=pltpu.CompilerParams(vmem_limit_bytes=limit * MIB),
         cost_estimate=pl.CostEstimate(flops=flops, bytes_accessed=touched, transcendentals=exps),
@@ -256,9 +262,9 @@
         "pick",
         [((rows, depth), BF16)] * 3 + [((5 * depth // 18, depth), BF16), ((2 * depth // 9, depth), BF16)],
         (img_feats, txt_feats, img_proj.T, txt_proj.T),
-        scratch=(pltpu.SemaphoreType.DMA((5,)),),
-        specs=[pl.BlockSpec(memory_space=pltpu.HBM)] * 4,
-        limit=60,
+        scratch=(pltpu.SemaphoreType.DMA((width // 64 + 3,)),),
+        anywhere=True,
+        limit=54,
     )
     far_top = lax.ppermute(top, AXES, NEAR_SWAP)
     far_bottom = lax.ppermute(bottom, AXES, FAR_SWAP)
@@ -275,16 +281,13 @@
 
     rows_of = ((pair, full), BF16)
     work = 2 * pair * depth * full
-    emb_a, raw_a, head = kernel_call(
-        embed_first_kernel,
-        "embed_first",
-        [rows_of, rows_of, ((depth, full), BF16)],
-        (top, bottom, far_top, far_bottom, *units_a),
-        flops=work,
+    (head,) = kernel_call(head_kernel, "head", [((depth, full), BF16)], (top, bottom, far_top, far_bottom))
+    emb_a, raw_a = kernel_call(
+        embed_kernel, "embed_first", [rows_of, rows_of], (head, *units_a), flops=work
     )
     far_a = swap(emb_a)
     emb_b, raw_b = kernel_call(
-        embed_second_kernel, "embed_second", [rows_of, rows_of], (head, *units_b), flops=work
+        embed_kernel, "embed_second", [rows_of, rows_of], (head, *units_b), flops=work
     )
     far_b = swap(emb_b)
     square = ((pair, pair), BF16)
@@ -299,28 +302,32 @@
         flops=4 * pair * pair * full,
         exps=2 * pair * pair,
     )
-    grad_a, grad_b = kernel_call(
+    term = ((part, full), BF16)
+    grad_a, grad_b, piece = kernel_call(
         score_second_kernel,
         "score_second",
-        [rows_of, rows_of],
-        (emb_a, emb_b, far_a, far_b, raw_a, raw_b, coef_a, coef_b),
+        [rows_of, rows_of, term],
+        (emb_a, emb_b, far_a, far_b, raw_a, raw_b, coef_a, coef_b, flip_a, flip_b),
         scratch=[turned],
-        flops=12 * pair * pair * full,
+        flops=12 * pair * pair * full + work // 2,
         exps=2 * pair * pair,
     )
 
-    def term(turn):
+    def terms(name, *turns):
         return kernel_call(
-            lambda *refs: term_kernel(turn, *refs),
-            "term_" + str(turn),
-            [((part, full), BF16)],
+            lambda *refs: terms_kernel(turns, *refs),
+            name,
+            [term] * len(turns),
             (flip_a, flip_b, grad_a, grad_b),
-            flops=work // 2,
-        )[0]
-
-    sent = [lax.ppermute(term(turn), AXES, ring(turn)) for turn in (2, 1, 3)]
+            flops=len(turns) * work // 2,
+        )
+
+    pieces = [piece, *terms("terms_near", 1, 3)]
+    sent = [lax.ppermute(piece, AXES, ring(turn)) for piece, turn in zip(pieces, (2, 1, 3))]
+    (kept,) = terms("term_own", 0)
+    (early,) = kernel_call(add_kernel, "add_far", [((part, full), F32)], (kept, sent[0]))
     (sums,) = kernel_call(
-        sum_kernel, "sum_terms", [((RING * RING, part // RING // 4, full), BF16)], (term(0), *sent)
+        sum_kernel, "sum_terms", [((RING * RING, part // RING // 4, full), BF16)], (early, *sent[1:])
     )
     swapped = lax.all_to_all(sums, AXES, 0, 0, axis_index_groups=REDUCE_GROUPS, tiled=True)
     total = jnp.sum(swapped.astype(F32), axis=0)

time: 92.6 us -> 159 us (1.72)
  Pallas kernels: 21.3 us -> 87.1 us
    pallas_call x10, Pallas kernels: 21.3 us -> 87.1 us  [kernel_call(): pl.pallas_call(body, out_shape=shapes, in_specs=[space] * len(operands),...]
    ppermute x1, starting transfers between devices: 2.72 us -> 0.19 us  [local(): far_bottom = lax.ppermute(bottom, AXES, FAR_SWAP)]
    ppermute x4, starting transfers between devices: 6.28 us -> 8.64 us  [swap(): return lax.ppermute(value, AXES, CORES_SWAP)]
    ppermute x3, waiting for transfers between devices: 12.3 us -> 10.4 us  [local(): lax.ppermute(piece, AXES, ring(turn))]
    ppermute x3, waiting for transfers between devices: 0.01 us -> 1.82 us  [local(): lax.ppermute(second, AXES, ring(turn))]
    all_to_all x1, starting transfers between devices: 5.77 us -> 4.12 us  [local(): lax.all_to_all(sums, AXES, 0, 0, axis_index_groups=REDUCE_GROUPS, tiled=T...]
  transfers between devices with their start and end apart: 17 -> 17, of which waited for: 7 -> 9; matrix products, arithmetic and copies ran while one was open for 1% -> 1% of each run, Pallas kernels for 9% -> 7%
where the time goes in v5:
time: 159 us
  Pallas kernels  87.1 us (55%)
  waiting for transfers between devices  35 us (22%)
  starting transfers between devices  34.2 us (22%)
  other arithmetic  1.98 us (1%)
    pallas_call x10, Pallas kernels, kernel_call(): pl.pallas_call(body, out_shape=shapes, in_specs=[space] * len(operands),...  87.1 us
    all_to_all x1, waiting for transfers between devices, local(): lax.all_to_all(sums, AXES, 0, 0, axis_index_groups=REDUCE_GROUPS, tiled=T...  14.5 us
    ppermute x3, waiting for transfers between devices, local(): lax.ppermute(piece, AXES, ring(turn))  10.4 us
    ppermute x4, starting transfers between devices, swap(): return lax.ppermute(value, AXES, CORES_SWAP)  8.64 us
    ppermute x3, starting transfers between devices, local(): lax.ppermute(second, AXES, ring(turn))  5.87 us
    ppermute x1, waiting for transfers between devices, local(): far_bottom = lax.ppermute(bottom, AXES, FAR_SWAP)  5.81 us
    ppermute x3, starting transfers between devices, local(): lax.ppermute(piece, AXES, ring(turn))  5.74 us
    ppermute x3, starting transfers between devices, local(): units_a = [lax.ppermute(send, AXES, first_ring(turn)) for turn in turns]  5.07 us
  transfers between devices with their start and end apart: 17, of which 9 were waited for; matrix products, arithmetic and copies ran while one was open for 1% of the time, Pallas kernels for 7%

profile of v5, /device:TPU:1, one launch (start us, length us, event | category | flops | bytes accessed | tf_op | source)
XLA Modules:
  0.0 159.0 jit_solution(9484858483719203669)
XLA Ops:
  0.6 68.2 %pick.1 = (bf16[128,1152]{1,0:T(8,128)(2,1)}, bf16[128,1152]{1,0:T(8,128)(2,1)}, bf16[128,1152]{1,0:T(8,128)(2,1)}, bf16[320,1152]{1,0:T(8,128)(2,1)}, bf16[256,1152]{1,0:T(8,128)(2,1)}) custom-call(bf16[128,1152]{1,0:T(8,128)(2,1)} %img_feats.1, bf16[128,1152]{1,0:T(8,128)(2,1)} %txt_feats.1, bf16[576,1152]{1,0:T(8,128)(2,1)} %bitcast.2, ...), custom_call_target="tpu_custom_call" | custom-call | bytes 5455872 | tf_op jit(solution)/shard_map/pick/pallas_call | solution.py:238
  68.9 1.5 collective-permute-start.2
  70.4 4.5 %collective-permute-start.6 = (bf16[128,1152]{1,0:T(8,128)(2,1)}, bf16[128,1152]{1,0:T(8,128)(2,1)S(1)}, u32[]{:S(2)}, u32[]{:S(2)}) collective-permute-start(bf16[128,1152]{1,0:T(8,128)(2,1)} %get-tuple-element.24), channel_id=1, source_target_pairs={{2,7},{1,6},{4,3},{7,2},{10,15},{9,14},{12,11},{15,10},{18,23},{17... | collective-permute-start | bytes 884744 | tf_op jit(solution)/shard_map/ppermute | solution.py:271
  74.9 0.1 collective-permute-start
  74.9 0.2 collective-permute-start.1
  75.1 3.0 %collective-permute-start.5 = (bf16[128,1152]{1,0:T(8,128)(2,1)}, bf16[128,1152]{1,0:T(8,128)(2,1)S(1)}, u32[]{:S(2)}, u32[]{:S(2)}) collective-permute-start(bf16[128,1152]{1,0:T(8,128)(2,1)} %get-tuple-element.24), channel_id=1, source_target_pairs={{0,64},{3,65},{6,68},{5,69},{8,72},{11,73},{14,76},{13,77},{16,80}... | collective-permute-start | bytes 884744 | tf_op jit(solution)/shard_map/ppermute | solution.py:273
  78.1 0.0 collective-permute-done.2
  78.1 0.8 collective-permute-start.4
  78.9 0.9 collective-permute-done.6
  79.9 1.3 collective-permute-start.3
  81.2 1.0 select_select_fusion
  82.2 0.6 collective-permute-done.5.refs_3_.refs_6_
  82.8 3.0 %collective-permute-start.9 = (bf16[128,1152]{1,0:T(8,128)(2,1)S(1)}, bf16[128,1152]{1,0:T(8,128)(2,1)S(1)}, u32[]{:S(2)}, u32[]{:S(2)}) collective-permute-start(bf16[128,1152]{1,0:T(8,128)(2,1)S(1)} %get-tuple-element.38.refs_0_.refs_7_), channel_id=1, source_target_pairs={{0,64},{2,18},{1,65},{3,19},{4,68},{6,22},{5,69},{7,23},{8,72},{10... | collective-permute-start | bytes 884744 | tf_op jit(solution)/shard_map/ppermute | solution.py:280
  85.7 5.8 %collective-permute-done.1.far_bottom = bf16[256,1152]{1,0:T(8,128)(2,1)S(1)} collective-permute-done((bf16[256,1152]{1,0:T(8,128)(2,1)}, bf16[256,1152]{1,0:T(8,128)(2,1)S(1)}, u32[]{:S(2)}, u32[]{:S(2)}) %collective-permute-start.1) | collective-permute-done | bytes 589856 | tf_op jit(solution)/shard_map/ppermute | solution.py:270
  91.5 2.9 %collective-permute-start.8 = (bf16[128,1152]{1,0:T(8,128)(2,1)S(1)}, bf16[128,1152]{1,0:T(8,128)(2,1)S(1)}, u32[]{:S(2)}, u32[]{:S(2)}) collective-permute-start(bf16[128,1152]{1,0:T(8,128)(2,1)S(1)} %get-tuple-element.38.refs_0_.refs_7_), channel_id=1, source_target_pairs={{0,96},{2,26},{1,97},{3,27},{4,100},{6,30},{5,101},{7,31},{8,104},... | collective-permute-start | bytes 884744 | tf_op jit(solution)/shard_map/ppermute | solution.py:280
  94.4 0.0 collective-permute-done.far_top
  94.4 0.0 collective-permute-start.7
  94.5 0.7 head.1.head_ref
  95.2 0.0 collective-permute-done.4.refs_2_.refs_5_
  95.2 0.0 collective-permute-done.3.refs_1_.refs_4_
  95.2 2.1 %embed_first.1 = (bf16[512,1152]{1,0:T(8,128)(2,1)S(1)}, bf16[512,1152]{1,0:T(8,128)(2,1)S(1)}) custom-call(bf16[1152,1152]{1,0:T(8,128)(2,1)S(1)} %head.1.head_ref, bf16[128,1152]{1,0:T(8,128)(2,1)S(1)} %get-tuple-element.39.refs_0_.refs_3_, bf16[128,1152]{1,0:T(8,128)(2,1)S(1)} %collective-permute-done.3.refs_1_.refs_4_, ...), custom_call_target="tpu_custom_call" | custom-call | flops 1358954496 | bytes 6193152 | tf_op jit(solution)/shard_map/embed_first/pallas_call | solution.py:238
  97.3 2.4 %collective-permute-start.10 = (bf16[512,1152]{1,0:T(8,128)(2,1)S(1)}, bf16[512,1152]{1,0:T(8,128)(2,1)S(1)}, u32[]{:S(2)}, u32[]{:S(2)}) collective-permute-start(bf16[512,1152]{1,0:T(8,128)(2,1)S(1)} %get-tuple-element.25.refs_0_.emb_a), channel_id=1, source_target_pairs={{0,2},{2,0},{1,3},{3,1},{4,6},{6,4},{5,7},{7,5},{8,10},{10,8},{9,1... | collective-permute-start | bytes 3538952 | tf_op jit(solution)/shard_map/ppermute | solution.py:258
  99.7 0.0 collective-permute-done.9.refs_3_.refs_10_
  99.7 0.0 collective-permute-done.8.refs_2_.refs_9_
  99.7 1.8 %collective-permute-done.7.refs_1_.refs_8_ = bf16[128,1152]{1,0:T(8,128)(2,1)S(1)} collective-permute-done((bf16[128,1152]{1,0:T(8,128)(2,1)S(1)}, bf16[128,1152]{1,0:T(8,128)(2,1)S(1)}, u32[]{:S(2)}, u32[]{:S(2)}) %collective-permute-start.7) | collective-permute-done | bytes 294944 | tf_op jit(solution)/shard_map/ppermute | solution.py:280
  101.5 2.1 %embed_second.1 = (bf16[512,1152]{1,0:T(8,128)(2,1)S(1)}, bf16[512,1152]{1,0:T(8,128)(2,1)S(1)}) custom-call(bf16[1152,1152]{1,0:T(8,128)(2,1)S(1)} %head.1.head_ref, bf16[128,1152]{1,0:T(8,128)(2,1)S(1)} %get-tuple-element.38.refs_0_.refs_7_, bf16[128,1152]{1,0:T(8,128)(2,1)S(1)} %collective-permute-done.7.refs_1_.refs_8_, ...), custom_call_target="tpu_custom_call" | custom-call | flops 1358954496 | bytes 6193152 | tf_op jit(solution)/shard_map/embed_second/pallas_call | solution.py:238
  103.6 3.2 %collective-permute-start.11 = (bf16[512,1152]{1,0:T(8,128)(2,1)S(1)}, bf16[512,1152]{1,0:T(8,128)(2,1)S(1)}, u32[]{:S(2)}, u32[]{:S(2)}) collective-permute-start(bf16[512,1152]{1,0:T(8,128)(2,1)S(1)} %get-tuple-element.26.refs_1_.emb_b), channel_id=1, source_target_pairs={{0,2},{2,0},{1,3},{3,1},{4,6},{6,4},{5,7},{7,5},{8,10},{10,8},{9,1... | collective-permute-start | bytes 3538952 | tf_op jit(solution)/shard_map/ppermute | solution.py:258
  106.8 0.0 collective-permute-done.10.refs_2_.far_a
  106.8 3.3 %score_first.1 = (bf16[512,512]{1,0:T(8,128)(2,1)S(1)}, bf16[512,512]{1,0:T(8,128)(2,1)S(1)}, bf16[4,288,512]{2,1,0:T(8,128)(2,1)S(1)}, bf16[4,288,512]{2,1,0:T(8,128)(2,1)S(1)}) custom-call(bf16[512,1152]{1,0:T(8,128)(2,1)S(1)} %get-tuple-element.25.refs_0_.emb_a, bf16[512,1152]{1,0:T(8,128)(2,1)S(1)} %get-tuple-element.26.refs_1_.emb_b, ...), custom_call_target="tpu_custom_call" | custom-call | flops 1207959552 | bytes 9306112 | tf_op jit(solution)/shard_map/score_first/pallas_call | solution.py:238
  110.1 0.0 collective-permute-done.11.far_b
  110.1 6.6 %score_second.1 = (bf16[512,1152]{1,0:T(8,128)(2,1)S(1)}, bf16[512,1152]{1,0:T(8,128)(2,1)S(1)}, bf16[288,1152]{1,0:T(8,128)(2,1)S(1)}) custom-call(bf16[512,1152]{1,0:T(8,128)(2,1)S(1)} %get-tuple-element.25.refs_0_.emb_a, bf16[512,1152]{1,0:T(8,128)(2,1)S(1)} %get-tuple-element.26.refs_1_.emb_b, ...), custom_call_target="tpu_custom_call" | custom-call | flops 4303355904 | bytes 13508608 | tf_op jit(solution)/shard_map/score_second/pallas_call | solution.py:238
  116.7 3.0 %collective-permute-start.12 = (bf16[288,1152]{1,0:T(8,128)(2,1)S(1)}, bf16[288,1152]{1,0:T(8,128)(2,1)S(1)}, u32[]{:S(2)}, u32[]{:S(2)}) collective-permute-start(bf16[288,1152]{1,0:T(8,128)(2,1)S(1)} %get-tuple-element.35), channel_id=1, source_target_pairs={{0,64},{2,18},{1,65},{3,19},{4,68},{6,22},{5,69},{7,23},{8,72},{10... | collective-permute-start | bytes 1990664 | tf_op jit(solution)/shard_map/ppermute | solution.py:326
  119.7 1.7 %terms_near.1 = (bf16[288,1152]{1,0:T(8,128)(2,1)S(1)}, bf16[288,1152]{1,0:T(8,128)(2,1)S(1)}) custom-call(bf16[4,288,512]{2,1,0:T(8,128)(2,1)S(1)} %get-tuple-element.27.flip_a.refs_0_, bf16[4,288,512]{2,1,0:T(8,128)(2,1)S(1)} %get-tuple-element.28.flip_b.refs_1_, bf16[512,1152]{1,0:T(8,128)(2,1)S(1)} %get-tuple-element.33.refs_2_, ...), custom_call_target="tpu_custom_call" | custom-call | flops 1358954496 | bytes 6045696 | tf_op jit(solution)/shard_map/terms_near/pallas_call | solution.py:238
  121.4 0.5 collective-permute-start.13
  121.9 2.3 %collective-permute-start.14 = (bf16[288,1152]{1,0:T(8,128)(2,1)S(1)}, bf16[288,1152]{1,0:T(8,128)(2,1)S(1)}, u32[]{:S(2)}, u32[]{:S(2)}) collective-permute-start(bf16[288,1152]{1,0:T(8,128)(2,1)S(1)} %get-tuple-element.37), channel_id=1, source_target_pairs={{0,96},{2,26},{1,97},{3,27},{4,100},{6,30},{5,101},{7,31},{8,104},... | collective-permute-start | bytes 1990664 | tf_op jit(solution)/shard_map/ppermute | solution.py:326
  124.2 0.9 term_own.1.left
  125.1 3.1 %collective-permute-done.12.right = bf16[288,1152]{1,0:T(8,128)(2,1)S(1)} collective-permute-done((bf16[288,1152]{1,0:T(8,128)(2,1)S(1)}, bf16[288,1152]{1,0:T(8,128)(2,1)S(1)}, u32[]{:S(2)}, u32[]{:S(2)}) %collective-permute-start.12) | collective-permute-done | bytes 663584 | tf_op jit(solution)/shard_map/ppermute | solution.py:326
  128.2 0.1 add_far.1.refs_0_
  128.3 6.9 %collective-permute-done.13.refs_1_ = bf16[288,1152]{1,0:T(8,128)(2,1)S(1)} collective-permute-done((bf16[288,1152]{1,0:T(8,128)(2,1)S(1)}, bf16[288,1152]{1,0:T(8,128)(2,1)S(1)}, u32[]{:S(2)}, u32[]{:S(2)}) %collective-permute-start.13) | collective-permute-done | bytes 663584 | tf_op jit(solution)/shard_map/ppermute | solution.py:326
  135.2 0.4 collective-permute-done.14.refs_2_
  135.6 1.3 sum_terms.1
  136.9 4.1 %all-to-all-start = ((bf16[16,18,1152]{2,1,0:T(8,128)(2,1)}), bf16[16,18,1152]{2,1,0:T(8,128)(2,1)S(1)}, u32[]{:S(2)}, u32[]{:S(2)}) async-start(bf16[16,18,1152]{2,1,0:T(8,128)(2,1)} %sum_terms.1), calls=%async_computation | async-start | bytes 1769472 | tf_op jit(solution)/shard_map/all_to_all | solution.py:332
  141.1 14.5 %all-to-all-done = bf16[16,18,1152]{2,1,0:T(8,128)(2,1)S(1)} async-done(((bf16[16,18,1152]{2,1,0:T(8,128)(2,1)}), bf16[16,18,1152]{2,1,0:T(8,128)(2,1)S(1)}, u32[]{:S(2)}, u32[]{:S(2)}) %all-to-all-start) | async-done | bytes 663584 | tf_op jit(solution)/shard_map/all_to_all | solution.py:332
  155.6 0.1 convert_reduce_fusion
  155.8 0.1 slice_select_fusion
  155.8 1.6 collective-permute-start.15
  157.4 0.9 collective-permute-done.15
  158.3 0.7 broadcast_select_fusion.1
  (4 shorter events, 0.0 us)
Async XLA Ops:
  68.9 25.6 %copy-start = (bf16[320,1152]{1,0:T(8,128)(2,1)S(1)}, bf16[320,1152]{1,0:T(8,128)(2,1)}, u32[]{:S(2)}) copy-start(bf16[320,1152]{1,0:T(8,128)(2,1)} %get-tuple-element.20.top) | copy-start | bytes 2211844
  68.9 25.6 %copy-start.1 = (bf16[256,1152]{1,0:T(8,128)(2,1)S(1)}, bf16[256,1152]{1,0:T(8,128)(2,1)}, u32[]{:S(2)}) copy-start(bf16[256,1152]{1,0:T(8,128)(2,1)} %get-tuple-element.21.bottom) | copy-start | bytes 1769476
  68.9 9.3 %collective-permute-start.2 = (bf16[128,1152]{1,0:T(8,128)(2,1)}, bf16[128,1152]{1,0:T(8,128)(2,1)S(1)}, u32[]{:S(2)}, u32[]{:S(2)}) collective-permute-start(bf16[128,1152]{1,0:T(8,128)(2,1)} %get-tuple-element.23), channel_id=1, source_target_pairs={{0,2},{2,0},{1,3},{3,1},{4,6},{6,4},{5,7},{7,5},{8,10},{10,8},{9,1... | collective-permute-start | bytes 884744 | tf_op jit(solution)/shard_map/ppermute | solution.py:258
  70.4 9.5 %collective-permute-start.6 = (bf16[128,1152]{1,0:T(8,128)(2,1)}, bf16[128,1152]{1,0:T(8,128)(2,1)S(1)}, u32[]{:S(2)}, u32[]{:S(2)}) collective-permute-start(bf16[128,1152]{1,0:T(8,128)(2,1)} %get-tuple-element.24), channel_id=1, source_target_pairs={{2,7},{1,6},{4,3},{7,2},{10,15},{9,14},{12,11},{15,10},{18,23},{17... | collective-permute-start | bytes 884744 | tf_op jit(solution)/shard_map/ppermute | solution.py:271
  74.9 19.6 %collective-permute-start = (bf16[320,1152]{1,0:T(8,128)(2,1)}, bf16[320,1152]{1,0:T(8,128)(2,1)S(1)}, u32[]{:S(2)}, u32[]{:S(2)}) collective-permute-start(bf16[320,1152]{1,0:T(8,128)(2,1)} %get-tuple-element.20.top), channel_id=1, source_target_pairs={{0,1},{2,3},{1,0},{3,2},{4,5},{6,7},{5,4},{7,6},{8,9},{10,11},{9,8... | collective-permute-start | bytes 2211848 | tf_op jit(solution)/shard_map/ppermute | solution.py:269
  74.9 16.6 %collective-permute-start.1 = (bf16[256,1152]{1,0:T(8,128)(2,1)}, bf16[256,1152]{1,0:T(8,128)(2,1)S(1)}, u32[]{:S(2)}, u32[]{:S(2)}) collective-permute-start(bf16[256,1152]{1,0:T(8,128)(2,1)} %get-tuple-element.21.bottom), channel_id=1, source_target_pairs={{0,5},{2,7},{1,4},{3,6},{4,1},{6,3},{5,0},{7,2},{8,13},{10,15},{9,... | collective-permute-start | bytes 1769480 | tf_op jit(solution)/shard_map/ppermute | solution.py:270
  75.1 7.6 %collective-permute-start.5 = (bf16[128,1152]{1,0:T(8,128)(2,1)}, bf16[128,1152]{1,0:T(8,128)(2,1)S(1)}, u32[]{:S(2)}, u32[]{:S(2)}) collective-permute-start(bf16[128,1152]{1,0:T(8,128)(2,1)} %get-tuple-element.24), channel_id=1, source_target_pairs={{0,64},{3,65},{6,68},{5,69},{8,72},{11,73},{14,76},{13,77},{16,80}... | collective-permute-start | bytes 884744 | tf_op jit(solution)/shard_map/ppermute | solution.py:273
  78.1 17.1 %collective-permute-start.4 = (bf16[128,1152]{1,0:T(8,128)(2,1)}, bf16[128,1152]{1,0:T(8,128)(2,1)S(1)}, u32[]{:S(2)}, u32[]{:S(2)}) collective-permute-start(bf16[128,1152]{1,0:T(8,128)(2,1)} %get-tuple-element.24), channel_id=1, source_target_pairs={{0,96},{3,97},{6,100},{5,101},{8,104},{11,105},{14,108},{13,109},{... | collective-permute-start | bytes 884744 | tf_op jit(solution)/shard_map/ppermute | solution.py:273
  79.9 15.4 %collective-permute-start.3 = (bf16[128,1152]{1,0:T(8,128)(2,1)}, bf16[128,1152]{1,0:T(8,128)(2,1)S(1)}, u32[]{:S(2)}, u32[]{:S(2)}) collective-permute-start(bf16[128,1152]{1,0:T(8,128)(2,1)} %get-tuple-element.24), channel_id=1, source_target_pairs={{0,32},{3,33},{6,36},{5,37},{8,40},{11,41},{14,44},{13,45},{16,48}... | collective-permute-start | bytes 884744 | tf_op jit(solution)/shard_map/ppermute | solution.py:273
  82.8 16.9 %collective-permute-start.9 = (bf16[128,1152]{1,0:T(8,128)(2,1)S(1)}, bf16[128,1152]{1,0:T(8,128)(2,1)S(1)}, u32[]{:S(2)}, u32[]{:S(2)}) collective-permute-start(bf16[128,1152]{1,0:T(8,128)(2,1)S(1)} %get-tuple-element.38.refs_0_.refs_7_), channel_id=1, source_target_pairs={{0,64},{2,18},{1,65},{3,19},{4,68},{6,22},{5,69},{7,23},{8,72},{10... | collective-permute-start | bytes 884744 | tf_op jit(solution)/shard_map/ppermute | solution.py:280
  91.5 8.2 %collective-permute-start.8 = (bf16[128,1152]{1,0:T(8,128)(2,1)S(1)}, bf16[128,1152]{1,0:T(8,128)(2,1)S(1)}, u32[]{:S(2)}, u32[]{:S(2)}) collective-permute-start(bf16[128,1152]{1,0:T(8,128)(2,1)S(1)} %get-tuple-element.38.refs_0_.refs_7_), channel_id=1, source_target_pairs={{0,96},{2,26},{1,97},{3,27},{4,100},{6,30},{5,101},{7,31},{8,104},... | collective-permute-start | bytes 884744 | tf_op jit(solution)/shard_map/ppermute | solution.py:280
  94.4 7.1 %collective-permute-start.7 = (bf16[128,1152]{1,0:T(8,128)(2,1)S(1)}, bf16[128,1152]{1,0:T(8,128)(2,1)S(1)}, u32[]{:S(2)}, u32[]{:S(2)}) collective-permute-start(bf16[128,1152]{1,0:T(8,128)(2,1)S(1)} %get-tuple-element.38.refs_0_.refs_7_), channel_id=1, source_target_pairs={{0,32},{2,10},{1,33},{3,11},{4,36},{6,14},{5,37},{7,15},{8,40},{10... | collective-permute-start | bytes 884744 | tf_op jit(solution)/shard_map/ppermute | solution.py:280
  97.3 9.5 %collective-permute-start.10 = (bf16[512,1152]{1,0:T(8,128)(2,1)S(1)}, bf16[512,1152]{1,0:T(8,128)(2,1)S(1)}, u32[]{:S(2)}, u32[]{:S(2)}) collective-permute-start(bf16[512,1152]{1,0:T(8,128)(2,1)S(1)} %get-tuple-element.25.refs_0_.emb_a), channel_id=1, source_target_pairs={{0,2},{2,0},{1,3},{3,1},{4,6},{6,4},{5,7},{7,5},{8,10},{10,8},{9,1... | collective-permute-start | bytes 3538952 | tf_op jit(solution)/shard_map/ppermute | solution.py:258
  103.6 6.5 %collective-permute-start.11 = (bf16[512,1152]{1,0:T(8,128)(2,1)S(1)}, bf16[512,1152]{1,0:T(8,128)(2,1)S(1)}, u32[]{:S(2)}, u32[]{:S(2)}) collective-permute-start(bf16[512,1152]{1,0:T(8,128)(2,1)S(1)} %get-tuple-element.26.refs_1_.emb_b), channel_id=1, source_target_pairs={{0,2},{2,0},{1,3},{3,1},{4,6},{6,4},{5,7},{7,5},{8,10},{10,8},{9,1... | collective-permute-start | bytes 3538952 | tf_op jit(solution)/shard_map/ppermute | solution.py:258
  116.7 11.4 %collective-permute-start.12 = (bf16[288,1152]{1,0:T(8,128)(2,1)S(1)}, bf16[288,1152]{1,0:T(8,128)(2,1)S(1)}, u32[]{:S(2)}, u32[]{:S(2)}) collective-permute-start(bf16[288,1152]{1,0:T(8,128)(2,1)S(1)} %get-tuple-element.35), channel_id=1, source_target_pairs={{0,64},{2,18},{1,65},{3,19},{4,68},{6,22},{5,69},{7,23},{8,72},{10... | collective-permute-start | bytes 1990664 | tf_op jit(solution)/shard_map/ppermute | solution.py:326
  121.4 13.8 %collective-permute-start.13 = (bf16[288,1152]{1,0:T(8,128)(2,1)S(1)}, bf16[288,1152]{1,0:T(8,128)(2,1)S(1)}, u32[]{:S(2)}, u32[]{:S(2)}) collective-permute-start(bf16[288,1152]{1,0:T(8,128)(2,1)S(1)} %get-tuple-element.36), channel_id=1, source_target_pairs={{0,32},{2,10},{1,33},{3,11},{4,36},{6,14},{5,37},{7,15},{8,40},{10... | collective-permute-start | bytes 1990664 | tf_op jit(solution)/shard_map/ppermute | solution.py:326
  121.9 13.7 %collective-permute-start.14 = (bf16[288,1152]{1,0:T(8,128)(2,1)S(1)}, bf16[288,1152]{1,0:T(8,128)(2,1)S(1)}, u32[]{:S(2)}, u32[]{:S(2)}) collective-permute-start(bf16[288,1152]{1,0:T(8,128)(2,1)S(1)} %get-tuple-element.37), channel_id=1, source_target_pairs={{0,96},{2,26},{1,97},{3,27},{4,100},{6,30},{5,101},{7,31},{8,104},... | collective-permute-start | bytes 1990664 | tf_op jit(solution)/shard_map/ppermute | solution.py:326
  136.9 18.7 %all-to-all-start = ((bf16[16,18,1152]{2,1,0:T(8,128)(2,1)}), bf16[16,18,1152]{2,1,0:T(8,128)(2,1)S(1)}, u32[]{:S(2)}, u32[]{:S(2)}) async-start(bf16[16,18,1152]{2,1,0:T(8,128)(2,1)} %sum_terms.1), calls=%async_computation | async-start | bytes 1769472 | tf_op jit(solution)/shard_map/all_to_all | solution.py:332
  155.8 2.5 %collective-permute-start.15 = (f32[18,576]{1,0:T(8,128)S(1)}, f32[18,576]{1,0:T(8,128)S(1)}, u32[]{:S(2)}, u32[]{:S(2)}) collective-permute-start(f32[18,576]{1,0:T(8,128)S(1)} %slice_select_fusion), channel_id=1, source_target_pairs={{0,2},{2,0},{1,3},{3,1},{4,6},{6,4},{5,7},{7,5},{8,10},{10,8},{9,1... | collective-permute-start | bytes 124424 | tf_op jit(solution)/shard_map/ppermute | solution.py:258

commit v6 on v5

--- a/solution.py
+++ b/solution.py
@@ -62,6 +62,14 @@
     )
 
 
+def vmem():
+    return pl.BlockSpec(memory_space=pltpu.VMEM)
+
+
+def anywhere_spec():
+    return pl.BlockSpec(memory_space=pl.ANY)
+
+
 def pick_kernel(img_feats, txt_feats, img_head, txt_head, mine, give, send, top, bottom, sems):
     _, _, high, core, tower = position()
     split, step = top.shape[0], 64
@@ -103,6 +111,10 @@
     choice(img_feats).wait()
 
 
+def inverse_norm(wide):
+    return 1.0 / jnp.sqrt(jnp.sum(wide * wide, axis=1, keepdims=True) + norm_eps)
+
+
 def embed_units(head, units, emb_ref, raw_ref):
     rows = units[0].shape[0]
     for i in range(0, len(units), 2):
@@ -110,12 +122,17 @@
         feats = jnp.concatenate([units[i][...], units[i + 1][...]], axis=0)
         raw = jnp.dot(feats, head, preferred_element_type=F32).astype(BF16)
         wide = raw.astype(F32)
-        norm = jnp.sqrt(jnp.sum(wide * wide, axis=1, keepdims=True) + norm_eps)
-        emb_ref[here, :] = (wide / norm).astype(BF16)
+        emb_ref[here, :] = (wide * inverse_norm(wide)).astype(BF16)
         raw_ref[here, :] = raw
 
 
-def head_kernel(top, bottom, far_top, far_bottom, head_ref):
+def flip_kernel(*refs):
+    *units, flip_ref = refs
+    for i, unit in enumerate(units):
+        flip_rows(unit[...], flip_ref, i * unit.shape[0])
+
+
+def head_kernel(top, bottom, far_top, far_bottom, _, head_ref):
     head_ref[...] = jnp.concatenate([top[...], bottom[...], far_top[...], far_bottom[...]], axis=0).T
 
 
@@ -166,7 +183,7 @@
 def score_first_kernel(*refs):
     core = position()[3]
     emb_a, emb_b, far_a = refs[:3]
-    *units, coef_a, coef_b, flip_a, flip_b, turned = refs[3:]
+    *units, coef_a, coef_b, flip_b, turned = refs[3:]
     turned[...] = far_a[...].T
     rows = emb_a.shape[0] // 2
     for emb, coef_ref in ((emb_a, coef_a), (emb_b, coef_b)):
@@ -177,8 +194,7 @@
             if emb is emb_b and i == 0:
                 result = with_positives(products, result, core == 0)
             coef_ref[here, :] = result
-    for i, unit in enumerate(units):
-        flip_rows(unit[...], flip_a if i < RING else flip_b, i % RING * unit.shape[0])
+    flip_kernel(*units, flip_b)
 
 
 def score_second_kernel(emb_a, emb_b, far_a, far_b, raw_a, raw_b, coef_a, coef_b, flip_a, flip_b, grad_a, grad_b, piece, turned):
@@ -196,10 +212,10 @@
                 result, far_b[...], preferred_element_type=F32
             )
             wide = raw[here, :].astype(F32)
-            norm = jnp.sqrt(jnp.sum(wide * wide, axis=1, keepdims=True) + norm_eps)
-            unit = wide / norm
+            inverse = inverse_norm(wide)
+            unit = wide * inverse
             inner = jnp.sum(unit * direction, axis=1, keepdims=True)
-            grad[here, :] = ((direction - unit * inner) / norm).astype(BF16)
+            grad[here, :] = ((direction - unit * inner) * inverse).astype(BF16)
     terms_kernel((2,), flip_a, flip_b, grad_a, grad_b, piece)
 
 
@@ -231,15 +247,14 @@
             out_ref[slot, :, width:] = total[(2 * j + 1) * part : (2 * j + 2) * part, columns]
 
 
-def kernel_call(body, name, shapes, operands, scratch=(), flops=0, exps=0, anywhere=False, limit=40):
+def kernel_call(body, name, shapes, operands, scratch=(), flops=0, exps=0, anywhere=(), limit=40):
     shapes = [jax.ShapeDtypeStruct(*shape) for shape in shapes]
-    space = pl.BlockSpec(memory_space=pl.ANY if anywhere else pltpu.VMEM)
     touched = sum(a.size * a.dtype.itemsize for a in (*shapes, *operands))
     return pl.pallas_call(
         body,
         out_shape=shapes,
-        in_specs=[space] * len(operands),
-        out_specs=[space] * len(shapes),
+        in_specs=[anywhere_spec() if i in anywhere else vmem() for i in range(len(operands))],
+        out_specs=[vmem()] * len(shapes),
         scratch_shapes=list(scratch),
         compiler_params=pltpu.CompilerParams(vmem_limit_bytes=limit * MIB),
         cost_estimate=pl.CostEstimate(flops=flops, bytes_accessed=touched, transcendentals=exps),
@@ -263,8 +278,8 @@
         [((rows, depth), BF16)] * 3 + [((5 * depth // 18, depth), BF16), ((2 * depth // 9, depth), BF16)],
         (img_feats, txt_feats, img_proj.T, txt_proj.T),
         scratch=(pltpu.SemaphoreType.DMA((width // 64 + 3,)),),
-        anywhere=True,
-        limit=54,
+        anywhere=range(4),
+        limit=56,
     )
     far_top = lax.ppermute(top, AXES, NEAR_SWAP)
     far_bottom = lax.ppermute(bottom, AXES, FAR_SWAP)
@@ -281,7 +296,11 @@
 
     rows_of = ((pair, full), BF16)
     work = 2 * pair * depth * full
-    (head,) = kernel_call(head_kernel, "head", [((depth, full), BF16)], (top, bottom, far_top, far_bottom))
+    flips = ((RING, part, pair), BF16)
+    (flip_a,) = kernel_call(flip_kernel, "flip_first", [flips], units_a)
+    (head,) = kernel_call(
+        head_kernel, "head", [((depth, full), BF16)], (top, bottom, far_top, far_bottom, flip_a), anywhere=(4,)
+    )
     emb_a, raw_a = kernel_call(
         embed_kernel, "embed_first", [rows_of, rows_of], (head, *units_a), flops=work
     )
@@ -291,13 +310,12 @@
     )
     far_b = swap(emb_b)
     square = ((pair, pair), BF16)
-    flips = ((RING, part, pair), BF16)
     turned = pltpu.VMEM((full, pair), BF16)
-    coef_a, coef_b, flip_a, flip_b = kernel_call(
+    coef_a, coef_b, flip_b = kernel_call(
         score_first_kernel,
         "score_first",
-        [square, square, flips, flips],
-        (emb_a, emb_b, far_a, *units_a, *units_b),
+        [square, square, flips],
+        (emb_a, emb_b, far_a, *units_b),
         scratch=[turned],
         flops=4 * pair * pair * full,
         exps=2 * pair * pair,

time: 159 us -> 90.8 us (0.57)
  Pallas kernels: 87.1 us -> 22.1 us
  waiting for transfers between devices: 35 us -> 31 us
    pallas_call x10 -> x11, Pallas kernels: 87.1 us -> 22.1 us  [kernel_call(): pl.pallas_call(body, out_shape=shapes, in_specs=[anywhere_spec() if i in...]
    ppermute x1, starting transfers between devices: 0.19 us -> 2.72 us  [local(): far_bottom = lax.ppermute(bottom, AXES, FAR_SWAP)]
    ppermute x4, starting transfers between devices: 8.64 us -> 6.13 us  [swap(): return lax.ppermute(value, AXES, CORES_SWAP)]
    ppermute x3, waiting for transfers between devices: 1.82 us -> 0.01 us  [local(): lax.ppermute(second, AXES, ring(turn))]
    all_to_all x1, starting transfers between devices: 4.12 us -> 5.76 us  [local(): lax.all_to_all(sums, AXES, 0, 0, axis_index_groups=REDUCE_GROUPS, tiled=T...]
  transfers between devices with their start and end apart: 17 -> 17, of which waited for: 9 -> 7; matrix products, arithmetic and copies ran while one was open for 1% -> 1% of each run, Pallas kernels for 7% -> 12%
where the time goes in v6:
time: 90.8 us; the launch traced here: 90.6 us
  starting transfers between devices  34.7 us (38%)
  waiting for transfers between devices  31 us (34%)
  Pallas kernels  22.1 us (24%)
  other arithmetic  1.98 us (2%)
    pallas_call x11, Pallas kernels, kernel_call(): pl.pallas_call(body, out_shape=shapes, in_specs=[anywhere_spec() if i in...  22.1 us
    all_to_all x1, waiting for transfers between devices, local(): lax.all_to_all(sums, AXES, 0, 0, axis_index_groups=REDUCE_GROUPS, tiled=T...  13.8 us
    ppermute x3, waiting for transfers between devices, local(): lax.ppermute(piece, AXES, ring(turn))  10.4 us
    ppermute x4, starting transfers between devices, swap(): return lax.ppermute(value, AXES, CORES_SWAP)  6.13 us
    all_to_all x1, starting transfers between devices, local(): lax.all_to_all(sums, AXES, 0, 0, axis_index_groups=REDUCE_GROUPS, tiled=T...  5.76 us
    ppermute x3, starting transfers between devices, local(): lax.ppermute(piece, AXES, ring(turn))  5.73 us
    ppermute x1, waiting for transfers between devices, local(): far_bottom = lax.ppermute(bottom, AXES, FAR_SWAP)  5.71 us
    ppermute x3, starting transfers between devices, local(): lax.ppermute(second, AXES, ring(turn))  5.32 us
  transfers between devices with their start and end apart: 17, of which 7 were waited for; matrix products, arithmetic and copies ran while one was open for 1% of the time, Pallas kernels for 12%

profile of v6, /device:TPU:1, one launch (start us, length us, event | category | flops | bytes accessed | tf_op | source)
XLA Modules:
  0.0 90.6 jit_solution(12223138439011902655)
XLA Ops:
  0.6 3.1 %pick.1 = (bf16[128,1152]{1,0:T(8,128)(2,1)}, bf16[128,1152]{1,0:T(8,128)(2,1)}, bf16[128,1152]{1,0:T(8,128)(2,1)}, bf16[320,1152]{1,0:T(8,128)(2,1)}, bf16[256,1152]{1,0:T(8,128)(2,1)}) custom-call(bf16[128,1152]{1,0:T(8,128)(2,1)} %img_feats.1, bf16[128,1152]{1,0:T(8,128)(2,1)} %txt_feats.1, bf16[576,1152]{1,0:T(8,128)(2,1)} %bitcast.2, ...), custom_call_target="tpu_custom_call" | custom-call | bytes 5455872 | tf_op jit(solution)/shard_map/pick/pallas_call | solution.py:253
  3.7 1.5 %collective-permute-start = (bf16[128,1152]{1,0:T(8,128)(2,1)}, bf16[128,1152]{1,0:T(8,128)(2,1)S(1)}, u32[]{:S(2)}, u32[]{:S(2)}) collective-permute-start(bf16[128,1152]{1,0:T(8,128)(2,1)} %get-tuple-element.20), channel_id=1, source_target_pairs={{0,2},{2,0},{1,3},{3,1},{4,6},{6,4},{5,7},{7,5},{8,10},{10,8},{9,1... | collective-permute-start | bytes 884744 | tf_op jit(solution)/shard_map/ppermute | solution.py:273
  5.2 4.5 %collective-permute-start.6 = (bf16[128,1152]{1,0:T(8,128)(2,1)}, bf16[128,1152]{1,0:T(8,128)(2,1)S(1)}, u32[]{:S(2)}, u32[]{:S(2)}) collective-permute-start(bf16[128,1152]{1,0:T(8,128)(2,1)} %get-tuple-element.21), channel_id=1, source_target_pairs={{2,7},{1,6},{4,3},{7,2},{10,15},{9,14},{12,11},{15,10},{18,23},{17... | collective-permute-start | bytes 884744 | tf_op jit(solution)/shard_map/ppermute | solution.py:286
  9.7 0.1 collective-permute-start.4
  9.8 3.0 %collective-permute-start.3 = (bf16[128,1152]{1,0:T(8,128)(2,1)}, bf16[128,1152]{1,0:T(8,128)(2,1)S(1)}, u32[]{:S(2)}, u32[]{:S(2)}) collective-permute-start(bf16[128,1152]{1,0:T(8,128)(2,1)} %get-tuple-element.21), channel_id=1, source_target_pairs={{0,64},{3,65},{6,68},{5,69},{8,72},{11,73},{14,76},{13,77},{16,80}... | collective-permute-start | bytes 884744 | tf_op jit(solution)/shard_map/ppermute | solution.py:288
  12.8 0.8 collective-permute-start.2
  13.6 0.0 collective-permute-done
  13.6 0.7 collective-permute-start.1
  14.3 0.0 collective-permute-done.6
  14.3 2.7 %collective-permute-start.5 = (bf16[256,1152]{1,0:T(8,128)(2,1)}, bf16[256,1152]{1,0:T(8,128)(2,1)S(1)}, u32[]{:S(2)}, u32[]{:S(2)}) collective-permute-start(bf16[256,1152]{1,0:T(8,128)(2,1)} %get-tuple-element.23.bottom), channel_id=1, source_target_pairs={{0,5},{2,7},{1,4},{3,6},{4,1},{6,3},{5,0},{7,2},{8,13},{10,15},{9,... | collective-permute-start | bytes 1769480 | tf_op jit(solution)/shard_map/ppermute | solution.py:285
  17.0 1.0 %select_select_fusion = (bf16[128,1152]{1,0:T(8,128)(2,1)S(1)}, bf16[128,1152]{1,0:T(8,128)(2,1)S(1)}) fusion(bf16[128,1152]{1,0:T(8,128)(2,1)S(1)} %collective-permute-done.6, bf16[128,1152]{1,0:T(8,128)(2,1)} %get-tuple-element.19, bf16[128,1152]{1,0:T(8,128)(2,1)S(1)} %collective-permute-done, pred[]{:T(512)S(6)} %eq.19, pred[]{:T(512)S(6)} %eq.18, pred[]{:T(512)S(6)} %eq.17), kind=kLoop, calls=%fused_computation.1 | loop fusion | flops 442368 | bytes 1474563 | tf_op jit(solution)/shard_map/jit(_where)/select_n | solution.py:293
  18.0 0.0 collective-permute-done.3.refs_3_
  18.0 3.0 %collective-permute-start.9 = (bf16[128,1152]{1,0:T(8,128)(2,1)S(1)}, bf16[128,1152]{1,0:T(8,128)(2,1)S(1)}, u32[]{:S(2)}, u32[]{:S(2)}) collective-permute-start(bf16[128,1152]{1,0:T(8,128)(2,1)S(1)} %get-tuple-element.36.refs_0_.refs_3_), channel_id=1, source_target_pairs={{0,64},{2,18},{1,65},{3,19},{4,68},{6,22},{5,69},{7,23},{8,72},{10... | collective-permute-start | bytes 884744 | tf_op jit(solution)/shard_map/ppermute | solution.py:295
  21.0 0.0 collective-permute-done.2.refs_2_
  21.0 2.3 %collective-permute-start.8 = (bf16[128,1152]{1,0:T(8,128)(2,1)S(1)}, bf16[128,1152]{1,0:T(8,128)(2,1)S(1)}, u32[]{:S(2)}, u32[]{:S(2)}) collective-permute-start(bf16[128,1152]{1,0:T(8,128)(2,1)S(1)} %get-tuple-element.36.refs_0_.refs_3_), channel_id=1, source_target_pairs={{0,96},{2,26},{1,97},{3,27},{4,100},{6,30},{5,101},{7,31},{8,104},... | collective-permute-start | bytes 884744 | tf_op jit(solution)/shard_map/ppermute | solution.py:295
  23.3 0.0 collective-permute-done.1.refs_1_
  23.3 0.0 collective-permute-start.7
  23.4 0.7 flip_first.1._.flip_a.refs_0_
  24.1 5.7 %collective-permute-done.5.far_bottom = bf16[256,1152]{1,0:T(8,128)(2,1)S(1)} collective-permute-done((bf16[256,1152]{1,0:T(8,128)(2,1)}, bf16[256,1152]{1,0:T(8,128)(2,1)S(1)}, u32[]{:S(2)}, u32[]{:S(2)}) %collective-permute-start.5) | collective-permute-done | bytes 589856 | tf_op jit(solution)/shard_map/ppermute | solution.py:285
  29.8 0.0 collective-permute-done.4.far_top
  29.8 0.7 head.1.head_ref
  30.6 2.1 %embed_first.1 = (bf16[512,1152]{1,0:T(8,128)(2,1)S(1)}, bf16[512,1152]{1,0:T(8,128)(2,1)S(1)}) custom-call(bf16[1152,1152]{1,0:T(8,128)(2,1)S(1)} %head.1.head_ref, bf16[128,1152]{1,0:T(8,128)(2,1)S(1)} %get-tuple-element.37.refs_0_, bf16[128,1152]{1,0:T(8,128)(2,1)S(1)} %collective-permute-done.1.refs_1_, ...), custom_call_target="tpu_custom_call" | custom-call | flops 1358954496 | bytes 6193152 | tf_op jit(solution)/shard_map/embed_first/pallas_call | solution.py:253
  32.7 1.7 %collective-permute-start.10 = (bf16[512,1152]{1,0:T(8,128)(2,1)S(1)}, bf16[512,1152]{1,0:T(8,128)(2,1)S(1)}, u32[]{:S(2)}, u32[]{:S(2)}) collective-permute-start(bf16[512,1152]{1,0:T(8,128)(2,1)S(1)} %get-tuple-element.24.refs_0_.emb_a), channel_id=1, source_target_pairs={{0,2},{2,0},{1,3},{3,1},{4,6},{6,4},{5,7},{7,5},{8,10},{10,8},{9,1... | collective-permute-start | bytes 3538952 | tf_op jit(solution)/shard_map/ppermute | solution.py:273
  34.4 0.0 collective-permute-done.8.refs_2_.refs_5_
  34.4 0.0 collective-permute-done.7.refs_1_.refs_4_
  34.4 2.1 %embed_second.1 = (bf16[512,1152]{1,0:T(8,128)(2,1)S(1)}, bf16[512,1152]{1,0:T(8,128)(2,1)S(1)}) custom-call(bf16[1152,1152]{1,0:T(8,128)(2,1)S(1)} %head.1.head_ref, bf16[128,1152]{1,0:T(8,128)(2,1)S(1)} %get-tuple-element.36.refs_0_.refs_3_, bf16[128,1152]{1,0:T(8,128)(2,1)S(1)} %collective-permute-done.7.refs_1_.refs_4_, ...), custom_call_target="tpu_custom_call" | custom-call | flops 1358954496 | bytes 6193152 | tf_op jit(solution)/shard_map/embed_second/pallas_call | solution.py:253
  36.5 0.1 collective-permute-start.11
  36.7 0.2 collective-permute-done.10.refs_2_.far_a
  36.9 2.6 %score_first.1 = (bf16[512,512]{1,0:T(8,128)(2,1)S(1)}, bf16[512,512]{1,0:T(8,128)(2,1)S(1)}, bf16[4,288,512]{2,1,0:T(8,128)(2,1)S(1)}) custom-call(bf16[512,1152]{1,0:T(8,128)(2,1)S(1)} %get-tuple-element.24.refs_0_.emb_a, bf16[512,1152]{1,0:T(8,128)(2,1)S(1)} %get-tuple-element.25.refs_1_.emb_b, ...), custom_call_target="tpu_custom_call" | custom-call | flops 1207959552 | bytes 6946816 | tf_op jit(solution)/shard_map/score_first/pallas_call | solution.py:253
  39.5 0.0 collective-permute-done.11.far_b
  39.5 6.7 %score_second.1 = (bf16[512,1152]{1,0:T(8,128)(2,1)S(1)}, bf16[512,1152]{1,0:T(8,128)(2,1)S(1)}, bf16[288,1152]{1,0:T(8,128)(2,1)S(1)}) custom-call(bf16[512,1152]{1,0:T(8,128)(2,1)S(1)} %get-tuple-element.24.refs_0_.emb_a, bf16[512,1152]{1,0:T(8,128)(2,1)S(1)} %get-tuple-element.25.refs_1_.emb_b, ...), custom_call_target="tpu_custom_call" | custom-call | flops 4303355904 | bytes 13508608 | tf_op jit(solution)/shard_map/score_second/pallas_call | solution.py:253
  46.2 3.0 %collective-permute-start.12 = (bf16[288,1152]{1,0:T(8,128)(2,1)S(1)}, bf16[288,1152]{1,0:T(8,128)(2,1)S(1)}, u32[]{:S(2)}, u32[]{:S(2)}) collective-permute-start(bf16[288,1152]{1,0:T(8,128)(2,1)S(1)} %get-tuple-element.33), channel_id=1, source_target_pairs={{0,64},{2,18},{1,65},{3,19},{4,68},{6,22},{5,69},{7,23},{8,72},{10... | collective-permute-start | bytes 1990664 | tf_op jit(solution)/shard_map/ppermute | solution.py:344
  49.2 1.7 %terms_near.1 = (bf16[288,1152]{1,0:T(8,128)(2,1)S(1)}, bf16[288,1152]{1,0:T(8,128)(2,1)S(1)}) custom-call(bf16[4,288,512]{2,1,0:T(8,128)(2,1)S(1)} %flip_first.1._.flip_a.refs_0_, bf16[4,288,512]{2,1,0:T(8,128)(2,1)S(1)} %get-tuple-element.26.flip_b.refs_1_, bf16[512,1152]{1,0:T(8,128)(2,1)S(1)} %get-tuple-element.31.refs_2_, ...), custom_call_target="tpu_custom_call" | custom-call | flops 1358954496 | bytes 6045696 | tf_op jit(solution)/shard_map/terms_near/pallas_call | solution.py:253
  50.8 0.5 collective-permute-start.13
  51.3 2.3 %collective-permute-start.14 = (bf16[288,1152]{1,0:T(8,128)(2,1)S(1)}, bf16[288,1152]{1,0:T(8,128)(2,1)S(1)}, u32[]{:S(2)}, u32[]{:S(2)}) collective-permute-start(bf16[288,1152]{1,0:T(8,128)(2,1)S(1)} %get-tuple-element.35), channel_id=1, source_target_pairs={{0,96},{2,26},{1,97},{3,27},{4,100},{6,30},{5,101},{7,31},{8,104},... | collective-permute-start | bytes 1990664 | tf_op jit(solution)/shard_map/ppermute | solution.py:344
  53.6 0.9 %term_own.1.left = bf16[288,1152]{1,0:T(8,128)(2,1)S(1)} custom-call(bf16[4,288,512]{2,1,0:T(8,128)(2,1)S(1)} %flip_first.1._.flip_a.refs_0_, bf16[4,288,512]{2,1,0:T(8,128)(2,1)S(1)} %get-tuple-element.26.flip_b.refs_1_, bf16[512,1152]{1,0:T(8,128)(2,1)S(1)} %get-tuple-element.31.refs_2_, bf16[512,1152]{1,0:T(8,128)(2,1)S(1)} %get-tuple-element.32.refs_3_), custom_call_target="tpu_custom_call" | custom-call | flops 679477248 | bytes 5382144 | tf_op jit(solution)/shard_map/term_own/pallas_call | solution.py:253
  54.5 3.1 %collective-permute-done.12.right = bf16[288,1152]{1,0:T(8,128)(2,1)S(1)} collective-permute-done((bf16[288,1152]{1,0:T(8,128)(2,1)S(1)}, bf16[288,1152]{1,0:T(8,128)(2,1)S(1)}, u32[]{:S(2)}, u32[]{:S(2)}) %collective-permute-start.12) | collective-permute-done | bytes 663584 | tf_op jit(solution)/shard_map/ppermute | solution.py:344
  57.6 0.1 add_far.1.refs_0_
  57.7 6.9 %collective-permute-done.13.refs_1_ = bf16[288,1152]{1,0:T(8,128)(2,1)S(1)} collective-permute-done((bf16[288,1152]{1,0:T(8,128)(2,1)S(1)}, bf16[288,1152]{1,0:T(8,128)(2,1)S(1)}, u32[]{:S(2)}, u32[]{:S(2)}) %collective-permute-start.13) | collective-permute-done | bytes 663584 | tf_op jit(solution)/shard_map/ppermute | solution.py:344
  64.7 0.4 collective-permute-done.14.refs_2_
  65.1 1.3 %sum_terms.1 = bf16[16,18,1152]{2,1,0:T(8,128)(2,1)} custom-call(f32[288,1152]{1,0:T(8,128)S(1)} %add_far.1.refs_0_, bf16[288,1152]{1,0:T(8,128)(2,1)S(1)} %collective-permute-done.13.refs_1_, bf16[288,1152]{1,0:T(8,128)(2,1)S(1)} %collective-permute-done.14.refs_2_), custom_call_target="tpu_custom_call" | custom-call | bytes 3317760 | tf_op jit(solution)/shard_map/sum_terms/pallas_call | solution.py:253
  66.4 5.8 %all-to-all-start = ((bf16[16,18,1152]{2,1,0:T(8,128)(2,1)}), bf16[16,18,1152]{2,1,0:T(8,128)(2,1)S(1)}, u32[]{:S(2)}, u32[]{:S(2)}) async-start(bf16[16,18,1152]{2,1,0:T(8,128)(2,1)} %sum_terms.1), calls=%async_computation | async-start | bytes 1769472 | tf_op jit(solution)/shard_map/all_to_all | solution.py:350
  72.1 13.8 %all-to-all-done = bf16[16,18,1152]{2,1,0:T(8,128)(2,1)S(1)} async-done(((bf16[16,18,1152]{2,1,0:T(8,128)(2,1)}), bf16[16,18,1152]{2,1,0:T(8,128)(2,1)S(1)}, u32[]{:S(2)}, u32[]{:S(2)}) %all-to-all-start) | async-done | bytes 663584 | tf_op jit(solution)/shard_map/all_to_all | solution.py:350
  85.9 0.1 convert_reduce_fusion
  86.1 0.1 slice_select_fusion
  86.1 2.8 %collective-permute-start.15 = (f32[18,576]{1,0:T(8,128)S(1)}, f32[18,576]{1,0:T(8,128)S(1)}, u32[]{:S(2)}, u32[]{:S(2)}) collective-permute-start(f32[18,576]{1,0:T(8,128)S(1)} %slice_select_fusion), channel_id=1, source_target_pairs={{0,2},{2,0},{1,3},{3,1},{4,6},{6,4},{5,7},{7,5},{8,10},{10,8},{9,1... | collective-permute-start | bytes 124424 | tf_op jit(solution)/shard_map/ppermute | solution.py:273
  88.9 0.9 collective-permute-done.15
  89.8 0.7 broadcast_select_fusion.1
  (5 shorter events, 0.0 us)
Async XLA Ops:
  3.7 9.8 %collective-permute-start = (bf16[128,1152]{1,0:T(8,128)(2,1)}, bf16[128,1152]{1,0:T(8,128)(2,1)S(1)}, u32[]{:S(2)}, u32[]{:S(2)}) collective-permute-start(bf16[128,1152]{1,0:T(8,128)(2,1)} %get-tuple-element.20), channel_id=1, source_target_pairs={{0,2},{2,0},{1,3},{3,1},{4,6},{6,4},{5,7},{7,5},{8,10},{10,8},{9,1... | collective-permute-start | bytes 884744 | tf_op jit(solution)/shard_map/ppermute | solution.py:273
  5.2 9.0 %collective-permute-start.6 = (bf16[128,1152]{1,0:T(8,128)(2,1)}, bf16[128,1152]{1,0:T(8,128)(2,1)S(1)}, u32[]{:S(2)}, u32[]{:S(2)}) collective-permute-start(bf16[128,1152]{1,0:T(8,128)(2,1)} %get-tuple-element.21), channel_id=1, source_target_pairs={{2,7},{1,6},{4,3},{7,2},{10,15},{9,14},{12,11},{15,10},{18,23},{17... | collective-permute-start | bytes 884744 | tf_op jit(solution)/shard_map/ppermute | solution.py:286
  9.7 20.1 %collective-permute-start.4 = (bf16[320,1152]{1,0:T(8,128)(2,1)}, bf16[320,1152]{1,0:T(8,128)(2,1)S(1)}, u32[]{:S(2)}, u32[]{:S(2)}) collective-permute-start(bf16[320,1152]{1,0:T(8,128)(2,1)} %get-tuple-element.22.top), channel_id=1, source_target_pairs={{0,1},{2,3},{1,0},{3,2},{4,5},{6,7},{5,4},{7,6},{8,9},{10,11},{9,8... | collective-permute-start | bytes 2211848 | tf_op jit(solution)/shard_map/ppermute | solution.py:284
  9.8 8.2 %collective-permute-start.3 = (bf16[128,1152]{1,0:T(8,128)(2,1)}, bf16[128,1152]{1,0:T(8,128)(2,1)S(1)}, u32[]{:S(2)}, u32[]{:S(2)}) collective-permute-start(bf16[128,1152]{1,0:T(8,128)(2,1)} %get-tuple-element.21), channel_id=1, source_target_pairs={{0,64},{3,65},{6,68},{5,69},{8,72},{11,73},{14,76},{13,77},{16,80}... | collective-permute-start | bytes 884744 | tf_op jit(solution)/shard_map/ppermute | solution.py:288
  12.8 8.2 %collective-permute-start.2 = (bf16[128,1152]{1,0:T(8,128)(2,1)}, bf16[128,1152]{1,0:T(8,128)(2,1)S(1)}, u32[]{:S(2)}, u32[]{:S(2)}) collective-permute-start(bf16[128,1152]{1,0:T(8,128)(2,1)} %get-tuple-element.21), channel_id=1, source_target_pairs={{0,96},{3,97},{6,100},{5,101},{8,104},{11,105},{14,108},{13,109},{... | collective-permute-start | bytes 884744 | tf_op jit(solution)/shard_map/ppermute | solution.py:288
  13.6 9.8 %collective-permute-start.1 = (bf16[128,1152]{1,0:T(8,128)(2,1)}, bf16[128,1152]{1,0:T(8,128)(2,1)S(1)}, u32[]{:S(2)}, u32[]{:S(2)}) collective-permute-start(bf16[128,1152]{1,0:T(8,128)(2,1)} %get-tuple-element.21), channel_id=1, source_target_pairs={{0,32},{3,33},{6,36},{5,37},{8,40},{11,41},{14,44},{13,45},{16,48}... | collective-permute-start | bytes 884744 | tf_op jit(solution)/shard_map/ppermute | solution.py:288
  14.3 15.6 %collective-permute-start.5 = (bf16[256,1152]{1,0:T(8,128)(2,1)}, bf16[256,1152]{1,0:T(8,128)(2,1)S(1)}, u32[]{:S(2)}, u32[]{:S(2)}) collective-permute-start(bf16[256,1152]{1,0:T(8,128)(2,1)} %get-tuple-element.23.bottom), channel_id=1, source_target_pairs={{0,5},{2,7},{1,4},{3,6},{4,1},{6,3},{5,0},{7,2},{8,13},{10,15},{9,... | collective-permute-start | bytes 1769480 | tf_op jit(solution)/shard_map/ppermute | solution.py:285
  18.0 16.4 %collective-permute-start.9 = (bf16[128,1152]{1,0:T(8,128)(2,1)S(1)}, bf16[128,1152]{1,0:T(8,128)(2,1)S(1)}, u32[]{:S(2)}, u32[]{:S(2)}) collective-permute-start(bf16[128,1152]{1,0:T(8,128)(2,1)S(1)} %get-tuple-element.36.refs_0_.refs_3_), channel_id=1, source_target_pairs={{0,64},{2,18},{1,65},{3,19},{4,68},{6,22},{5,69},{7,23},{8,72},{10... | collective-permute-start | bytes 884744 | tf_op jit(solution)/shard_map/ppermute | solution.py:295
  21.0 13.4 %collective-permute-start.8 = (bf16[128,1152]{1,0:T(8,128)(2,1)S(1)}, bf16[128,1152]{1,0:T(8,128)(2,1)S(1)}, u32[]{:S(2)}, u32[]{:S(2)}) collective-permute-start(bf16[128,1152]{1,0:T(8,128)(2,1)S(1)} %get-tuple-element.36.refs_0_.refs_3_), channel_id=1, source_target_pairs={{0,96},{2,26},{1,97},{3,27},{4,100},{6,30},{5,101},{7,31},{8,104},... | collective-permute-start | bytes 884744 | tf_op jit(solution)/shard_map/ppermute | solution.py:295
  23.3 11.1 %collective-permute-start.7 = (bf16[128,1152]{1,0:T(8,128)(2,1)S(1)}, bf16[128,1152]{1,0:T(8,128)(2,1)S(1)}, u32[]{:S(2)}, u32[]{:S(2)}) collective-permute-start(bf16[128,1152]{1,0:T(8,128)(2,1)S(1)} %get-tuple-element.36.refs_0_.refs_3_), channel_id=1, source_target_pairs={{0,32},{2,10},{1,33},{3,11},{4,36},{6,14},{5,37},{7,15},{8,40},{10... | collective-permute-start | bytes 884744 | tf_op jit(solution)/shard_map/ppermute | solution.py:295
  23.4 6.5 %copy-start = (bf16[320,1152]{1,0:T(8,128)(2,1)S(1)}, bf16[320,1152]{1,0:T(8,128)(2,1)}, u32[]{:S(2)}) copy-start(bf16[320,1152]{1,0:T(8,128)(2,1)} %get-tuple-element.22.top) | copy-start | bytes 2211844
  23.4 6.5 %copy-start.1 = (bf16[256,1152]{1,0:T(8,128)(2,1)S(1)}, bf16[256,1152]{1,0:T(8,128)(2,1)}, u32[]{:S(2)}) copy-start(bf16[256,1152]{1,0:T(8,128)(2,1)} %get-tuple-element.23.bottom) | copy-start | bytes 1769476
  32.7 4.2 %collective-permute-start.10 = (bf16[512,1152]{1,0:T(8,128)(2,1)S(1)}, bf16[512,1152]{1,0:T(8,128)(2,1)S(1)}, u32[]{:S(2)}, u32[]{:S(2)}) collective-permute-start(bf16[512,1152]{1,0:T(8,128)(2,1)S(1)} %get-tuple-element.24.refs_0_.emb_a), channel_id=1, source_target_pairs={{0,2},{2,0},{1,3},{3,1},{4,6},{6,4},{5,7},{7,5},{8,10},{10,8},{9,1... | collective-permute-start | bytes 3538952 | tf_op jit(solution)/shard_map/ppermute | solution.py:273
  36.5 2.9 %collective-permute-start.11 = (bf16[512,1152]{1,0:T(8,128)(2,1)S(1)}, bf16[512,1152]{1,0:T(8,128)(2,1)S(1)}, u32[]{:S(2)}, u32[]{:S(2)}) collective-permute-start(bf16[512,1152]{1,0:T(8,128)(2,1)S(1)} %get-tuple-element.25.refs_1_.emb_b), channel_id=1, source_target_pairs={{0,2},{2,0},{1,3},{3,1},{4,6},{6,4},{5,7},{7,5},{8,10},{10,8},{9,1... | collective-permute-start | bytes 3538952 | tf_op jit(solution)/shard_map/ppermute | solution.py:273
  46.2 11.4 %collective-permute-start.12 = (bf16[288,1152]{1,0:T(8,128)(2,1)S(1)}, bf16[288,1152]{1,0:T(8,128)(2,1)S(1)}, u32[]{:S(2)}, u32[]{:S(2)}) collective-permute-start(bf16[288,1152]{1,0:T(8,128)(2,1)S(1)} %get-tuple-element.33), channel_id=1, source_target_pairs={{0,64},{2,18},{1,65},{3,19},{4,68},{6,22},{5,69},{7,23},{8,72},{10... | collective-permute-start | bytes 1990664 | tf_op jit(solution)/shard_map/ppermute | solution.py:344
  50.8 13.8 %collective-permute-start.13 = (bf16[288,1152]{1,0:T(8,128)(2,1)S(1)}, bf16[288,1152]{1,0:T(8,128)(2,1)S(1)}, u32[]{:S(2)}, u32[]{:S(2)}) collective-permute-start(bf16[288,1152]{1,0:T(8,128)(2,1)S(1)} %get-tuple-element.34), channel_id=1, source_target_pairs={{0,32},{2,10},{1,33},{3,11},{4,36},{6,14},{5,37},{7,15},{8,40},{10... | collective-permute-start | bytes 1990664 | tf_op jit(solution)/shard_map/ppermute | solution.py:344
  51.3 13.7 %collective-permute-start.14 = (bf16[288,1152]{1,0:T(8,128)(2,1)S(1)}, bf16[288,1152]{1,0:T(8,128)(2,1)S(1)}, u32[]{:S(2)}, u32[]{:S(2)}) collective-permute-start(bf16[288,1152]{1,0:T(8,128)(2,1)S(1)} %get-tuple-element.35), channel_id=1, source_target_pairs={{0,96},{2,26},{1,97},{3,27},{4,100},{6,30},{5,101},{7,31},{8,104},... | collective-permute-start | bytes 1990664 | tf_op jit(solution)/shard_map/ppermute | solution.py:344
  66.4 19.5 %all-to-all-start = ((bf16[16,18,1152]{2,1,0:T(8,128)(2,1)}), bf16[16,18,1152]{2,1,0:T(8,128)(2,1)S(1)}, u32[]{:S(2)}, u32[]{:S(2)}) async-start(bf16[16,18,1152]{2,1,0:T(8,128)(2,1)} %sum_terms.1), calls=%async_computation | async-start | bytes 1769472 | tf_op jit(solution)/shard_map/all_to_all | solution.py:350
  86.1 3.7 %collective-permute-start.15 = (f32[18,576]{1,0:T(8,128)S(1)}, f32[18,576]{1,0:T(8,128)S(1)}, u32[]{:S(2)}, u32[]{:S(2)}) collective-permute-start(f32[18,576]{1,0:T(8,128)S(1)} %slice_select_fusion), channel_id=1, source_target_pairs={{0,2},{2,0},{1,3},{3,1},{4,6},{6,4},{5,7},{7,5},{8,10},{10,8},{9,1... | collective-permute-start | bytes 124424 | tf_op jit(solution)/shard_map/ppermute | solution.py:273

commit v7 on v6

--- a/solution.py
+++ b/solution.py
@@ -42,8 +42,8 @@
 
 
 CORES_SWAP = [(device(*chip, core), device(*chip, 1 - core)) for chip in CHIPS for core in range(2)]
-NEAR_SWAP = per_core(*[lambda z, y, x: (z, y, x ^ 1)] * 2)
-FAR_SWAP = per_core(*[lambda z, y, x: (z, y, 3 - x)] * 2)
+IMG_HEADS = [(device(z, y, x, 0), device(z, y, x ^ 1, 0)) for z, y, x in CHIPS]
+TXT_HEADS = [(device(z, y, x, 1), device(z, y, 3 - x, 1)) for z, y, x in CHIPS]
 TEXTS_SWAP = [(device(z, y, x, block_of(x)), device(z, y, 3 - x, 1)) for z, y, x in CHIPS]
 
 REDUCE_GROUPS = [[device(z, y, x, 0) for y in range(RING) for x in range(RING)] for z in range(RING)] + [
@@ -64,51 +64,6 @@
 
 def vmem():
     return pl.BlockSpec(memory_space=pltpu.VMEM)
-
-
-def anywhere_spec():
-    return pl.BlockSpec(memory_space=pl.ANY)
-
-
-def pick_kernel(img_feats, txt_feats, img_head, txt_head, mine, give, send, top, bottom, sems):
-    _, _, high, core, tower = position()
-    split, step = top.shape[0], 64
-
-    def copies(feats, other, head):
-        moves = [(head.at[pl.ds(i, step)], top.at[pl.ds(i, step)]) for i in range(0, split, step)]
-        moves += [
-            (head.at[pl.ds(split + i, step)], bottom.at[pl.ds(i, step)])
-            for i in range(0, bottom.shape[0], step)
-        ]
-        moves += [(other, give), (feats, mine)]
-        return [pltpu.make_async_copy(*move, sems.at[i]) for i, move in enumerate(moves)]
-
-    def choice(feats):
-        return pltpu.make_async_copy(feats, send, sems.at[sems.shape[0] - 1])
-
-    holds_block = (high == tower).astype(jnp.int32) == core
-
-    @pl.when(holds_block)
-    def _():
-        choice(txt_feats).start()
-
-    @pl.when(jnp.logical_not(holds_block))
-    def _():
-        choice(img_feats).start()
-
-    @pl.when(core == 0)
-    def _():
-        for copy in copies(img_feats, txt_feats, img_head):
-            copy.start()
-
-    @pl.when(core == 1)
-    def _():
-        for copy in copies(txt_feats, img_feats, txt_head):
-            copy.start()
-
-    for copy in copies(img_feats, txt_feats, img_head):
-        copy.wait()
-    choice(img_feats).wait()
 
 
 def inverse_norm(wide):
@@ -132,8 +87,16 @@
         flip_rows(unit[...], flip_ref, i * unit.shape[0])
 
 
-def head_kernel(top, bottom, far_top, far_bottom, _, head_ref):
-    head_ref[...] = jnp.concatenate([top[...], bottom[...], far_top[...], far_bottom[...]], axis=0).T
+def head_kernel(img_head, txt_head, far_img, far_txt, head_ref):
+    core = position()[3]
+
+    @pl.when(core == 0)
+    def _():
+        head_ref[...] = jnp.concatenate([img_head[...], far_img[...]], axis=0).T
+
+    @pl.when(core == 1)
+    def _():
+        head_ref[...] = jnp.concatenate([txt_head[...], far_txt[...]], axis=0).T
 
 
 def embed_kernel(head_ref, *refs):
@@ -183,7 +146,7 @@
 def score_first_kernel(*refs):
     core = position()[3]
     emb_a, emb_b, far_a = refs[:3]
-    *units, coef_a, coef_b, flip_b, turned = refs[3:]
+    *units, coef_a, coef_b, flip_a, flip_b, turned = refs[3:]
     turned[...] = far_a[...].T
     rows = emb_a.shape[0] // 2
     for emb, coef_ref in ((emb_a, coef_a), (emb_b, coef_b)):
@@ -194,7 +157,8 @@
             if emb is emb_b and i == 0:
                 result = with_positives(products, result, core == 0)
             coef_ref[here, :] = result
-    flip_kernel(*units, flip_b)
+    flip_kernel(*units[:RING], flip_a)
+    flip_kernel(*units[RING:], flip_b)
 
 
 def score_second_kernel(emb_a, emb_b, far_a, far_b, raw_a, raw_b, coef_a, coef_b, flip_a, flip_b, grad_a, grad_b, piece, turned):
@@ -247,13 +211,13 @@
             out_ref[slot, :, width:] = total[(2 * j + 1) * part : (2 * j + 2) * part, columns]
 
 
-def kernel_call(body, name, shapes, operands, scratch=(), flops=0, exps=0, anywhere=(), limit=40):
+def kernel_call(body, name, shapes, operands, scratch=(), flops=0, exps=0, limit=40):
     shapes = [jax.ShapeDtypeStruct(*shape) for shape in shapes]
     touched = sum(a.size * a.dtype.itemsize for a in (*shapes, *operands))
     return pl.pallas_call(
         body,
         out_shape=shapes,
-        in_specs=[anywhere_spec() if i in anywhere else vmem() for i in range(len(operands))],
+        in_specs=[vmem()] * len(operands),
         out_specs=[vmem()] * len(shapes),
         scratch_shapes=list(scratch),
         compiler_params=pltpu.CompilerParams(vmem_limit_bytes=limit * MIB),
@@ -272,34 +236,28 @@
     def swap(value):
         return lax.ppermute(value, AXES, CORES_SWAP)
 
-    mine, give, send, top, bottom = kernel_call(
-        pick_kernel,
-        "pick",
-        [((rows, depth), BF16)] * 3 + [((5 * depth // 18, depth), BF16), ((2 * depth // 9, depth), BF16)],
-        (img_feats, txt_feats, img_proj.T, txt_proj.T),
-        scratch=(pltpu.SemaphoreType.DMA((width // 64 + 3,)),),
-        anywhere=range(4),
-        limit=56,
-    )
-    far_top = lax.ppermute(top, AXES, NEAR_SWAP)
-    far_bottom = lax.ppermute(bottom, AXES, FAR_SWAP)
+    _, _, high, core, tower = position()
+    block = (high == tower).astype(jnp.int32)
+    is_img = core == 0
+    img_head, txt_head = img_proj.T, txt_proj.T
+    far_img = lax.ppermute(img_head, AXES, IMG_HEADS)
+    far_txt = lax.ppermute(txt_head, AXES, TXT_HEADS)
+    send = jnp.where(block == core, txt_feats, img_feats)
     far_texts = lax.ppermute(send, AXES, TEXTS_SWAP)
     turns = (1, 3, 2)
     units_a = [lax.ppermute(send, AXES, first_ring(turn)) for turn in turns]
-    other = swap(give)
-    _, _, high, core, tower = position()
-    block = (high == tower).astype(jnp.int32)
+    mine = jnp.where(is_img, img_feats, txt_feats)
+    other = swap(jnp.where(is_img, txt_feats, img_feats))
     first = jnp.where(block == 1, mine, other)
-    second = jnp.where(core == 1, far_texts, jnp.where(block == 0, mine, other))
+    second = jnp.where(is_img, jnp.where(block == 0, mine, other), far_texts)
     units_a = [first, *units_a]
     units_b = [second] + [lax.ppermute(second, AXES, ring(turn)) for turn in turns]
 
     rows_of = ((pair, full), BF16)
     work = 2 * pair * depth * full
     flips = ((RING, part, pair), BF16)
-    (flip_a,) = kernel_call(flip_kernel, "flip_first", [flips], units_a)
     (head,) = kernel_call(
-        head_kernel, "head", [((depth, full), BF16)], (top, bottom, far_top, far_bottom, flip_a), anywhere=(4,)
+        head_kernel, "head", [((depth, full), BF16)], (img_head, txt_head, far_img, far_txt)
     )
     emb_a, raw_a = kernel_call(
         embed_kernel, "embed_first", [rows_of, rows_of], (head, *units_a), flops=work
@@ -311,11 +269,11 @@
     far_b = swap(emb_b)
     square = ((pair, pair), BF16)
     turned = pltpu.VMEM((full, pair), BF16)
-    coef_a, coef_b, flip_b = kernel_call(
+    coef_a, coef_b, flip_a, flip_b = kernel_call(
         score_first_kernel,
         "score_first",
-        [square, square, flips],
-        (emb_a, emb_b, far_a, *units_b),
+        [square, square, flips, flips],
+        (emb_a, emb_b, far_a, *units_a, *units_b),
         scratch=[turned],
         flops=4 * pair * pair * full,
         exps=2 * pair * pair,
@@ -349,7 +307,6 @@
     )
     swapped = lax.all_to_all(sums, AXES, 0, 0, axis_index_groups=REDUCE_GROUPS, tiled=True)
     total = jnp.sum(swapped.astype(F32), axis=0)
-    is_img = position()[3] == 0
     low, high = total[:, :width], total[:, width:]
     keep = jnp.where(is_img, low, high)
     got = swap(jnp.where(is_img, high, low))

time: 90.8 us -> 97.5 us (1.074)
  blocking collectives: 0 us -> 22.5 us
  starting transfers between devices: 34.7 us -> 23.7 us
  waiting for transfers between devices: 31 us -> 26.4 us
  Pallas kernels: 22.1 us -> 19.8 us
  other arithmetic: 1.98 us -> 4.03 us
    all_to_all x0 -> x1, blocking collectives: none -> 22.5 us  [local(): lax.all_to_all(sums, AXES, 0, 0, axis_index_groups=REDUCE_GROUPS, tiled=T...]
    all_to_all x1 -> x0, waiting for transfers between devices: 13.8 us -> none  [local(): lax.all_to_all(sums, AXES, 0, 0, axis_index_groups=REDUCE_GROUPS, tiled=T...]
    ppermute x1, waiting for transfers between devices: 0.01 us -> 9.62 us  [local(): far_texts = lax.ppermute(send, AXES, TEXTS_SWAP)]
    ppermute x4, starting transfers between devices: 6.13 us -> 0.26 us  [swap(): return lax.ppermute(value, AXES, CORES_SWAP)]
    all_to_all x1 -> x0, starting transfers between devices: 5.76 us -> none  [local(): lax.all_to_all(sums, AXES, 0, 0, axis_index_groups=REDUCE_GROUPS, tiled=T...]
    ppermute x2, waiting for transfers between devices: 5.72 us -> 0.01 us  [the longest x1 0.01 us: local(): far_img = lax.ppermute(img_head, AXES, IMG_HEADS)]
    ppermute x2, starting transfers between devices: 2.8 us -> 7.08 us  [the longest x1 5.21 us: local(): far_txt = lax.ppermute(txt_head, AXES, TXT_HEADS)]
    ppermute x3, waiting for transfers between devices: 0.01 us -> 3.32 us  [local(): lax.ppermute(second, AXES, ring(turn))]
  transfers between devices with their start and end apart: 17 -> 16, of which waited for: 7 -> 7; matrix products, arithmetic and copies ran while one was open for 1% -> 3% of each run, Pallas kernels for 12% -> 13%
where the time goes in v7:
time: 97.5 us; the launch traced here: 97.3 us
  waiting for transfers between devices  26.4 us (27%)
  starting transfers between devices  23.7 us (24%)
  blocking collectives  22.5 us (23%)
  Pallas kernels  19.8 us (20%)
  other arithmetic  4.03 us (4%)
    all_to_all x1, blocking collectives, local(): lax.all_to_all(sums, AXES, 0, 0, axis_index_groups=REDUCE_GROUPS, tiled=T...  22.5 us
    pallas_call x9, Pallas kernels, kernel_call(): pl.pallas_call(body, out_shape=shapes, in_specs=[vmem()] * len(operands),...  19.8 us
    ppermute x3, waiting for transfers between devices, local(): lax.ppermute(piece, AXES, ring(turn))  12.2 us
    ppermute x1, waiting for transfers between devices, local(): far_texts = lax.ppermute(send, AXES, TEXTS_SWAP)  9.62 us
    ppermute x3, starting transfers between devices, local(): units_a = [lax.ppermute(send, AXES, first_ring(turn)) for turn in turns]  5.24 us
    ppermute x1, starting transfers between devices, local(): far_txt = lax.ppermute(txt_head, AXES, TXT_HEADS)  5.21 us
    ppermute x3, starting transfers between devices, local(): lax.ppermute(second, AXES, ring(turn))  4.17 us
    ppermute x3, starting transfers between devices, local(): lax.ppermute(piece, AXES, ring(turn))  3.57 us
  transfers between devices with their start and end apart: 16, of which 7 were waited for; matrix products, arithmetic and copies ran while one was open for 3% of the time, Pallas kernels for 13%

profile of v7, /device:TPU:1, one launch (start us, length us, event | category | flops | bytes accessed | tf_op | source)
XLA Modules:
  0.0 97.3 jit_solution(17155877773705158284)
XLA Ops:
  0.6 0.0 copy-start.2
  0.6 1.9 %collective-permute-start = (bf16[576,1152]{1,0:T(8,128)(2,1)}, bf16[576,1152]{1,0:T(8,128)(2,1)}, u32[]{:S(2)}, u32[]{:S(2)}) collective-permute-start(bf16[576,1152]{1,0:T(8,128)(2,1)} %bitcast.2), channel_id=1, source_target_pairs={{0,1},{1,0},{4,5},{5,4},{8,9},{9,8},{12,13},{13,12},{16,17},{17,16... | collective-permute-start | bytes 3981320 | tf_op jit(solution)/shard_map/ppermute | solution.py:243
  2.5 5.2 %collective-permute-start.1 = (bf16[576,1152]{1,0:T(8,128)(2,1)}, bf16[576,1152]{1,0:T(8,128)(2,1)}, u32[]{:S(2)}, u32[]{:S(2)}) collective-permute-start(bf16[576,1152]{1,0:T(8,128)(2,1)} %bitcast.4), channel_id=1, source_target_pairs={{2,7},{3,6},{6,3},{7,2},{10,15},{11,14},{14,11},{15,10},{18,23},{1... | collective-permute-start | bytes 3981320 | tf_op jit(solution)/shard_map/ppermute | solution.py:244
  7.8 2.0 %broadcast_select_fusion = (bf16[128,1152]{1,0:T(8,128)(2,1)}, bf16[128,1152]{1,0:T(8,128)(2,1)}) fusion(bf16[128,1152]{1,0:T(8,128)(2,1)} %param.5, bf16[128,1152]{1,0:T(8,128)(2,1)} %param.4, pred[]{:T(512)S(6)} %eq.18, pred[]{:T(512)S(6)} %eq.15), kind=kLoop, calls=%fused_computation.2 | loop fusion | flops 294912 | bytes 1179650 | tf_op jit(solution)/shard_map/jit(_where)/select_n | solution.py:245
  9.8 0.0 collective-permute-start.2
  9.8 3.4 %collective-permute-start.6 = (bf16[128,1152]{1,0:T(8,128)(2,1)}, bf16[128,1152]{1,0:T(8,128)(2,1)}, u32[]{:S(2)}, u32[]{:S(2)}) collective-permute-start(bf16[128,1152]{1,0:T(8,128)(2,1)} %get-tuple-element.30), channel_id=1, source_target_pairs={{2,7},{1,6},{4,3},{7,2},{10,15},{9,14},{12,11},{15,10},{18,23},{17... | collective-permute-start | bytes 884744 | tf_op jit(solution)/shard_map/ppermute | solution.py:246
  13.2 3.0 %collective-permute-start.5 = (bf16[128,1152]{1,0:T(8,128)(2,1)}, bf16[128,1152]{1,0:T(8,128)(2,1)S(1)}, u32[]{:S(2)}, u32[]{:S(2)}) collective-permute-start(bf16[128,1152]{1,0:T(8,128)(2,1)} %get-tuple-element.30), channel_id=1, source_target_pairs={{0,64},{3,65},{6,68},{5,69},{8,72},{11,73},{14,76},{13,77},{16,80}... | collective-permute-start | bytes 884744 | tf_op jit(solution)/shard_map/ppermute | solution.py:248
  16.1 0.0 collective-permute-done.2
  16.2 0.8 collective-permute-start.4
  16.9 9.6 %collective-permute-done.6 = bf16[128,1152]{1,0:T(8,128)(2,1)} collective-permute-done((bf16[128,1152]{1,0:T(8,128)(2,1)}, bf16[128,1152]{1,0:T(8,128)(2,1)}, u32[]{:S(2)}, u32[]{:S(2)}) %collective-permute-start.6) | collective-permute-done | bytes 294944 | tf_op jit(solution)/shard_map/ppermute | solution.py:246
  26.5 1.5 %collective-permute-start.3 = (bf16[128,1152]{1,0:T(8,128)(2,1)}, bf16[128,1152]{1,0:T(8,128)(2,1)S(1)}, u32[]{:S(2)}, u32[]{:S(2)}) collective-permute-start(bf16[128,1152]{1,0:T(8,128)(2,1)} %get-tuple-element.30), channel_id=1, source_target_pairs={{0,32},{3,33},{6,36},{5,37},{8,40},{11,41},{14,44},{13,45},{16,48}... | collective-permute-start | bytes 884744 | tf_op jit(solution)/shard_map/ppermute | solution.py:248
  28.0 1.0 %select_select_fusion = (bf16[128,1152]{1,0:T(8,128)(2,1)S(1)}, bf16[128,1152]{1,0:T(8,128)(2,1)S(1)}) fusion(bf16[128,1152]{1,0:T(8,128)(2,1)} %collective-permute-done.6, bf16[128,1152]{1,0:T(8,128)(2,1)S(1)} %collective-permute-done.2, pred[]{:T(512)S(6)} %eq.19, pred[]{:T(512)S(6)} %eq.15, bf16[128,1152]{1,0:T(8,128)(2,1)} %param.4, ...), kind=kLoop, calls=%fused_computation.1 | loop fusion | flops 589824 | bytes 1769475 | tf_op jit(solution)/shard_map/jit(_where)/select_n | solution.py:252
  29.1 0.0 collective-permute-done.5.refs_3_.refs_6_
  29.1 2.7 %collective-permute-start.9 = (bf16[128,1152]{1,0:T(8,128)(2,1)S(1)}, bf16[128,1152]{1,0:T(8,128)(2,1)S(1)}, u32[]{:S(2)}, u32[]{:S(2)}) collective-permute-start(bf16[128,1152]{1,0:T(8,128)(2,1)S(1)} %get-tuple-element.28.refs_0_.refs_7_), channel_id=1, source_target_pairs={{0,64},{2,18},{1,65},{3,19},{4,68},{6,22},{5,69},{7,23},{8,72},{10... | collective-permute-start | bytes 884744 | tf_op jit(solution)/shard_map/ppermute | solution.py:254
  31.8 0.0 collective-permute-done.far_img
  31.8 1.1 %collective-permute-start.8 = (bf16[128,1152]{1,0:T(8,128)(2,1)S(1)}, bf16[128,1152]{1,0:T(8,128)(2,1)S(1)}, u32[]{:S(2)}, u32[]{:S(2)}) collective-permute-start(bf16[128,1152]{1,0:T(8,128)(2,1)S(1)} %get-tuple-element.28.refs_0_.refs_7_), channel_id=1, source_target_pairs={{0,96},{2,26},{1,97},{3,27},{4,100},{6,30},{5,101},{7,31},{8,104},... | collective-permute-start | bytes 884744 | tf_op jit(solution)/shard_map/ppermute | solution.py:254
  32.9 0.0 collective-permute-done.1.far_txt
  32.9 0.4 collective-permute-start.7
  33.3 2.5 %head.1.head_ref = bf16[1152,1152]{1,0:T(8,128)(2,1)S(1)} custom-call(bf16[576,1152]{1,0:T(8,128)(2,1)S(1)} %bitcast.3, bf16[576,1152]{1,0:T(8,128)(2,1)S(1)} %bitcast.5, bf16[576,1152]{1,0:T(8,128)(2,1)} %collective-permute-done.far_img, bf16[576,1152]{1,0:T(8,128)(2,1)} %collective-permute-done.1.far_txt), custom_call_target="tpu_custom_call" | custom-call | bytes 7962624 | tf_op jit(solution)/shard_map/head/pallas_call | solution.py:217
  35.7 0.0 collective-permute-done.4.refs_2_.refs_5_
  35.8 0.0 collective-permute-done.3.refs_1_.refs_4_
  35.8 2.1 %embed_first.1 = (bf16[512,1152]{1,0:T(8,128)(2,1)S(1)}, bf16[512,1152]{1,0:T(8,128)(2,1)S(1)}) custom-call(bf16[1152,1152]{1,0:T(8,128)(2,1)S(1)} %head.1.head_ref, bf16[128,1152]{1,0:T(8,128)(2,1)S(1)} %get-tuple-element.29.refs_0_.refs_3_, bf16[128,1152]{1,0:T(8,128)(2,1)S(1)} %collective-permute-done.3.refs_1_.refs_4_, ...), custom_call_target="tpu_custom_call" | custom-call | flops 1358954496 | bytes 6193152 | tf_op jit(solution)/shard_map/embed_first/pallas_call | solution.py:217
  37.9 0.1 collective-permute-start.10
  38.0 0.3 collective-permute-done.9.refs_3_.refs_10_
  38.2 0.2 collective-permute-done.8.refs_2_.refs_9_
  38.5 2.8 %collective-permute-done.7.refs_1_.refs_8_ = bf16[128,1152]{1,0:T(8,128)(2,1)S(1)} collective-permute-done((bf16[128,1152]{1,0:T(8,128)(2,1)S(1)}, bf16[128,1152]{1,0:T(8,128)(2,1)S(1)}, u32[]{:S(2)}, u32[]{:S(2)}) %collective-permute-start.7) | collective-permute-done | bytes 294944 | tf_op jit(solution)/shard_map/ppermute | solution.py:254
  41.3 2.1 %embed_second.1 = (bf16[512,1152]{1,0:T(8,128)(2,1)S(1)}, bf16[512,1152]{1,0:T(8,128)(2,1)S(1)}) custom-call(bf16[1152,1152]{1,0:T(8,128)(2,1)S(1)} %head.1.head_ref, bf16[128,1152]{1,0:T(8,128)(2,1)S(1)} %get-tuple-element.28.refs_0_.refs_7_, bf16[128,1152]{1,0:T(8,128)(2,1)S(1)} %collective-permute-done.7.refs_1_.refs_8_, ...), custom_call_target="tpu_custom_call" | custom-call | flops 1358954496 | bytes 6193152 | tf_op jit(solution)/shard_map/embed_second/pallas_call | solution.py:217
  43.4 0.1 collective-permute-start.11
  43.5 0.0 collective-permute-done.10.refs_2_.far_a
  43.5 3.3 %score_first.1 = (bf16[512,512]{1,0:T(8,128)(2,1)S(1)}, bf16[512,512]{1,0:T(8,128)(2,1)S(1)}, bf16[4,288,512]{2,1,0:T(8,128)(2,1)S(1)}, bf16[4,288,512]{2,1,0:T(8,128)(2,1)S(1)}) custom-call(bf16[512,1152]{1,0:T(8,128)(2,1)S(1)} %get-tuple-element.15.refs_0_.emb_a, bf16[512,1152]{1,0:T(8,128)(2,1)S(1)} %get-tuple-element.16.refs_1_.emb_b, ...), custom_call_target="tpu_custom_call" | custom-call | flops 1207959552 | bytes 9306112 | tf_op jit(solution)/shard_map/score_first/pallas_call | solution.py:217
  46.8 0.0 collective-permute-done.11.far_b
  46.8 6.7 %score_second.1 = (bf16[512,1152]{1,0:T(8,128)(2,1)S(1)}, bf16[512,1152]{1,0:T(8,128)(2,1)S(1)}, bf16[288,1152]{1,0:T(8,128)(2,1)S(1)}) custom-call(bf16[512,1152]{1,0:T(8,128)(2,1)S(1)} %get-tuple-element.15.refs_0_.emb_a, bf16[512,1152]{1,0:T(8,128)(2,1)S(1)} %get-tuple-element.16.refs_1_.emb_b, ...), custom_call_target="tpu_custom_call" | custom-call | flops 4303355904 | bytes 13508608 | tf_op jit(solution)/shard_map/score_second/pallas_call | solution.py:217
  53.5 0.8 collective-permute-start.12
  54.4 1.7 %terms_near.1 = (bf16[288,1152]{1,0:T(8,128)(2,1)S(1)}, bf16[288,1152]{1,0:T(8,128)(2,1)S(1)}) custom-call(bf16[4,288,512]{2,1,0:T(8,128)(2,1)S(1)} %get-tuple-element.17.flip_a.refs_0_, bf16[4,288,512]{2,1,0:T(8,128)(2,1)S(1)} %get-tuple-element.18.flip_b.refs_1_, bf16[512,1152]{1,0:T(8,128)(2,1)S(1)} %get-tuple-element.23.refs_2_, ...), custom_call_target="tpu_custom_call" | custom-call | flops 1358954496 | bytes 6045696 | tf_op jit(solution)/shard_map/terms_near/pallas_call | solution.py:217
  56.1 0.2 collective-permute-start.13
  56.3 2.5 %collective-permute-start.14 = (bf16[288,1152]{1,0:T(8,128)(2,1)S(1)}, bf16[288,1152]{1,0:T(8,128)(2,1)S(1)}, u32[]{:S(2)}, u32[]{:S(2)}) collective-permute-start(bf16[288,1152]{1,0:T(8,128)(2,1)S(1)} %get-tuple-element.27), channel_id=1, source_target_pairs={{0,96},{2,26},{1,97},{3,27},{4,100},{6,30},{5,101},{7,31},{8,104},... | collective-permute-start | bytes 1990664 | tf_op jit(solution)/shard_map/ppermute | solution.py:302
  58.8 0.9 term_own.1.left
  59.7 5.2 %collective-permute-done.12.right = bf16[288,1152]{1,0:T(8,128)(2,1)S(1)} collective-permute-done((bf16[288,1152]{1,0:T(8,128)(2,1)S(1)}, bf16[288,1152]{1,0:T(8,128)(2,1)S(1)}, u32[]{:S(2)}, u32[]{:S(2)}) %collective-permute-start.12) | collective-permute-done | bytes 663584 | tf_op jit(solution)/shard_map/ppermute | solution.py:302
  65.0 0.1 add_far.1.refs_0_
  65.1 6.9 %collective-permute-done.13.refs_1_ = bf16[288,1152]{1,0:T(8,128)(2,1)S(1)} collective-permute-done((bf16[288,1152]{1,0:T(8,128)(2,1)S(1)}, bf16[288,1152]{1,0:T(8,128)(2,1)S(1)}, u32[]{:S(2)}, u32[]{:S(2)}) %collective-permute-start.13) | collective-permute-done | bytes 663584 | tf_op jit(solution)/shard_map/ppermute | solution.py:302
  72.0 0.0 collective-permute-done.14.refs_2_
  72.0 0.4 sum_terms.1
  72.4 22.5 %all_to_all.5 = bf16[16,18,1152]{2,1,0:T(8,128)(2,1)S(1)} all-to-all(bf16[16,18,1152]{2,1,0:T(8,128)(2,1)S(1)} %sum_terms.1), channel_id=1, replica_groups={{0,1,4,5,8,9,12,13,16,17,20,21,24,25,28,29},{32,33,36,37,40,41,44,45,48..., dimensions={0} | all-to-all | bytes 1327104 | tf_op jit(solution)/shard_map/all_to_all | solution.py:308
  95.0 0.1 convert_reduce_fusion
  95.1 0.1 slice_select_fusion
  95.2 0.1 collective-permute-start.15
  95.3 1.2 %collective-permute-done.15 = f32[18,576]{1,0:T(8,128)S(1)} collective-permute-done((f32[18,576]{1,0:T(8,128)S(1)}, f32[18,576]{1,0:T(8,128)S(1)}, u32[]{:S(2)}, u32[]{:S(2)}) %collective-permute-start.15) | collective-permute-done | bytes 41504 | tf_op jit(solution)/shard_map/ppermute | solution.py:237
  96.5 0.7 broadcast_select_fusion.4
  (5 shorter events, 0.0 us)
Async XLA Ops:
  0.6 27.4 %copy-start.2 = (bf16[128,1152]{1,0:T(8,128)(2,1)S(1)}, bf16[128,1152]{1,0:T(8,128)(2,1)}, u32[]{:S(2)}) copy-start(bf16[128,1152]{1,0:T(8,128)(2,1)} %param.5) | copy-start | bytes 884740
  0.6 31.2 %collective-permute-start = (bf16[576,1152]{1,0:T(8,128)(2,1)}, bf16[576,1152]{1,0:T(8,128)(2,1)}, u32[]{:S(2)}, u32[]{:S(2)}) collective-permute-start(bf16[576,1152]{1,0:T(8,128)(2,1)} %bitcast.2), channel_id=1, source_target_pairs={{0,1},{1,0},{4,5},{5,4},{8,9},{9,8},{12,13},{13,12},{16,17},{17,16... | collective-permute-start | bytes 3981320 | tf_op jit(solution)/shard_map/ppermute | solution.py:243
  2.5 30.4 %collective-permute-start.1 = (bf16[576,1152]{1,0:T(8,128)(2,1)}, bf16[576,1152]{1,0:T(8,128)(2,1)}, u32[]{:S(2)}, u32[]{:S(2)}) collective-permute-start(bf16[576,1152]{1,0:T(8,128)(2,1)} %bitcast.4), channel_id=1, source_target_pairs={{2,7},{3,6},{6,3},{7,2},{10,15},{11,14},{14,11},{15,10},{18,23},{1... | collective-permute-start | bytes 3981320 | tf_op jit(solution)/shard_map/ppermute | solution.py:244
  7.7 25.5 %copy-start.1 = (bf16[1152,576]{0,1:T(8,128)(2,1)S(1)}, bf16[1152,576]{0,1:T(8,128)(2,1)}, u32[]{:S(2)}) copy-start(bf16[1152,576]{0,1:T(8,128)(2,1)} %param.7) | copy-start | bytes 3981316
  9.8 23.5 %copy-start = (bf16[1152,576]{0,1:T(8,128)(2,1)S(1)}, bf16[1152,576]{0,1:T(8,128)(2,1)}, u32[]{:S(2)}) copy-start(bf16[1152,576]{0,1:T(8,128)(2,1)} %param.6) | copy-start | bytes 3981316
  9.8 6.4 %collective-permute-start.2 = (bf16[128,1152]{1,0:T(8,128)(2,1)}, bf16[128,1152]{1,0:T(8,128)(2,1)S(1)}, u32[]{:S(2)}, u32[]{:S(2)}) collective-permute-start(bf16[128,1152]{1,0:T(8,128)(2,1)} %get-tuple-element.31), channel_id=1, source_target_pairs={{0,2},{2,0},{1,3},{3,1},{4,6},{6,4},{5,7},{7,5},{8,10},{10,8},{9,1... | collective-permute-start | bytes 884744 | tf_op jit(solution)/shard_map/ppermute | solution.py:237
  9.8 16.8 %collective-permute-start.6 = (bf16[128,1152]{1,0:T(8,128)(2,1)}, bf16[128,1152]{1,0:T(8,128)(2,1)}, u32[]{:S(2)}, u32[]{:S(2)}) collective-permute-start(bf16[128,1152]{1,0:T(8,128)(2,1)} %get-tuple-element.30), channel_id=1, source_target_pairs={{2,7},{1,6},{4,3},{7,2},{10,15},{9,14},{12,11},{15,10},{18,23},{17... | collective-permute-start | bytes 884744 | tf_op jit(solution)/shard_map/ppermute | solution.py:246
  13.2 15.9 %collective-permute-start.5 = (bf16[128,1152]{1,0:T(8,128)(2,1)}, bf16[128,1152]{1,0:T(8,128)(2,1)S(1)}, u32[]{:S(2)}, u32[]{:S(2)}) collective-permute-start(bf16[128,1152]{1,0:T(8,128)(2,1)} %get-tuple-element.30), channel_id=1, source_target_pairs={{0,64},{3,65},{6,68},{5,69},{8,72},{11,73},{14,76},{13,77},{16,80}... | collective-permute-start | bytes 884744 | tf_op jit(solution)/shard_map/ppermute | solution.py:248
  16.2 19.6 %collective-permute-start.4 = (bf16[128,1152]{1,0:T(8,128)(2,1)}, bf16[128,1152]{1,0:T(8,128)(2,1)S(1)}, u32[]{:S(2)}, u32[]{:S(2)}) collective-permute-start(bf16[128,1152]{1,0:T(8,128)(2,1)} %get-tuple-element.30), channel_id=1, source_target_pairs={{0,96},{3,97},{6,100},{5,101},{8,104},{11,105},{14,108},{13,109},{... | collective-permute-start | bytes 884744 | tf_op jit(solution)/shard_map/ppermute | solution.py:248
  26.5 9.2 %collective-permute-start.3 = (bf16[128,1152]{1,0:T(8,128)(2,1)}, bf16[128,1152]{1,0:T(8,128)(2,1)S(1)}, u32[]{:S(2)}, u32[]{:S(2)}) collective-permute-start(bf16[128,1152]{1,0:T(8,128)(2,1)} %get-tuple-element.30), channel_id=1, source_target_pairs={{0,32},{3,33},{6,36},{5,37},{8,40},{11,41},{14,44},{13,45},{16,48}... | collective-permute-start | bytes 884744 | tf_op jit(solution)/shard_map/ppermute | solution.py:248
  29.1 9.1 %collective-permute-start.9 = (bf16[128,1152]{1,0:T(8,128)(2,1)S(1)}, bf16[128,1152]{1,0:T(8,128)(2,1)S(1)}, u32[]{:S(2)}, u32[]{:S(2)}) collective-permute-start(bf16[128,1152]{1,0:T(8,128)(2,1)S(1)} %get-tuple-element.28.refs_0_.refs_7_), channel_id=1, source_target_pairs={{0,64},{2,18},{1,65},{3,19},{4,68},{6,22},{5,69},{7,23},{8,72},{10... | collective-permute-start | bytes 884744 | tf_op jit(solution)/shard_map/ppermute | solution.py:254
  31.8 6.7 %collective-permute-start.8 = (bf16[128,1152]{1,0:T(8,128)(2,1)S(1)}, bf16[128,1152]{1,0:T(8,128)(2,1)S(1)}, u32[]{:S(2)}, u32[]{:S(2)}) collective-permute-start(bf16[128,1152]{1,0:T(8,128)(2,1)S(1)} %get-tuple-element.28.refs_0_.refs_7_), channel_id=1, source_target_pairs={{0,96},{2,26},{1,97},{3,27},{4,100},{6,30},{5,101},{7,31},{8,104},... | collective-permute-start | bytes 884744 | tf_op jit(solution)/shard_map/ppermute | solution.py:254
  32.9 8.4 %collective-permute-start.7 = (bf16[128,1152]{1,0:T(8,128)(2,1)S(1)}, bf16[128,1152]{1,0:T(8,128)(2,1)S(1)}, u32[]{:S(2)}, u32[]{:S(2)}) collective-permute-start(bf16[128,1152]{1,0:T(8,128)(2,1)S(1)} %get-tuple-element.28.refs_0_.refs_7_), channel_id=1, source_target_pairs={{0,32},{2,10},{1,33},{3,11},{4,36},{6,14},{5,37},{7,15},{8,40},{10... | collective-permute-start | bytes 884744 | tf_op jit(solution)/shard_map/ppermute | solution.py:254
  37.9 5.6 %collective-permute-start.10 = (bf16[512,1152]{1,0:T(8,128)(2,1)S(1)}, bf16[512,1152]{1,0:T(8,128)(2,1)S(1)}, u32[]{:S(2)}, u32[]{:S(2)}) collective-permute-start(bf16[512,1152]{1,0:T(8,128)(2,1)S(1)} %get-tuple-element.15.refs_0_.emb_a), channel_id=1, source_target_pairs={{0,2},{2,0},{1,3},{3,1},{4,6},{6,4},{5,7},{7,5},{8,10},{10,8},{9,1... | collective-permute-start | bytes 3538952 | tf_op jit(solution)/shard_map/ppermute | solution.py:237
  43.4 3.4 %collective-permute-start.11 = (bf16[512,1152]{1,0:T(8,128)(2,1)S(1)}, bf16[512,1152]{1,0:T(8,128)(2,1)S(1)}, u32[]{:S(2)}, u32[]{:S(2)}) collective-permute-start(bf16[512,1152]{1,0:T(8,128)(2,1)S(1)} %get-tuple-element.16.refs_1_.emb_b), channel_id=1, source_target_pairs={{0,2},{2,0},{1,3},{3,1},{4,6},{6,4},{5,7},{7,5},{8,10},{10,8},{9,1... | collective-permute-start | bytes 3538952 | tf_op jit(solution)/shard_map/ppermute | solution.py:237
  53.5 11.4 %collective-permute-start.12 = (bf16[288,1152]{1,0:T(8,128)(2,1)S(1)}, bf16[288,1152]{1,0:T(8,128)(2,1)S(1)}, u32[]{:S(2)}, u32[]{:S(2)}) collective-permute-start(bf16[288,1152]{1,0:T(8,128)(2,1)S(1)} %get-tuple-element.25), channel_id=1, source_target_pairs={{0,64},{2,18},{1,65},{3,19},{4,68},{6,22},{5,69},{7,23},{8,72},{10... | collective-permute-start | bytes 1990664 | tf_op jit(solution)/shard_map/ppermute | solution.py:302
  56.1 16.0 %collective-permute-start.13 = (bf16[288,1152]{1,0:T(8,128)(2,1)S(1)}, bf16[288,1152]{1,0:T(8,128)(2,1)S(1)}, u32[]{:S(2)}, u32[]{:S(2)}) collective-permute-start(bf16[288,1152]{1,0:T(8,128)(2,1)S(1)} %get-tuple-element.26), channel_id=1, source_target_pairs={{0,32},{2,10},{1,33},{3,11},{4,36},{6,14},{5,37},{7,15},{8,40},{10... | collective-permute-start | bytes 1990664 | tf_op jit(solution)/shard_map/ppermute | solution.py:302
  56.3 15.8 %collective-permute-start.14 = (bf16[288,1152]{1,0:T(8,128)(2,1)S(1)}, bf16[288,1152]{1,0:T(8,128)(2,1)S(1)}, u32[]{:S(2)}, u32[]{:S(2)}) collective-permute-start(bf16[288,1152]{1,0:T(8,128)(2,1)S(1)} %get-tuple-element.27), channel_id=1, source_target_pairs={{0,96},{2,26},{1,97},{3,27},{4,100},{6,30},{5,101},{7,31},{8,104},... | collective-permute-start | bytes 1990664 | tf_op jit(solution)/shard_map/ppermute | solution.py:302
  95.2 1.3 %collective-permute-start.15 = (f32[18,576]{1,0:T(8,128)S(1)}, f32[18,576]{1,0:T(8,128)S(1)}, u32[]{:S(2)}, u32[]{:S(2)}) collective-permute-start(f32[18,576]{1,0:T(8,128)S(1)} %slice_select_fusion), channel_id=1, source_target_pairs={{0,2},{2,0},{1,3},{3,1},{4,6},{6,4},{5,7},{7,5},{8,10},{10,8},{9,1... | collective-permute-start | bytes 124424 | tf_op jit(solution)/shard_map/ppermute | solution.py:237

commit v8 on v7

--- a/solution.py
+++ b/solution.py
@@ -42,6 +42,8 @@
 
 
 CORES_SWAP = [(device(*chip, core), device(*chip, 1 - core)) for chip in CHIPS for core in range(2)]
+IMAGES_DOWN = [(device(*chip, 1), device(*chip, 0)) for chip in CHIPS]
+TEXTS_UP = [(device(*chip, 0), device(*chip, 1)) for chip in CHIPS]
 IMG_HEADS = [(device(z, y, x, 0), device(z, y, x ^ 1, 0)) for z, y, x in CHIPS]
 TXT_HEADS = [(device(z, y, x, 1), device(z, y, 3 - x, 1)) for z, y, x in CHIPS]
 TEXTS_SWAP = [(device(z, y, x, block_of(x)), device(z, y, 3 - x, 1)) for z, y, x in CHIPS]
@@ -87,16 +89,76 @@
         flip_rows(unit[...], flip_ref, i * unit.shape[0])
 
 
-def head_kernel(img_head, txt_head, far_img, far_txt, head_ref):
+def send_kernel(img_feats, txt_feats, send):
+    _, _, high, core, tower = position()
+    holds_block = (high == tower).astype(jnp.int32) == core
+
+    @pl.when(holds_block)
+    def _():
+        send[...] = txt_feats[...]
+
+    @pl.when(jnp.logical_not(holds_block))
+    def _():
+        send[...] = img_feats[...]
+
+
+def own_kernel(img_head, txt_head, img_feats, txt_feats, other_img, other_txt, far_texts, first, second, head, sems):
+    _, _, high, core, tower = position()
+    block = (high == tower).astype(jnp.int32)
+    step = head.shape[0] // sems.shape[0]
+
+    def copies(source):
+        return [
+            pltpu.make_async_copy(source.at[pl.ds(i * step, step)], head.at[pl.ds(i * step, step)], sems.at[i])
+            for i in range(sems.shape[0])
+        ]
+
+    @pl.when(core == 0)
+    def _():
+        for copy in copies(img_head):
+            copy.start()
+
+    @pl.when(core == 1)
+    def _():
+        for copy in copies(txt_head):
+            copy.start()
+
+    @pl.when((core == 0) & (block == 0))
+    def _():
+        first[...] = other_img[...]
+        second[...] = img_feats[...]
+
+    @pl.when((core == 0) & (block == 1))
+    def _():
+        first[...] = img_feats[...]
+        second[...] = other_img[...]
+
+    @pl.when(core == 1)
+    def _():
+        second[...] = far_texts[...]
+
+    @pl.when((core == 1) & (block == 0))
+    def _():
+        first[...] = other_txt[...]
+
+    @pl.when((core == 1) & (block == 1))
+    def _():
+        first[...] = txt_feats[...]
+
+    for copy in copies(img_head):
+        copy.wait()
+
+
+def head_kernel(own, far_img, far_txt, head_ref):
     core = position()[3]
 
     @pl.when(core == 0)
     def _():
-        head_ref[...] = jnp.concatenate([img_head[...], far_img[...]], axis=0).T
+        head_ref[...] = jnp.concatenate([own[...], far_img[...]], axis=0).T
 
     @pl.when(core == 1)
     def _():
-        head_ref[...] = jnp.concatenate([txt_head[...], far_txt[...]], axis=0).T
+        head_ref[...] = jnp.concatenate([own[...], far_txt[...]], axis=0).T
 
 
 def embed_kernel(head_ref, *refs):
@@ -211,13 +273,13 @@
             out_ref[slot, :, width:] = total[(2 * j + 1) * part : (2 * j + 2) * part, columns]
 
 
-def kernel_call(body, name, shapes, operands, scratch=(), flops=0, exps=0, limit=40):
+def kernel_call(body, name, shapes, operands, scratch=(), flops=0, exps=0, anywhere=0, limit=40):
     shapes = [jax.ShapeDtypeStruct(*shape) for shape in shapes]
     touched = sum(a.size * a.dtype.itemsize for a in (*shapes, *operands))
     return pl.pallas_call(
         body,
         out_shape=shapes,
-        in_specs=[vmem()] * len(operands),
+        in_specs=[pl.BlockSpec(memory_space=pl.ANY)] * anywhere + [vmem()] * (len(operands) - anywhere),
         out_specs=[vmem()] * len(shapes),
         scratch_shapes=list(scratch),
         compiler_params=pltpu.CompilerParams(vmem_limit_bytes=limit * MIB),
@@ -236,20 +298,25 @@
     def swap(value):
         return lax.ppermute(value, AXES, CORES_SWAP)
 
-    _, _, high, core, tower = position()
-    block = (high == tower).astype(jnp.int32)
-    is_img = core == 0
+    is_img = position()[3] == 0
     img_head, txt_head = img_proj.T, txt_proj.T
+    unit = ((rows, depth), BF16)
+    far_texts = lax.ppermute(txt_feats, AXES, TEXTS_SWAP)
     far_img = lax.ppermute(img_head, AXES, IMG_HEADS)
     far_txt = lax.ppermute(txt_head, AXES, TXT_HEADS)
-    send = jnp.where(block == core, txt_feats, img_feats)
-    far_texts = lax.ppermute(send, AXES, TEXTS_SWAP)
+    other_img = lax.ppermute(img_feats, AXES, IMAGES_DOWN)
+    other_txt = lax.ppermute(txt_feats, AXES, TEXTS_UP)
+    (send,) = kernel_call(send_kernel, "send", [unit], (img_feats, txt_feats))
     turns = (1, 3, 2)
     units_a = [lax.ppermute(send, AXES, first_ring(turn)) for turn in turns]
-    mine = jnp.where(is_img, img_feats, txt_feats)
-    other = swap(jnp.where(is_img, txt_feats, img_feats))
-    first = jnp.where(block == 1, mine, other)
-    second = jnp.where(is_img, jnp.where(block == 0, mine, other), far_texts)
+    first, second, own_head = kernel_call(
+        own_kernel,
+        "own",
+        [unit, unit, ((width, depth), BF16)],
+        (img_head, txt_head, img_feats, txt_feats, other_img, other_txt, far_texts),
+        scratch=(pltpu.SemaphoreType.DMA((4,)),),
+        anywhere=2,
+    )
     units_a = [first, *units_a]
     units_b = [second] + [lax.ppermute(second, AXES, ring(turn)) for turn in turns]
 
@@ -257,7 +324,7 @@
     work = 2 * pair * depth * full
     flips = ((RING, part, pair), BF16)
     (head,) = kernel_call(
-        head_kernel, "head", [((depth, full), BF16)], (img_head, txt_head, far_img, far_txt)
+        head_kernel, "head", [((depth, full), BF16)], (own_head, far_img, far_txt)
     )
     emb_a, raw_a = kernel_call(
         embed_kernel, "embed_first", [rows_of, rows_of], (head, *units_a), flops=work

time: 97.5 us -> 101 us (1.036)
  blocking collectives: 22.5 us -> 0 us
  waiting for transfers between devices: 26.4 us -> 39.1 us
  starting transfers between devices: 23.7 us -> 33.4 us
  local copies, waits for them, and re-layouts: 0.01 us -> 6.48 us
  other arithmetic: 4.03 us -> 0.95 us
    all_to_all x1 -> x0, blocking collectives: 22.5 us -> none  [local(): lax.all_to_all(sums, AXES, 0, 0, axis_index_groups=REDUCE_GROUPS, tiled=T...]
    all_to_all x0 -> x1, waiting for transfers between devices: none -> 14.8 us  [local(): lax.all_to_all(sums, AXES, 0, 0, axis_index_groups=REDUCE_GROUPS, tiled=T...]
    all_to_all x0 -> x1, starting transfers between devices: none -> 7.33 us  [local(): lax.all_to_all(sums, AXES, 0, 0, axis_index_groups=REDUCE_GROUPS, tiled=T...]
    unnamed x6 -> x12, local copies, waits for them, and re-layouts: 0.01 us -> 6.48 us
    ppermute x1 -> x3, starting transfers between devices: 3.37 us -> 6.63 us  [the longest x1 3.73 us: local(): far_texts = lax.ppermute(txt_feats, AXES, TEXTS_SWAP)]
    select_n x2 -> x0, other arithmetic: 3.07 us -> none  [the longest x1 2.03 us: local(): send = jnp.where(block == core, txt_feats, img_feats)]
    ppermute x1 -> x3, waiting for transfers between devices: 9.62 us -> 7.31 us  [the longest x1 7.3 us: local(): far_texts = lax.ppermute(txt_feats, AXES, TEXTS_SWAP)]
    ppermute x3, starting transfers between devices: 4.17 us -> 2.93 us  [local(): lax.ppermute(second, AXES, ring(turn))]
  transfers between devices with their start and end apart: 16 -> 18, of which waited for: 7 -> 7; matrix products, arithmetic and copies ran while one was open for 3% -> 0% of each run, Pallas kernels for 13% -> 11%
where the time goes in v8:
time: 101 us; the launch traced here: 100 us
  waiting for transfers between devices  39.1 us (39%)
  starting transfers between devices  33.4 us (33%)
  Pallas kernels  19.5 us (19%)
  local copies, waits for them, and re-layouts  6.48 us (6%)
    pallas_call x11, Pallas kernels, kernel_call(): pl.pallas_call(body, out_shape=shapes, in_specs=[pl.BlockSpec(memory_spac...  19.5 us
    all_to_all x1, waiting for transfers between devices, local(): lax.all_to_all(sums, AXES, 0, 0, axis_index_groups=REDUCE_GROUPS, tiled=T...  14.8 us
    ppermute x3, waiting for transfers between devices, local(): lax.ppermute(piece, AXES, ring(turn))  11.7 us
    all_to_all x1, starting transfers between devices, local(): lax.all_to_all(sums, AXES, 0, 0, axis_index_groups=REDUCE_GROUPS, tiled=T...  7.33 us
    ppermute x1, waiting for transfers between devices, local(): far_texts = lax.ppermute(txt_feats, AXES, TEXTS_SWAP)  7.3 us
    unnamed x12, local copies, waits for them, and re-layouts  6.48 us
    ppermute x3, starting transfers between devices, local(): units_a = [lax.ppermute(send, AXES, first_ring(turn)) for turn in turns]  5.99 us
    ppermute x1, starting transfers between devices, local(): far_txt = lax.ppermute(txt_head, AXES, TXT_HEADS)  5.22 us
  transfers between devices with their start and end apart: 18, of which 7 were waited for; matrix products, arithmetic and copies ran while one was open for 0% of the time, Pallas kernels for 11%

profile of v8, /device:TPU:1, one launch (start us, length us, event | category | flops | bytes accessed | tf_op | source)
XLA Modules:
  0.0 100.3 jit_solution(8899325822705367374)
XLA Ops:
  0.6 0.7 collective-permute-start.3
  1.4 5.2 %collective-permute-start.4 = (bf16[576,1152]{1,0:T(8,128)(2,1)}, bf16[576,1152]{1,0:T(8,128)(2,1)S(1)}, u32[]{:S(2)}, u32[]{:S(2)}) collective-permute-start(bf16[576,1152]{1,0:T(8,128)(2,1)} %bitcast.4), channel_id=1, source_target_pairs={{2,7},{3,6},{6,3},{7,2},{10,15},{11,14},{14,11},{15,10},{18,23},{1... | collective-permute-start | bytes 3981320 | tf_op jit(solution)/shard_map/ppermute | solution.py:306
  6.6 1.6 %collective-permute-start = (bf16[128,1152]{1,0:T(8,128)(2,1)}, bf16[128,1152]{1,0:T(8,128)(2,1)S(1)}, u32[]{:S(2)}, u32[]{:S(2)}) collective-permute-start(bf16[128,1152]{1,0:T(8,128)(2,1)} %img_feats.3), channel_id=1, source_target_pairs={{2,0},{3,1},{6,4},{7,5},{10,8},{11,9},{14,12},{15,13},{18,16},{19,... | collective-permute-start | bytes 884744 | tf_op jit(solution)/shard_map/ppermute | solution.py:307
  8.2 1.3 %collective-permute-start.1 = (bf16[128,1152]{1,0:T(8,128)(2,1)}, bf16[128,1152]{1,0:T(8,128)(2,1)S(1)}, u32[]{:S(2)}, u32[]{:S(2)}) collective-permute-start(bf16[128,1152]{1,0:T(8,128)(2,1)} %txt_feats.3), channel_id=1, source_target_pairs={{0,2},{1,3},{4,6},{5,7},{8,10},{9,11},{12,14},{13,15},{16,18},{17,... | collective-permute-start | bytes 884744 | tf_op jit(solution)/shard_map/ppermute | solution.py:308
  9.5 3.7 %collective-permute-start.2 = (bf16[128,1152]{1,0:T(8,128)(2,1)}, bf16[128,1152]{1,0:T(8,128)(2,1)S(1)}, u32[]{:S(2)}, u32[]{:S(2)}) collective-permute-start(bf16[128,1152]{1,0:T(8,128)(2,1)} %txt_feats.3), channel_id=1, source_target_pairs={{2,7},{1,6},{4,3},{7,2},{10,15},{9,14},{12,11},{15,10},{18,23},{17... | collective-permute-start | bytes 884744 | tf_op jit(solution)/shard_map/ppermute | solution.py:304
  13.3 0.0 copy-start.2
  13.3 1.0 copy-done.2
  14.2 1.0 copy-done.4
  15.2 1.4 %collective-permute-start.5 = (bf16[128,1152]{1,0:T(8,128)(2,1)S(1)}, bf16[128,1152]{1,0:T(8,128)(2,1)S(1)}, u32[]{:S(2)}, u32[]{:S(2)}) collective-permute-start(bf16[128,1152]{1,0:T(8,128)(2,1)S(1)} %send.1), channel_id=1, source_target_pairs={{0,32},{3,33},{6,36},{5,37},{8,40},{11,41},{14,44},{13,45},{16,48}... | collective-permute-start | bytes 884744 | tf_op jit(solution)/shard_map/ppermute | solution.py:311
  16.6 0.0 collective-permute-done.1.other_txt
  16.6 1.5 %collective-permute-start.6 = (bf16[128,1152]{1,0:T(8,128)(2,1)S(1)}, bf16[128,1152]{1,0:T(8,128)(2,1)S(1)}, u32[]{:S(2)}, u32[]{:S(2)}) collective-permute-start(bf16[128,1152]{1,0:T(8,128)(2,1)S(1)} %send.1), channel_id=1, source_target_pairs={{0,96},{3,97},{6,100},{5,101},{8,104},{11,105},{14,108},{13,109},{... | collective-permute-start | bytes 884744 | tf_op jit(solution)/shard_map/ppermute | solution.py:311
  18.1 7.3 %collective-permute-done.2.far_texts = bf16[128,1152]{1,0:T(8,128)(2,1)S(1)} collective-permute-done((bf16[128,1152]{1,0:T(8,128)(2,1)}, bf16[128,1152]{1,0:T(8,128)(2,1)S(1)}, u32[]{:S(2)}, u32[]{:S(2)}) %collective-permute-start.2) | collective-permute-done | bytes 294944 | tf_op jit(solution)/shard_map/ppermute | solution.py:304
  25.4 3.1 %collective-permute-start.7 = (bf16[128,1152]{1,0:T(8,128)(2,1)S(1)}, bf16[128,1152]{1,0:T(8,128)(2,1)S(1)}, u32[]{:S(2)}, u32[]{:S(2)}) collective-permute-start(bf16[128,1152]{1,0:T(8,128)(2,1)S(1)} %send.1), channel_id=1, source_target_pairs={{0,64},{3,65},{6,68},{5,69},{8,72},{11,73},{14,76},{13,77},{16,80}... | collective-permute-start | bytes 884744 | tf_op jit(solution)/shard_map/ppermute | solution.py:311
  28.5 1.3 %copy-done = bf16[1152,576]{0,1:T(8,128)(2,1)S(1)} copy-done((bf16[1152,576]{0,1:T(8,128)(2,1)S(1)}, bf16[1152,576]{0,1:T(8,128)(2,1)}, u32[]{:S(2)}) %copy-start) | copy-done | bytes 1327128
  29.9 1.3 %copy-done.1 = bf16[1152,576]{0,1:T(8,128)(2,1)S(1)} copy-done((bf16[1152,576]{0,1:T(8,128)(2,1)S(1)}, bf16[1152,576]{0,1:T(8,128)(2,1)}, u32[]{:S(2)}) %copy-start.1) | copy-done | bytes 1327128
  31.2 1.0 copy-done.3
  32.1 1.0 copy-done.5
  33.1 0.5 own.1
  33.6 0.0 collective-permute-done.5.refs_1_.refs_4_
  33.6 0.1 collective-permute-start.10
  33.7 1.3 %collective-permute-start.8 = (bf16[128,1152]{1,0:T(8,128)(2,1)S(1)}, bf16[128,1152]{1,0:T(8,128)(2,1)S(1)}, u32[]{:S(2)}, u32[]{:S(2)}) collective-permute-start(bf16[128,1152]{1,0:T(8,128)(2,1)S(1)} %get-tuple-element.21.refs_0_.refs_7_), channel_id=1, source_target_pairs={{0,32},{2,10},{1,33},{3,11},{4,36},{6,14},{5,37},{7,15},{8,40},{10... | collective-permute-start | bytes 884744 | tf_op jit(solution)/shard_map/ppermute | solution.py:321
  35.1 1.5 %collective-permute-start.9 = (bf16[128,1152]{1,0:T(8,128)(2,1)S(1)}, bf16[128,1152]{1,0:T(8,128)(2,1)S(1)}, u32[]{:S(2)}, u32[]{:S(2)}) collective-permute-start(bf16[128,1152]{1,0:T(8,128)(2,1)S(1)} %get-tuple-element.21.refs_0_.refs_7_), channel_id=1, source_target_pairs={{0,96},{2,26},{1,97},{3,27},{4,100},{6,30},{5,101},{7,31},{8,104},... | collective-permute-start | bytes 884744 | tf_op jit(solution)/shard_map/ppermute | solution.py:321
  36.6 0.7 head.1.head_ref
  37.3 0.0 collective-permute-done.6.refs_2_.refs_5_
  37.4 2.1 %embed_first.1 = (bf16[512,1152]{1,0:T(8,128)(2,1)S(1)}, bf16[512,1152]{1,0:T(8,128)(2,1)S(1)}) custom-call(bf16[1152,1152]{1,0:T(8,128)(2,1)S(1)} %head.1.head_ref, bf16[128,1152]{1,0:T(8,128)(2,1)S(1)} %get-tuple-element.19.refs_0_.refs_3_, bf16[128,1152]{1,0:T(8,128)(2,1)S(1)} %collective-permute-done.5.refs_1_.refs_4_, ...), custom_call_target="tpu_custom_call" | custom-call | flops 1358954496 | bytes 6193152 | tf_op jit(solution)/shard_map/embed_first/pallas_call | solution.py:279
  39.5 0.1 collective-permute-start.11
  39.6 1.3 %collective-permute-done.10.refs_3_.refs_10_ = bf16[128,1152]{1,0:T(8,128)(2,1)S(1)} collective-permute-done((bf16[128,1152]{1,0:T(8,128)(2,1)S(1)}, bf16[128,1152]{1,0:T(8,128)(2,1)S(1)}, u32[]{:S(2)}, u32[]{:S(2)}) %collective-permute-start.10) | collective-permute-done | bytes 294944 | tf_op jit(solution)/shard_map/ppermute | solution.py:321
  40.9 2.9 %collective-permute-done.8.refs_1_.refs_8_ = bf16[128,1152]{1,0:T(8,128)(2,1)S(1)} collective-permute-done((bf16[128,1152]{1,0:T(8,128)(2,1)S(1)}, bf16[128,1152]{1,0:T(8,128)(2,1)S(1)}, u32[]{:S(2)}, u32[]{:S(2)}) %collective-permute-start.8) | collective-permute-done | bytes 294944 | tf_op jit(solution)/shard_map/ppermute | solution.py:321
  43.8 2.1 %embed_second.1 = (bf16[512,1152]{1,0:T(8,128)(2,1)S(1)}, bf16[512,1152]{1,0:T(8,128)(2,1)S(1)}) custom-call(bf16[1152,1152]{1,0:T(8,128)(2,1)S(1)} %head.1.head_ref, bf16[128,1152]{1,0:T(8,128)(2,1)S(1)} %get-tuple-element.21.refs_0_.refs_7_, bf16[128,1152]{1,0:T(8,128)(2,1)S(1)} %collective-permute-done.8.refs_1_.refs_8_, ...), custom_call_target="tpu_custom_call" | custom-call | flops 1358954496 | bytes 6193152 | tf_op jit(solution)/shard_map/embed_second/pallas_call | solution.py:279
  45.9 0.1 collective-permute-start.12
  46.0 3.3 %score_first.1 = (bf16[512,512]{1,0:T(8,128)(2,1)S(1)}, bf16[512,512]{1,0:T(8,128)(2,1)S(1)}, bf16[4,288,512]{2,1,0:T(8,128)(2,1)S(1)}, bf16[4,288,512]{2,1,0:T(8,128)(2,1)S(1)}) custom-call(bf16[512,1152]{1,0:T(8,128)(2,1)S(1)} %get-tuple-element.20.refs_0_.emb_a, bf16[512,1152]{1,0:T(8,128)(2,1)S(1)} %get-tuple-element.22.refs_1_.emb_b, ...), custom_call_target="tpu_custom_call" | custom-call | flops 1207959552 | bytes 9306112 | tf_op jit(solution)/shard_map/score_first/pallas_call | solution.py:279
  49.3 6.7 %score_second.1 = (bf16[512,1152]{1,0:T(8,128)(2,1)S(1)}, bf16[512,1152]{1,0:T(8,128)(2,1)S(1)}, bf16[288,1152]{1,0:T(8,128)(2,1)S(1)}) custom-call(bf16[512,1152]{1,0:T(8,128)(2,1)S(1)} %get-tuple-element.20.refs_0_.emb_a, bf16[512,1152]{1,0:T(8,128)(2,1)S(1)} %get-tuple-element.22.refs_1_.emb_b, ...), custom_call_target="tpu_custom_call" | custom-call | flops 4303355904 | bytes 13508608 | tf_op jit(solution)/shard_map/score_second/pallas_call | solution.py:279
  56.0 1.3 %collective-permute-start.13 = (bf16[288,1152]{1,0:T(8,128)(2,1)S(1)}, bf16[288,1152]{1,0:T(8,128)(2,1)S(1)}, u32[]{:S(2)}, u32[]{:S(2)}) collective-permute-start(bf16[288,1152]{1,0:T(8,128)(2,1)S(1)} %get-tuple-element.31), channel_id=1, source_target_pairs={{0,64},{2,18},{1,65},{3,19},{4,68},{6,22},{5,69},{7,23},{8,72},{10... | collective-permute-start | bytes 1990664 | tf_op jit(solution)/shard_map/ppermute | solution.py:369
  57.3 1.7 %terms_near.1 = (bf16[288,1152]{1,0:T(8,128)(2,1)S(1)}, bf16[288,1152]{1,0:T(8,128)(2,1)S(1)}) custom-call(bf16[4,288,512]{2,1,0:T(8,128)(2,1)S(1)} %get-tuple-element.23.flip_a.refs_0_, bf16[4,288,512]{2,1,0:T(8,128)(2,1)S(1)} %get-tuple-element.24.flip_b.refs_1_, bf16[512,1152]{1,0:T(8,128)(2,1)S(1)} %get-tuple-element.29.refs_2_, ...), custom_call_target="tpu_custom_call" | custom-call | flops 1358954496 | bytes 6045696 | tf_op jit(solution)/shard_map/terms_near/pallas_call | solution.py:279
  59.0 0.4 collective-permute-start.14
  59.4 2.4 %collective-permute-start.15 = (bf16[288,1152]{1,0:T(8,128)(2,1)S(1)}, bf16[288,1152]{1,0:T(8,128)(2,1)S(1)}, u32[]{:S(2)}, u32[]{:S(2)}) collective-permute-start(bf16[288,1152]{1,0:T(8,128)(2,1)S(1)} %get-tuple-element.33), channel_id=1, source_target_pairs={{0,96},{2,26},{1,97},{3,27},{4,100},{6,30},{5,101},{7,31},{8,104},... | collective-permute-start | bytes 1990664 | tf_op jit(solution)/shard_map/ppermute | solution.py:369
  61.7 0.9 term_own.1.left
  62.7 4.8 %collective-permute-done.13.right = bf16[288,1152]{1,0:T(8,128)(2,1)S(1)} collective-permute-done((bf16[288,1152]{1,0:T(8,128)(2,1)S(1)}, bf16[288,1152]{1,0:T(8,128)(2,1)S(1)}, u32[]{:S(2)}, u32[]{:S(2)}) %collective-permute-start.13) | collective-permute-done | bytes 663584 | tf_op jit(solution)/shard_map/ppermute | solution.py:369
  67.4 0.1 add_far.1.refs_0_
  67.6 6.9 %collective-permute-done.14.refs_1_ = bf16[288,1152]{1,0:T(8,128)(2,1)S(1)} collective-permute-done((bf16[288,1152]{1,0:T(8,128)(2,1)S(1)}, bf16[288,1152]{1,0:T(8,128)(2,1)S(1)}, u32[]{:S(2)}, u32[]{:S(2)}) %collective-permute-start.14) | collective-permute-done | bytes 663584 | tf_op jit(solution)/shard_map/ppermute | solution.py:369
  74.5 1.3 %sum_terms.1 = bf16[16,18,1152]{2,1,0:T(8,128)(2,1)} custom-call(f32[288,1152]{1,0:T(8,128)S(1)} %add_far.1.refs_0_, bf16[288,1152]{1,0:T(8,128)(2,1)S(1)} %collective-permute-done.14.refs_1_, bf16[288,1152]{1,0:T(8,128)(2,1)S(1)} %collective-permute-done.15.refs_2_), custom_call_target="tpu_custom_call" | custom-call | bytes 3317760 | tf_op jit(solution)/shard_map/sum_terms/pallas_call | solution.py:279
  75.8 7.3 %all-to-all-start = ((bf16[16,18,1152]{2,1,0:T(8,128)(2,1)}), bf16[16,18,1152]{2,1,0:T(8,128)(2,1)S(1)}, u32[]{:S(2)}, u32[]{:S(2)}) async-start(bf16[16,18,1152]{2,1,0:T(8,128)(2,1)} %sum_terms.1), calls=%async_computation | async-start | bytes 1769472 | tf_op jit(solution)/shard_map/all_to_all | solution.py:375
  83.2 14.8 %all-to-all-done = bf16[16,18,1152]{2,1,0:T(8,128)(2,1)S(1)} async-done(((bf16[16,18,1152]{2,1,0:T(8,128)(2,1)}), bf16[16,18,1152]{2,1,0:T(8,128)(2,1)S(1)}, u32[]{:S(2)}, u32[]{:S(2)}) %all-to-all-start) | async-done | bytes 663584 | tf_op jit(solution)/shard_map/all_to_all | solution.py:375
  98.0 0.1 convert_reduce_fusion
  98.1 0.1 slice_select_fusion
  98.2 0.3 collective-permute-start.16
  98.5 1.0 collective-permute-done.16
  99.5 0.7 broadcast_select_fusion
  (14 shorter events, 0.1 us)
Async XLA Ops:
  0.6 33.1 %collective-permute-start.3 = (bf16[576,1152]{1,0:T(8,128)(2,1)}, bf16[576,1152]{1,0:T(8,128)(2,1)S(1)}, u32[]{:S(2)}, u32[]{:S(2)}) collective-permute-start(bf16[576,1152]{1,0:T(8,128)(2,1)} %bitcast.2), channel_id=1, source_target_pairs={{0,1},{1,0},{4,5},{5,4},{8,9},{9,8},{12,13},{13,12},{16,17},{17,16... | collective-permute-start | bytes 3981320 | tf_op jit(solution)/shard_map/ppermute | solution.py:305
  1.4 33.7 %collective-permute-start.4 = (bf16[576,1152]{1,0:T(8,128)(2,1)}, bf16[576,1152]{1,0:T(8,128)(2,1)S(1)}, u32[]{:S(2)}, u32[]{:S(2)}) collective-permute-start(bf16[576,1152]{1,0:T(8,128)(2,1)} %bitcast.4), channel_id=1, source_target_pairs={{2,7},{3,6},{6,3},{7,2},{10,15},{11,14},{14,11},{15,10},{18,23},{1... | collective-permute-start | bytes 3981320 | tf_op jit(solution)/shard_map/ppermute | solution.py:306
  6.6 8.6 %collective-permute-start = (bf16[128,1152]{1,0:T(8,128)(2,1)}, bf16[128,1152]{1,0:T(8,128)(2,1)S(1)}, u32[]{:S(2)}, u32[]{:S(2)}) collective-permute-start(bf16[128,1152]{1,0:T(8,128)(2,1)} %img_feats.3), channel_id=1, source_target_pairs={{2,0},{3,1},{6,4},{7,5},{10,8},{11,9},{14,12},{15,13},{18,16},{19,... | collective-permute-start | bytes 884744 | tf_op jit(solution)/shard_map/ppermute | solution.py:307
  8.2 8.4 %collective-permute-start.1 = (bf16[128,1152]{1,0:T(8,128)(2,1)}, bf16[128,1152]{1,0:T(8,128)(2,1)S(1)}, u32[]{:S(2)}, u32[]{:S(2)}) collective-permute-start(bf16[128,1152]{1,0:T(8,128)(2,1)} %txt_feats.3), channel_id=1, source_target_pairs={{0,2},{1,3},{4,6},{5,7},{8,10},{9,11},{12,14},{13,15},{16,18},{17,... | collective-permute-start | bytes 884744 | tf_op jit(solution)/shard_map/ppermute | solution.py:308
  9.5 15.9 %collective-permute-start.2 = (bf16[128,1152]{1,0:T(8,128)(2,1)}, bf16[128,1152]{1,0:T(8,128)(2,1)S(1)}, u32[]{:S(2)}, u32[]{:S(2)}) collective-permute-start(bf16[128,1152]{1,0:T(8,128)(2,1)} %txt_feats.3), channel_id=1, source_target_pairs={{2,7},{1,6},{4,3},{7,2},{10,15},{9,14},{12,11},{15,10},{18,23},{17... | collective-permute-start | bytes 884744 | tf_op jit(solution)/shard_map/ppermute | solution.py:304
  13.3 1.0 copy-start.2
  14.2 1.0 copy-start.4
  15.2 18.4 %collective-permute-start.5 = (bf16[128,1152]{1,0:T(8,128)(2,1)S(1)}, bf16[128,1152]{1,0:T(8,128)(2,1)S(1)}, u32[]{:S(2)}, u32[]{:S(2)}) collective-permute-start(bf16[128,1152]{1,0:T(8,128)(2,1)S(1)} %send.1), channel_id=1, source_target_pairs={{0,32},{3,33},{6,36},{5,37},{8,40},{11,41},{14,44},{13,45},{16,48}... | collective-permute-start | bytes 884744 | tf_op jit(solution)/shard_map/ppermute | solution.py:311
  16.6 20.7 %collective-permute-start.6 = (bf16[128,1152]{1,0:T(8,128)(2,1)S(1)}, bf16[128,1152]{1,0:T(8,128)(2,1)S(1)}, u32[]{:S(2)}, u32[]{:S(2)}) collective-permute-start(bf16[128,1152]{1,0:T(8,128)(2,1)S(1)} %send.1), channel_id=1, source_target_pairs={{0,96},{3,97},{6,100},{5,101},{8,104},{11,105},{14,108},{13,109},{... | collective-permute-start | bytes 884744 | tf_op jit(solution)/shard_map/ppermute | solution.py:311
  25.4 11.9 %collective-permute-start.7 = (bf16[128,1152]{1,0:T(8,128)(2,1)S(1)}, bf16[128,1152]{1,0:T(8,128)(2,1)S(1)}, u32[]{:S(2)}, u32[]{:S(2)}) collective-permute-start(bf16[128,1152]{1,0:T(8,128)(2,1)S(1)} %send.1), channel_id=1, source_target_pairs={{0,64},{3,65},{6,68},{5,69},{8,72},{11,73},{14,76},{13,77},{16,80}... | collective-permute-start | bytes 884744 | tf_op jit(solution)/shard_map/ppermute | solution.py:311
  28.5 1.3 %copy-start = (bf16[1152,576]{0,1:T(8,128)(2,1)S(1)}, bf16[1152,576]{0,1:T(8,128)(2,1)}, u32[]{:S(2)}) copy-start(bf16[1152,576]{0,1:T(8,128)(2,1)} %param.6) | copy-start | bytes 3981316
  29.9 1.3 %copy-start.1 = (bf16[1152,576]{0,1:T(8,128)(2,1)S(1)}, bf16[1152,576]{0,1:T(8,128)(2,1)}, u32[]{:S(2)}) copy-start(bf16[1152,576]{0,1:T(8,128)(2,1)} %param.7) | copy-start | bytes 3981316
  31.2 1.0 copy-start.3
  32.1 1.0 copy-start.5
  33.6 7.3 %collective-permute-start.10 = (bf16[128,1152]{1,0:T(8,128)(2,1)S(1)}, bf16[128,1152]{1,0:T(8,128)(2,1)S(1)}, u32[]{:S(2)}, u32[]{:S(2)}) collective-permute-start(bf16[128,1152]{1,0:T(8,128)(2,1)S(1)} %get-tuple-element.21.refs_0_.refs_7_), channel_id=1, source_target_pairs={{0,64},{2,18},{1,65},{3,19},{4,68},{6,22},{5,69},{7,23},{8,72},{10... | collective-permute-start | bytes 884744 | tf_op jit(solution)/shard_map/ppermute | solution.py:321
  33.7 10.0 %collective-permute-start.8 = (bf16[128,1152]{1,0:T(8,128)(2,1)S(1)}, bf16[128,1152]{1,0:T(8,128)(2,1)S(1)}, u32[]{:S(2)}, u32[]{:S(2)}) collective-permute-start(bf16[128,1152]{1,0:T(8,128)(2,1)S(1)} %get-tuple-element.21.refs_0_.refs_7_), channel_id=1, source_target_pairs={{0,32},{2,10},{1,33},{3,11},{4,36},{6,14},{5,37},{7,15},{8,40},{10... | collective-permute-start | bytes 884744 | tf_op jit(solution)/shard_map/ppermute | solution.py:321
  35.1 8.7 %collective-permute-start.9 = (bf16[128,1152]{1,0:T(8,128)(2,1)S(1)}, bf16[128,1152]{1,0:T(8,128)(2,1)S(1)}, u32[]{:S(2)}, u32[]{:S(2)}) collective-permute-start(bf16[128,1152]{1,0:T(8,128)(2,1)S(1)} %get-tuple-element.21.refs_0_.refs_7_), channel_id=1, source_target_pairs={{0,96},{2,26},{1,97},{3,27},{4,100},{6,30},{5,101},{7,31},{8,104},... | collective-permute-start | bytes 884744 | tf_op jit(solution)/shard_map/ppermute | solution.py:321
  39.5 6.5 %collective-permute-start.11 = (bf16[512,1152]{1,0:T(8,128)(2,1)S(1)}, bf16[512,1152]{1,0:T(8,128)(2,1)S(1)}, u32[]{:S(2)}, u32[]{:S(2)}) collective-permute-start(bf16[512,1152]{1,0:T(8,128)(2,1)S(1)} %get-tuple-element.20.refs_0_.emb_a), channel_id=1, source_target_pairs={{0,2},{2,0},{1,3},{3,1},{4,6},{6,4},{5,7},{7,5},{8,10},{10,8},{9,1... | collective-permute-start | bytes 3538952 | tf_op jit(solution)/shard_map/ppermute | solution.py:299
  45.9 3.4 %collective-permute-start.12 = (bf16[512,1152]{1,0:T(8,128)(2,1)S(1)}, bf16[512,1152]{1,0:T(8,128)(2,1)S(1)}, u32[]{:S(2)}, u32[]{:S(2)}) collective-permute-start(bf16[512,1152]{1,0:T(8,128)(2,1)S(1)} %get-tuple-element.22.refs_1_.emb_b), channel_id=1, source_target_pairs={{0,2},{2,0},{1,3},{3,1},{4,6},{6,4},{5,7},{7,5},{8,10},{10,8},{9,1... | collective-permute-start | bytes 3538952 | tf_op jit(solution)/shard_map/ppermute | solution.py:299
  56.0 11.4 %collective-permute-start.13 = (bf16[288,1152]{1,0:T(8,128)(2,1)S(1)}, bf16[288,1152]{1,0:T(8,128)(2,1)S(1)}, u32[]{:S(2)}, u32[]{:S(2)}) collective-permute-start(bf16[288,1152]{1,0:T(8,128)(2,1)S(1)} %get-tuple-element.31), channel_id=1, source_target_pairs={{0,64},{2,18},{1,65},{3,19},{4,68},{6,22},{5,69},{7,23},{8,72},{10... | collective-permute-start | bytes 1990664 | tf_op jit(solution)/shard_map/ppermute | solution.py:369
  59.0 15.5 %collective-permute-start.14 = (bf16[288,1152]{1,0:T(8,128)(2,1)S(1)}, bf16[288,1152]{1,0:T(8,128)(2,1)S(1)}, u32[]{:S(2)}, u32[]{:S(2)}) collective-permute-start(bf16[288,1152]{1,0:T(8,128)(2,1)S(1)} %get-tuple-element.32), channel_id=1, source_target_pairs={{0,32},{2,10},{1,33},{3,11},{4,36},{6,14},{5,37},{7,15},{8,40},{10... | collective-permute-start | bytes 1990664 | tf_op jit(solution)/shard_map/ppermute | solution.py:369
  59.4 15.2 %collective-permute-start.15 = (bf16[288,1152]{1,0:T(8,128)(2,1)S(1)}, bf16[288,1152]{1,0:T(8,128)(2,1)S(1)}, u32[]{:S(2)}, u32[]{:S(2)}) collective-permute-start(bf16[288,1152]{1,0:T(8,128)(2,1)S(1)} %get-tuple-element.33), channel_id=1, source_target_pairs={{0,96},{2,26},{1,97},{3,27},{4,100},{6,30},{5,101},{7,31},{8,104},... | collective-permute-start | bytes 1990664 | tf_op jit(solution)/shard_map/ppermute | solution.py:369
  75.8 22.1 %all-to-all-start = ((bf16[16,18,1152]{2,1,0:T(8,128)(2,1)}), bf16[16,18,1152]{2,1,0:T(8,128)(2,1)S(1)}, u32[]{:S(2)}, u32[]{:S(2)}) async-start(bf16[16,18,1152]{2,1,0:T(8,128)(2,1)} %sum_terms.1), calls=%async_computation | async-start | bytes 1769472 | tf_op jit(solution)/shard_map/all_to_all | solution.py:375
  98.2 1.3 %collective-permute-start.16 = (f32[18,576]{1,0:T(8,128)S(1)}, f32[18,576]{1,0:T(8,128)S(1)}, u32[]{:S(2)}, u32[]{:S(2)}) collective-permute-start(f32[18,576]{1,0:T(8,128)S(1)} %slice_select_fusion), channel_id=1, source_target_pairs={{0,2},{2,0},{1,3},{3,1},{4,6},{6,4},{5,7},{7,5},{8,10},{10,8},{9,1... | collective-permute-start | bytes 124424 | tf_op jit(solution)/shard_map/ppermute | solution.py:299

commit v9 on v6

--- a/solution.py
+++ b/solution.py
@@ -46,9 +46,15 @@
 FAR_SWAP = per_core(*[lambda z, y, x: (z, y, 3 - x)] * 2)
 TEXTS_SWAP = [(device(z, y, x, block_of(x)), device(z, y, 3 - x, 1)) for z, y, x in CHIPS]
 
-REDUCE_GROUPS = [[device(z, y, x, 0) for y in range(RING) for x in range(RING)] for z in range(RING)] + [
-    [device(z, y, x, 1) for z in range(RING) for x in range(RING)] for y in range(RING)
-]
+def reduce_pairs(turn, flip):
+    return per_core(
+        lambda z, y, x: (z + turn, y, x ^ flip), lambda z, y, x: (z, y + turn, 3 - x if flip else x)
+    )
+
+
+REDUCE_GROUPS = [
+    [device(z, y, x, 0) for y in range(RING) for x in pair] for z in range(RING) for pair in ((0, 3), (1, 2))
+] + [[device(z, y, x, 1) for z in range(RING) for x in pair] for y in range(RING) for pair in ((0, 1), (2, 3))]
 
 
 def position():
@@ -70,21 +76,30 @@
     return pl.BlockSpec(memory_space=pl.ANY)
 
 
-def pick_kernel(img_feats, txt_feats, img_head, txt_head, mine, give, send, top, bottom, sems):
+def pick_kernel(img_feats, txt_feats, img_head, txt_head, mine, give, send, top, bottom, *scratch):
     _, _, high, core, tower = position()
+    head, units, into, out = scratch
     split, step = top.shape[0], 64
-
-    def copies(feats, other, head):
-        moves = [(head.at[pl.ds(i, step)], top.at[pl.ds(i, step)]) for i in range(0, split, step)]
-        moves += [
-            (head.at[pl.ds(split + i, step)], bottom.at[pl.ds(i, step)])
-            for i in range(0, bottom.shape[0], step)
-        ]
-        moves += [(other, give), (feats, mine)]
-        return [pltpu.make_async_copy(*move, sems.at[i]) for i, move in enumerate(moves)]
+    cuts = range(0, head.shape[0], step)
+    count = len(cuts) + 3
+
+    def loads(feats, other, source):
+        moves = [(source.at[pl.ds(i, step)], head.at[pl.ds(i, step)]) for i in cuts]
+        moves += [(other, units.at[0]), (feats, units.at[1])]
+        return [pltpu.make_async_copy(*move, into.at[i]) for i, move in enumerate(moves)]
 
     def choice(feats):
-        return pltpu.make_async_copy(feats, send, sems.at[sems.shape[0] - 1])
+        return pltpu.make_async_copy(feats, units.at[2], into.at[count - 1])
+
+    @pl.when(core == 0)
+    def _():
+        for copy in loads(img_feats, txt_feats, img_head):
+            copy.start()
+
+    @pl.when(core == 1)
+    def _():
+        for copy in loads(txt_feats, img_feats, txt_head):
+            copy.start()
 
     holds_block = (high == tower).astype(jnp.int32) == core
 
@@ -96,19 +111,16 @@
     def _():
         choice(img_feats).start()
 
-    @pl.when(core == 0)
-    def _():
-        for copy in copies(img_feats, txt_feats, img_head):
-            copy.start()
-
-    @pl.when(core == 1)
-    def _():
-        for copy in copies(txt_feats, img_feats, txt_head):
-            copy.start()
-
-    for copy in copies(img_feats, txt_feats, img_head):
-        copy.wait()
-    choice(img_feats).wait()
+    arrivals = [*loads(img_feats, txt_feats, img_head), choice(img_feats)]
+    targets = [top.at[pl.ds(i, step)] if i < split else bottom.at[pl.ds(i - split, step)] for i in cuts]
+    sources = [head.at[pl.ds(i, step)] for i in cuts] + [units.at[i] for i in range(3)]
+    targets += [give, mine, send]
+    stores = [pltpu.make_async_copy(sources[i], targets[i], out.at[i]) for i in range(count)]
+    for arrival, store in zip(arrivals, stores):
+        arrival.wait()
+        store.start()
+    for store in stores:
+        store.wait()
 
 
 def inverse_norm(wide):
@@ -142,16 +154,16 @@
 
 
 def flip_rows(feats, flip_ref, lane):
-    z, y, _, core, _ = position()
-    part = flip_ref.shape[1] // RING
+    z, y, high, core, _ = position()
+    part = flip_ref.shape[2] // RING
     turned = feats.T
 
     def store(own, ring_first):
-        for block in range(RING * RING):
-            first, second = divmod(block, RING)
-            place, other = (first, second) if ring_first else (second, first)
-            turn = lax.rem(place - own + RING, RING)
-            flip_ref[turn, pl.ds(other * part, part), pl.ds(lane, feats.shape[0])] = (
+        for block in range(2 * RING * RING):
+            first, second, side = block // 8, block // 2 % 4, block % 2
+            ring, other = (first, second) if ring_first else (second, first)
+            turn = lax.rem(ring - own + RING, RING)
+            flip_ref[turn, lax.rem(side + high, 2), pl.ds(other * part, part), pl.ds(lane, feats.shape[0])] = (
                 turned[block * part : (block + 1) * part, :]
             )
 
@@ -197,7 +209,7 @@
     flip_kernel(*units, flip_b)
 
 
-def score_second_kernel(emb_a, emb_b, far_a, far_b, raw_a, raw_b, coef_a, coef_b, flip_a, flip_b, grad_a, grad_b, piece, turned):
+def score_second_kernel(emb_a, emb_b, far_a, far_b, raw_a, raw_b, coef_a, coef_b, flip_a, flip_b, grad_a, grad_b, straight, crossed, turned):
     core = position()[3]
     turned[...] = far_b[...].T
     rows = emb_a.shape[0] // 2
@@ -216,45 +228,65 @@
             unit = wide * inverse
             inner = jnp.sum(unit * direction, axis=1, keepdims=True)
             grad[here, :] = ((direction - unit * inner) * inverse).astype(BF16)
-    terms_kernel((2,), flip_a, flip_b, grad_a, grad_b, piece)
+    terms_kernel((2,), flip_a, flip_b, grad_a, grad_b, straight, crossed)
 
 
 def terms_kernel(turns, flip_a, flip_b, grad_a, grad_b, *pieces):
-    for turn, piece in zip(turns, pieces):
-        piece[...] = (
-            jnp.dot(flip_a[turn], grad_a[...], preferred_element_type=F32)
-            + jnp.dot(flip_b[turn], grad_b[...], preferred_element_type=F32)
-        ).astype(piece.dtype)
-
-
-def add_kernel(left, right, out_ref):
-    out_ref[...] = left[...].astype(F32) + right[...].astype(F32)
+    core = position()[3]
+    for k, turn in enumerate(turns):
+        half, rows = flip_a.shape[2], grad_a.shape[0]
+        width = grad_a.shape[1] // 2
+        term = jnp.dot(
+            flip_a[turn].reshape(2 * half, rows), grad_a[...], preferred_element_type=F32
+        ) + jnp.dot(flip_b[turn].reshape(2 * half, rows), grad_b[...], preferred_element_type=F32)
+        term = term.astype(BF16)
+        straight, crossed = pieces[2 * k], pieces[2 * k + 1]
+        straight[:, :width] = term[:half, :width]
+        crossed[:, width:] = term[half:, :width]
+
+        @pl.when(core == 0)
+        def _():
+            straight[:, width:] = term[half:, width:]
+            crossed[:, :width] = term[:half, width:]
+
+        @pl.when(core == 1)
+        def _():
+            straight[:, width:] = term[:half, width:]
+            crossed[:, :width] = term[half:, width:]
+
+
+def add_kernel(*refs):
+    total = refs[0][...].astype(F32)
+    for ref in refs[1:-1]:
+        total += ref[...].astype(F32)
+    refs[-1][...] = total
 
 
 def sum_kernel(*refs):
-    tower = position()[4]
+    _, _, high, core, tower = position()
     out_ref = refs[-1]
     total = refs[0][...].astype(F32)
     for ref in refs[1:-1]:
         total += ref[...].astype(F32)
     total = total.astype(out_ref.dtype)
+    twist = jnp.where(core == 0, high, tower)
     part, width = out_ref.shape[1], out_ref.shape[2] // 2
-    for j in range(2 * RING):
-        for half in range(2):
-            slot = 2 * j + lax.rem(half + tower, 2)
-            columns = slice(half * width, (half + 1) * width)
+    for j in range(RING):
+        for side in range(2):
+            slot = 2 * j + lax.rem(side + twist, 2)
+            columns = slice(side * width, (side + 1) * width)
             out_ref[slot, :, :width] = total[2 * j * part : (2 * j + 1) * part, columns]
             out_ref[slot, :, width:] = total[(2 * j + 1) * part : (2 * j + 2) * part, columns]
 
 
-def kernel_call(body, name, shapes, operands, scratch=(), flops=0, exps=0, anywhere=(), limit=40):
+def kernel_call(body, name, shapes, operands, scratch=(), flops=0, exps=0, anywhere=(), anywhere_out=False, limit=40):
     shapes = [jax.ShapeDtypeStruct(*shape) for shape in shapes]
     touched = sum(a.size * a.dtype.itemsize for a in (*shapes, *operands))
     return pl.pallas_call(
         body,
         out_shape=shapes,
         in_specs=[anywhere_spec() if i in anywhere else vmem() for i in range(len(operands))],
-        out_specs=[vmem()] * len(shapes),
+        out_specs=[anywhere_spec() if anywhere_out else vmem()] * len(shapes),
         scratch_shapes=list(scratch),
         compiler_params=pltpu.CompilerParams(vmem_limit_bytes=limit * MIB),
         cost_estimate=pl.CostEstimate(flops=flops, bytes_accessed=touched, transcendentals=exps),
@@ -272,18 +304,24 @@
     def swap(value):
         return lax.ppermute(value, AXES, CORES_SWAP)
 
+    far_texts = lax.ppermute(txt_feats, AXES, TEXTS_SWAP)
     mine, give, send, top, bottom = kernel_call(
         pick_kernel,
         "pick",
         [((rows, depth), BF16)] * 3 + [((5 * depth // 18, depth), BF16), ((2 * depth // 9, depth), BF16)],
         (img_feats, txt_feats, img_proj.T, txt_proj.T),
-        scratch=(pltpu.SemaphoreType.DMA((width // 64 + 3,)),),
+        scratch=(
+            pltpu.VMEM((width, depth), BF16),
+            pltpu.VMEM((3, rows, depth), BF16),
+            pltpu.SemaphoreType.DMA((width // 64 + 3,)),
+            pltpu.SemaphoreType.DMA((width // 64 + 3,)),
+        ),
+        anywhere_out=True,
         anywhere=range(4),
         limit=56,
     )
     far_top = lax.ppermute(top, AXES, NEAR_SWAP)
     far_bottom = lax.ppermute(bottom, AXES, FAR_SWAP)
-    far_texts = lax.ppermute(send, AXES, TEXTS_SWAP)
     turns = (1, 3, 2)
     units_a = [lax.ppermute(send, AXES, first_ring(turn)) for turn in turns]
     other = swap(give)
@@ -296,7 +334,7 @@
 
     rows_of = ((pair, full), BF16)
     work = 2 * pair * depth * full
-    flips = ((RING, part, pair), BF16)
+    flips = ((RING, 2, part // 2, pair), BF16)
     (flip_a,) = kernel_call(flip_kernel, "flip_first", [flips], units_a)
     (head,) = kernel_call(
         head_kernel, "head", [((depth, full), BF16)], (top, bottom, far_top, far_bottom, flip_a), anywhere=(4,)
@@ -320,11 +358,11 @@
         flops=4 * pair * pair * full,
         exps=2 * pair * pair,
     )
-    term = ((part, full), BF16)
-    grad_a, grad_b, piece = kernel_call(
+    term = ((part // 2, full), BF16)
+    grad_a, grad_b, *far = kernel_call(
         score_second_kernel,
         "score_second",
-        [rows_of, rows_of, term],
+        [rows_of, rows_of, term, term],
         (emb_a, emb_b, far_a, far_b, raw_a, raw_b, coef_a, coef_b, flip_a, flip_b),
         scratch=[turned],
         flops=12 * pair * pair * full + work // 2,
@@ -335,17 +373,25 @@
         return kernel_call(
             lambda *refs: terms_kernel(turns, *refs),
             name,
-            [term] * len(turns),
+            [term] * (2 * len(turns)),
             (flip_a, flip_b, grad_a, grad_b),
             flops=len(turns) * work // 2,
         )
 
-    pieces = [piece, *terms("terms_near", 1, 3)]
-    sent = [lax.ppermute(piece, AXES, ring(turn)) for piece, turn in zip(pieces, (2, 1, 3))]
-    (kept,) = terms("term_own", 0)
-    (early,) = kernel_call(add_kernel, "add_far", [((part, full), F32)], (kept, sent[0]))
+    def send_pieces(pieces, *turns):
+        return [
+            lax.ppermute(pieces[2 * k + flip], AXES, reduce_pairs(turn, flip))
+            for k, turn in enumerate(turns)
+            for flip in (1, 0)
+        ]
+
+    far = send_pieces(far, 2)
+    near = send_pieces(terms("terms_near", 1, 3), 1, 3)
+    kept, crossed = terms("term_own", 0)
+    crossed = lax.ppermute(crossed, AXES, reduce_pairs(0, 1))
+    (early,) = kernel_call(add_kernel, "add_far", [((part // 2, full), F32)], (kept, *far))
     (sums,) = kernel_call(
-        sum_kernel, "sum_terms", [((RING * RING, part // RING // 4, full), BF16)], (early, *sent[1:])
+        sum_kernel, "sum_terms", [((2 * RING, part // RING // 4, full), BF16)], (early, *near, crossed)
     )
     swapped = lax.all_to_all(sums, AXES, 0, 0, axis_index_groups=REDUCE_GROUPS, tiled=True)
     total = jnp.sum(swapped.astype(F32), axis=0)

time: 90.8 us -> 88.6 us (0.976)
  waiting for transfers between devices: 31 us -> 23.5 us
  starting transfers between devices: 34.7 us -> 39.6 us
    ppermute x4 -> x8, starting transfers between devices: 10.2 us -> 17.1 us  [the longest x6 9.96 us: send_pieces(): lax.ppermute(pieces[2 * k + flip], AXES, reduce_pairs(turn, flip))]
    all_to_all x1, waiting for transfers between devices: 13.8 us -> 7.39 us  [local(): lax.all_to_all(sums, AXES, 0, 0, axis_index_groups=REDUCE_GROUPS, tiled=T...]
    ppermute x3, waiting for transfers between devices: 0.01 us -> 1.89 us  [local(): units_a = [lax.ppermute(send, AXES, first_ring(turn)) for turn in turns]]
    ppermute x1, starting transfers between devices: 2.72 us -> 0.86 us  [local(): far_bottom = lax.ppermute(bottom, AXES, FAR_SWAP)]
    ppermute x4 -> x8, waiting for transfers between devices: 10.4 us -> 8.68 us  [the longest x6 8.67 us: send_pieces(): lax.ppermute(pieces[2 * k + flip], AXES, reduce_pairs(turn, flip))]
    ppermute x1, waiting for transfers between devices: 5.71 us -> 4.42 us  [local(): far_bottom = lax.ppermute(bottom, AXES, FAR_SWAP)]
    all_to_all x1, starting transfers between devices: 5.76 us -> 4.8 us  [local(): lax.all_to_all(sums, AXES, 0, 0, axis_index_groups=REDUCE_GROUPS, tiled=T...]
  transfers between devices with their start and end apart: 17 -> 21, of which waited for: 7 -> 9; matrix products, arithmetic and copies ran while one was open for 1% -> 1% of each run, Pallas kernels for 12% -> 17%
where the time goes in v9:
time: 88.6 us; the launch traced here: 88.3 us
  starting transfers between devices  39.6 us (45%)
  waiting for transfers between devices  23.5 us (27%)
  Pallas kernels  22.5 us (25%)
  other arithmetic  1.91 us (2%)
    pallas_call x11, Pallas kernels, kernel_call(): pl.pallas_call(body, out_shape=shapes, in_specs=[anywhere_spec() if i in...  22.5 us
    ppermute x6, starting transfers between devices, send_pieces(): lax.ppermute(pieces[2 * k + flip], AXES, reduce_pairs(turn, flip))  9.96 us
    ppermute x6, waiting for transfers between devices, send_pieces(): lax.ppermute(pieces[2 * k + flip], AXES, reduce_pairs(turn, flip))  8.67 us
    all_to_all x1, waiting for transfers between devices, local(): lax.all_to_all(sums, AXES, 0, 0, axis_index_groups=REDUCE_GROUPS, tiled=T...  7.39 us
    ppermute x4, starting transfers between devices, swap(): return lax.ppermute(value, AXES, CORES_SWAP)  6.81 us
    ppermute x3, starting transfers between devices, local(): lax.ppermute(second, AXES, ring(turn))  5.31 us
    ppermute x1, starting transfers between devices, local(): far_texts = lax.ppermute(txt_feats, AXES, TEXTS_SWAP)  5.22 us
    all_to_all x1, starting transfers between devices, local(): lax.all_to_all(sums, AXES, 0, 0, axis_index_groups=REDUCE_GROUPS, tiled=T...  4.8 us
  transfers between devices with their start and end apart: 21, of which 9 were waited for; matrix products, arithmetic and copies ran while one was open for 1% of the time, Pallas kernels for 17%

profile of v9, /device:TPU:1, one launch (start us, length us, event | category | flops | bytes accessed | tf_op | source)
XLA Modules:
  0.0 88.3 jit_solution(9156997743311513608)
XLA Ops:
  0.6 5.2 %collective-permute-start.6 = (bf16[128,1152]{1,0:T(8,128)(2,1)}, bf16[128,1152]{1,0:T(8,128)(2,1)S(1)}, u32[]{:S(2)}, u32[]{:S(2)}) collective-permute-start(bf16[128,1152]{1,0:T(8,128)(2,1)} %txt_feats.1), channel_id=1, source_target_pairs={{2,7},{1,6},{4,3},{7,2},{10,15},{9,14},{12,11},{15,10},{18,23},{17... | collective-permute-start | bytes 884744 | tf_op jit(solution)/shard_map/ppermute | solution.py:307
  5.9 2.6 %pick.1 = (bf16[128,1152]{1,0:T(8,128)(2,1)}, bf16[128,1152]{1,0:T(8,128)(2,1)}, bf16[128,1152]{1,0:T(8,128)(2,1)}, bf16[320,1152]{1,0:T(8,128)(2,1)}, bf16[256,1152]{1,0:T(8,128)(2,1)}) custom-call(bf16[128,1152]{1,0:T(8,128)(2,1)} %img_feats.1, bf16[128,1152]{1,0:T(8,128)(2,1)} %txt_feats.1, bf16[576,1152]{1,0:T(8,128)(2,1)} %bitcast.2, ...), custom_call_target="tpu_custom_call" | custom-call | bytes 5455872 | tf_op jit(solution)/shard_map/pick/pallas_call | solution.py:285
  8.5 0.1 collective-permute-start
  8.6 0.3 collective-permute-start.4
  8.9 2.9 %collective-permute-start.3 = (bf16[128,1152]{1,0:T(8,128)(2,1)}, bf16[128,1152]{1,0:T(8,128)(2,1)S(1)}, u32[]{:S(2)}, u32[]{:S(2)}) collective-permute-start(bf16[128,1152]{1,0:T(8,128)(2,1)} %get-tuple-element.26), channel_id=1, source_target_pairs={{0,64},{3,65},{6,68},{5,69},{8,72},{11,73},{14,76},{13,77},{16,80}... | collective-permute-start | bytes 884744 | tf_op jit(solution)/shard_map/ppermute | solution.py:326
  11.8 0.8 collective-permute-start.2
  12.6 0.7 collective-permute-start.1
  13.3 0.9 collective-permute-start.5
  14.2 1.0 %select_select_fusion = (bf16[128,1152]{1,0:T(8,128)(2,1)S(1)}, bf16[128,1152]{1,0:T(8,128)(2,1)S(1)}) fusion(bf16[128,1152]{1,0:T(8,128)(2,1)S(1)} %collective-permute-done.6, bf16[128,1152]{1,0:T(8,128)(2,1)} %get-tuple-element.24, bf16[128,1152]{1,0:T(8,128)(2,1)S(1)} %collective-permute-done, pred[]{:T(512)S(6)} %eq.19, pred[]{:T(512)S(6)} %eq.18, pred[]{:T(512)S(6)} %eq.17), kind=kLoop, calls=%fused_computation.1 | loop fusion | flops 442368 | bytes 1474563 | tf_op jit(solution)/shard_map/jit(_where)/select_n | solution.py:331
  15.2 1.3 %collective-permute-done.3.refs_3_ = bf16[128,1152]{1,0:T(8,128)(2,1)S(1)} collective-permute-done((bf16[128,1152]{1,0:T(8,128)(2,1)}, bf16[128,1152]{1,0:T(8,128)(2,1)S(1)}, u32[]{:S(2)}, u32[]{:S(2)}) %collective-permute-start.3) | collective-permute-done | bytes 294944 | tf_op jit(solution)/shard_map/ppermute | solution.py:326
  16.5 3.0 %collective-permute-start.9 = (bf16[128,1152]{1,0:T(8,128)(2,1)S(1)}, bf16[128,1152]{1,0:T(8,128)(2,1)S(1)}, u32[]{:S(2)}, u32[]{:S(2)}) collective-permute-start(bf16[128,1152]{1,0:T(8,128)(2,1)S(1)} %get-tuple-element.46.refs_0_.refs_3_), channel_id=1, source_target_pairs={{0,64},{2,18},{1,65},{3,19},{4,68},{6,22},{5,69},{7,23},{8,72},{10... | collective-permute-start | bytes 884744 | tf_op jit(solution)/shard_map/ppermute | solution.py:333
  19.5 0.6 collective-permute-done.2.refs_2_
  20.1 2.3 %collective-permute-start.8 = (bf16[128,1152]{1,0:T(8,128)(2,1)S(1)}, bf16[128,1152]{1,0:T(8,128)(2,1)S(1)}, u32[]{:S(2)}, u32[]{:S(2)}) collective-permute-start(bf16[128,1152]{1,0:T(8,128)(2,1)S(1)} %get-tuple-element.46.refs_0_.refs_3_), channel_id=1, source_target_pairs={{0,96},{2,26},{1,97},{3,27},{4,100},{6,30},{5,101},{7,31},{8,104},... | collective-permute-start | bytes 884744 | tf_op jit(solution)/shard_map/ppermute | solution.py:333
  22.4 0.8 flip_first.1._.flip_a.refs_0_
  23.3 4.4 %collective-permute-done.5.far_bottom = bf16[256,1152]{1,0:T(8,128)(2,1)S(1)} collective-permute-done((bf16[256,1152]{1,0:T(8,128)(2,1)}, bf16[256,1152]{1,0:T(8,128)(2,1)S(1)}, u32[]{:S(2)}, u32[]{:S(2)}) %collective-permute-start.5) | collective-permute-done | bytes 589856 | tf_op jit(solution)/shard_map/ppermute | solution.py:324
  27.7 0.0 collective-permute-done.4.far_top
  27.7 0.7 head.1.head_ref
  28.4 2.1 %embed_first.1 = (bf16[512,1152]{1,0:T(8,128)(2,1)S(1)}, bf16[512,1152]{1,0:T(8,128)(2,1)S(1)}) custom-call(bf16[1152,1152]{1,0:T(8,128)(2,1)S(1)} %head.1.head_ref, bf16[128,1152]{1,0:T(8,128)(2,1)S(1)} %get-tuple-element.47.refs_0_, bf16[128,1152]{1,0:T(8,128)(2,1)S(1)} %collective-permute-done.1.refs_1_, ...), custom_call_target="tpu_custom_call" | custom-call | flops 1358954496 | bytes 6193152 | tf_op jit(solution)/shard_map/embed_first/pallas_call | solution.py:285
  30.6 2.9 %collective-permute-start.10 = (bf16[512,1152]{1,0:T(8,128)(2,1)S(1)}, bf16[512,1152]{1,0:T(8,128)(2,1)S(1)}, u32[]{:S(2)}, u32[]{:S(2)}) collective-permute-start(bf16[512,1152]{1,0:T(8,128)(2,1)S(1)} %get-tuple-element.29.refs_0_.emb_a), channel_id=1, source_target_pairs={{0,2},{2,0},{1,3},{3,1},{4,6},{6,4},{5,7},{7,5},{8,10},{10,8},{9,1... | collective-permute-start | bytes 3538952 | tf_op jit(solution)/shard_map/ppermute | solution.py:305
  33.4 0.0 collective-permute-done.7.refs_1_.refs_4_
  33.5 2.1 %embed_second.1 = (bf16[512,1152]{1,0:T(8,128)(2,1)S(1)}, bf16[512,1152]{1,0:T(8,128)(2,1)S(1)}) custom-call(bf16[1152,1152]{1,0:T(8,128)(2,1)S(1)} %head.1.head_ref, bf16[128,1152]{1,0:T(8,128)(2,1)S(1)} %get-tuple-element.46.refs_0_.refs_3_, bf16[128,1152]{1,0:T(8,128)(2,1)S(1)} %collective-permute-done.7.refs_1_.refs_4_, ...), custom_call_target="tpu_custom_call" | custom-call | flops 1358954496 | bytes 6193152 | tf_op jit(solution)/shard_map/embed_second/pallas_call | solution.py:285
  35.6 0.1 collective-permute-start.11
  35.7 0.2 collective-permute-done.10.refs_2_.far_a
  35.9 2.6 %score_first.1 = (bf16[512,512]{1,0:T(8,128)(2,1)S(1)}, bf16[512,512]{1,0:T(8,128)(2,1)S(1)}, bf16[4,2,144,512]{3,2,1,0:T(8,128)(2,1)S(1)}) custom-call(bf16[512,1152]{1,0:T(8,128)(2,1)S(1)} %get-tuple-element.29.refs_0_.emb_a, bf16[512,1152]{1,0:T(8,128)(2,1)S(1)} %get-tuple-element.30.refs_1_.emb_b, ...), custom_call_target="tpu_custom_call" | custom-call | flops 1207959552 | bytes 6946816 | tf_op jit(solution)/shard_map/score_first/pallas_call | solution.py:285
  38.6 0.0 collective-permute-done.11.far_b
  38.6 6.8 %score_second.1 = (bf16[512,1152]{1,0:T(8,128)(2,1)S(1)}, bf16[512,1152]{1,0:T(8,128)(2,1)S(1)}, bf16[144,1152]{1,0:T(8,128)(2,1)S(1)}, bf16[144,1152]{1,0:T(8,128)(2,1)S(1)}) custom-call(bf16[512,1152]{1,0:T(8,128)(2,1)S(1)} %get-tuple-element.29.refs_0_.emb_a, bf16[512,1152]{1,0:T(8,128)(2,1)S(1)} %get-tuple-element.30.refs_1_.emb_b, ...), custom_call_target="tpu_custom_call" | custom-call | flops 4303355904 | bytes 13508608 | tf_op jit(solution)/shard_map/score_second/pallas_call | solution.py:285
  45.4 3.2 %collective-permute-start.12 = (bf16[144,1152]{1,0:T(8,128)(2,1)S(1)}, bf16[144,1152]{1,0:T(8,128)(2,1)S(1)}, u32[]{:S(2)}, u32[]{:S(2)}) collective-permute-start(bf16[144,1152]{1,0:T(8,128)(2,1)S(1)} %get-tuple-element.39), channel_id=1, source_target_pairs={{0,65},{2,23},{1,64},{3,22},{4,69},{6,19},{5,68},{7,18},{8,73},{10... | collective-permute-start | bytes 995336 | tf_op jit(solution)/shard_map/ppermute | solution.py:383
  48.6 0.4 collective-permute-start.13
  49.0 1.1 %term_own.1 = (bf16[144,1152]{1,0:T(8,128)(2,1)S(1)}, bf16[144,1152]{1,0:T(8,128)(2,1)S(1)}) custom-call(bf16[4,2,144,512]{3,2,1,0:T(8,128)(2,1)S(1)} %flip_first.1._.flip_a.refs_0_, bf16[4,2,144,512]{3,2,1,0:T(8,128)(2,1)S(1)} %get-tuple-element.31.flip_b.refs_1_, bf16[512,1152]{1,0:T(8,128)(2,1)S(1)} %get-tuple-element.36.refs_2_, ...), custom_call_target="tpu_custom_call" | custom-call | flops 679477248 | bytes 5382144 | tf_op jit(solution)/shard_map/term_own/pallas_call | solution.py:285
  50.1 1.9 %collective-permute-start.18 = (bf16[144,1152]{1,0:T(8,128)(2,1)S(1)}, bf16[144,1152]{1,0:T(8,128)(2,1)S(1)}, u32[]{:S(2)}, u32[]{:S(2)}) collective-permute-start(bf16[144,1152]{1,0:T(8,128)(2,1)S(1)} %get-tuple-element.45), channel_id=1, source_target_pairs={{0,1},{2,7},{1,0},{3,6},{4,5},{6,3},{5,4},{7,2},{8,9},{10,15},{9,8... | collective-permute-start | bytes 995336 | tf_op jit(solution)/shard_map/ppermute | solution.py:391
  51.9 2.4 %terms_near.1 = (bf16[144,1152]{1,0:T(8,128)(2,1)S(1)}, bf16[144,1152]{1,0:T(8,128)(2,1)S(1)}, bf16[144,1152]{1,0:T(8,128)(2,1)S(1)}, bf16[144,1152]{1,0:T(8,128)(2,1)S(1)}) custom-call(bf16[4,2,144,512]{3,2,1,0:T(8,128)(2,1)S(1)} %flip_first.1._.flip_a.refs_0_, bf16[4,2,144,512]{3,2,1,0:T(8,128)(2,1)S(1)} %get-tuple-element.31.flip_b.refs_1_, ...), custom_call_target="tpu_custom_call" | custom-call | flops 1358954496 | bytes 6045696 | tf_op jit(solution)/shard_map/terms_near/pallas_call | solution.py:285
  54.4 1.9 %collective-permute-start.14 = (bf16[144,1152]{1,0:T(8,128)(2,1)S(1)}, bf16[144,1152]{1,0:T(8,128)(2,1)S(1)}, u32[]{:S(2)}, u32[]{:S(2)}) collective-permute-start(bf16[144,1152]{1,0:T(8,128)(2,1)S(1)} %get-tuple-element.41), channel_id=1, source_target_pairs={{0,33},{2,15},{1,32},{3,14},{4,37},{6,11},{5,36},{7,10},{8,41},{10... | collective-permute-start | bytes 995336 | tf_op jit(solution)/shard_map/ppermute | solution.py:383
  56.2 1.0 %collective-permute-start.15 = (bf16[144,1152]{1,0:T(8,128)(2,1)S(1)}, bf16[144,1152]{1,0:T(8,128)(2,1)S(1)}, u32[]{:S(2)}, u32[]{:S(2)}) collective-permute-start(bf16[144,1152]{1,0:T(8,128)(2,1)S(1)} %get-tuple-element.42), channel_id=1, source_target_pairs={{0,32},{2,10},{1,33},{3,11},{4,36},{6,14},{5,37},{7,15},{8,40},{10... | collective-permute-start | bytes 995336 | tf_op jit(solution)/shard_map/ppermute | solution.py:383
  57.2 2.4 %collective-permute-start.16 = (bf16[144,1152]{1,0:T(8,128)(2,1)S(1)}, bf16[144,1152]{1,0:T(8,128)(2,1)S(1)}, u32[]{:S(2)}, u32[]{:S(2)}) collective-permute-start(bf16[144,1152]{1,0:T(8,128)(2,1)S(1)} %get-tuple-element.43), channel_id=1, source_target_pairs={{0,97},{2,31},{1,96},{3,30},{4,101},{6,27},{5,100},{7,26},{8,105},... | collective-permute-start | bytes 995336 | tf_op jit(solution)/shard_map/ppermute | solution.py:383
  59.7 0.0 collective-permute-done.13.refs_2_
  59.7 1.0 %collective-permute-start.17 = (bf16[144,1152]{1,0:T(8,128)(2,1)S(1)}, bf16[144,1152]{1,0:T(8,128)(2,1)S(1)}, u32[]{:S(2)}, u32[]{:S(2)}) collective-permute-start(bf16[144,1152]{1,0:T(8,128)(2,1)S(1)} %get-tuple-element.44), channel_id=1, source_target_pairs={{0,96},{2,26},{1,97},{3,27},{4,100},{6,30},{5,101},{7,31},{8,104},... | collective-permute-start | bytes 995336 | tf_op jit(solution)/shard_map/ppermute | solution.py:383
  60.7 0.1 add_far.1.refs_0_
  60.8 3.0 %collective-permute-done.14.refs_1_ = bf16[144,1152]{1,0:T(8,128)(2,1)S(1)} collective-permute-done((bf16[144,1152]{1,0:T(8,128)(2,1)S(1)}, bf16[144,1152]{1,0:T(8,128)(2,1)S(1)}, u32[]{:S(2)}, u32[]{:S(2)}) %collective-permute-start.14) | collective-permute-done | bytes 331808 | tf_op jit(solution)/shard_map/ppermute | solution.py:383
  63.8 3.4 %collective-permute-done.15.refs_2_ = bf16[144,1152]{1,0:T(8,128)(2,1)S(1)} collective-permute-done((bf16[144,1152]{1,0:T(8,128)(2,1)S(1)}, bf16[144,1152]{1,0:T(8,128)(2,1)S(1)}, u32[]{:S(2)}, u32[]{:S(2)}) %collective-permute-start.15) | collective-permute-done | bytes 331808 | tf_op jit(solution)/shard_map/ppermute | solution.py:383
  67.3 2.2 %collective-permute-done.17.refs_4_ = bf16[144,1152]{1,0:T(8,128)(2,1)S(1)} collective-permute-done((bf16[144,1152]{1,0:T(8,128)(2,1)S(1)}, bf16[144,1152]{1,0:T(8,128)(2,1)S(1)}, u32[]{:S(2)}, u32[]{:S(2)}) %collective-permute-start.17) | collective-permute-done | bytes 331808 | tf_op jit(solution)/shard_map/ppermute | solution.py:383
  69.5 1.1 %sum_terms.1 = bf16[8,18,1152]{2,1,0:T(8,128)(2,1)} custom-call(f32[144,1152]{1,0:T(8,128)S(1)} %add_far.1.refs_0_, bf16[144,1152]{1,0:T(8,128)(2,1)S(1)} %collective-permute-done.14.refs_1_, bf16[144,1152]{1,0:T(8,128)(2,1)S(1)} %collective-permute-done.15.refs_2_, bf16[144,1152]{1,0:T(8,128)(2,1)S(1)} %collective-permute-done.16.refs_3_, ...), custom_call_target="tpu_custom_call" | custom-call | bytes 2654208 | tf_op jit(solution)/shard_map/sum_terms/pallas_call | solution.py:285
  70.6 4.8 %all-to-all-start = ((bf16[8,18,1152]{2,1,0:T(8,128)(2,1)}), bf16[8,18,1152]{2,1,0:T(8,128)(2,1)S(1)}, u32[]{:S(2)}, u32[]{:S(2)}) async-start(bf16[8,18,1152]{2,1,0:T(8,128)(2,1)} %sum_terms.1), calls=%async_computation | async-start | bytes 884736 | tf_op jit(solution)/shard_map/all_to_all | solution.py:396
  75.4 7.4 %all-to-all-done = bf16[8,18,1152]{2,1,0:T(8,128)(2,1)S(1)} async-done(((bf16[8,18,1152]{2,1,0:T(8,128)(2,1)}), bf16[8,18,1152]{2,1,0:T(8,128)(2,1)S(1)}, u32[]{:S(2)}, u32[]{:S(2)}) %all-to-all-start) | async-done | bytes 331808 | tf_op jit(solution)/shard_map/all_to_all | solution.py:396
  82.8 0.1 convert_reduce_fusion
  82.9 0.1 slice_select_fusion
  82.9 3.7 %collective-permute-start.19 = (f32[18,576]{1,0:T(8,128)S(1)}, f32[18,576]{1,0:T(8,128)S(1)}, u32[]{:S(2)}, u32[]{:S(2)}) collective-permute-start(f32[18,576]{1,0:T(8,128)S(1)} %slice_select_fusion), channel_id=1, source_target_pairs={{0,2},{2,0},{1,3},{3,1},{4,6},{6,4},{5,7},{7,5},{8,10},{10,8},{9,1... | collective-permute-start | bytes 124424 | tf_op jit(solution)/shard_map/ppermute | solution.py:305
  86.7 0.9 %collective-permute-done.19 = f32[18,576]{1,0:T(8,128)S(1)} collective-permute-done((f32[18,576]{1,0:T(8,128)S(1)}, f32[18,576]{1,0:T(8,128)S(1)}, u32[]{:S(2)}, u32[]{:S(2)}) %collective-permute-start.19) | collective-permute-done | bytes 41504 | tf_op jit(solution)/shard_map/ppermute | solution.py:305
  87.6 0.7 broadcast_select_fusion.1
  (13 shorter events, 0.0 us)
Async XLA Ops:
  0.6 12.0 %collective-permute-start.6 = (bf16[128,1152]{1,0:T(8,128)(2,1)}, bf16[128,1152]{1,0:T(8,128)(2,1)S(1)}, u32[]{:S(2)}, u32[]{:S(2)}) collective-permute-start(bf16[128,1152]{1,0:T(8,128)(2,1)} %txt_feats.1), channel_id=1, source_target_pairs={{2,7},{1,6},{4,3},{7,2},{10,15},{9,14},{12,11},{15,10},{18,23},{17... | collective-permute-start | bytes 884744 | tf_op jit(solution)/shard_map/ppermute | solution.py:307
  8.5 4.8 %collective-permute-start = (bf16[128,1152]{1,0:T(8,128)(2,1)}, bf16[128,1152]{1,0:T(8,128)(2,1)S(1)}, u32[]{:S(2)}, u32[]{:S(2)}) collective-permute-start(bf16[128,1152]{1,0:T(8,128)(2,1)} %get-tuple-element.25), channel_id=1, source_target_pairs={{0,2},{2,0},{1,3},{3,1},{4,6},{6,4},{5,7},{7,5},{8,10},{10,8},{9,1... | collective-permute-start | bytes 884744 | tf_op jit(solution)/shard_map/ppermute | solution.py:305
  8.6 19.1 %collective-permute-start.4 = (bf16[320,1152]{1,0:T(8,128)(2,1)}, bf16[320,1152]{1,0:T(8,128)(2,1)S(1)}, u32[]{:S(2)}, u32[]{:S(2)}) collective-permute-start(bf16[320,1152]{1,0:T(8,128)(2,1)} %get-tuple-element.27.top), channel_id=1, source_target_pairs={{0,1},{2,3},{1,0},{3,2},{4,5},{6,7},{5,4},{7,6},{8,9},{10,11},{9,8... | collective-permute-start | bytes 2211848 | tf_op jit(solution)/shard_map/ppermute | solution.py:323
  8.9 7.6 %collective-permute-start.3 = (bf16[128,1152]{1,0:T(8,128)(2,1)}, bf16[128,1152]{1,0:T(8,128)(2,1)S(1)}, u32[]{:S(2)}, u32[]{:S(2)}) collective-permute-start(bf16[128,1152]{1,0:T(8,128)(2,1)} %get-tuple-element.26), channel_id=1, source_target_pairs={{0,64},{3,65},{6,68},{5,69},{8,72},{11,73},{14,76},{13,77},{16,80}... | collective-permute-start | bytes 884744 | tf_op jit(solution)/shard_map/ppermute | solution.py:326
  11.8 8.2 %collective-permute-start.2 = (bf16[128,1152]{1,0:T(8,128)(2,1)}, bf16[128,1152]{1,0:T(8,128)(2,1)S(1)}, u32[]{:S(2)}, u32[]{:S(2)}) collective-permute-start(bf16[128,1152]{1,0:T(8,128)(2,1)} %get-tuple-element.26), channel_id=1, source_target_pairs={{0,96},{3,97},{6,100},{5,101},{8,104},{11,105},{14,108},{13,109},{... | collective-permute-start | bytes 884744 | tf_op jit(solution)/shard_map/ppermute | solution.py:326
  12.6 9.8 %collective-permute-start.1 = (bf16[128,1152]{1,0:T(8,128)(2,1)}, bf16[128,1152]{1,0:T(8,128)(2,1)S(1)}, u32[]{:S(2)}, u32[]{:S(2)}) collective-permute-start(bf16[128,1152]{1,0:T(8,128)(2,1)} %get-tuple-element.26), channel_id=1, source_target_pairs={{0,32},{3,33},{6,36},{5,37},{8,40},{11,41},{14,44},{13,45},{16,48}... | collective-permute-start | bytes 884744 | tf_op jit(solution)/shard_map/ppermute | solution.py:326
  13.3 14.4 %collective-permute-start.5 = (bf16[256,1152]{1,0:T(8,128)(2,1)}, bf16[256,1152]{1,0:T(8,128)(2,1)S(1)}, u32[]{:S(2)}, u32[]{:S(2)}) collective-permute-start(bf16[256,1152]{1,0:T(8,128)(2,1)} %get-tuple-element.28.bottom), channel_id=1, source_target_pairs={{0,5},{2,7},{1,4},{3,6},{4,1},{6,3},{5,0},{7,2},{8,13},{10,15},{9,... | collective-permute-start | bytes 1769480 | tf_op jit(solution)/shard_map/ppermute | solution.py:324
  16.5 16.9 %collective-permute-start.9 = (bf16[128,1152]{1,0:T(8,128)(2,1)S(1)}, bf16[128,1152]{1,0:T(8,128)(2,1)S(1)}, u32[]{:S(2)}, u32[]{:S(2)}) collective-permute-start(bf16[128,1152]{1,0:T(8,128)(2,1)S(1)} %get-tuple-element.46.refs_0_.refs_3_), channel_id=1, source_target_pairs={{0,64},{2,18},{1,65},{3,19},{4,68},{6,22},{5,69},{7,23},{8,72},{10... | collective-permute-start | bytes 884744 | tf_op jit(solution)/shard_map/ppermute | solution.py:333
  20.1 13.4 %collective-permute-start.8 = (bf16[128,1152]{1,0:T(8,128)(2,1)S(1)}, bf16[128,1152]{1,0:T(8,128)(2,1)S(1)}, u32[]{:S(2)}, u32[]{:S(2)}) collective-permute-start(bf16[128,1152]{1,0:T(8,128)(2,1)S(1)} %get-tuple-element.46.refs_0_.refs_3_), channel_id=1, source_target_pairs={{0,96},{2,26},{1,97},{3,27},{4,100},{6,30},{5,101},{7,31},{8,104},... | collective-permute-start | bytes 884744 | tf_op jit(solution)/shard_map/ppermute | solution.py:333
  22.4 11.0 %collective-permute-start.7 = (bf16[128,1152]{1,0:T(8,128)(2,1)S(1)}, bf16[128,1152]{1,0:T(8,128)(2,1)S(1)}, u32[]{:S(2)}, u32[]{:S(2)}) collective-permute-start(bf16[128,1152]{1,0:T(8,128)(2,1)S(1)} %get-tuple-element.46.refs_0_.refs_3_), channel_id=1, source_target_pairs={{0,32},{2,10},{1,33},{3,11},{4,36},{6,14},{5,37},{7,15},{8,40},{10... | collective-permute-start | bytes 884744 | tf_op jit(solution)/shard_map/ppermute | solution.py:333
  22.4 5.3 %copy-start = (bf16[320,1152]{1,0:T(8,128)(2,1)S(1)}, bf16[320,1152]{1,0:T(8,128)(2,1)}, u32[]{:S(2)}) copy-start(bf16[320,1152]{1,0:T(8,128)(2,1)} %get-tuple-element.27.top) | copy-start | bytes 2211844
  22.4 5.3 %copy-start.1 = (bf16[256,1152]{1,0:T(8,128)(2,1)S(1)}, bf16[256,1152]{1,0:T(8,128)(2,1)}, u32[]{:S(2)}) copy-start(bf16[256,1152]{1,0:T(8,128)(2,1)} %get-tuple-element.28.bottom) | copy-start | bytes 1769476
  30.6 5.4 %collective-permute-start.10 = (bf16[512,1152]{1,0:T(8,128)(2,1)S(1)}, bf16[512,1152]{1,0:T(8,128)(2,1)S(1)}, u32[]{:S(2)}, u32[]{:S(2)}) collective-permute-start(bf16[512,1152]{1,0:T(8,128)(2,1)S(1)} %get-tuple-element.29.refs_0_.emb_a), channel_id=1, source_target_pairs={{0,2},{2,0},{1,3},{3,1},{4,6},{6,4},{5,7},{7,5},{8,10},{10,8},{9,1... | collective-permute-start | bytes 3538952 | tf_op jit(solution)/shard_map/ppermute | solution.py:305
  35.6 3.0 %collective-permute-start.11 = (bf16[512,1152]{1,0:T(8,128)(2,1)S(1)}, bf16[512,1152]{1,0:T(8,128)(2,1)S(1)}, u32[]{:S(2)}, u32[]{:S(2)}) collective-permute-start(bf16[512,1152]{1,0:T(8,128)(2,1)S(1)} %get-tuple-element.30.refs_1_.emb_b), channel_id=1, source_target_pairs={{0,2},{2,0},{1,3},{3,1},{4,6},{6,4},{5,7},{7,5},{8,10},{10,8},{9,1... | collective-permute-start | bytes 3538952 | tf_op jit(solution)/shard_map/ppermute | solution.py:305
  45.4 11.9 %collective-permute-start.12 = (bf16[144,1152]{1,0:T(8,128)(2,1)S(1)}, bf16[144,1152]{1,0:T(8,128)(2,1)S(1)}, u32[]{:S(2)}, u32[]{:S(2)}) collective-permute-start(bf16[144,1152]{1,0:T(8,128)(2,1)S(1)} %get-tuple-element.39), channel_id=1, source_target_pairs={{0,65},{2,23},{1,64},{3,22},{4,69},{6,19},{5,68},{7,18},{8,73},{10... | collective-permute-start | bytes 995336 | tf_op jit(solution)/shard_map/ppermute | solution.py:383
  48.6 11.1 %collective-permute-start.13 = (bf16[144,1152]{1,0:T(8,128)(2,1)S(1)}, bf16[144,1152]{1,0:T(8,128)(2,1)S(1)}, u32[]{:S(2)}, u32[]{:S(2)}) collective-permute-start(bf16[144,1152]{1,0:T(8,128)(2,1)S(1)} %get-tuple-element.40), channel_id=1, source_target_pairs={{0,64},{2,18},{1,65},{3,19},{4,68},{6,22},{5,69},{7,23},{8,72},{10... | collective-permute-start | bytes 995336 | tf_op jit(solution)/shard_map/ppermute | solution.py:383
  50.1 10.8 %collective-permute-start.18 = (bf16[144,1152]{1,0:T(8,128)(2,1)S(1)}, bf16[144,1152]{1,0:T(8,128)(2,1)S(1)}, u32[]{:S(2)}, u32[]{:S(2)}) collective-permute-start(bf16[144,1152]{1,0:T(8,128)(2,1)S(1)} %get-tuple-element.45), channel_id=1, source_target_pairs={{0,1},{2,7},{1,0},{3,6},{4,5},{6,3},{5,4},{7,2},{8,9},{10,15},{9,8... | collective-permute-start | bytes 995336 | tf_op jit(solution)/shard_map/ppermute | solution.py:391
  54.4 9.5 %collective-permute-start.14 = (bf16[144,1152]{1,0:T(8,128)(2,1)S(1)}, bf16[144,1152]{1,0:T(8,128)(2,1)S(1)}, u32[]{:S(2)}, u32[]{:S(2)}) collective-permute-start(bf16[144,1152]{1,0:T(8,128)(2,1)S(1)} %get-tuple-element.41), channel_id=1, source_target_pairs={{0,33},{2,15},{1,32},{3,14},{4,37},{6,11},{5,36},{7,10},{8,41},{10... | collective-permute-start | bytes 995336 | tf_op jit(solution)/shard_map/ppermute | solution.py:383
  56.2 11.0 %collective-permute-start.15 = (bf16[144,1152]{1,0:T(8,128)(2,1)S(1)}, bf16[144,1152]{1,0:T(8,128)(2,1)S(1)}, u32[]{:S(2)}, u32[]{:S(2)}) collective-permute-start(bf16[144,1152]{1,0:T(8,128)(2,1)S(1)} %get-tuple-element.42), channel_id=1, source_target_pairs={{0,32},{2,10},{1,33},{3,11},{4,36},{6,14},{5,37},{7,15},{8,40},{10... | collective-permute-start | bytes 995336 | tf_op jit(solution)/shard_map/ppermute | solution.py:383
  57.2 10.0 %collective-permute-start.16 = (bf16[144,1152]{1,0:T(8,128)(2,1)S(1)}, bf16[144,1152]{1,0:T(8,128)(2,1)S(1)}, u32[]{:S(2)}, u32[]{:S(2)}) collective-permute-start(bf16[144,1152]{1,0:T(8,128)(2,1)S(1)} %get-tuple-element.43), channel_id=1, source_target_pairs={{0,97},{2,31},{1,96},{3,30},{4,101},{6,27},{5,100},{7,26},{8,105},... | collective-permute-start | bytes 995336 | tf_op jit(solution)/shard_map/ppermute | solution.py:383
  59.7 9.8 %collective-permute-start.17 = (bf16[144,1152]{1,0:T(8,128)(2,1)S(1)}, bf16[144,1152]{1,0:T(8,128)(2,1)S(1)}, u32[]{:S(2)}, u32[]{:S(2)}) collective-permute-start(bf16[144,1152]{1,0:T(8,128)(2,1)S(1)} %get-tuple-element.44), channel_id=1, source_target_pairs={{0,96},{2,26},{1,97},{3,27},{4,100},{6,30},{5,101},{7,31},{8,104},... | collective-permute-start | bytes 995336 | tf_op jit(solution)/shard_map/ppermute | solution.py:383
  70.6 12.2 %all-to-all-start = ((bf16[8,18,1152]{2,1,0:T(8,128)(2,1)}), bf16[8,18,1152]{2,1,0:T(8,128)(2,1)S(1)}, u32[]{:S(2)}, u32[]{:S(2)}) async-start(bf16[8,18,1152]{2,1,0:T(8,128)(2,1)} %sum_terms.1), calls=%async_computation | async-start | bytes 884736 | tf_op jit(solution)/shard_map/all_to_all | solution.py:396
  82.9 4.6 %collective-permute-start.19 = (f32[18,576]{1,0:T(8,128)S(1)}, f32[18,576]{1,0:T(8,128)S(1)}, u32[]{:S(2)}, u32[]{:S(2)}) collective-permute-start(f32[18,576]{1,0:T(8,128)S(1)} %slice_select_fusion), channel_id=1, source_target_pairs={{0,2},{2,0},{1,3},{3,1},{4,6},{6,4},{5,7},{7,5},{8,10},{10,8},{9,1... | collective-permute-start | bytes 124424 | tf_op jit(solution)/shard_map/ppermute | solution.py:305

commit v10 on v9

--- a/solution.py
+++ b/solution.py
@@ -79,7 +79,7 @@
 def pick_kernel(img_feats, txt_feats, img_head, txt_head, mine, give, send, top, bottom, *scratch):
     _, _, high, core, tower = position()
     head, units, into, out = scratch
-    split, step = top.shape[0], 64
+    split, step = top.shape[0], 32
     cuts = range(0, head.shape[0], step)
     count = len(cuts) + 3
 
@@ -144,8 +144,33 @@
         flip_rows(unit[...], flip_ref, i * unit.shape[0])
 
 
-def head_kernel(top, bottom, far_top, far_bottom, _, head_ref):
-    head_ref[...] = jnp.concatenate([top[...], bottom[...], far_top[...], far_bottom[...]], axis=0).T
+def own_half_kernel(top, bottom, *refs):
+    *units, flip_ref, turned_ref, raw_ref = refs
+    turned_ref[...] = jnp.concatenate([top[...], bottom[...]], axis=0).T
+    flip_kernel(*units, flip_ref)
+    rows = units[0].shape[0]
+    for i in range(0, len(units), 2):
+        feats = jnp.concatenate([units[i][...], units[i + 1][...]], axis=0)
+        raw_ref[pl.ds(i * rows, 2 * rows), :] = jnp.dot(
+            feats, turned_ref[...], preferred_element_type=F32
+        ).astype(BF16)
+
+
+def embed_first_kernel(turned, own_raw, far_top, far_bottom, *refs):
+    *units, emb_ref, raw_ref, head_ref = refs
+    width = turned.shape[1]
+    far = jnp.concatenate([far_top[...], far_bottom[...]], axis=0).T
+    rows = units[0].shape[0]
+    for i in range(0, len(units), 2):
+        here = pl.ds(i * rows, 2 * rows)
+        feats = jnp.concatenate([units[i][...], units[i + 1][...]], axis=0)
+        far_raw = jnp.dot(feats, far, preferred_element_type=F32).astype(BF16)
+        raw = jnp.concatenate([own_raw[here, :], far_raw], axis=1)
+        wide = raw.astype(F32)
+        emb_ref[here, :] = (wide * inverse_norm(wide)).astype(BF16)
+        raw_ref[here, :] = raw
+    head_ref[:, :width] = turned[...]
+    head_ref[:, width:] = far
 
 
 def embed_kernel(head_ref, *refs):
@@ -308,13 +333,13 @@
     mine, give, send, top, bottom = kernel_call(
         pick_kernel,
         "pick",
-        [((rows, depth), BF16)] * 3 + [((5 * depth // 18, depth), BF16), ((2 * depth // 9, depth), BF16)],
+        [((rows, depth), BF16)] * 3 + [((22 * depth // 72, depth), BF16), ((14 * depth // 72, depth), BF16)],
         (img_feats, txt_feats, img_proj.T, txt_proj.T),
         scratch=(
             pltpu.VMEM((width, depth), BF16),
             pltpu.VMEM((3, rows, depth), BF16),
-            pltpu.SemaphoreType.DMA((width // 64 + 3,)),
-            pltpu.SemaphoreType.DMA((width // 64 + 3,)),
+            pltpu.SemaphoreType.DMA((width // 32 + 3,)),
+            pltpu.SemaphoreType.DMA((width // 32 + 3,)),
         ),
         anywhere_out=True,
         anywhere=range(4),
@@ -335,12 +360,19 @@
     rows_of = ((pair, full), BF16)
     work = 2 * pair * depth * full
     flips = ((RING, 2, part // 2, pair), BF16)
-    (flip_a,) = kernel_call(flip_kernel, "flip_first", [flips], units_a)
-    (head,) = kernel_call(
-        head_kernel, "head", [((depth, full), BF16)], (top, bottom, far_top, far_bottom, flip_a), anywhere=(4,)
-    )
-    emb_a, raw_a = kernel_call(
-        embed_kernel, "embed_first", [rows_of, rows_of], (head, *units_a), flops=work
+    flip_a, turned_head, own_raw = kernel_call(
+        own_half_kernel,
+        "own_half",
+        [flips, ((depth, width), BF16), ((pair, width), BF16)],
+        (top, bottom, *units_a),
+        flops=work // 2,
+    )
+    emb_a, raw_a, head = kernel_call(
+        embed_first_kernel,
+        "embed_first",
+        [rows_of, rows_of, ((depth, full), BF16)],
+        (turned_head, own_raw, far_top, far_bottom, *units_a),
+        flops=work // 2,
     )
     far_a = swap(emb_a)
     emb_b, raw_b = kernel_call(
@@ -386,7 +418,7 @@
         ]
 
     far = send_pieces(far, 2)
-    near = send_pieces(terms("terms_near", 1, 3), 1, 3)
+    near = send_pieces(terms("term_up", 1), 1) + send_pieces(terms("term_down", 3), 3)
     kept, crossed = terms("term_own", 0)
     crossed = lax.ppermute(crossed, AXES, reduce_pairs(0, 1))
     (early,) = kernel_call(add_kernel, "add_far", [((part // 2, full), F32)], (kept, *far))

time: 88.6 us -> 85.4 us (0.964)
  starting transfers between devices: 39.6 us -> 37.4 us
  waiting for transfers between devices: 23.5 us -> 21.6 us
    ppermute x1, waiting for transfers between devices: 4.42 us -> 1.29 us  [local(): far_bottom = lax.ppermute(bottom, AXES, FAR_SWAP)]
    ppermute x1, waiting for transfers between devices: 0.01 us -> 2.01 us  [local(): far_top = lax.ppermute(top, AXES, NEAR_SWAP)]
    all_to_all x1, starting transfers between devices: 4.8 us -> 3.57 us  [local(): lax.all_to_all(sums, AXES, 0, 0, axis_index_groups=REDUCE_GROUPS, tiled=T...]
    ppermute x4, starting transfers between devices: 6.81 us -> 5.69 us  [swap(): return lax.ppermute(value, AXES, CORES_SWAP)]
  transfers between devices with their start and end apart: 21 -> 21, of which waited for: 9 -> 8; matrix products, arithmetic and copies ran while one was open for 1% -> 1% of each run, Pallas kernels for 17% -> 18%
where the time goes in v10:
time: 85.4 us; the launch traced here: 84.7 us
  starting transfers between devices  37.4 us (44%)
  Pallas kernels  23 us (27%)
  waiting for transfers between devices  21.6 us (25%)
  other arithmetic  1.91 us (2%)
    pallas_call x11, Pallas kernels, kernel_call(): pl.pallas_call(body, out_shape=shapes, in_specs=[anywhere_spec() if i in...  23 us
    ppermute x6, starting transfers between devices, send_pieces(): lax.ppermute(pieces[2 * k + flip], AXES, reduce_pairs(turn, flip))  10.2 us
    ppermute x6, waiting for transfers between devices, send_pieces(): lax.ppermute(pieces[2 * k + flip], AXES, reduce_pairs(turn, flip))  8.08 us
    all_to_all x1, waiting for transfers between devices, local(): lax.all_to_all(sums, AXES, 0, 0, axis_index_groups=REDUCE_GROUPS, tiled=T...  7.39 us
    ppermute x4, starting transfers between devices, swap(): return lax.ppermute(value, AXES, CORES_SWAP)  5.69 us
    ppermute x3, starting transfers between devices, local(): lax.ppermute(second, AXES, ring(turn))  5.31 us
    ppermute x1, starting transfers between devices, local(): far_texts = lax.ppermute(txt_feats, AXES, TEXTS_SWAP)  5.22 us
    ppermute x3, starting transfers between devices, local(): units_a = [lax.ppermute(send, AXES, first_ring(turn)) for turn in turns]  4.38 us
  transfers between devices with their start and end apart: 21, of which 8 were waited for; matrix products, arithmetic and copies ran while one was open for 1% of the time, Pallas kernels for 18%

profile of v10, /device:TPU:1, one launch (start us, length us, event | category | flops | bytes accessed | tf_op | source)
XLA Modules:
  0.0 84.7 jit_solution(9599011565727393751)
XLA Ops:
  0.6 5.2 %collective-permute-start.6 = (bf16[128,1152]{1,0:T(8,128)(2,1)}, bf16[128,1152]{1,0:T(8,128)(2,1)S(1)}, u32[]{:S(2)}, u32[]{:S(2)}) collective-permute-start(bf16[128,1152]{1,0:T(8,128)(2,1)} %txt_feats.1), channel_id=1, source_target_pairs={{2,7},{1,6},{4,3},{7,2},{10,15},{9,14},{12,11},{15,10},{18,23},{17... | collective-permute-start | bytes 884744 | tf_op jit(solution)/shard_map/ppermute | solution.py:332
  5.9 2.8 %pick.1 = (bf16[128,1152]{1,0:T(8,128)(2,1)}, bf16[128,1152]{1,0:T(8,128)(2,1)}, bf16[128,1152]{1,0:T(8,128)(2,1)}, bf16[352,1152]{1,0:T(8,128)(2,1)}, bf16[224,1152]{1,0:T(8,128)(2,1)}) custom-call(bf16[128,1152]{1,0:T(8,128)(2,1)} %img_feats.1, bf16[128,1152]{1,0:T(8,128)(2,1)} %txt_feats.1, bf16[576,1152]{1,0:T(8,128)(2,1)} %bitcast.2, ...), custom_call_target="tpu_custom_call" | custom-call | bytes 5455872 | tf_op jit(solution)/shard_map/pick/pallas_call | solution.py:310
  8.7 0.1 collective-permute-start
  8.8 0.3 collective-permute-start.4
  9.1 2.9 %collective-permute-start.3 = (bf16[128,1152]{1,0:T(8,128)(2,1)}, bf16[128,1152]{1,0:T(8,128)(2,1)S(1)}, u32[]{:S(2)}, u32[]{:S(2)}) collective-permute-start(bf16[128,1152]{1,0:T(8,128)(2,1)} %get-tuple-element.32), channel_id=1, source_target_pairs={{0,64},{3,65},{6,68},{5,69},{8,72},{11,73},{14,76},{13,77},{16,80}... | collective-permute-start | bytes 884744 | tf_op jit(solution)/shard_map/ppermute | solution.py:351
  12.0 0.8 collective-permute-start.2
  12.8 0.7 collective-permute-start.1
  13.5 0.0 collective-permute-done
  13.5 0.9 %collective-permute-start.5 = (bf16[224,1152]{1,0:T(8,128)(2,1)}, bf16[224,1152]{1,0:T(8,128)(2,1)S(1)}, u32[]{:S(2)}, u32[]{:S(2)}) collective-permute-start(bf16[224,1152]{1,0:T(8,128)(2,1)} %get-tuple-element.29.bottom), channel_id=1, source_target_pairs={{0,5},{2,7},{1,4},{3,6},{4,1},{6,3},{5,0},{7,2},{8,13},{10,15},{9,... | collective-permute-start | bytes 1548296 | tf_op jit(solution)/shard_map/ppermute | solution.py:349
  14.4 1.0 %select_select_fusion = (bf16[128,1152]{1,0:T(8,128)(2,1)S(1)}, bf16[128,1152]{1,0:T(8,128)(2,1)S(1)}) fusion(bf16[128,1152]{1,0:T(8,128)(2,1)S(1)} %collective-permute-done.6, bf16[128,1152]{1,0:T(8,128)(2,1)} %get-tuple-element.30, bf16[128,1152]{1,0:T(8,128)(2,1)S(1)} %collective-permute-done, pred[]{:T(512)S(6)} %eq.19, pred[]{:T(512)S(6)} %eq.18, pred[]{:T(512)S(6)} %eq.17), kind=kLoop, calls=%fused_computation.1 | loop fusion | flops 442368 | bytes 1474563 | tf_op jit(solution)/shard_map/jit(_where)/select_n | solution.py:356
  15.4 1.3 %collective-permute-done.3.refs_3_ = bf16[128,1152]{1,0:T(8,128)(2,1)S(1)} collective-permute-done((bf16[128,1152]{1,0:T(8,128)(2,1)}, bf16[128,1152]{1,0:T(8,128)(2,1)S(1)}, u32[]{:S(2)}, u32[]{:S(2)}) %collective-permute-start.3) | collective-permute-done | bytes 294944 | tf_op jit(solution)/shard_map/ppermute | solution.py:351
  16.7 3.0 %collective-permute-start.9 = (bf16[128,1152]{1,0:T(8,128)(2,1)S(1)}, bf16[128,1152]{1,0:T(8,128)(2,1)S(1)}, u32[]{:S(2)}, u32[]{:S(2)}) collective-permute-start(bf16[128,1152]{1,0:T(8,128)(2,1)S(1)} %get-tuple-element.54.refs_0_.refs_3_), channel_id=1, source_target_pairs={{0,64},{2,18},{1,65},{3,19},{4,68},{6,22},{5,69},{7,23},{8,72},{10... | collective-permute-start | bytes 884744 | tf_op jit(solution)/shard_map/ppermute | solution.py:358
  19.7 0.6 collective-permute-done.2.refs_2_
  20.3 2.3 %collective-permute-start.8 = (bf16[128,1152]{1,0:T(8,128)(2,1)S(1)}, bf16[128,1152]{1,0:T(8,128)(2,1)S(1)}, u32[]{:S(2)}, u32[]{:S(2)}) collective-permute-start(bf16[128,1152]{1,0:T(8,128)(2,1)S(1)} %get-tuple-element.54.refs_0_.refs_3_), channel_id=1, source_target_pairs={{0,96},{2,26},{1,97},{3,27},{4,100},{6,30},{5,101},{7,31},{8,104},... | collective-permute-start | bytes 884744 | tf_op jit(solution)/shard_map/ppermute | solution.py:358
  22.6 2.4 %own_half.1 = (bf16[4,2,144,512]{3,2,1,0:T(8,128)(2,1)S(1)}, bf16[1152,576]{1,0:T(8,128)(2,1)S(1)}, bf16[512,576]{1,0:T(8,128)(2,1)S(1)}) custom-call(bf16[352,1152]{1,0:T(8,128)(2,1)S(1)} %copy-done, bf16[224,1152]{1,0:T(8,128)(2,1)S(1)} %copy-done.1, bf16[128,1152]{1,0:T(8,128)(2,1)S(1)} %get-tuple-element.55.refs_0_, ...), custom_call_target="tpu_custom_call" | custom-call | flops 679477248 | bytes 5603328 | tf_op jit(solution)/shard_map/own_half/pallas_call | solution.py:310
  25.0 1.3 %collective-permute-done.5.far_bottom = bf16[224,1152]{1,0:T(8,128)(2,1)S(1)} collective-permute-done((bf16[224,1152]{1,0:T(8,128)(2,1)}, bf16[224,1152]{1,0:T(8,128)(2,1)S(1)}, u32[]{:S(2)}, u32[]{:S(2)}) %collective-permute-start.5) | collective-permute-done | bytes 516128 | tf_op jit(solution)/shard_map/ppermute | solution.py:349
  26.3 2.0 %collective-permute-done.4.far_top = bf16[352,1152]{1,0:T(8,128)(2,1)S(1)} collective-permute-done((bf16[352,1152]{1,0:T(8,128)(2,1)}, bf16[352,1152]{1,0:T(8,128)(2,1)S(1)}, u32[]{:S(2)}, u32[]{:S(2)}) %collective-permute-start.4) | collective-permute-done | bytes 811040 | tf_op jit(solution)/shard_map/ppermute | solution.py:348
  28.3 1.8 %embed_first.1 = (bf16[512,1152]{1,0:T(8,128)(2,1)S(1)}, bf16[512,1152]{1,0:T(8,128)(2,1)S(1)}, bf16[1152,1152]{1,0:T(8,128)(2,1)S(1)}) custom-call(bf16[1152,576]{1,0:T(8,128)(2,1)S(1)} %get-tuple-element.34.turned, bf16[512,576]{1,0:T(8,128)(2,1)S(1)} %get-tuple-element.35.own_raw, bf16[352,1152]{1,0:T(8,128)(2,1)S(1)} %collective-permute-done.4.far_top, ...), custom_call_target="tpu_custom_call" | custom-call | flops 679477248 | bytes 9437184 | tf_op jit(solution)/shard_map/embed_first/pallas_call | solution.py:310
  30.1 1.3 %collective-permute-start.10 = (bf16[512,1152]{1,0:T(8,128)(2,1)S(1)}, bf16[512,1152]{1,0:T(8,128)(2,1)S(1)}, u32[]{:S(2)}, u32[]{:S(2)}) collective-permute-start(bf16[512,1152]{1,0:T(8,128)(2,1)S(1)} %get-tuple-element.36.refs_0_.emb_a), channel_id=1, source_target_pairs={{0,2},{2,0},{1,3},{3,1},{4,6},{6,4},{5,7},{7,5},{8,10},{10,8},{9,1... | collective-permute-start | bytes 3538952 | tf_op jit(solution)/shard_map/ppermute | solution.py:330
  31.4 0.0 collective-permute-done.9.refs_3_.refs_6_
  31.4 2.1 %embed_second.1 = (bf16[512,1152]{1,0:T(8,128)(2,1)S(1)}, bf16[512,1152]{1,0:T(8,128)(2,1)S(1)}) custom-call(bf16[1152,1152]{1,0:T(8,128)(2,1)S(1)} %get-tuple-element.37.head_ref, bf16[128,1152]{1,0:T(8,128)(2,1)S(1)} %get-tuple-element.54.refs_0_.refs_3_, bf16[128,1152]{1,0:T(8,128)(2,1)S(1)} %collective-permute-done.7.refs_1_.refs_4_, ...), custom_call_target="tpu_custom_call" | custom-call | flops 1358954496 | bytes 6193152 | tf_op jit(solution)/shard_map/embed_second/pallas_call | solution.py:310
  33.6 1.7 %collective-permute-start.11 = (bf16[512,1152]{1,0:T(8,128)(2,1)S(1)}, bf16[512,1152]{1,0:T(8,128)(2,1)S(1)}, u32[]{:S(2)}, u32[]{:S(2)}) collective-permute-start(bf16[512,1152]{1,0:T(8,128)(2,1)S(1)} %get-tuple-element.38.refs_1_.emb_b), channel_id=1, source_target_pairs={{0,2},{2,0},{1,3},{3,1},{4,6},{6,4},{5,7},{7,5},{8,10},{10,8},{9,1... | collective-permute-start | bytes 3538952 | tf_op jit(solution)/shard_map/ppermute | solution.py:330
  35.3 2.7 %score_first.1 = (bf16[512,512]{1,0:T(8,128)(2,1)S(1)}, bf16[512,512]{1,0:T(8,128)(2,1)S(1)}, bf16[4,2,144,512]{3,2,1,0:T(8,128)(2,1)S(1)}) custom-call(bf16[512,1152]{1,0:T(8,128)(2,1)S(1)} %get-tuple-element.36.refs_0_.emb_a, bf16[512,1152]{1,0:T(8,128)(2,1)S(1)} %get-tuple-element.38.refs_1_.emb_b, ...), custom_call_target="tpu_custom_call" | custom-call | flops 1207959552 | bytes 6946816 | tf_op jit(solution)/shard_map/score_first/pallas_call | solution.py:310
  38.0 0.0 collective-permute-done.11.far_b
  38.0 6.9 %score_second.1 = (bf16[512,1152]{1,0:T(8,128)(2,1)S(1)}, bf16[512,1152]{1,0:T(8,128)(2,1)S(1)}, bf16[144,1152]{1,0:T(8,128)(2,1)S(1)}, bf16[144,1152]{1,0:T(8,128)(2,1)S(1)}) custom-call(bf16[512,1152]{1,0:T(8,128)(2,1)S(1)} %get-tuple-element.36.refs_0_.emb_a, bf16[512,1152]{1,0:T(8,128)(2,1)S(1)} %get-tuple-element.38.refs_1_.emb_b, ...), custom_call_target="tpu_custom_call" | custom-call | flops 4303355904 | bytes 13508608 | tf_op jit(solution)/shard_map/score_second/pallas_call | solution.py:310
  44.9 3.6 %collective-permute-start.12 = (bf16[144,1152]{1,0:T(8,128)(2,1)S(1)}, bf16[144,1152]{1,0:T(8,128)(2,1)S(1)}, u32[]{:S(2)}, u32[]{:S(2)}) collective-permute-start(bf16[144,1152]{1,0:T(8,128)(2,1)S(1)} %get-tuple-element.47), channel_id=1, source_target_pairs={{0,65},{2,23},{1,64},{3,22},{4,69},{6,19},{5,68},{7,18},{8,73},{10... | collective-permute-start | bytes 995336 | tf_op jit(solution)/shard_map/ppermute | solution.py:415
  48.4 0.1 collective-permute-start.13
  48.5 1.1 %term_down.1 = (bf16[144,1152]{1,0:T(8,128)(2,1)S(1)}, bf16[144,1152]{1,0:T(8,128)(2,1)S(1)}) custom-call(bf16[4,2,144,512]{3,2,1,0:T(8,128)(2,1)S(1)} %get-tuple-element.33.flip_a.refs_0_, bf16[4,2,144,512]{3,2,1,0:T(8,128)(2,1)S(1)} %get-tuple-element.39.flip_b.refs_1_, bf16[512,1152]{1,0:T(8,128)(2,1)S(1)} %get-tuple-element.44.refs_2_, ...), custom_call_target="tpu_custom_call" | custom-call | flops 679477248 | bytes 5382144 | tf_op jit(solution)/shard_map/term_down/pallas_call | solution.py:310
  49.5 4.3 %collective-permute-start.16 = (bf16[144,1152]{1,0:T(8,128)(2,1)S(1)}, bf16[144,1152]{1,0:T(8,128)(2,1)S(1)}, u32[]{:S(2)}, u32[]{:S(2)}) collective-permute-start(bf16[144,1152]{1,0:T(8,128)(2,1)S(1)} %get-tuple-element.51), channel_id=1, source_target_pairs={{0,97},{2,31},{1,96},{3,30},{4,101},{6,27},{5,100},{7,26},{8,105},... | collective-permute-start | bytes 995336 | tf_op jit(solution)/shard_map/ppermute | solution.py:415
  53.9 0.5 collective-permute-start.17
  54.4 1.1 %term_up.1 = (bf16[144,1152]{1,0:T(8,128)(2,1)S(1)}, bf16[144,1152]{1,0:T(8,128)(2,1)S(1)}) custom-call(bf16[4,2,144,512]{3,2,1,0:T(8,128)(2,1)S(1)} %get-tuple-element.33.flip_a.refs_0_, bf16[4,2,144,512]{3,2,1,0:T(8,128)(2,1)S(1)} %get-tuple-element.39.flip_b.refs_1_, bf16[512,1152]{1,0:T(8,128)(2,1)S(1)} %get-tuple-element.44.refs_2_, ...), custom_call_target="tpu_custom_call" | custom-call | flops 679477248 | bytes 5382144 | tf_op jit(solution)/shard_map/term_up/pallas_call | solution.py:310
  55.4 1.6 %collective-permute-start.14 = (bf16[144,1152]{1,0:T(8,128)(2,1)S(1)}, bf16[144,1152]{1,0:T(8,128)(2,1)S(1)}, u32[]{:S(2)}, u32[]{:S(2)}) collective-permute-start(bf16[144,1152]{1,0:T(8,128)(2,1)S(1)} %get-tuple-element.49), channel_id=1, source_target_pairs={{0,33},{2,15},{1,32},{3,14},{4,37},{6,11},{5,36},{7,10},{8,41},{10... | collective-permute-start | bytes 995336 | tf_op jit(solution)/shard_map/ppermute | solution.py:415
  57.1 1.1 %term_own.1 = (bf16[144,1152]{1,0:T(8,128)(2,1)S(1)}, bf16[144,1152]{1,0:T(8,128)(2,1)S(1)}) custom-call(bf16[4,2,144,512]{3,2,1,0:T(8,128)(2,1)S(1)} %get-tuple-element.33.flip_a.refs_0_, bf16[4,2,144,512]{3,2,1,0:T(8,128)(2,1)S(1)} %get-tuple-element.39.flip_b.refs_1_, bf16[512,1152]{1,0:T(8,128)(2,1)S(1)} %get-tuple-element.44.refs_2_, ...), custom_call_target="tpu_custom_call" | custom-call | flops 679477248 | bytes 5382144 | tf_op jit(solution)/shard_map/term_own/pallas_call | solution.py:310
  58.1 0.1 collective-permute-start.15
  58.2 0.0 collective-permute-done.13.refs_2_
  58.2 1.9 %collective-permute-start.18 = (bf16[144,1152]{1,0:T(8,128)(2,1)S(1)}, bf16[144,1152]{1,0:T(8,128)(2,1)S(1)}, u32[]{:S(2)}, u32[]{:S(2)}) collective-permute-start(bf16[144,1152]{1,0:T(8,128)(2,1)S(1)} %get-tuple-element.53), channel_id=1, source_target_pairs={{0,1},{2,7},{1,0},{3,6},{4,5},{6,3},{5,4},{7,2},{8,9},{10,15},{9,8... | collective-permute-start | bytes 995336 | tf_op jit(solution)/shard_map/ppermute | solution.py:423
  60.1 0.1 add_far.1.refs_0_
  60.2 0.0 collective-permute-done.16.refs_3_
  60.3 5.8 %collective-permute-done.17.refs_4_ = bf16[144,1152]{1,0:T(8,128)(2,1)S(1)} collective-permute-done((bf16[144,1152]{1,0:T(8,128)(2,1)S(1)}, bf16[144,1152]{1,0:T(8,128)(2,1)S(1)}, u32[]{:S(2)}, u32[]{:S(2)}) %collective-permute-start.17) | collective-permute-done | bytes 331808 | tf_op jit(solution)/shard_map/ppermute | solution.py:415
  66.0 2.3 %collective-permute-done.15.refs_2_ = bf16[144,1152]{1,0:T(8,128)(2,1)S(1)} collective-permute-done((bf16[144,1152]{1,0:T(8,128)(2,1)S(1)}, bf16[144,1152]{1,0:T(8,128)(2,1)S(1)}, u32[]{:S(2)}, u32[]{:S(2)}) %collective-permute-start.15) | collective-permute-done | bytes 331808 | tf_op jit(solution)/shard_map/ppermute | solution.py:415
  68.3 1.1 %sum_terms.1 = bf16[8,18,1152]{2,1,0:T(8,128)(2,1)} custom-call(f32[144,1152]{1,0:T(8,128)S(1)} %add_far.1.refs_0_, bf16[144,1152]{1,0:T(8,128)(2,1)S(1)} %collective-permute-done.14.refs_1_, bf16[144,1152]{1,0:T(8,128)(2,1)S(1)} %collective-permute-done.15.refs_2_, bf16[144,1152]{1,0:T(8,128)(2,1)S(1)} %collective-permute-done.16.refs_3_, ...), custom_call_target="tpu_custom_call" | custom-call | bytes 2654208 | tf_op jit(solution)/shard_map/sum_terms/pallas_call | solution.py:310
  69.4 3.6 %all-to-all-start = ((bf16[8,18,1152]{2,1,0:T(8,128)(2,1)}), bf16[8,18,1152]{2,1,0:T(8,128)(2,1)S(1)}, u32[]{:S(2)}, u32[]{:S(2)}) async-start(bf16[8,18,1152]{2,1,0:T(8,128)(2,1)} %sum_terms.1), calls=%async_computation | async-start | bytes 884736 | tf_op jit(solution)/shard_map/all_to_all | solution.py:428
  73.0 7.4 %all-to-all-done = bf16[8,18,1152]{2,1,0:T(8,128)(2,1)S(1)} async-done(((bf16[8,18,1152]{2,1,0:T(8,128)(2,1)}), bf16[8,18,1152]{2,1,0:T(8,128)(2,1)S(1)}, u32[]{:S(2)}, u32[]{:S(2)}) %all-to-all-start) | async-done | bytes 331808 | tf_op jit(solution)/shard_map/all_to_all | solution.py:428
  80.4 0.1 convert_reduce_fusion
  80.5 0.1 slice_select_fusion
  80.6 2.6 %collective-permute-start.19 = (f32[18,576]{1,0:T(8,128)S(1)}, f32[18,576]{1,0:T(8,128)S(1)}, u32[]{:S(2)}, u32[]{:S(2)}) collective-permute-start(f32[18,576]{1,0:T(8,128)S(1)} %slice_select_fusion), channel_id=1, source_target_pairs={{0,2},{2,0},{1,3},{3,1},{4,6},{6,4},{5,7},{7,5},{8,10},{10,8},{9,1... | collective-permute-start | bytes 124424 | tf_op jit(solution)/shard_map/ppermute | solution.py:330
  83.1 0.9 %collective-permute-done.19 = f32[18,576]{1,0:T(8,128)S(1)} collective-permute-done((f32[18,576]{1,0:T(8,128)S(1)}, f32[18,576]{1,0:T(8,128)S(1)}, u32[]{:S(2)}, u32[]{:S(2)}) %collective-permute-start.19) | collective-permute-done | bytes 41504 | tf_op jit(solution)/shard_map/ppermute | solution.py:330
  84.0 0.7 broadcast_select_fusion.1
  (13 shorter events, 0.0 us)
Async XLA Ops:
  0.6 12.2 %collective-permute-start.6 = (bf16[128,1152]{1,0:T(8,128)(2,1)}, bf16[128,1152]{1,0:T(8,128)(2,1)S(1)}, u32[]{:S(2)}, u32[]{:S(2)}) collective-permute-start(bf16[128,1152]{1,0:T(8,128)(2,1)} %txt_feats.1), channel_id=1, source_target_pairs={{2,7},{1,6},{4,3},{7,2},{10,15},{9,14},{12,11},{15,10},{18,23},{17... | collective-permute-start | bytes 884744 | tf_op jit(solution)/shard_map/ppermute | solution.py:332
  8.7 13.9 %copy-start = (bf16[352,1152]{1,0:T(8,128)(2,1)S(1)}, bf16[352,1152]{1,0:T(8,128)(2,1)}, u32[]{:S(2)}) copy-start(bf16[352,1152]{1,0:T(8,128)(2,1)} %get-tuple-element.28.top) | copy-start | bytes 2433028
  8.7 13.9 %copy-start.1 = (bf16[224,1152]{1,0:T(8,128)(2,1)S(1)}, bf16[224,1152]{1,0:T(8,128)(2,1)}, u32[]{:S(2)}) copy-start(bf16[224,1152]{1,0:T(8,128)(2,1)} %get-tuple-element.29.bottom) | copy-start | bytes 1548292
  8.7 4.8 %collective-permute-start = (bf16[128,1152]{1,0:T(8,128)(2,1)}, bf16[128,1152]{1,0:T(8,128)(2,1)S(1)}, u32[]{:S(2)}, u32[]{:S(2)}) collective-permute-start(bf16[128,1152]{1,0:T(8,128)(2,1)} %get-tuple-element.31), channel_id=1, source_target_pairs={{0,2},{2,0},{1,3},{3,1},{4,6},{6,4},{5,7},{7,5},{8,10},{10,8},{9,1... | collective-permute-start | bytes 884744 | tf_op jit(solution)/shard_map/ppermute | solution.py:330
  8.8 19.5 %collective-permute-start.4 = (bf16[352,1152]{1,0:T(8,128)(2,1)}, bf16[352,1152]{1,0:T(8,128)(2,1)S(1)}, u32[]{:S(2)}, u32[]{:S(2)}) collective-permute-start(bf16[352,1152]{1,0:T(8,128)(2,1)} %get-tuple-element.28.top), channel_id=1, source_target_pairs={{0,1},{2,3},{1,0},{3,2},{4,5},{6,7},{5,4},{7,6},{8,9},{10,11},{9,8... | collective-permute-start | bytes 2433032 | tf_op jit(solution)/shard_map/ppermute | solution.py:348
  9.1 7.6 %collective-permute-start.3 = (bf16[128,1152]{1,0:T(8,128)(2,1)}, bf16[128,1152]{1,0:T(8,128)(2,1)S(1)}, u32[]{:S(2)}, u32[]{:S(2)}) collective-permute-start(bf16[128,1152]{1,0:T(8,128)(2,1)} %get-tuple-element.32), channel_id=1, source_target_pairs={{0,64},{3,65},{6,68},{5,69},{8,72},{11,73},{14,76},{13,77},{16,80}... | collective-permute-start | bytes 884744 | tf_op jit(solution)/shard_map/ppermute | solution.py:351
  12.0 8.2 %collective-permute-start.2 = (bf16[128,1152]{1,0:T(8,128)(2,1)}, bf16[128,1152]{1,0:T(8,128)(2,1)S(1)}, u32[]{:S(2)}, u32[]{:S(2)}) collective-permute-start(bf16[128,1152]{1,0:T(8,128)(2,1)} %get-tuple-element.32), channel_id=1, source_target_pairs={{0,96},{3,97},{6,100},{5,101},{8,104},{11,105},{14,108},{13,109},{... | collective-permute-start | bytes 884744 | tf_op jit(solution)/shard_map/ppermute | solution.py:351
  12.8 9.8 %collective-permute-start.1 = (bf16[128,1152]{1,0:T(8,128)(2,1)}, bf16[128,1152]{1,0:T(8,128)(2,1)S(1)}, u32[]{:S(2)}, u32[]{:S(2)}) collective-permute-start(bf16[128,1152]{1,0:T(8,128)(2,1)} %get-tuple-element.32), channel_id=1, source_target_pairs={{0,32},{3,33},{6,36},{5,37},{8,40},{11,41},{14,44},{13,45},{16,48}... | collective-permute-start | bytes 884744 | tf_op jit(solution)/shard_map/ppermute | solution.py:351
  13.5 12.8 %collective-permute-start.5 = (bf16[224,1152]{1,0:T(8,128)(2,1)}, bf16[224,1152]{1,0:T(8,128)(2,1)S(1)}, u32[]{:S(2)}, u32[]{:S(2)}) collective-permute-start(bf16[224,1152]{1,0:T(8,128)(2,1)} %get-tuple-element.29.bottom), channel_id=1, source_target_pairs={{0,5},{2,7},{1,4},{3,6},{4,1},{6,3},{5,0},{7,2},{8,13},{10,15},{9,... | collective-permute-start | bytes 1548296 | tf_op jit(solution)/shard_map/ppermute | solution.py:349
  16.7 14.7 %collective-permute-start.9 = (bf16[128,1152]{1,0:T(8,128)(2,1)S(1)}, bf16[128,1152]{1,0:T(8,128)(2,1)S(1)}, u32[]{:S(2)}, u32[]{:S(2)}) collective-permute-start(bf16[128,1152]{1,0:T(8,128)(2,1)S(1)} %get-tuple-element.54.refs_0_.refs_3_), channel_id=1, source_target_pairs={{0,64},{2,18},{1,65},{3,19},{4,68},{6,22},{5,69},{7,23},{8,72},{10... | collective-permute-start | bytes 884744 | tf_op jit(solution)/shard_map/ppermute | solution.py:358
  20.3 11.2 %collective-permute-start.8 = (bf16[128,1152]{1,0:T(8,128)(2,1)S(1)}, bf16[128,1152]{1,0:T(8,128)(2,1)S(1)}, u32[]{:S(2)}, u32[]{:S(2)}) collective-permute-start(bf16[128,1152]{1,0:T(8,128)(2,1)S(1)} %get-tuple-element.54.refs_0_.refs_3_), channel_id=1, source_target_pairs={{0,96},{2,26},{1,97},{3,27},{4,100},{6,30},{5,101},{7,31},{8,104},... | collective-permute-start | bytes 884744 | tf_op jit(solution)/shard_map/ppermute | solution.py:358
  22.6 8.8 %collective-permute-start.7 = (bf16[128,1152]{1,0:T(8,128)(2,1)S(1)}, bf16[128,1152]{1,0:T(8,128)(2,1)S(1)}, u32[]{:S(2)}, u32[]{:S(2)}) collective-permute-start(bf16[128,1152]{1,0:T(8,128)(2,1)S(1)} %get-tuple-element.54.refs_0_.refs_3_), channel_id=1, source_target_pairs={{0,32},{2,10},{1,33},{3,11},{4,36},{6,14},{5,37},{7,15},{8,40},{10... | collective-permute-start | bytes 884744 | tf_op jit(solution)/shard_map/ppermute | solution.py:358
  30.1 5.2 %collective-permute-start.10 = (bf16[512,1152]{1,0:T(8,128)(2,1)S(1)}, bf16[512,1152]{1,0:T(8,128)(2,1)S(1)}, u32[]{:S(2)}, u32[]{:S(2)}) collective-permute-start(bf16[512,1152]{1,0:T(8,128)(2,1)S(1)} %get-tuple-element.36.refs_0_.emb_a), channel_id=1, source_target_pairs={{0,2},{2,0},{1,3},{3,1},{4,6},{6,4},{5,7},{7,5},{8,10},{10,8},{9,1... | collective-permute-start | bytes 3538952 | tf_op jit(solution)/shard_map/ppermute | solution.py:330
  33.6 4.4 %collective-permute-start.11 = (bf16[512,1152]{1,0:T(8,128)(2,1)S(1)}, bf16[512,1152]{1,0:T(8,128)(2,1)S(1)}, u32[]{:S(2)}, u32[]{:S(2)}) collective-permute-start(bf16[512,1152]{1,0:T(8,128)(2,1)S(1)} %get-tuple-element.38.refs_1_.emb_b), channel_id=1, source_target_pairs={{0,2},{2,0},{1,3},{3,1},{4,6},{6,4},{5,7},{7,5},{8,10},{10,8},{9,1... | collective-permute-start | bytes 3538952 | tf_op jit(solution)/shard_map/ppermute | solution.py:330
  44.9 13.3 %collective-permute-start.12 = (bf16[144,1152]{1,0:T(8,128)(2,1)S(1)}, bf16[144,1152]{1,0:T(8,128)(2,1)S(1)}, u32[]{:S(2)}, u32[]{:S(2)}) collective-permute-start(bf16[144,1152]{1,0:T(8,128)(2,1)S(1)} %get-tuple-element.47), channel_id=1, source_target_pairs={{0,65},{2,23},{1,64},{3,22},{4,69},{6,19},{5,68},{7,18},{8,73},{10... | collective-permute-start | bytes 995336 | tf_op jit(solution)/shard_map/ppermute | solution.py:415
  48.4 9.8 %collective-permute-start.13 = (bf16[144,1152]{1,0:T(8,128)(2,1)S(1)}, bf16[144,1152]{1,0:T(8,128)(2,1)S(1)}, u32[]{:S(2)}, u32[]{:S(2)}) collective-permute-start(bf16[144,1152]{1,0:T(8,128)(2,1)S(1)} %get-tuple-element.48), channel_id=1, source_target_pairs={{0,64},{2,18},{1,65},{3,19},{4,68},{6,22},{5,69},{7,23},{8,72},{10... | collective-permute-start | bytes 995336 | tf_op jit(solution)/shard_map/ppermute | solution.py:415
  49.5 10.7 %collective-permute-start.16 = (bf16[144,1152]{1,0:T(8,128)(2,1)S(1)}, bf16[144,1152]{1,0:T(8,128)(2,1)S(1)}, u32[]{:S(2)}, u32[]{:S(2)}) collective-permute-start(bf16[144,1152]{1,0:T(8,128)(2,1)S(1)} %get-tuple-element.51), channel_id=1, source_target_pairs={{0,97},{2,31},{1,96},{3,30},{4,101},{6,27},{5,100},{7,26},{8,105},... | collective-permute-start | bytes 995336 | tf_op jit(solution)/shard_map/ppermute | solution.py:415
  53.9 12.1 %collective-permute-start.17 = (bf16[144,1152]{1,0:T(8,128)(2,1)S(1)}, bf16[144,1152]{1,0:T(8,128)(2,1)S(1)}, u32[]{:S(2)}, u32[]{:S(2)}) collective-permute-start(bf16[144,1152]{1,0:T(8,128)(2,1)S(1)} %get-tuple-element.52), channel_id=1, source_target_pairs={{0,96},{2,26},{1,97},{3,27},{4,100},{6,30},{5,101},{7,31},{8,104},... | collective-permute-start | bytes 995336 | tf_op jit(solution)/shard_map/ppermute | solution.py:415
  55.4 10.6 %collective-permute-start.14 = (bf16[144,1152]{1,0:T(8,128)(2,1)S(1)}, bf16[144,1152]{1,0:T(8,128)(2,1)S(1)}, u32[]{:S(2)}, u32[]{:S(2)}) collective-permute-start(bf16[144,1152]{1,0:T(8,128)(2,1)S(1)} %get-tuple-element.49), channel_id=1, source_target_pairs={{0,33},{2,15},{1,32},{3,14},{4,37},{6,11},{5,36},{7,10},{8,41},{10... | collective-permute-start | bytes 995336 | tf_op jit(solution)/shard_map/ppermute | solution.py:415
  58.1 10.2 %collective-permute-start.15 = (bf16[144,1152]{1,0:T(8,128)(2,1)S(1)}, bf16[144,1152]{1,0:T(8,128)(2,1)S(1)}, u32[]{:S(2)}, u32[]{:S(2)}) collective-permute-start(bf16[144,1152]{1,0:T(8,128)(2,1)S(1)} %get-tuple-element.50), channel_id=1, source_target_pairs={{0,32},{2,10},{1,33},{3,11},{4,36},{6,14},{5,37},{7,15},{8,40},{10... | collective-permute-start | bytes 995336 | tf_op jit(solution)/shard_map/ppermute | solution.py:415
  58.2 10.1 %collective-permute-start.18 = (bf16[144,1152]{1,0:T(8,128)(2,1)S(1)}, bf16[144,1152]{1,0:T(8,128)(2,1)S(1)}, u32[]{:S(2)}, u32[]{:S(2)}) collective-permute-start(bf16[144,1152]{1,0:T(8,128)(2,1)S(1)} %get-tuple-element.53), channel_id=1, source_target_pairs={{0,1},{2,7},{1,0},{3,6},{4,5},{6,3},{5,4},{7,2},{8,9},{10,15},{9,8... | collective-permute-start | bytes 995336 | tf_op jit(solution)/shard_map/ppermute | solution.py:423
  69.4 11.0 %all-to-all-start = ((bf16[8,18,1152]{2,1,0:T(8,128)(2,1)}), bf16[8,18,1152]{2,1,0:T(8,128)(2,1)S(1)}, u32[]{:S(2)}, u32[]{:S(2)}) async-start(bf16[8,18,1152]{2,1,0:T(8,128)(2,1)} %sum_terms.1), calls=%async_computation | async-start | bytes 884736 | tf_op jit(solution)/shard_map/all_to_all | solution.py:428
  80.6 3.5 %collective-permute-start.19 = (f32[18,576]{1,0:T(8,128)S(1)}, f32[18,576]{1,0:T(8,128)S(1)}, u32[]{:S(2)}, u32[]{:S(2)}) collective-permute-start(f32[18,576]{1,0:T(8,128)S(1)} %slice_select_fusion), channel_id=1, source_target_pairs={{0,2},{2,0},{1,3},{3,1},{4,6},{6,4},{5,7},{7,5},{8,10},{10,8},{9,1... | collective-permute-start | bytes 124424 | tf_op jit(solution)/shard_map/ppermute | solution.py:330

commit v11 on v10

--- a/solution.py
+++ b/solution.py
@@ -79,12 +79,12 @@
 def pick_kernel(img_feats, txt_feats, img_head, txt_head, mine, give, send, top, bottom, *scratch):
     _, _, high, core, tower = position()
     head, units, into, out = scratch
-    split, step = top.shape[0], 32
-    cuts = range(0, head.shape[0], step)
+    split = top.shape[0]
+    cuts = ((0, split // 2), (split // 2, split // 2), (split, bottom.shape[0]))
     count = len(cuts) + 3
 
     def loads(feats, other, source):
-        moves = [(source.at[pl.ds(i, step)], head.at[pl.ds(i, step)]) for i in cuts]
+        moves = [(source.at[pl.ds(*cut)], head.at[pl.ds(*cut)]) for cut in cuts]
         moves += [(other, units.at[0]), (feats, units.at[1])]
         return [pltpu.make_async_copy(*move, into.at[i]) for i, move in enumerate(moves)]
 
@@ -112,8 +112,8 @@
         choice(img_feats).start()
 
     arrivals = [*loads(img_feats, txt_feats, img_head), choice(img_feats)]
-    targets = [top.at[pl.ds(i, step)] if i < split else bottom.at[pl.ds(i - split, step)] for i in cuts]
-    sources = [head.at[pl.ds(i, step)] for i in cuts] + [units.at[i] for i in range(3)]
+    targets = [top.at[pl.ds(i, n)] if i < split else bottom.at[pl.ds(i - split, n)] for i, n in cuts]
+    sources = [head.at[pl.ds(*cut)] for cut in cuts] + [units.at[i] for i in range(3)]
     targets += [give, mine, send]
     stores = [pltpu.make_async_copy(sources[i], targets[i], out.at[i]) for i in range(count)]
     for arrival, store in zip(arrivals, stores):
@@ -338,8 +338,8 @@
         scratch=(
             pltpu.VMEM((width, depth), BF16),
             pltpu.VMEM((3, rows, depth), BF16),
-            pltpu.SemaphoreType.DMA((width // 32 + 3,)),
-            pltpu.SemaphoreType.DMA((width // 32 + 3,)),
+            pltpu.SemaphoreType.DMA((6,)),
+            pltpu.SemaphoreType.DMA((6,)),
         ),
         anywhere_out=True,
         anywhere=range(4),

time: 85.4 us -> 85.1 us (level)
  transfers between devices with their start and end apart: 21 -> 21, of which waited for: 8 -> 8; matrix products, arithmetic and copies ran while one was open for 1% -> 1% of each run, Pallas kernels for 18% -> 17%
where the time goes in v11:
time: 85.1 us; the launch traced here: 84.5 us
  starting transfers between devices  37.5 us (44%)
  Pallas kernels  22.7 us (27%)
  waiting for transfers between devices  21.5 us (25%)
  other arithmetic  1.91 us (2%)
    pallas_call x11, Pallas kernels, kernel_call(): pl.pallas_call(body, out_shape=shapes, in_specs=[anywhere_spec() if i in...  22.7 us
    ppermute x6, starting transfers between devices, send_pieces(): lax.ppermute(pieces[2 * k + flip], AXES, reduce_pairs(turn, flip))  10.2 us
    ppermute x6, waiting for transfers between devices, send_pieces(): lax.ppermute(pieces[2 * k + flip], AXES, reduce_pairs(turn, flip))  8.08 us
    all_to_all x1, waiting for transfers between devices, local(): lax.all_to_all(sums, AXES, 0, 0, axis_index_groups=REDUCE_GROUPS, tiled=T...  7.39 us
    ppermute x4, starting transfers between devices, swap(): return lax.ppermute(value, AXES, CORES_SWAP)  5.71 us
    ppermute x3, starting transfers between devices, local(): lax.ppermute(second, AXES, ring(turn))  5.31 us
    ppermute x1, starting transfers between devices, local(): far_texts = lax.ppermute(txt_feats, AXES, TEXTS_SWAP)  5.22 us
    ppermute x3, starting transfers between devices, local(): units_a = [lax.ppermute(send, AXES, first_ring(turn)) for turn in turns]  4.38 us
  transfers between devices with their start and end apart: 21, of which 8 were waited for; matrix products, arithmetic and copies ran while one was open for 1% of the time, Pallas kernels for 17%

profile of v11, /device:TPU:1, one launch (start us, length us, event | category | flops | bytes accessed | tf_op | source)
XLA Modules:
  0.0 84.5 jit_solution(3771737588630308836)
XLA Ops:
  0.6 5.2 %collective-permute-start.6 = (bf16[128,1152]{1,0:T(8,128)(2,1)}, bf16[128,1152]{1,0:T(8,128)(2,1)S(1)}, u32[]{:S(2)}, u32[]{:S(2)}) collective-permute-start(bf16[128,1152]{1,0:T(8,128)(2,1)} %txt_feats.1), channel_id=1, source_target_pairs={{2,7},{1,6},{4,3},{7,2},{10,15},{9,14},{12,11},{15,10},{18,23},{17... | collective-permute-start | bytes 884744 | tf_op jit(solution)/shard_map/ppermute | solution.py:332
  5.9 2.5 %pick.1 = (bf16[128,1152]{1,0:T(8,128)(2,1)}, bf16[128,1152]{1,0:T(8,128)(2,1)}, bf16[128,1152]{1,0:T(8,128)(2,1)}, bf16[352,1152]{1,0:T(8,128)(2,1)}, bf16[224,1152]{1,0:T(8,128)(2,1)}) custom-call(bf16[128,1152]{1,0:T(8,128)(2,1)} %img_feats.1, bf16[128,1152]{1,0:T(8,128)(2,1)} %txt_feats.1, bf16[576,1152]{1,0:T(8,128)(2,1)} %bitcast.2, ...), custom_call_target="tpu_custom_call" | custom-call | bytes 5455872 | tf_op jit(solution)/shard_map/pick/pallas_call | solution.py:310
  8.4 0.1 collective-permute-start
  8.5 0.4 collective-permute-start.4
  8.9 2.9 %collective-permute-start.3 = (bf16[128,1152]{1,0:T(8,128)(2,1)}, bf16[128,1152]{1,0:T(8,128)(2,1)S(1)}, u32[]{:S(2)}, u32[]{:S(2)}) collective-permute-start(bf16[128,1152]{1,0:T(8,128)(2,1)} %get-tuple-element.32), channel_id=1, source_target_pairs={{0,64},{3,65},{6,68},{5,69},{8,72},{11,73},{14,76},{13,77},{16,80}... | collective-permute-start | bytes 884744 | tf_op jit(solution)/shard_map/ppermute | solution.py:351
  11.8 0.8 collective-permute-start.2
  12.5 0.7 collective-permute-start.1
  13.2 0.0 collective-permute-done
  13.2 0.9 %collective-permute-start.5 = (bf16[224,1152]{1,0:T(8,128)(2,1)}, bf16[224,1152]{1,0:T(8,128)(2,1)S(1)}, u32[]{:S(2)}, u32[]{:S(2)}) collective-permute-start(bf16[224,1152]{1,0:T(8,128)(2,1)} %get-tuple-element.29.bottom), channel_id=1, source_target_pairs={{0,5},{2,7},{1,4},{3,6},{4,1},{6,3},{5,0},{7,2},{8,13},{10,15},{9,... | collective-permute-start | bytes 1548296 | tf_op jit(solution)/shard_map/ppermute | solution.py:349
  14.1 1.0 %select_select_fusion = (bf16[128,1152]{1,0:T(8,128)(2,1)S(1)}, bf16[128,1152]{1,0:T(8,128)(2,1)S(1)}) fusion(bf16[128,1152]{1,0:T(8,128)(2,1)S(1)} %collective-permute-done.6, bf16[128,1152]{1,0:T(8,128)(2,1)} %get-tuple-element.30, bf16[128,1152]{1,0:T(8,128)(2,1)S(1)} %collective-permute-done, pred[]{:T(512)S(6)} %eq.19, pred[]{:T(512)S(6)} %eq.18, pred[]{:T(512)S(6)} %eq.17), kind=kLoop, calls=%fused_computation.1 | loop fusion | flops 442368 | bytes 1474563 | tf_op jit(solution)/shard_map/jit(_where)/select_n | solution.py:356
  15.2 1.3 %collective-permute-done.3.refs_3_ = bf16[128,1152]{1,0:T(8,128)(2,1)S(1)} collective-permute-done((bf16[128,1152]{1,0:T(8,128)(2,1)}, bf16[128,1152]{1,0:T(8,128)(2,1)S(1)}, u32[]{:S(2)}, u32[]{:S(2)}) %collective-permute-start.3) | collective-permute-done | bytes 294944 | tf_op jit(solution)/shard_map/ppermute | solution.py:351
  16.4 3.0 %collective-permute-start.9 = (bf16[128,1152]{1,0:T(8,128)(2,1)S(1)}, bf16[128,1152]{1,0:T(8,128)(2,1)S(1)}, u32[]{:S(2)}, u32[]{:S(2)}) collective-permute-start(bf16[128,1152]{1,0:T(8,128)(2,1)S(1)} %get-tuple-element.54.refs_0_.refs_3_), channel_id=1, source_target_pairs={{0,64},{2,18},{1,65},{3,19},{4,68},{6,22},{5,69},{7,23},{8,72},{10... | collective-permute-start | bytes 884744 | tf_op jit(solution)/shard_map/ppermute | solution.py:358
  19.4 0.6 collective-permute-done.2.refs_2_
  20.0 2.3 %collective-permute-start.8 = (bf16[128,1152]{1,0:T(8,128)(2,1)S(1)}, bf16[128,1152]{1,0:T(8,128)(2,1)S(1)}, u32[]{:S(2)}, u32[]{:S(2)}) collective-permute-start(bf16[128,1152]{1,0:T(8,128)(2,1)S(1)} %get-tuple-element.54.refs_0_.refs_3_), channel_id=1, source_target_pairs={{0,96},{2,26},{1,97},{3,27},{4,100},{6,30},{5,101},{7,31},{8,104},... | collective-permute-start | bytes 884744 | tf_op jit(solution)/shard_map/ppermute | solution.py:358
  22.3 0.0 collective-permute-done.1.refs_1_
  22.4 2.4 %own_half.1 = (bf16[4,2,144,512]{3,2,1,0:T(8,128)(2,1)S(1)}, bf16[1152,576]{1,0:T(8,128)(2,1)S(1)}, bf16[512,576]{1,0:T(8,128)(2,1)S(1)}) custom-call(bf16[352,1152]{1,0:T(8,128)(2,1)S(1)} %copy-done, bf16[224,1152]{1,0:T(8,128)(2,1)S(1)} %copy-done.1, bf16[128,1152]{1,0:T(8,128)(2,1)S(1)} %get-tuple-element.55.refs_0_, ...), custom_call_target="tpu_custom_call" | custom-call | flops 679477248 | bytes 5603328 | tf_op jit(solution)/shard_map/own_half/pallas_call | solution.py:310
  24.7 1.3 %collective-permute-done.5.far_bottom = bf16[224,1152]{1,0:T(8,128)(2,1)S(1)} collective-permute-done((bf16[224,1152]{1,0:T(8,128)(2,1)}, bf16[224,1152]{1,0:T(8,128)(2,1)S(1)}, u32[]{:S(2)}, u32[]{:S(2)}) %collective-permute-start.5) | collective-permute-done | bytes 516128 | tf_op jit(solution)/shard_map/ppermute | solution.py:349
  26.0 2.0 %collective-permute-done.4.far_top = bf16[352,1152]{1,0:T(8,128)(2,1)S(1)} collective-permute-done((bf16[352,1152]{1,0:T(8,128)(2,1)}, bf16[352,1152]{1,0:T(8,128)(2,1)S(1)}, u32[]{:S(2)}, u32[]{:S(2)}) %collective-permute-start.4) | collective-permute-done | bytes 811040 | tf_op jit(solution)/shard_map/ppermute | solution.py:348
  28.0 1.8 %embed_first.1 = (bf16[512,1152]{1,0:T(8,128)(2,1)S(1)}, bf16[512,1152]{1,0:T(8,128)(2,1)S(1)}, bf16[1152,1152]{1,0:T(8,128)(2,1)S(1)}) custom-call(bf16[1152,576]{1,0:T(8,128)(2,1)S(1)} %get-tuple-element.34.turned, bf16[512,576]{1,0:T(8,128)(2,1)S(1)} %get-tuple-element.35.own_raw, bf16[352,1152]{1,0:T(8,128)(2,1)S(1)} %collective-permute-done.4.far_top, ...), custom_call_target="tpu_custom_call" | custom-call | flops 679477248 | bytes 9437184 | tf_op jit(solution)/shard_map/embed_first/pallas_call | solution.py:310
  29.8 1.3 %collective-permute-start.10 = (bf16[512,1152]{1,0:T(8,128)(2,1)S(1)}, bf16[512,1152]{1,0:T(8,128)(2,1)S(1)}, u32[]{:S(2)}, u32[]{:S(2)}) collective-permute-start(bf16[512,1152]{1,0:T(8,128)(2,1)S(1)} %get-tuple-element.36.refs_0_.emb_a), channel_id=1, source_target_pairs={{0,2},{2,0},{1,3},{3,1},{4,6},{6,4},{5,7},{7,5},{8,10},{10,8},{9,1... | collective-permute-start | bytes 3538952 | tf_op jit(solution)/shard_map/ppermute | solution.py:330
  31.1 0.0 collective-permute-done.9.refs_3_.refs_6_
  31.1 0.0 collective-permute-done.8.refs_2_.refs_5_
  31.1 0.0 collective-permute-done.7.refs_1_.refs_4_
  31.1 2.1 %embed_second.1 = (bf16[512,1152]{1,0:T(8,128)(2,1)S(1)}, bf16[512,1152]{1,0:T(8,128)(2,1)S(1)}) custom-call(bf16[1152,1152]{1,0:T(8,128)(2,1)S(1)} %get-tuple-element.37.head_ref, bf16[128,1152]{1,0:T(8,128)(2,1)S(1)} %get-tuple-element.54.refs_0_.refs_3_, bf16[128,1152]{1,0:T(8,128)(2,1)S(1)} %collective-permute-done.7.refs_1_.refs_4_, ...), custom_call_target="tpu_custom_call" | custom-call | flops 1358954496 | bytes 6193152 | tf_op jit(solution)/shard_map/embed_second/pallas_call | solution.py:310
  33.3 1.7 %collective-permute-start.11 = (bf16[512,1152]{1,0:T(8,128)(2,1)S(1)}, bf16[512,1152]{1,0:T(8,128)(2,1)S(1)}, u32[]{:S(2)}, u32[]{:S(2)}) collective-permute-start(bf16[512,1152]{1,0:T(8,128)(2,1)S(1)} %get-tuple-element.38.refs_1_.emb_b), channel_id=1, source_target_pairs={{0,2},{2,0},{1,3},{3,1},{4,6},{6,4},{5,7},{7,5},{8,10},{10,8},{9,1... | collective-permute-start | bytes 3538952 | tf_op jit(solution)/shard_map/ppermute | solution.py:330
  35.0 2.7 %score_first.1 = (bf16[512,512]{1,0:T(8,128)(2,1)S(1)}, bf16[512,512]{1,0:T(8,128)(2,1)S(1)}, bf16[4,2,144,512]{3,2,1,0:T(8,128)(2,1)S(1)}) custom-call(bf16[512,1152]{1,0:T(8,128)(2,1)S(1)} %get-tuple-element.36.refs_0_.emb_a, bf16[512,1152]{1,0:T(8,128)(2,1)S(1)} %get-tuple-element.38.refs_1_.emb_b, ...), custom_call_target="tpu_custom_call" | custom-call | flops 1207959552 | bytes 6946816 | tf_op jit(solution)/shard_map/score_first/pallas_call | solution.py:310
  37.7 6.9 %score_second.1 = (bf16[512,1152]{1,0:T(8,128)(2,1)S(1)}, bf16[512,1152]{1,0:T(8,128)(2,1)S(1)}, bf16[144,1152]{1,0:T(8,128)(2,1)S(1)}, bf16[144,1152]{1,0:T(8,128)(2,1)S(1)}) custom-call(bf16[512,1152]{1,0:T(8,128)(2,1)S(1)} %get-tuple-element.36.refs_0_.emb_a, bf16[512,1152]{1,0:T(8,128)(2,1)S(1)} %get-tuple-element.38.refs_1_.emb_b, ...), custom_call_target="tpu_custom_call" | custom-call | flops 4303355904 | bytes 13508608 | tf_op jit(solution)/shard_map/score_second/pallas_call | solution.py:310
  44.6 3.6 %collective-permute-start.12 = (bf16[144,1152]{1,0:T(8,128)(2,1)S(1)}, bf16[144,1152]{1,0:T(8,128)(2,1)S(1)}, u32[]{:S(2)}, u32[]{:S(2)}) collective-permute-start(bf16[144,1152]{1,0:T(8,128)(2,1)S(1)} %get-tuple-element.47), channel_id=1, source_target_pairs={{0,65},{2,23},{1,64},{3,22},{4,69},{6,19},{5,68},{7,18},{8,73},{10... | collective-permute-start | bytes 995336 | tf_op jit(solution)/shard_map/ppermute | solution.py:415
  48.2 0.1 collective-permute-start.13
  48.2 1.1 %term_down.1 = (bf16[144,1152]{1,0:T(8,128)(2,1)S(1)}, bf16[144,1152]{1,0:T(8,128)(2,1)S(1)}) custom-call(bf16[4,2,144,512]{3,2,1,0:T(8,128)(2,1)S(1)} %get-tuple-element.33.flip_a.refs_0_, bf16[4,2,144,512]{3,2,1,0:T(8,128)(2,1)S(1)} %get-tuple-element.39.flip_b.refs_1_, bf16[512,1152]{1,0:T(8,128)(2,1)S(1)} %get-tuple-element.44.refs_2_, ...), custom_call_target="tpu_custom_call" | custom-call | flops 679477248 | bytes 5382144 | tf_op jit(solution)/shard_map/term_down/pallas_call | solution.py:310
  49.3 4.3 %collective-permute-start.16 = (bf16[144,1152]{1,0:T(8,128)(2,1)S(1)}, bf16[144,1152]{1,0:T(8,128)(2,1)S(1)}, u32[]{:S(2)}, u32[]{:S(2)}) collective-permute-start(bf16[144,1152]{1,0:T(8,128)(2,1)S(1)} %get-tuple-element.51), channel_id=1, source_target_pairs={{0,97},{2,31},{1,96},{3,30},{4,101},{6,27},{5,100},{7,26},{8,105},... | collective-permute-start | bytes 995336 | tf_op jit(solution)/shard_map/ppermute | solution.py:415
  53.6 0.5 collective-permute-start.17
  54.1 1.1 %term_up.1 = (bf16[144,1152]{1,0:T(8,128)(2,1)S(1)}, bf16[144,1152]{1,0:T(8,128)(2,1)S(1)}) custom-call(bf16[4,2,144,512]{3,2,1,0:T(8,128)(2,1)S(1)} %get-tuple-element.33.flip_a.refs_0_, bf16[4,2,144,512]{3,2,1,0:T(8,128)(2,1)S(1)} %get-tuple-element.39.flip_b.refs_1_, bf16[512,1152]{1,0:T(8,128)(2,1)S(1)} %get-tuple-element.44.refs_2_, ...), custom_call_target="tpu_custom_call" | custom-call | flops 679477248 | bytes 5382144 | tf_op jit(solution)/shard_map/term_up/pallas_call | solution.py:310
  55.1 1.7 %collective-permute-start.14 = (bf16[144,1152]{1,0:T(8,128)(2,1)S(1)}, bf16[144,1152]{1,0:T(8,128)(2,1)S(1)}, u32[]{:S(2)}, u32[]{:S(2)}) collective-permute-start(bf16[144,1152]{1,0:T(8,128)(2,1)S(1)} %get-tuple-element.49), channel_id=1, source_target_pairs={{0,33},{2,15},{1,32},{3,14},{4,37},{6,11},{5,36},{7,10},{8,41},{10... | collective-permute-start | bytes 995336 | tf_op jit(solution)/shard_map/ppermute | solution.py:415
  56.8 1.1 %term_own.1 = (bf16[144,1152]{1,0:T(8,128)(2,1)S(1)}, bf16[144,1152]{1,0:T(8,128)(2,1)S(1)}) custom-call(bf16[4,2,144,512]{3,2,1,0:T(8,128)(2,1)S(1)} %get-tuple-element.33.flip_a.refs_0_, bf16[4,2,144,512]{3,2,1,0:T(8,128)(2,1)S(1)} %get-tuple-element.39.flip_b.refs_1_, bf16[512,1152]{1,0:T(8,128)(2,1)S(1)} %get-tuple-element.44.refs_2_, ...), custom_call_target="tpu_custom_call" | custom-call | flops 679477248 | bytes 5382144 | tf_op jit(solution)/shard_map/term_own/pallas_call | solution.py:310
  57.9 0.1 collective-permute-start.15
  58.0 1.9 %collective-permute-start.18 = (bf16[144,1152]{1,0:T(8,128)(2,1)S(1)}, bf16[144,1152]{1,0:T(8,128)(2,1)S(1)}, u32[]{:S(2)}, u32[]{:S(2)}) collective-permute-start(bf16[144,1152]{1,0:T(8,128)(2,1)S(1)} %get-tuple-element.53), channel_id=1, source_target_pairs={{0,1},{2,7},{1,0},{3,6},{4,5},{6,3},{5,4},{7,2},{8,9},{10,15},{9,8... | collective-permute-start | bytes 995336 | tf_op jit(solution)/shard_map/ppermute | solution.py:423
  59.9 0.1 add_far.1.refs_0_
  60.0 5.8 %collective-permute-done.17.refs_4_ = bf16[144,1152]{1,0:T(8,128)(2,1)S(1)} collective-permute-done((bf16[144,1152]{1,0:T(8,128)(2,1)S(1)}, bf16[144,1152]{1,0:T(8,128)(2,1)S(1)}, u32[]{:S(2)}, u32[]{:S(2)}) %collective-permute-start.17) | collective-permute-done | bytes 331808 | tf_op jit(solution)/shard_map/ppermute | solution.py:415
  65.8 2.3 %collective-permute-done.15.refs_2_ = bf16[144,1152]{1,0:T(8,128)(2,1)S(1)} collective-permute-done((bf16[144,1152]{1,0:T(8,128)(2,1)S(1)}, bf16[144,1152]{1,0:T(8,128)(2,1)S(1)}, u32[]{:S(2)}, u32[]{:S(2)}) %collective-permute-start.15) | collective-permute-done | bytes 331808 | tf_op jit(solution)/shard_map/ppermute | solution.py:415
  68.1 1.1 %sum_terms.1 = bf16[8,18,1152]{2,1,0:T(8,128)(2,1)} custom-call(f32[144,1152]{1,0:T(8,128)S(1)} %add_far.1.refs_0_, bf16[144,1152]{1,0:T(8,128)(2,1)S(1)} %collective-permute-done.14.refs_1_, bf16[144,1152]{1,0:T(8,128)(2,1)S(1)} %collective-permute-done.15.refs_2_, bf16[144,1152]{1,0:T(8,128)(2,1)S(1)} %collective-permute-done.16.refs_3_, ...), custom_call_target="tpu_custom_call" | custom-call | bytes 2654208 | tf_op jit(solution)/shard_map/sum_terms/pallas_call | solution.py:310
  69.2 3.6 %all-to-all-start = ((bf16[8,18,1152]{2,1,0:T(8,128)(2,1)}), bf16[8,18,1152]{2,1,0:T(8,128)(2,1)S(1)}, u32[]{:S(2)}, u32[]{:S(2)}) async-start(bf16[8,18,1152]{2,1,0:T(8,128)(2,1)} %sum_terms.1), calls=%async_computation | async-start | bytes 884736 | tf_op jit(solution)/shard_map/all_to_all | solution.py:428
  72.7 7.4 %all-to-all-done = bf16[8,18,1152]{2,1,0:T(8,128)(2,1)S(1)} async-done(((bf16[8,18,1152]{2,1,0:T(8,128)(2,1)}), bf16[8,18,1152]{2,1,0:T(8,128)(2,1)S(1)}, u32[]{:S(2)}, u32[]{:S(2)}) %all-to-all-start) | async-done | bytes 331808 | tf_op jit(solution)/shard_map/all_to_all | solution.py:428
  80.1 0.1 convert_reduce_fusion
  80.2 0.1 slice_select_fusion
  80.3 2.6 %collective-permute-start.19 = (f32[18,576]{1,0:T(8,128)S(1)}, f32[18,576]{1,0:T(8,128)S(1)}, u32[]{:S(2)}, u32[]{:S(2)}) collective-permute-start(f32[18,576]{1,0:T(8,128)S(1)} %slice_select_fusion), channel_id=1, source_target_pairs={{0,2},{2,0},{1,3},{3,1},{4,6},{6,4},{5,7},{7,5},{8,10},{10,8},{9,1... | collective-permute-start | bytes 124424 | tf_op jit(solution)/shard_map/ppermute | solution.py:330
  82.8 0.9 %collective-permute-done.19 = f32[18,576]{1,0:T(8,128)S(1)} collective-permute-done((f32[18,576]{1,0:T(8,128)S(1)}, f32[18,576]{1,0:T(8,128)S(1)}, u32[]{:S(2)}, u32[]{:S(2)}) %collective-permute-start.19) | collective-permute-done | bytes 41504 | tf_op jit(solution)/shard_map/ppermute | solution.py:330
  83.7 0.7 broadcast_select_fusion.1
  (13 shorter events, 0.0 us)
Async XLA Ops:
  0.6 11.9 %collective-permute-start.6 = (bf16[128,1152]{1,0:T(8,128)(2,1)}, bf16[128,1152]{1,0:T(8,128)(2,1)S(1)}, u32[]{:S(2)}, u32[]{:S(2)}) collective-permute-start(bf16[128,1152]{1,0:T(8,128)(2,1)} %txt_feats.1), channel_id=1, source_target_pairs={{2,7},{1,6},{4,3},{7,2},{10,15},{9,14},{12,11},{15,10},{18,23},{17... | collective-permute-start | bytes 884744 | tf_op jit(solution)/shard_map/ppermute | solution.py:332
  8.4 14.0 %copy-start = (bf16[352,1152]{1,0:T(8,128)(2,1)S(1)}, bf16[352,1152]{1,0:T(8,128)(2,1)}, u32[]{:S(2)}) copy-start(bf16[352,1152]{1,0:T(8,128)(2,1)} %get-tuple-element.28.top) | copy-start | bytes 2433028
  8.4 13.9 %copy-start.1 = (bf16[224,1152]{1,0:T(8,128)(2,1)S(1)}, bf16[224,1152]{1,0:T(8,128)(2,1)}, u32[]{:S(2)}) copy-start(bf16[224,1152]{1,0:T(8,128)(2,1)} %get-tuple-element.29.bottom) | copy-start | bytes 1548292
  8.4 4.8 %collective-permute-start = (bf16[128,1152]{1,0:T(8,128)(2,1)}, bf16[128,1152]{1,0:T(8,128)(2,1)S(1)}, u32[]{:S(2)}, u32[]{:S(2)}) collective-permute-start(bf16[128,1152]{1,0:T(8,128)(2,1)} %get-tuple-element.31), channel_id=1, source_target_pairs={{0,2},{2,0},{1,3},{3,1},{4,6},{6,4},{5,7},{7,5},{8,10},{10,8},{9,1... | collective-permute-start | bytes 884744 | tf_op jit(solution)/shard_map/ppermute | solution.py:330
  8.5 19.5 %collective-permute-start.4 = (bf16[352,1152]{1,0:T(8,128)(2,1)}, bf16[352,1152]{1,0:T(8,128)(2,1)S(1)}, u32[]{:S(2)}, u32[]{:S(2)}) collective-permute-start(bf16[352,1152]{1,0:T(8,128)(2,1)} %get-tuple-element.28.top), channel_id=1, source_target_pairs={{0,1},{2,3},{1,0},{3,2},{4,5},{6,7},{5,4},{7,6},{8,9},{10,11},{9,8... | collective-permute-start | bytes 2433032 | tf_op jit(solution)/shard_map/ppermute | solution.py:348
  8.9 7.6 %collective-permute-start.3 = (bf16[128,1152]{1,0:T(8,128)(2,1)}, bf16[128,1152]{1,0:T(8,128)(2,1)S(1)}, u32[]{:S(2)}, u32[]{:S(2)}) collective-permute-start(bf16[128,1152]{1,0:T(8,128)(2,1)} %get-tuple-element.32), channel_id=1, source_target_pairs={{0,64},{3,65},{6,68},{5,69},{8,72},{11,73},{14,76},{13,77},{16,80}... | collective-permute-start | bytes 884744 | tf_op jit(solution)/shard_map/ppermute | solution.py:351
  11.8 8.2 %collective-permute-start.2 = (bf16[128,1152]{1,0:T(8,128)(2,1)}, bf16[128,1152]{1,0:T(8,128)(2,1)S(1)}, u32[]{:S(2)}, u32[]{:S(2)}) collective-permute-start(bf16[128,1152]{1,0:T(8,128)(2,1)} %get-tuple-element.32), channel_id=1, source_target_pairs={{0,96},{3,97},{6,100},{5,101},{8,104},{11,105},{14,108},{13,109},{... | collective-permute-start | bytes 884744 | tf_op jit(solution)/shard_map/ppermute | solution.py:351
  12.5 9.8 %collective-permute-start.1 = (bf16[128,1152]{1,0:T(8,128)(2,1)}, bf16[128,1152]{1,0:T(8,128)(2,1)S(1)}, u32[]{:S(2)}, u32[]{:S(2)}) collective-permute-start(bf16[128,1152]{1,0:T(8,128)(2,1)} %get-tuple-element.32), channel_id=1, source_target_pairs={{0,32},{3,33},{6,36},{5,37},{8,40},{11,41},{14,44},{13,45},{16,48}... | collective-permute-start | bytes 884744 | tf_op jit(solution)/shard_map/ppermute | solution.py:351
  13.2 12.8 %collective-permute-start.5 = (bf16[224,1152]{1,0:T(8,128)(2,1)}, bf16[224,1152]{1,0:T(8,128)(2,1)S(1)}, u32[]{:S(2)}, u32[]{:S(2)}) collective-permute-start(bf16[224,1152]{1,0:T(8,128)(2,1)} %get-tuple-element.29.bottom), channel_id=1, source_target_pairs={{0,5},{2,7},{1,4},{3,6},{4,1},{6,3},{5,0},{7,2},{8,13},{10,15},{9,... | collective-permute-start | bytes 1548296 | tf_op jit(solution)/shard_map/ppermute | solution.py:349
  16.4 14.7 %collective-permute-start.9 = (bf16[128,1152]{1,0:T(8,128)(2,1)S(1)}, bf16[128,1152]{1,0:T(8,128)(2,1)S(1)}, u32[]{:S(2)}, u32[]{:S(2)}) collective-permute-start(bf16[128,1152]{1,0:T(8,128)(2,1)S(1)} %get-tuple-element.54.refs_0_.refs_3_), channel_id=1, source_target_pairs={{0,64},{2,18},{1,65},{3,19},{4,68},{6,22},{5,69},{7,23},{8,72},{10... | collective-permute-start | bytes 884744 | tf_op jit(solution)/shard_map/ppermute | solution.py:358
  20.0 11.1 %collective-permute-start.8 = (bf16[128,1152]{1,0:T(8,128)(2,1)S(1)}, bf16[128,1152]{1,0:T(8,128)(2,1)S(1)}, u32[]{:S(2)}, u32[]{:S(2)}) collective-permute-start(bf16[128,1152]{1,0:T(8,128)(2,1)S(1)} %get-tuple-element.54.refs_0_.refs_3_), channel_id=1, source_target_pairs={{0,96},{2,26},{1,97},{3,27},{4,100},{6,30},{5,101},{7,31},{8,104},... | collective-permute-start | bytes 884744 | tf_op jit(solution)/shard_map/ppermute | solution.py:358
  22.3 8.8 %collective-permute-start.7 = (bf16[128,1152]{1,0:T(8,128)(2,1)S(1)}, bf16[128,1152]{1,0:T(8,128)(2,1)S(1)}, u32[]{:S(2)}, u32[]{:S(2)}) collective-permute-start(bf16[128,1152]{1,0:T(8,128)(2,1)S(1)} %get-tuple-element.54.refs_0_.refs_3_), channel_id=1, source_target_pairs={{0,32},{2,10},{1,33},{3,11},{4,36},{6,14},{5,37},{7,15},{8,40},{10... | collective-permute-start | bytes 884744 | tf_op jit(solution)/shard_map/ppermute | solution.py:358
  29.8 5.2 %collective-permute-start.10 = (bf16[512,1152]{1,0:T(8,128)(2,1)S(1)}, bf16[512,1152]{1,0:T(8,128)(2,1)S(1)}, u32[]{:S(2)}, u32[]{:S(2)}) collective-permute-start(bf16[512,1152]{1,0:T(8,128)(2,1)S(1)} %get-tuple-element.36.refs_0_.emb_a), channel_id=1, source_target_pairs={{0,2},{2,0},{1,3},{3,1},{4,6},{6,4},{5,7},{7,5},{8,10},{10,8},{9,1... | collective-permute-start | bytes 3538952 | tf_op jit(solution)/shard_map/ppermute | solution.py:330
  33.3 4.4 %collective-permute-start.11 = (bf16[512,1152]{1,0:T(8,128)(2,1)S(1)}, bf16[512,1152]{1,0:T(8,128)(2,1)S(1)}, u32[]{:S(2)}, u32[]{:S(2)}) collective-permute-start(bf16[512,1152]{1,0:T(8,128)(2,1)S(1)} %get-tuple-element.38.refs_1_.emb_b), channel_id=1, source_target_pairs={{0,2},{2,0},{1,3},{3,1},{4,6},{6,4},{5,7},{7,5},{8,10},{10,8},{9,1... | collective-permute-start | bytes 3538952 | tf_op jit(solution)/shard_map/ppermute | solution.py:330
  44.6 13.3 %collective-permute-start.12 = (bf16[144,1152]{1,0:T(8,128)(2,1)S(1)}, bf16[144,1152]{1,0:T(8,128)(2,1)S(1)}, u32[]{:S(2)}, u32[]{:S(2)}) collective-permute-start(bf16[144,1152]{1,0:T(8,128)(2,1)S(1)} %get-tuple-element.47), channel_id=1, source_target_pairs={{0,65},{2,23},{1,64},{3,22},{4,69},{6,19},{5,68},{7,18},{8,73},{10... | collective-permute-start | bytes 995336 | tf_op jit(solution)/shard_map/ppermute | solution.py:415
  48.2 9.8 %collective-permute-start.13 = (bf16[144,1152]{1,0:T(8,128)(2,1)S(1)}, bf16[144,1152]{1,0:T(8,128)(2,1)S(1)}, u32[]{:S(2)}, u32[]{:S(2)}) collective-permute-start(bf16[144,1152]{1,0:T(8,128)(2,1)S(1)} %get-tuple-element.48), channel_id=1, source_target_pairs={{0,64},{2,18},{1,65},{3,19},{4,68},{6,22},{5,69},{7,23},{8,72},{10... | collective-permute-start | bytes 995336 | tf_op jit(solution)/shard_map/ppermute | solution.py:415
  49.3 10.7 %collective-permute-start.16 = (bf16[144,1152]{1,0:T(8,128)(2,1)S(1)}, bf16[144,1152]{1,0:T(8,128)(2,1)S(1)}, u32[]{:S(2)}, u32[]{:S(2)}) collective-permute-start(bf16[144,1152]{1,0:T(8,128)(2,1)S(1)} %get-tuple-element.51), channel_id=1, source_target_pairs={{0,97},{2,31},{1,96},{3,30},{4,101},{6,27},{5,100},{7,26},{8,105},... | collective-permute-start | bytes 995336 | tf_op jit(solution)/shard_map/ppermute | solution.py:415
  53.6 12.1 %collective-permute-start.17 = (bf16[144,1152]{1,0:T(8,128)(2,1)S(1)}, bf16[144,1152]{1,0:T(8,128)(2,1)S(1)}, u32[]{:S(2)}, u32[]{:S(2)}) collective-permute-start(bf16[144,1152]{1,0:T(8,128)(2,1)S(1)} %get-tuple-element.52), channel_id=1, source_target_pairs={{0,96},{2,26},{1,97},{3,27},{4,100},{6,30},{5,101},{7,31},{8,104},... | collective-permute-start | bytes 995336 | tf_op jit(solution)/shard_map/ppermute | solution.py:415
  55.1 10.6 %collective-permute-start.14 = (bf16[144,1152]{1,0:T(8,128)(2,1)S(1)}, bf16[144,1152]{1,0:T(8,128)(2,1)S(1)}, u32[]{:S(2)}, u32[]{:S(2)}) collective-permute-start(bf16[144,1152]{1,0:T(8,128)(2,1)S(1)} %get-tuple-element.49), channel_id=1, source_target_pairs={{0,33},{2,15},{1,32},{3,14},{4,37},{6,11},{5,36},{7,10},{8,41},{10... | collective-permute-start | bytes 995336 | tf_op jit(solution)/shard_map/ppermute | solution.py:415
  57.9 10.2 %collective-permute-start.15 = (bf16[144,1152]{1,0:T(8,128)(2,1)S(1)}, bf16[144,1152]{1,0:T(8,128)(2,1)S(1)}, u32[]{:S(2)}, u32[]{:S(2)}) collective-permute-start(bf16[144,1152]{1,0:T(8,128)(2,1)S(1)} %get-tuple-element.50), channel_id=1, source_target_pairs={{0,32},{2,10},{1,33},{3,11},{4,36},{6,14},{5,37},{7,15},{8,40},{10... | collective-permute-start | bytes 995336 | tf_op jit(solution)/shard_map/ppermute | solution.py:415
  58.0 10.1 %collective-permute-start.18 = (bf16[144,1152]{1,0:T(8,128)(2,1)S(1)}, bf16[144,1152]{1,0:T(8,128)(2,1)S(1)}, u32[]{:S(2)}, u32[]{:S(2)}) collective-permute-start(bf16[144,1152]{1,0:T(8,128)(2,1)S(1)} %get-tuple-element.53), channel_id=1, source_target_pairs={{0,1},{2,7},{1,0},{3,6},{4,5},{6,3},{5,4},{7,2},{8,9},{10,15},{9,8... | collective-permute-start | bytes 995336 | tf_op jit(solution)/shard_map/ppermute | solution.py:423
  69.2 10.9 %all-to-all-start = ((bf16[8,18,1152]{2,1,0:T(8,128)(2,1)}), bf16[8,18,1152]{2,1,0:T(8,128)(2,1)S(1)}, u32[]{:S(2)}, u32[]{:S(2)}) async-start(bf16[8,18,1152]{2,1,0:T(8,128)(2,1)} %sum_terms.1), calls=%async_computation | async-start | bytes 884736 | tf_op jit(solution)/shard_map/all_to_all | solution.py:428
  80.3 3.5 %collective-permute-start.19 = (f32[18,576]{1,0:T(8,128)S(1)}, f32[18,576]{1,0:T(8,128)S(1)}, u32[]{:S(2)}, u32[]{:S(2)}) collective-permute-start(f32[18,576]{1,0:T(8,128)S(1)} %slice_select_fusion), channel_id=1, source_target_pairs={{0,2},{2,0},{1,3},{3,1},{4,6},{6,4},{5,7},{7,5},{8,10},{10,8},{9,1... | collective-permute-start | bytes 124424 | tf_op jit(solution)/shard_map/ppermute | solution.py:330

commit v12 on v11

--- a/solution.py
+++ b/solution.py
@@ -76,29 +76,29 @@
     return pl.BlockSpec(memory_space=pl.ANY)
 
 
-def pick_kernel(img_feats, txt_feats, img_head, txt_head, mine, give, send, top, bottom, *scratch):
+def pick_kernel(img_feats, txt_feats, img_head, txt_head, give, send, top, bottom, *scratch):
     _, _, high, core, tower = position()
     head, units, into, out = scratch
     split = top.shape[0]
     cuts = ((0, split // 2), (split // 2, split // 2), (split, bottom.shape[0]))
-    count = len(cuts) + 3
-
-    def loads(feats, other, source):
+    count = len(cuts) + 2
+
+    def loads(other, source):
         moves = [(source.at[pl.ds(*cut)], head.at[pl.ds(*cut)]) for cut in cuts]
-        moves += [(other, units.at[0]), (feats, units.at[1])]
+        moves += [(other, units.at[0])]
         return [pltpu.make_async_copy(*move, into.at[i]) for i, move in enumerate(moves)]
 
     def choice(feats):
-        return pltpu.make_async_copy(feats, units.at[2], into.at[count - 1])
+        return pltpu.make_async_copy(feats, units.at[1], into.at[count - 1])
 
     @pl.when(core == 0)
     def _():
-        for copy in loads(img_feats, txt_feats, img_head):
+        for copy in loads(txt_feats, img_head):
             copy.start()
 
     @pl.when(core == 1)
     def _():
-        for copy in loads(txt_feats, img_feats, txt_head):
+        for copy in loads(img_feats, txt_head):
             copy.start()
 
     holds_block = (high == tower).astype(jnp.int32) == core
@@ -111,10 +111,10 @@
     def _():
         choice(img_feats).start()
 
-    arrivals = [*loads(img_feats, txt_feats, img_head), choice(img_feats)]
+    arrivals = [*loads(txt_feats, img_head), choice(img_feats)]
     targets = [top.at[pl.ds(i, n)] if i < split else bottom.at[pl.ds(i - split, n)] for i, n in cuts]
-    sources = [head.at[pl.ds(*cut)] for cut in cuts] + [units.at[i] for i in range(3)]
-    targets += [give, mine, send]
+    sources = [head.at[pl.ds(*cut)] for cut in cuts] + [units.at[i] for i in range(2)]
+    targets += [give, send]
     stores = [pltpu.make_async_copy(sources[i], targets[i], out.at[i]) for i in range(count)]
     for arrival, store in zip(arrivals, stores):
         arrival.wait()
@@ -330,16 +330,16 @@
         return lax.ppermute(value, AXES, CORES_SWAP)
 
     far_texts = lax.ppermute(txt_feats, AXES, TEXTS_SWAP)
-    mine, give, send, top, bottom = kernel_call(
+    give, send, top, bottom = kernel_call(
         pick_kernel,
         "pick",
-        [((rows, depth), BF16)] * 3 + [((22 * depth // 72, depth), BF16), ((14 * depth // 72, depth), BF16)],
+        [((rows, depth), BF16)] * 2 + [((22 * depth // 72, depth), BF16), ((14 * depth // 72, depth), BF16)],
         (img_feats, txt_feats, img_proj.T, txt_proj.T),
         scratch=(
             pltpu.VMEM((width, depth), BF16),
-            pltpu.VMEM((3, rows, depth), BF16),
-            pltpu.SemaphoreType.DMA((6,)),
-            pltpu.SemaphoreType.DMA((6,)),
+            pltpu.VMEM((2, rows, depth), BF16),
+            pltpu.SemaphoreType.DMA((5,)),
+            pltpu.SemaphoreType.DMA((5,)),
         ),
         anywhere_out=True,
         anywhere=range(4),
@@ -350,6 +350,7 @@
     turns = (1, 3, 2)
     units_a = [lax.ppermute(send, AXES, first_ring(turn)) for turn in turns]
     other = swap(give)
+    mine = jnp.where(position()[3] == 0, img_feats, txt_feats)
     _, _, high, core, tower = position()
     block = (high == tower).astype(jnp.int32)
     first = jnp.where(block == 1, mine, other)

time: 85.1 us -> 84.8 us (level)
  blocking collectives: 0 us -> 10.1 us
  waiting for transfers between devices: 21.5 us -> 13.4 us
  starting transfers between devices: 37.5 us -> 36 us
    all_to_all x0 -> x1, blocking collectives: none -> 10.1 us  [local(): lax.all_to_all(sums, AXES, 0, 0, axis_index_groups=REDUCE_GROUPS, tiled=T...]
    all_to_all x1 -> x0, waiting for transfers between devices: 7.39 us -> none  [local(): lax.all_to_all(sums, AXES, 0, 0, axis_index_groups=REDUCE_GROUPS, tiled=T...]
    all_to_all x1 -> x0, starting transfers between devices: 3.55 us -> none  [local(): lax.all_to_all(sums, AXES, 0, 0, axis_index_groups=REDUCE_GROUPS, tiled=T...]
    ppermute x4, starting transfers between devices: 5.71 us -> 7.15 us  [swap(): return lax.ppermute(value, AXES, CORES_SWAP)]
  transfers between devices with their start and end apart: 21 -> 20, of which waited for: 8 -> 7; matrix products, arithmetic and copies ran while one was open for 1% -> 1% of each run, Pallas kernels for 17% -> 17%
where the time goes in v12:
time: 84.8 us; the launch traced here: 84.3 us
  starting transfers between devices  36 us (42%)
  Pallas kernels  21.9 us (26%)
  waiting for transfers between devices  13.4 us (16%)
  blocking collectives  10.1 us (12%)
  other arithmetic  2.02 us (2%)
    pallas_call x11, Pallas kernels, kernel_call(): pl.pallas_call(body, out_shape=shapes, in_specs=[anywhere_spec() if i in...  21.9 us
    ppermute x6, starting transfers between devices, send_pieces(): lax.ppermute(pieces[2 * k + flip], AXES, reduce_pairs(turn, flip))  10.1 us
    all_to_all x1, blocking collectives, local(): lax.all_to_all(sums, AXES, 0, 0, axis_index_groups=REDUCE_GROUPS, tiled=T...  10.1 us
    ppermute x6, waiting for transfers between devices, send_pieces(): lax.ppermute(pieces[2 * k + flip], AXES, reduce_pairs(turn, flip))  8.08 us
    ppermute x4, starting transfers between devices, swap(): return lax.ppermute(value, AXES, CORES_SWAP)  7.15 us
    ppermute x3, starting transfers between devices, local(): lax.ppermute(second, AXES, ring(turn))  5.31 us
    ppermute x1, starting transfers between devices, local(): far_texts = lax.ppermute(txt_feats, AXES, TEXTS_SWAP)  5.22 us
    ppermute x3, starting transfers between devices, local(): units_a = [lax.ppermute(send, AXES, first_ring(turn)) for turn in turns]  4.38 us
  transfers between devices with their start and end apart: 20, of which 7 were waited for; matrix products, arithmetic and copies ran while one was open for 1% of the time, Pallas kernels for 17%

profile of v12, /device:TPU:1, one launch (start us, length us, event | category | flops | bytes accessed | tf_op | source)
XLA Modules:
  0.0 84.3 jit_solution(11110965387584752064)
XLA Ops:
  0.6 5.2 %collective-permute-start.6 = (bf16[128,1152]{1,0:T(8,128)(2,1)}, bf16[128,1152]{1,0:T(8,128)(2,1)}, u32[]{:S(2)}, u32[]{:S(2)}) collective-permute-start(bf16[128,1152]{1,0:T(8,128)(2,1)} %txt_feats.1), channel_id=1, source_target_pairs={{2,7},{1,6},{4,3},{7,2},{10,15},{9,14},{12,11},{15,10},{18,23},{17... | collective-permute-start | bytes 884744 | tf_op jit(solution)/shard_map/ppermute | solution.py:332
  5.9 2.5 %pick.1 = (bf16[128,1152]{1,0:T(8,128)(2,1)}, bf16[128,1152]{1,0:T(8,128)(2,1)}, bf16[352,1152]{1,0:T(8,128)(2,1)}, bf16[224,1152]{1,0:T(8,128)(2,1)}) custom-call(bf16[128,1152]{1,0:T(8,128)(2,1)} %img_feats.1, bf16[128,1152]{1,0:T(8,128)(2,1)} %txt_feats.1, bf16[576,1152]{1,0:T(8,128)(2,1)} %bitcast.2, bf16[576,1152]{1,0:T(8,128)(2,1)} %bitcast.3), custom_call_target="tpu_custom_call" | custom-call | bytes 5160960 | tf_op jit(solution)/shard_map/pick/pallas_call | solution.py:310
  8.4 0.1 collective-permute-start
  8.5 1.0 %collective-permute-start.4 = (bf16[352,1152]{1,0:T(8,128)(2,1)}, bf16[352,1152]{1,0:T(8,128)(2,1)S(1)}, u32[]{:S(2)}, u32[]{:S(2)}) collective-permute-start(bf16[352,1152]{1,0:T(8,128)(2,1)} %get-tuple-element.27.top), channel_id=1, source_target_pairs={{0,1},{2,3},{1,0},{3,2},{4,5},{6,7},{5,4},{7,6},{8,9},{10,11},{9,8... | collective-permute-start | bytes 2433032 | tf_op jit(solution)/shard_map/ppermute | solution.py:348
  9.5 2.9 %collective-permute-start.3 = (bf16[128,1152]{1,0:T(8,128)(2,1)}, bf16[128,1152]{1,0:T(8,128)(2,1)S(1)}, u32[]{:S(2)}, u32[]{:S(2)}) collective-permute-start(bf16[128,1152]{1,0:T(8,128)(2,1)} %get-tuple-element.30), channel_id=1, source_target_pairs={{0,64},{3,65},{6,68},{5,69},{8,72},{11,73},{14,76},{13,77},{16,80}... | collective-permute-start | bytes 884744 | tf_op jit(solution)/shard_map/ppermute | solution.py:351
  12.4 0.8 collective-permute-start.2
  13.2 0.0 collective-permute-done.6
  13.2 0.7 collective-permute-start.1
  13.9 0.0 collective-permute-done
  13.9 0.9 %collective-permute-start.5 = (bf16[224,1152]{1,0:T(8,128)(2,1)}, bf16[224,1152]{1,0:T(8,128)(2,1)S(1)}, u32[]{:S(2)}, u32[]{:S(2)}) collective-permute-start(bf16[224,1152]{1,0:T(8,128)(2,1)} %get-tuple-element.28.bottom), channel_id=1, source_target_pairs={{0,5},{2,7},{1,4},{3,6},{4,1},{6,3},{5,0},{7,2},{8,13},{10,15},{9,... | collective-permute-start | bytes 1548296 | tf_op jit(solution)/shard_map/ppermute | solution.py:349
  14.7 1.1 %select_select_fusion = (bf16[128,1152]{1,0:T(8,128)(2,1)S(1)}, bf16[128,1152]{1,0:T(8,128)(2,1)S(1)}) fusion(bf16[128,1152]{1,0:T(8,128)(2,1)} %collective-permute-done.6, bf16[128,1152]{1,0:T(8,128)(2,1)} %collective-permute-done, pred[]{:T(512)S(6)} %eq.20, pred[]{:T(512)S(6)} %eq.19, bf16[128,1152]{1,0:T(8,128)(2,1)S(1)} %copy-done.2, ...), kind=kLoop, calls=%fused_computation.1 | loop fusion | flops 589824 | bytes 1769476 | tf_op jit(solution)/shard_map/jit(_where)/select_n | solution.py:357
  15.9 1.2 %collective-permute-done.3.refs_3_ = bf16[128,1152]{1,0:T(8,128)(2,1)S(1)} collective-permute-done((bf16[128,1152]{1,0:T(8,128)(2,1)}, bf16[128,1152]{1,0:T(8,128)(2,1)S(1)}, u32[]{:S(2)}, u32[]{:S(2)}) %collective-permute-start.3) | collective-permute-done | bytes 294944 | tf_op jit(solution)/shard_map/ppermute | solution.py:351
  17.1 3.0 %collective-permute-start.9 = (bf16[128,1152]{1,0:T(8,128)(2,1)S(1)}, bf16[128,1152]{1,0:T(8,128)(2,1)S(1)}, u32[]{:S(2)}, u32[]{:S(2)}) collective-permute-start(bf16[128,1152]{1,0:T(8,128)(2,1)S(1)} %get-tuple-element.52.refs_0_.refs_3_), channel_id=1, source_target_pairs={{0,64},{2,18},{1,65},{3,19},{4,68},{6,22},{5,69},{7,23},{8,72},{10... | collective-permute-start | bytes 884744 | tf_op jit(solution)/shard_map/ppermute | solution.py:359
  20.0 0.6 collective-permute-done.2.refs_2_
  20.6 2.3 %collective-permute-start.8 = (bf16[128,1152]{1,0:T(8,128)(2,1)S(1)}, bf16[128,1152]{1,0:T(8,128)(2,1)S(1)}, u32[]{:S(2)}, u32[]{:S(2)}) collective-permute-start(bf16[128,1152]{1,0:T(8,128)(2,1)S(1)} %get-tuple-element.52.refs_0_.refs_3_), channel_id=1, source_target_pairs={{0,96},{2,26},{1,97},{3,27},{4,100},{6,30},{5,101},{7,31},{8,104},... | collective-permute-start | bytes 884744 | tf_op jit(solution)/shard_map/ppermute | solution.py:359
  23.0 2.4 %own_half.1 = (bf16[4,2,144,512]{3,2,1,0:T(8,128)(2,1)S(1)}, bf16[1152,576]{1,0:T(8,128)(2,1)S(1)}, bf16[512,576]{1,0:T(8,128)(2,1)S(1)}) custom-call(bf16[352,1152]{1,0:T(8,128)(2,1)S(1)} %copy-done, bf16[224,1152]{1,0:T(8,128)(2,1)S(1)} %copy-done.1, bf16[128,1152]{1,0:T(8,128)(2,1)S(1)} %get-tuple-element.53.refs_0_, ...), custom_call_target="tpu_custom_call" | custom-call | flops 679477248 | bytes 5603328 | tf_op jit(solution)/shard_map/own_half/pallas_call | solution.py:310
  25.4 1.3 %collective-permute-done.5.far_bottom = bf16[224,1152]{1,0:T(8,128)(2,1)S(1)} collective-permute-done((bf16[224,1152]{1,0:T(8,128)(2,1)}, bf16[224,1152]{1,0:T(8,128)(2,1)S(1)}, u32[]{:S(2)}, u32[]{:S(2)}) %collective-permute-start.5) | collective-permute-done | bytes 516128 | tf_op jit(solution)/shard_map/ppermute | solution.py:349
  26.7 1.3 %collective-permute-done.4.far_top = bf16[352,1152]{1,0:T(8,128)(2,1)S(1)} collective-permute-done((bf16[352,1152]{1,0:T(8,128)(2,1)}, bf16[352,1152]{1,0:T(8,128)(2,1)S(1)}, u32[]{:S(2)}, u32[]{:S(2)}) %collective-permute-start.4) | collective-permute-done | bytes 811040 | tf_op jit(solution)/shard_map/ppermute | solution.py:348
  28.0 1.8 %embed_first.1 = (bf16[512,1152]{1,0:T(8,128)(2,1)S(1)}, bf16[512,1152]{1,0:T(8,128)(2,1)S(1)}, bf16[1152,1152]{1,0:T(8,128)(2,1)S(1)}) custom-call(bf16[1152,576]{1,0:T(8,128)(2,1)S(1)} %get-tuple-element.32.turned, bf16[512,576]{1,0:T(8,128)(2,1)S(1)} %get-tuple-element.33.own_raw, bf16[352,1152]{1,0:T(8,128)(2,1)S(1)} %collective-permute-done.4.far_top, ...), custom_call_target="tpu_custom_call" | custom-call | flops 679477248 | bytes 9437184 | tf_op jit(solution)/shard_map/embed_first/pallas_call | solution.py:310
  29.8 1.6 %collective-permute-start.10 = (bf16[512,1152]{1,0:T(8,128)(2,1)S(1)}, bf16[512,1152]{1,0:T(8,128)(2,1)S(1)}, u32[]{:S(2)}, u32[]{:S(2)}) collective-permute-start(bf16[512,1152]{1,0:T(8,128)(2,1)S(1)} %get-tuple-element.34.refs_0_.emb_a), channel_id=1, source_target_pairs={{0,2},{2,0},{1,3},{3,1},{4,6},{6,4},{5,7},{7,5},{8,10},{10,8},{9,1... | collective-permute-start | bytes 3538952 | tf_op jit(solution)/shard_map/ppermute | solution.py:330
  31.3 2.1 %embed_second.1 = (bf16[512,1152]{1,0:T(8,128)(2,1)S(1)}, bf16[512,1152]{1,0:T(8,128)(2,1)S(1)}) custom-call(bf16[1152,1152]{1,0:T(8,128)(2,1)S(1)} %get-tuple-element.35.head_ref, bf16[128,1152]{1,0:T(8,128)(2,1)S(1)} %get-tuple-element.52.refs_0_.refs_3_, bf16[128,1152]{1,0:T(8,128)(2,1)S(1)} %collective-permute-done.7.refs_1_.refs_4_, ...), custom_call_target="tpu_custom_call" | custom-call | flops 1358954496 | bytes 6193152 | tf_op jit(solution)/shard_map/embed_second/pallas_call | solution.py:310
  33.5 2.2 %collective-permute-start.11 = (bf16[512,1152]{1,0:T(8,128)(2,1)S(1)}, bf16[512,1152]{1,0:T(8,128)(2,1)S(1)}, u32[]{:S(2)}, u32[]{:S(2)}) collective-permute-start(bf16[512,1152]{1,0:T(8,128)(2,1)S(1)} %get-tuple-element.36.refs_1_.emb_b), channel_id=1, source_target_pairs={{0,2},{2,0},{1,3},{3,1},{4,6},{6,4},{5,7},{7,5},{8,10},{10,8},{9,1... | collective-permute-start | bytes 3538952 | tf_op jit(solution)/shard_map/ppermute | solution.py:330
  35.6 0.0 collective-permute-done.10.refs_2_.far_a
  35.7 2.7 %score_first.1 = (bf16[512,512]{1,0:T(8,128)(2,1)S(1)}, bf16[512,512]{1,0:T(8,128)(2,1)S(1)}, bf16[4,2,144,512]{3,2,1,0:T(8,128)(2,1)S(1)}) custom-call(bf16[512,1152]{1,0:T(8,128)(2,1)S(1)} %get-tuple-element.34.refs_0_.emb_a, bf16[512,1152]{1,0:T(8,128)(2,1)S(1)} %get-tuple-element.36.refs_1_.emb_b, ...), custom_call_target="tpu_custom_call" | custom-call | flops 1207959552 | bytes 6946816 | tf_op jit(solution)/shard_map/score_first/pallas_call | solution.py:310
  38.3 0.0 collective-permute-done.11.far_b
  38.3 6.9 %score_second.1 = (bf16[512,1152]{1,0:T(8,128)(2,1)S(1)}, bf16[512,1152]{1,0:T(8,128)(2,1)S(1)}, bf16[144,1152]{1,0:T(8,128)(2,1)S(1)}, bf16[144,1152]{1,0:T(8,128)(2,1)S(1)}) custom-call(bf16[512,1152]{1,0:T(8,128)(2,1)S(1)} %get-tuple-element.34.refs_0_.emb_a, bf16[512,1152]{1,0:T(8,128)(2,1)S(1)} %get-tuple-element.36.refs_1_.emb_b, ...), custom_call_target="tpu_custom_call" | custom-call | flops 4303355904 | bytes 13508608 | tf_op jit(solution)/shard_map/score_second/pallas_call | solution.py:310
  45.2 3.6 %collective-permute-start.12 = (bf16[144,1152]{1,0:T(8,128)(2,1)S(1)}, bf16[144,1152]{1,0:T(8,128)(2,1)S(1)}, u32[]{:S(2)}, u32[]{:S(2)}) collective-permute-start(bf16[144,1152]{1,0:T(8,128)(2,1)S(1)} %get-tuple-element.45), channel_id=1, source_target_pairs={{0,65},{2,23},{1,64},{3,22},{4,69},{6,19},{5,68},{7,18},{8,73},{10... | collective-permute-start | bytes 995336 | tf_op jit(solution)/shard_map/ppermute | solution.py:416
  48.8 0.1 collective-permute-start.13
  48.9 1.1 %term_down.1 = (bf16[144,1152]{1,0:T(8,128)(2,1)S(1)}, bf16[144,1152]{1,0:T(8,128)(2,1)S(1)}) custom-call(bf16[4,2,144,512]{3,2,1,0:T(8,128)(2,1)S(1)} %get-tuple-element.31.flip_a.refs_0_, bf16[4,2,144,512]{3,2,1,0:T(8,128)(2,1)S(1)} %get-tuple-element.37.flip_b.refs_1_, bf16[512,1152]{1,0:T(8,128)(2,1)S(1)} %get-tuple-element.42.refs_2_, ...), custom_call_target="tpu_custom_call" | custom-call | flops 679477248 | bytes 5382144 | tf_op jit(solution)/shard_map/term_down/pallas_call | solution.py:310
  49.9 4.3 %collective-permute-start.16 = (bf16[144,1152]{1,0:T(8,128)(2,1)S(1)}, bf16[144,1152]{1,0:T(8,128)(2,1)S(1)}, u32[]{:S(2)}, u32[]{:S(2)}) collective-permute-start(bf16[144,1152]{1,0:T(8,128)(2,1)S(1)} %get-tuple-element.49), channel_id=1, source_target_pairs={{0,97},{2,31},{1,96},{3,30},{4,101},{6,27},{5,100},{7,26},{8,105},... | collective-permute-start | bytes 995336 | tf_op jit(solution)/shard_map/ppermute | solution.py:416
  54.3 0.5 collective-permute-start.17
  54.7 1.1 %term_up.1 = (bf16[144,1152]{1,0:T(8,128)(2,1)S(1)}, bf16[144,1152]{1,0:T(8,128)(2,1)S(1)}) custom-call(bf16[4,2,144,512]{3,2,1,0:T(8,128)(2,1)S(1)} %get-tuple-element.31.flip_a.refs_0_, bf16[4,2,144,512]{3,2,1,0:T(8,128)(2,1)S(1)} %get-tuple-element.37.flip_b.refs_1_, bf16[512,1152]{1,0:T(8,128)(2,1)S(1)} %get-tuple-element.42.refs_2_, ...), custom_call_target="tpu_custom_call" | custom-call | flops 679477248 | bytes 5382144 | tf_op jit(solution)/shard_map/term_up/pallas_call | solution.py:310
  55.8 1.6 %collective-permute-start.14 = (bf16[144,1152]{1,0:T(8,128)(2,1)S(1)}, bf16[144,1152]{1,0:T(8,128)(2,1)S(1)}, u32[]{:S(2)}, u32[]{:S(2)}) collective-permute-start(bf16[144,1152]{1,0:T(8,128)(2,1)S(1)} %get-tuple-element.47), channel_id=1, source_target_pairs={{0,33},{2,15},{1,32},{3,14},{4,37},{6,11},{5,36},{7,10},{8,41},{10... | collective-permute-start | bytes 995336 | tf_op jit(solution)/shard_map/ppermute | solution.py:416
  57.4 1.1 %term_own.1 = (bf16[144,1152]{1,0:T(8,128)(2,1)S(1)}, bf16[144,1152]{1,0:T(8,128)(2,1)S(1)}) custom-call(bf16[4,2,144,512]{3,2,1,0:T(8,128)(2,1)S(1)} %get-tuple-element.31.flip_a.refs_0_, bf16[4,2,144,512]{3,2,1,0:T(8,128)(2,1)S(1)} %get-tuple-element.37.flip_b.refs_1_, bf16[512,1152]{1,0:T(8,128)(2,1)S(1)} %get-tuple-element.42.refs_2_, ...), custom_call_target="tpu_custom_call" | custom-call | flops 679477248 | bytes 5382144 | tf_op jit(solution)/shard_map/term_own/pallas_call | solution.py:310
  58.5 0.1 collective-permute-start.15
  58.6 1.9 %collective-permute-start.18 = (bf16[144,1152]{1,0:T(8,128)(2,1)S(1)}, bf16[144,1152]{1,0:T(8,128)(2,1)S(1)}, u32[]{:S(2)}, u32[]{:S(2)}) collective-permute-start(bf16[144,1152]{1,0:T(8,128)(2,1)S(1)} %get-tuple-element.51), channel_id=1, source_target_pairs={{0,1},{2,7},{1,0},{3,6},{4,5},{6,3},{5,4},{7,2},{8,9},{10,15},{9,8... | collective-permute-start | bytes 995336 | tf_op jit(solution)/shard_map/ppermute | solution.py:424
  60.5 0.1 add_far.1.refs_0_
  60.6 0.0 collective-permute-done.16.refs_3_
  60.6 5.8 %collective-permute-done.17.refs_4_ = bf16[144,1152]{1,0:T(8,128)(2,1)S(1)} collective-permute-done((bf16[144,1152]{1,0:T(8,128)(2,1)S(1)}, bf16[144,1152]{1,0:T(8,128)(2,1)S(1)}, u32[]{:S(2)}, u32[]{:S(2)}) %collective-permute-start.17) | collective-permute-done | bytes 331808 | tf_op jit(solution)/shard_map/ppermute | solution.py:416
  66.4 2.3 %collective-permute-done.15.refs_2_ = bf16[144,1152]{1,0:T(8,128)(2,1)S(1)} collective-permute-done((bf16[144,1152]{1,0:T(8,128)(2,1)S(1)}, bf16[144,1152]{1,0:T(8,128)(2,1)S(1)}, u32[]{:S(2)}, u32[]{:S(2)}) %collective-permute-start.15) | collective-permute-done | bytes 331808 | tf_op jit(solution)/shard_map/ppermute | solution.py:416
  68.7 0.0 collective-permute-done.18.refs_5_
  68.7 0.3 sum_terms.1
  69.0 10.1 %all_to_all.5 = bf16[8,18,1152]{2,1,0:T(8,128)(2,1)S(1)} all-to-all(bf16[8,18,1152]{2,1,0:T(8,128)(2,1)S(1)} %sum_terms.1), channel_id=1, replica_groups={{0,5,8,13,16,21,24,29},{1,4,9,12,17,20,25,28},{32,37,40,45,48,53,56,61}..., dimensions={0} | all-to-all | bytes 663552 | tf_op jit(solution)/shard_map/all_to_all | solution.py:429
  79.2 0.1 convert_reduce_fusion
  79.2 0.1 slice_select_fusion
  79.3 3.3 %collective-permute-start.19 = (f32[18,576]{1,0:T(8,128)S(1)}, f32[18,576]{1,0:T(8,128)S(1)}, u32[]{:S(2)}, u32[]{:S(2)}) collective-permute-start(f32[18,576]{1,0:T(8,128)S(1)} %slice_select_fusion), channel_id=1, source_target_pairs={{0,2},{2,0},{1,3},{3,1},{4,6},{6,4},{5,7},{7,5},{8,10},{10,8},{9,1... | collective-permute-start | bytes 124424 | tf_op jit(solution)/shard_map/ppermute | solution.py:330
  82.6 0.9 %collective-permute-done.19 = f32[18,576]{1,0:T(8,128)S(1)} collective-permute-done((f32[18,576]{1,0:T(8,128)S(1)}, f32[18,576]{1,0:T(8,128)S(1)}, u32[]{:S(2)}, u32[]{:S(2)}) %collective-permute-start.19) | collective-permute-done | bytes 41504 | tf_op jit(solution)/shard_map/ppermute | solution.py:330
  83.5 0.7 broadcast_select_fusion.2
  (16 shorter events, 0.0 us)
Async XLA Ops:
  0.6 12.6 %collective-permute-start.6 = (bf16[128,1152]{1,0:T(8,128)(2,1)}, bf16[128,1152]{1,0:T(8,128)(2,1)}, u32[]{:S(2)}, u32[]{:S(2)}) collective-permute-start(bf16[128,1152]{1,0:T(8,128)(2,1)} %txt_feats.1), channel_id=1, source_target_pairs={{2,7},{1,6},{4,3},{7,2},{10,15},{9,14},{12,11},{15,10},{18,23},{17... | collective-permute-start | bytes 884744 | tf_op jit(solution)/shard_map/ppermute | solution.py:332
  5.9 8.9 %copy-start.2 = (bf16[128,1152]{1,0:T(8,128)(2,1)S(1)}, bf16[128,1152]{1,0:T(8,128)(2,1)}, u32[]{:S(2)}) copy-start(bf16[128,1152]{1,0:T(8,128)(2,1)} %img_feats.1) | copy-start | bytes 884740
  5.9 8.9 %copy-start.3 = (bf16[128,1152]{1,0:T(8,128)(2,1)S(1)}, bf16[128,1152]{1,0:T(8,128)(2,1)}, u32[]{:S(2)}) copy-start(bf16[128,1152]{1,0:T(8,128)(2,1)} %txt_feats.1) | copy-start | bytes 884740
  8.4 14.6 %copy-start = (bf16[352,1152]{1,0:T(8,128)(2,1)S(1)}, bf16[352,1152]{1,0:T(8,128)(2,1)}, u32[]{:S(2)}) copy-start(bf16[352,1152]{1,0:T(8,128)(2,1)} %get-tuple-element.27.top) | copy-start | bytes 2433028
  8.4 14.6 %copy-start.1 = (bf16[224,1152]{1,0:T(8,128)(2,1)S(1)}, bf16[224,1152]{1,0:T(8,128)(2,1)}, u32[]{:S(2)}) copy-start(bf16[224,1152]{1,0:T(8,128)(2,1)} %get-tuple-element.28.bottom) | copy-start | bytes 1548292
  8.4 5.5 %collective-permute-start = (bf16[128,1152]{1,0:T(8,128)(2,1)}, bf16[128,1152]{1,0:T(8,128)(2,1)}, u32[]{:S(2)}, u32[]{:S(2)}) collective-permute-start(bf16[128,1152]{1,0:T(8,128)(2,1)} %get-tuple-element.29), channel_id=1, source_target_pairs={{0,2},{2,0},{1,3},{3,1},{4,6},{6,4},{5,7},{7,5},{8,10},{10,8},{9,1... | collective-permute-start | bytes 884744 | tf_op jit(solution)/shard_map/ppermute | solution.py:330
  8.5 19.5 %collective-permute-start.4 = (bf16[352,1152]{1,0:T(8,128)(2,1)}, bf16[352,1152]{1,0:T(8,128)(2,1)S(1)}, u32[]{:S(2)}, u32[]{:S(2)}) collective-permute-start(bf16[352,1152]{1,0:T(8,128)(2,1)} %get-tuple-element.27.top), channel_id=1, source_target_pairs={{0,1},{2,3},{1,0},{3,2},{4,5},{6,7},{5,4},{7,6},{8,9},{10,11},{9,8... | collective-permute-start | bytes 2433032 | tf_op jit(solution)/shard_map/ppermute | solution.py:348
  9.5 7.6 %collective-permute-start.3 = (bf16[128,1152]{1,0:T(8,128)(2,1)}, bf16[128,1152]{1,0:T(8,128)(2,1)S(1)}, u32[]{:S(2)}, u32[]{:S(2)}) collective-permute-start(bf16[128,1152]{1,0:T(8,128)(2,1)} %get-tuple-element.30), channel_id=1, source_target_pairs={{0,64},{3,65},{6,68},{5,69},{8,72},{11,73},{14,76},{13,77},{16,80}... | collective-permute-start | bytes 884744 | tf_op jit(solution)/shard_map/ppermute | solution.py:351
  12.4 8.2 %collective-permute-start.2 = (bf16[128,1152]{1,0:T(8,128)(2,1)}, bf16[128,1152]{1,0:T(8,128)(2,1)S(1)}, u32[]{:S(2)}, u32[]{:S(2)}) collective-permute-start(bf16[128,1152]{1,0:T(8,128)(2,1)} %get-tuple-element.30), channel_id=1, source_target_pairs={{0,96},{3,97},{6,100},{5,101},{8,104},{11,105},{14,108},{13,109},{... | collective-permute-start | bytes 884744 | tf_op jit(solution)/shard_map/ppermute | solution.py:351
  13.2 9.8 %collective-permute-start.1 = (bf16[128,1152]{1,0:T(8,128)(2,1)}, bf16[128,1152]{1,0:T(8,128)(2,1)S(1)}, u32[]{:S(2)}, u32[]{:S(2)}) collective-permute-start(bf16[128,1152]{1,0:T(8,128)(2,1)} %get-tuple-element.30), channel_id=1, source_target_pairs={{0,32},{3,33},{6,36},{5,37},{8,40},{11,41},{14,44},{13,45},{16,48}... | collective-permute-start | bytes 884744 | tf_op jit(solution)/shard_map/ppermute | solution.py:351
  13.9 12.8 %collective-permute-start.5 = (bf16[224,1152]{1,0:T(8,128)(2,1)}, bf16[224,1152]{1,0:T(8,128)(2,1)S(1)}, u32[]{:S(2)}, u32[]{:S(2)}) collective-permute-start(bf16[224,1152]{1,0:T(8,128)(2,1)} %get-tuple-element.28.bottom), channel_id=1, source_target_pairs={{0,5},{2,7},{1,4},{3,6},{4,1},{6,3},{5,0},{7,2},{8,13},{10,15},{9,... | collective-permute-start | bytes 1548296 | tf_op jit(solution)/shard_map/ppermute | solution.py:349
  17.1 14.2 %collective-permute-start.9 = (bf16[128,1152]{1,0:T(8,128)(2,1)S(1)}, bf16[128,1152]{1,0:T(8,128)(2,1)S(1)}, u32[]{:S(2)}, u32[]{:S(2)}) collective-permute-start(bf16[128,1152]{1,0:T(8,128)(2,1)S(1)} %get-tuple-element.52.refs_0_.refs_3_), channel_id=1, source_target_pairs={{0,64},{2,18},{1,65},{3,19},{4,68},{6,22},{5,69},{7,23},{8,72},{10... | collective-permute-start | bytes 884744 | tf_op jit(solution)/shard_map/ppermute | solution.py:359
  20.6 10.7 %collective-permute-start.8 = (bf16[128,1152]{1,0:T(8,128)(2,1)S(1)}, bf16[128,1152]{1,0:T(8,128)(2,1)S(1)}, u32[]{:S(2)}, u32[]{:S(2)}) collective-permute-start(bf16[128,1152]{1,0:T(8,128)(2,1)S(1)} %get-tuple-element.52.refs_0_.refs_3_), channel_id=1, source_target_pairs={{0,96},{2,26},{1,97},{3,27},{4,100},{6,30},{5,101},{7,31},{8,104},... | collective-permute-start | bytes 884744 | tf_op jit(solution)/shard_map/ppermute | solution.py:359
  23.0 8.3 %collective-permute-start.7 = (bf16[128,1152]{1,0:T(8,128)(2,1)S(1)}, bf16[128,1152]{1,0:T(8,128)(2,1)S(1)}, u32[]{:S(2)}, u32[]{:S(2)}) collective-permute-start(bf16[128,1152]{1,0:T(8,128)(2,1)S(1)} %get-tuple-element.52.refs_0_.refs_3_), channel_id=1, source_target_pairs={{0,32},{2,10},{1,33},{3,11},{4,36},{6,14},{5,37},{7,15},{8,40},{10... | collective-permute-start | bytes 884744 | tf_op jit(solution)/shard_map/ppermute | solution.py:359
  29.8 5.9 %collective-permute-start.10 = (bf16[512,1152]{1,0:T(8,128)(2,1)S(1)}, bf16[512,1152]{1,0:T(8,128)(2,1)S(1)}, u32[]{:S(2)}, u32[]{:S(2)}) collective-permute-start(bf16[512,1152]{1,0:T(8,128)(2,1)S(1)} %get-tuple-element.34.refs_0_.emb_a), channel_id=1, source_target_pairs={{0,2},{2,0},{1,3},{3,1},{4,6},{6,4},{5,7},{7,5},{8,10},{10,8},{9,1... | collective-permute-start | bytes 3538952 | tf_op jit(solution)/shard_map/ppermute | solution.py:330
  33.5 4.9 %collective-permute-start.11 = (bf16[512,1152]{1,0:T(8,128)(2,1)S(1)}, bf16[512,1152]{1,0:T(8,128)(2,1)S(1)}, u32[]{:S(2)}, u32[]{:S(2)}) collective-permute-start(bf16[512,1152]{1,0:T(8,128)(2,1)S(1)} %get-tuple-element.36.refs_1_.emb_b), channel_id=1, source_target_pairs={{0,2},{2,0},{1,3},{3,1},{4,6},{6,4},{5,7},{7,5},{8,10},{10,8},{9,1... | collective-permute-start | bytes 3538952 | tf_op jit(solution)/shard_map/ppermute | solution.py:330
  45.2 13.3 %collective-permute-start.12 = (bf16[144,1152]{1,0:T(8,128)(2,1)S(1)}, bf16[144,1152]{1,0:T(8,128)(2,1)S(1)}, u32[]{:S(2)}, u32[]{:S(2)}) collective-permute-start(bf16[144,1152]{1,0:T(8,128)(2,1)S(1)} %get-tuple-element.45), channel_id=1, source_target_pairs={{0,65},{2,23},{1,64},{3,22},{4,69},{6,19},{5,68},{7,18},{8,73},{10... | collective-permute-start | bytes 995336 | tf_op jit(solution)/shard_map/ppermute | solution.py:416
  48.8 9.8 %collective-permute-start.13 = (bf16[144,1152]{1,0:T(8,128)(2,1)S(1)}, bf16[144,1152]{1,0:T(8,128)(2,1)S(1)}, u32[]{:S(2)}, u32[]{:S(2)}) collective-permute-start(bf16[144,1152]{1,0:T(8,128)(2,1)S(1)} %get-tuple-element.46), channel_id=1, source_target_pairs={{0,64},{2,18},{1,65},{3,19},{4,68},{6,22},{5,69},{7,23},{8,72},{10... | collective-permute-start | bytes 995336 | tf_op jit(solution)/shard_map/ppermute | solution.py:416
  49.9 10.7 %collective-permute-start.16 = (bf16[144,1152]{1,0:T(8,128)(2,1)S(1)}, bf16[144,1152]{1,0:T(8,128)(2,1)S(1)}, u32[]{:S(2)}, u32[]{:S(2)}) collective-permute-start(bf16[144,1152]{1,0:T(8,128)(2,1)S(1)} %get-tuple-element.49), channel_id=1, source_target_pairs={{0,97},{2,31},{1,96},{3,30},{4,101},{6,27},{5,100},{7,26},{8,105},... | collective-permute-start | bytes 995336 | tf_op jit(solution)/shard_map/ppermute | solution.py:416
  54.3 12.1 %collective-permute-start.17 = (bf16[144,1152]{1,0:T(8,128)(2,1)S(1)}, bf16[144,1152]{1,0:T(8,128)(2,1)S(1)}, u32[]{:S(2)}, u32[]{:S(2)}) collective-permute-start(bf16[144,1152]{1,0:T(8,128)(2,1)S(1)} %get-tuple-element.50), channel_id=1, source_target_pairs={{0,96},{2,26},{1,97},{3,27},{4,100},{6,30},{5,101},{7,31},{8,104},... | collective-permute-start | bytes 995336 | tf_op jit(solution)/shard_map/ppermute | solution.py:416
  55.8 10.6 %collective-permute-start.14 = (bf16[144,1152]{1,0:T(8,128)(2,1)S(1)}, bf16[144,1152]{1,0:T(8,128)(2,1)S(1)}, u32[]{:S(2)}, u32[]{:S(2)}) collective-permute-start(bf16[144,1152]{1,0:T(8,128)(2,1)S(1)} %get-tuple-element.47), channel_id=1, source_target_pairs={{0,33},{2,15},{1,32},{3,14},{4,37},{6,11},{5,36},{7,10},{8,41},{10... | collective-permute-start | bytes 995336 | tf_op jit(solution)/shard_map/ppermute | solution.py:416
  58.5 10.2 %collective-permute-start.15 = (bf16[144,1152]{1,0:T(8,128)(2,1)S(1)}, bf16[144,1152]{1,0:T(8,128)(2,1)S(1)}, u32[]{:S(2)}, u32[]{:S(2)}) collective-permute-start(bf16[144,1152]{1,0:T(8,128)(2,1)S(1)} %get-tuple-element.48), channel_id=1, source_target_pairs={{0,32},{2,10},{1,33},{3,11},{4,36},{6,14},{5,37},{7,15},{8,40},{10... | collective-permute-start | bytes 995336 | tf_op jit(solution)/shard_map/ppermute | solution.py:416
  58.6 10.1 %collective-permute-start.18 = (bf16[144,1152]{1,0:T(8,128)(2,1)S(1)}, bf16[144,1152]{1,0:T(8,128)(2,1)S(1)}, u32[]{:S(2)}, u32[]{:S(2)}) collective-permute-start(bf16[144,1152]{1,0:T(8,128)(2,1)S(1)} %get-tuple-element.51), channel_id=1, source_target_pairs={{0,1},{2,7},{1,0},{3,6},{4,5},{6,3},{5,4},{7,2},{8,9},{10,15},{9,8... | collective-permute-start | bytes 995336 | tf_op jit(solution)/shard_map/ppermute | solution.py:424
  79.3 4.2 %collective-permute-start.19 = (f32[18,576]{1,0:T(8,128)S(1)}, f32[18,576]{1,0:T(8,128)S(1)}, u32[]{:S(2)}, u32[]{:S(2)}) collective-permute-start(f32[18,576]{1,0:T(8,128)S(1)} %slice_select_fusion), channel_id=1, source_target_pairs={{0,2},{2,0},{1,3},{3,1},{4,6},{6,4},{5,7},{7,5},{8,10},{10,8},{9,1... | collective-permute-start | bytes 124424 | tf_op jit(solution)/shard_map/ppermute | solution.py:330
